TPU v7x, 32 devices: a whole 2x2x4 slice. The times are simulated.
32 devices in a mesh: parts: 2 (over x), il: 8 (over z, y), xl: 2 (over core).
Axes of the slice: x: 2, y: 2, z: 4, core: 2. Of those that a mesh axis runs over, the one named last changes fastest.
Arguments:
- volume: bfloat16 [18, 2048, 512], P(None, ('parts', 'il'), 'xl'), parts along dimension 1, may hold values from -8 to 8
Outputs:
- inline_dip: float32 [16, 2048, 512], P(None, ('parts', 'il'), 'xl'), parts along dimension 1
- cross_dip: float32 [16, 2048, 512], P(None, ('parts', 'il'), 'xl'), parts along dimension 1
- planarity: float32 [16, 2048, 512], P(None, ('parts', 'il'), 'xl'), parts along dimension 1
There are 2 independent parts, one for each index of `parts`. A program takes and returns all parts, laid end to end along the dimension named above; each array names one. Nothing has to cross between parts.
All inputs are finite; a program needn't handle non-finite values.
Results may differ from a plain program's by a relative error of at most 0.0021.
Values may be sent and summed in bfloat16 or wider, within the bound.
No kernel may reach another device: no remote copies, remote signals or barrier semaphores. Data moves between devices by JAX's collectives and lax.ppermute only.
A program may use at most 64 MiB of HBM per device.

v0:
```python
import jax
import jax.numpy as jnp
from jax import lax
from jax.sharding import PartitionSpec as P

RADIUS = 9


def padded_2(block, sides, width):
    for axis, dim in sides:
        count = lax.axis_size(axis)
        forward = [(i, i + 1) for i in range(count - 1)]
        backward = [(target, source) for source, target in forward]
        low = lax.ppermute(
            lax.slice_in_dim(block, block.shape[dim] - width, None, axis=dim), axis, forward
        )
        high = lax.ppermute(lax.slice_in_dim(block, 0, width, axis=dim), axis, backward)
        block = jnp.concatenate([low, block, high], axis=dim)
    return block


def band_matrix(window, count):
    rowplace = lax.broadcasted_iota(jnp.int32, (window, count), 0)
    colplace = lax.broadcasted_iota(jnp.int32, (window, count), 1)
    offset = (rowplace - colplace).astype(jnp.float32)
    sigma = RADIUS / 3.0
    offsets = jnp.arange(2 * RADIUS + 1).astype(jnp.float32)
    total = jnp.sum(jnp.exp(-0.5 * ((offsets - RADIUS) / sigma) ** 2))
    weights = jnp.exp(-0.5 * ((offset - RADIUS) / sigma) ** 2) / total
    inside = (rowplace >= colplace) & (rowplace <= colplace + 2 * RADIUS)
    return jnp.where(inside, weights, 0.0).astype(jnp.bfloat16)


def smooth_rows(padded):
    length = padded.shape[2] - 2 * RADIUS
    blocks = length // 128
    extended = jnp.pad(padded, ((0, 0), (0, 0), (0, 128 - 2 * RADIUS), (0, 0)))
    shaped = extended.reshape(padded.shape[0], padded.shape[1], blocks + 1, 128, padded.shape[3])
    windows = jnp.concatenate([shaped[:, :, :blocks], shaped[:, :, 1:, : 2 * RADIUS]], axis=3)
    result = jnp.einsum(
        "kdnjb,jo->kdnob",
        windows,
        band_matrix(128 + 2 * RADIUS, 128),
        preferred_element_type=jnp.float32,
    )
    return result.reshape(padded.shape[0], padded.shape[1], length, padded.shape[3])


def smooth_columns(padded):
    length = padded.shape[3] - 2 * RADIUS
    blocks = length // 128
    extended = jnp.pad(padded, ((0, 0), (0, 0), (0, 0), (0, 128 - 2 * RADIUS)))
    shaped = extended.reshape(padded.shape[0], padded.shape[1], padded.shape[2], blocks + 1, 128)
    windows = jnp.concatenate([shaped[:, :, :, :blocks], shaped[:, :, :, 1:, : 2 * RADIUS]], axis=4)
    result = jnp.einsum(
        "kdanj,jo->kdano",
        windows,
        band_matrix(128 + 2 * RADIUS, 128),
        preferred_element_type=jnp.float32,
    )
    return result.reshape(padded.shape[0], padded.shape[1], padded.shape[2], length)


def attributes(tensor):
    comp_a, comp_b, comp_c, comp_d, comp_e, comp_f = [tensor[index] for index in range(6)]
    inline_dip = -comp_e / (comp_c + 1e-06)
    cross_dip = -comp_f / (comp_c + 1e-06)
    spread = 0.5 * ((comp_a - comp_b) ** 2 + (comp_b - comp_c) ** 2 + (comp_c - comp_a) ** 2)
    spread = spread + 3.0 * (comp_d * comp_d + comp_e * comp_e + comp_f * comp_f)
    planarity = jnp.sqrt(spread) / (comp_a + comp_b + comp_c + 1e-06)
    return jnp.stack([inline_dip, cross_dip, planarity])


def moment_terms(padded):
    centre = padded[1:-1]
    grad_i = 0.5 * (
        centre[:, 2:, 1:-1].astype(jnp.float32) - centre[:, :-2, 1:-1].astype(jnp.float32)
    )
    grad_x = 0.5 * (
        centre[:, 1:-1, 2:].astype(jnp.float32) - centre[:, 1:-1, :-2].astype(jnp.float32)
    )
    grad_z = 0.5 * (
        padded[2:, 1:-1, 1:-1].astype(jnp.float32) - padded[:-2, 1:-1, 1:-1].astype(jnp.float32)
    )
    return jnp.stack(
        [
            grad_i * grad_i,
            grad_x * grad_x,
            grad_z * grad_z,
            grad_i * grad_x,
            grad_i * grad_z,
            grad_x * grad_z,
        ]
    )


def inline_pass(pieces):
    padded = jnp.pad(pieces, ((0, 0), (0, 0), (RADIUS, RADIUS), (0, 0)))
    smoothed = smooth_rows(padded).astype(jnp.bfloat16)
    return lax.all_to_all(smoothed, "il", split_axis=2, concat_axis=1, tiled=True)


def cross_pass(pieces):
    padded = jnp.pad(pieces, ((0, 0), (0, 0), (0, 0), (RADIUS, RADIUS)))
    results = attributes(smooth_columns(padded))
    return lax.all_to_all(results, "xl", split_axis=3, concat_axis=1, tiled=True)


def body(volume):
    padded = padded_2(volume, (("il", 1), ("xl", 2)), 1)
    products = moment_terms(padded)
    moments = products.astype(jnp.bfloat16)
    lined = inline_pass(lax.all_to_all(moments, "il", split_axis=1, concat_axis=2, tiled=True))
    results = cross_pass(lax.all_to_all(lined, "xl", split_axis=1, concat_axis=3, tiled=True))
    return (results[0], results[1], results[2])


def solution(mesh):
    placed = (P(None, ("parts", "il"), "xl"),)
    return jax.shard_map(
        body,
        mesh=mesh,
        in_specs=placed,
        out_specs=(
            P(None, ("parts", "il"), "xl"),
            P(None, ("parts", "il"), "xl"),
            P(None, ("parts", "il"), "xl"),
        ),
        check_vma=False,
    )
```

profile of v0, /device:TPU:0, one launch (start us, length us, event | category | flops | bytes accessed | tf_op | source)
XLA Modules:
  0.0 443.5 jit_solution(9486976443787063022)
XLA Ops:
  1.6 4.9 %collective-permute-start.1 = (bf16[18,1,256]{2,0,1:T(8,128)(2,1)S(1)}, bf16[18,1,256]{2,0,1:T(8,128)(2,1)S(1)}, u32[]{:S(2)}, u32[]{:S(2)}) collective-permute-start(bf16[18,1,256]{2,0,1:T(8,128)(2,1)S(1)} %copy.154), channel_id=1, source_target_pairs={{0,2},{2,4},{4,6},{6,8},{8,10},{10,12},{12,14},{1,3},{3,5},{5,7},{... | collective-permute-start | bytes 27656 | tf_op jit(solution)/shard_map/ppermute | solution.py:14
  6.5 1.3 collective-permute-start
  7.8 1.9 copy.117
  10.7 1.4 collective-permute-done
  12.1 1.7 copy.118
  16.0 1.3 collective-permute-start.2
  17.3 3.1 fusion.17
  20.4 5.8 %fusion.19 = (bf16[6,16,128,256]{2,1,3,0:T(8,128)(2,1)}, bf16[16,128,256]{1,0,2:T(8,128)(2,1)S(1)}, bf16[16,128,256]{1,0,2:T(8,128)(2,1)S(1)}) fusion(bf16[6,16,128,256]{2,1,3,0:T(8,128)(2,1)} %get-tuple-element.6, bf16[18,130,1]{1,0,2:T(8,128)(2,1)S(1)} %collective-permute-done.2, bf16[18,1,256]{1,0,2:T(8,128)(2,1)S(1)} %copy-done, ...), kind=kLoop, calls=%fused_computation.34 | loop fusion | flops 11534336 | bytes 4353168
  26.2 1.7 fusion.21
  27.9 1.6 fusion.23
  29.5 1.9 fusion.25
  31.4 1.9 fusion.27
  33.4 9.0 %copy.127 = bf16[6,16,128,256]{3,2,0,1:T(8,128)(2,1)} copy(bf16[6,16,128,256]{2,1,3,0:T(8,128)(2,1)} %fusion.27) | data formatting | bytes 12582912 | tf_op jit(solution)/shard_map/stack | solution.py:85
  42.4 5.7 %all-to-all-start = ((bf16[6,16,128,256]{3,2,0,1:T(8,128)(2,1)}), bf16[6,16,128,256]{3,2,0,1:T(8,128)(2,1)}, u32[]{:S(2)}, u32[]{:S(2)}) async-start(bf16[6,16,128,256]{3,2,0,1:T(8,128)(2,1)} %copy.127), calls=%async_computation | async-start | bytes 12582912 | tf_op jit(solution)/shard_map/all_to_all | solution.py:113
  48.7 139.1 %all-to-all-done = bf16[6,16,128,256]{3,2,0,1:T(8,128)(2,1)} async-done(((bf16[6,16,128,256]{3,2,0,1:T(8,128)(2,1)}), bf16[6,16,128,256]{3,2,0,1:T(8,128)(2,1)}, u32[]{:S(2)}, u32[]{:S(2)}) %all-to-all-start) | async-done | bytes 6291488 | tf_op jit(solution)/shard_map/all_to_all | solution.py:113
  187.9 3.5 copy.128
  191.4 1.7 pad.60
  194.1 2.9 fusion.8
  197.0 31.9 %copy.129 = bf16[6,2,1024,256]{3,1,0,2:T(2,128)(2,1)S(1)} copy(bf16[6,2,1024,256]{3,2,1,0:T(8,128)(2,1)S(1)} %bitcast.64) | data formatting | bytes 12582912 | tf_op jit(solution)/shard_map/convert_element_type | solution.py:99
  228.8 141.6 %all_to_all.69 = bf16[6,2,1024,256]{3,1,0,2:T(2,128)(2,1)S(1)} all-to-all(bf16[6,2,1024,256]{3,1,0,2:T(2,128)(2,1)S(1)} %copy.129), channel_id=1, replica_groups=mesh['parts'=2,'il'=8,'xl'=2] {'il'}, dimensions={2} | all-to-all | bytes 12582912 | tf_op jit(solution)/shard_map/all_to_all | solution.py:100
  372.9 9.9 %all_to_all.70 = bf16[6,16,128,256]{3,2,0,1:T(8,128)(2,1)} all-to-all(bf16[6,16,128,256]{3,2,0,1:T(8,128)(2,1)S(1)} %copy.132), channel_id=1, replica_groups=mesh['parts'=2,'il'=8,'xl'=2] {'xl'}, dimensions={1} | all-to-all | bytes 12582912 | tf_op jit(solution)/shard_map/all_to_all | solution.py:114
  382.9 8.6 %copy.134 = bf16[6,8,128,2,256]{2,4,3,1,0:T(8,128)(2,1)} copy(bf16[6,8,128,2,256]{4,2,0,1,3:T(8,128)(2,1)} %bitcast.68) | data formatting | bytes 12582912 | tf_op jit(solution)/shard_map/all_to_all | solution.py:114
  391.5 5.4 %pad.61 = bf16[6,8,128,640]{2,3,1,0:T(8,128)(2,1)S(1)} pad(bf16[6,8,128,512]{2,3,1,0:T(8,128)(2,1)} %bitcast.65, bf16[]{:T(256)} %constant.7.clone.1), padding=0_0x0_0x0_0x9_119 | pad | bytes 14155778 | tf_op jit(solution)/shard_map/jit(_pad)/pad | solution.py:52
  397.2 1.4 slice.116
  398.5 6.2 %fusion.4 = f32[6,8,128,4,128]{2,4,3,1,0:T(8,128)} fusion(bf16[6,8,128,4,18]{2,4,3,1,0:T(8,128)(2,1)S(1)} %slice.117, bf16[6,8,128,4,128]{2,4,3,1,0:T(8,128)(2,1)S(1)} %slice.116, f32[]{:T(128)} %exponential_reduce_fusion, s32[128]{0:T(128)S(1)} %iota_add_fusion), kind=kOutput, calls=%fused_computation.4 | convolution fusion | flops 933129216 | bytes 19759620 | tf_op jit(solution)/shard_map/kdanj,jo->kdano/dot_general | solution.py:55
  404.8 8.6 %slice_negate_fusion.1 = (f32[1,8,128,4,128]{2,4,3,1,0:T(8,128)S(1)}, f32[1,8,128,4,128]{2,4,3,1,0:T(8,128)S(1)}, f32[1,8,128,4,128]{2,4,3,1,0:T(8,128)S(1)}, f3...) fusion(f32[6,8,128,4,128]{2,4,3,1,0:T(8,128)} %fusion.4), kind=kLoop, calls=%fused_computation.29 | loop fusion | flops 4194304 | bytes 25165824 | tf_op jit(solution)/shard_map/neg | solution.py:66
  413.4 10.9 %copy_divide_fusion.1 = (f32[1,8,128,512]{2,1,0,3:T(8,128)S(1)}, f32[1,8,128,512]{2,1,0,3:T(8,128)S(1)}, f32[1,8,128,512]{2,1,0,3:T(8,128)S(1)}) fusion(f32[1,8,128,512]{2,3,1,0:T(8,128)S(1)} %bitcast.70, f32[1,8,128,512]{2,3,1,0:T(8,128)} %bitcast.75, f32[1,8,128,512]{2,3,1,0:T(8,128)} %bitcast.74, f32[1,8,128,512]{2,3,1,0:T(8,128)S(1)} %bitcast.71, ...), kind=kLoop, calls=%fused_computation.18 | loop fusion | flops 8912896 | bytes 18874368 | tf_op jit(solution)/shard_map/div | solution.py:66
  424.8 8.8 %all_to_all.71 = f32[3,8,128,512]{2,1,0,3:T(8,128)S(1)} all-to-all(f32[3,8,128,512]{2,1,0,3:T(8,128)S(1)} %pad_maximum_fusion), channel_id=1, replica_groups=mesh['parts'=2,'il'=8,'xl'=2] {'xl'}, dimensions={3} | all-to-all | bytes 12582912 | tf_op jit(solution)/shard_map/all_to_all | solution.py:106
  433.5 2.4 fusion.48
  436.0 2.9 copy.150
  438.8 2.9 copy.149
  441.7 1.8 copy.148
  (20 shorter events, 8.9 us)
Async XLA Ops:
  1.6 8.1 %collective-permute-start.1 = (bf16[18,1,256]{2,0,1:T(8,128)(2,1)S(1)}, bf16[18,1,256]{2,0,1:T(8,128)(2,1)S(1)}, u32[]{:S(2)}, u32[]{:S(2)}) collective-permute-start(bf16[18,1,256]{2,0,1:T(8,128)(2,1)S(1)} %copy.154), channel_id=1, source_target_pairs={{0,2},{2,4},{4,6},{6,8},{8,10},{10,12},{12,14},{1,3},{3,5},{5,7},{... | collective-permute-start | bytes 27656 | tf_op jit(solution)/shard_map/ppermute | solution.py:14
  6.5 5.6 %collective-permute-start = (bf16[18,1,256]{2,0,1:T(8,128)(2,1)S(1)}, bf16[18,1,256]{2,0,1:T(8,128)(2,1)S(1)}, u32[]{:S(2)}, u32[]{:S(2)}) collective-permute-start(bf16[18,1,256]{2,0,1:T(8,128)(2,1)S(1)} %copy.153), channel_id=1, source_target_pairs={{2,0},{4,2},{6,4},{8,6},{10,8},{12,10},{14,12},{3,1},{5,3},{7,5},{... | collective-permute-start | bytes 27656 | tf_op jit(solution)/shard_map/ppermute | solution.py:17
  13.8 3.5 copy-start
  14.7 5.7 %collective-permute-start.3 = (bf16[18,130,1]{1,0,2:T(8,128)(2,1)S(1)}, bf16[18,130,1]{1,0,2:T(8,128)(2,1)S(1)}, u32[]{:S(2)}, u32[]{:S(2)}) collective-permute-start(bf16[18,130,1]{1,0,2:T(8,128)(2,1)S(1)} %get-tuple-element.18), channel_id=1, source_target_pairs={{0,1},{2,3},{4,5},{6,7},{8,9},{10,11},{12,13},{14,15},{16,17},{18,... | collective-permute-start | bytes 14048 | tf_op jit(solution)/shard_map/ppermute | solution.py:14
  16.0 4.4 collective-permute-start.2
  42.4 145.5 %all-to-all-start = ((bf16[6,16,128,256]{3,2,0,1:T(8,128)(2,1)}), bf16[6,16,128,256]{3,2,0,1:T(8,128)(2,1)}, u32[]{:S(2)}, u32[]{:S(2)}) async-start(bf16[6,16,128,256]{3,2,0,1:T(8,128)(2,1)} %copy.127), calls=%async_computation | async-start | bytes 12582912 | tf_op jit(solution)/shard_map/all_to_all | solution.py:113
where the time goes:
time: 445 us; the launch traced here: 444 us
  blocking collectives  160 us (36%)
  waiting for transfers between devices  141 us (32%)
  local copies, waits for them, and re-layouts  80.7 us (18%)
  other arithmetic  37.6 us (8%)
  starting transfers between devices  14.5 us (3%)
  matrix products  9.09 us (2%)
    all_to_all x1, blocking collectives, inline_pass(): lax.all_to_all(smoothed, 'il', split_axis=2, concat_axis=1, tiled=True)  142 us
    all_to_all x1, waiting for transfers between devices, body(): lax.all_to_all(moments, 'il', split_axis=1, concat_axis=2, tiled=True)  139 us
    convert_element_type x1, local copies, waits for them, and re-layouts, inline_pass(): smoothed = smooth_rows(padded).astype(jnp.bfloat16)  31.9 us
    unnamed x5, other arithmetic  14.1 us
    div x1, other arithmetic, attributes(): inline_dip = -comp_e / (comp_c + 1e-06)  10.9 us
    slice x4, local copies, waits for them, and re-layouts, body(): return (results[0], results[1], results[2])  10 us
    all_to_all x1, blocking collectives, body(): lax.all_to_all(lined, 'xl', split_axis=1, concat_axis=3, tiled=True)  9.95 us
    another operation x1, local copies, waits for them, and re-layouts, moment_terms(): jnp.stack([grad_i * grad_i, grad_x * grad_x, grad_z * grad_z, grad_i * gr...  9 us
  transfers between devices with their start and end apart: 5, of which 2 were waited for; matrix products, arithmetic and copies ran while one was open for 1% of the time, Pallas kernels for 0%

commit v1 on v0

v1 whole, which is shorter than its diff:
```python
import jax
import jax.numpy as jnp
import ml_dtypes
import numpy as np
from jax import lax
from jax.experimental import pallas as pl
from jax.experimental.pallas import tpu as pltpu
from jax.sharding import PartitionSpec as P

RADIUS = 9
SIDE = 16
SLOTS = 8
BF16 = ml_dtypes.bfloat16


def filter_taps():
    offsets = np.arange(2 * RADIUS + 1).astype(np.float32)
    sigma = np.float32(RADIUS / 3.0)
    shape = np.exp(np.float32(-0.5) * ((offsets - RADIUS) / sigma) ** 2)
    return (shape / np.sum(shape, dtype=np.float32)).astype(BF16).astype(np.float32)


def band(source, target):
    offset = source[:, None] - target[None, :] + RADIUS
    inside = (offset >= 0) & (offset <= 2 * RADIUS)
    return np.where(inside, filter_taps()[np.clip(offset, 0, 2 * RADIUS)], 0.0)


def difference(source, target):
    offset = source[:, None] - target[None, :]
    return (offset == 1).astype(np.float32) - (offset == -1).astype(np.float32)


class Tables:
    def __init__(self, rows, cols):
        self.rows, self.cols = rows, cols
        self.parts, self.at, self.total = [], {}, 0
        slots = np.arange(128) // SIDE
        place = np.arange(128) % SIDE
        row = np.arange(rows)
        position = np.concatenate([row, rows + np.arange(SIDE), np.arange(SIDE) - SIDE])
        self.add("lines", 0.25 * band(position, row).T)
        self.add("diff_i", difference(position, position).T)
        col = np.arange(cols)
        self.add("diff_x", difference(col, col))
        self.add("smooth_x", band(col, col))
        halo_0, halo_1 = cols + place, place - SIDE
        for x, halo in enumerate((halo_0, halo_1)):
            self.add(f"edge{x}", difference(col, halo))
            self.add(f"diff_h{x}", difference(halo, col))
            self.add(f"smooth_h{x}", band(halo, col))
        plane = np.concatenate(
            [1 + slots, 1 + SLOTS + slots, np.where(slots == 0, 0, np.where(slots == 1, 2 * SLOTS + 1, -99))]
        )
        places = np.concatenate([place, place, place])
        for group in range(2):
            centre = 1 + SLOTS * group + slots
            same = (places[:, None] == place[None, :]).astype(np.float32)
            depth = difference(plane, centre) * same
            level = (plane[:, None] == centre[None, :]).astype(np.float32)
            across = difference(places, place) * level
            self.add(f"halo{group}", np.concatenate([depth, across], axis=1))
        self.table = np.concatenate(self.parts, axis=0)

    def add(self, name, matrix):
        count, width = matrix.shape
        padded = np.zeros((-(-count // 16) * 16, self.cols), np.float32)
        padded[:count, :width] = matrix
        self.at[name] = (self.total, count, width)
        self.parts.append(padded.astype(BF16))
        self.total += padded.shape[0]

    def load(self, ref, name):
        start, count, width = self.at[name]
        return ref[start : start + count, :width]


def dot(left, right):
    return jnp.dot(left, right, preferred_element_type=jnp.float32)


def side_kernel(vol_ref, side_ref, top_ref, bottom_ref, top_corner_ref, bottom_corner_ref):
    depths, rows, cols = vol_ref.shape
    x = lax.axis_index("xl")
    first = jnp.where(x == 0, cols - SIDE, 0)
    lane = lax.broadcasted_iota(jnp.int32, (cols, 128), 0)
    place = lax.broadcasted_iota(jnp.int32, (cols, 128), 1)
    pick = (lane == first + lax.rem(place, SIDE)).astype(jnp.float32).astype(jnp.bfloat16)
    slot = lax.div(lax.broadcasted_iota(jnp.int32, (rows, 128), 1), SIDE)

    def piece(depth, index):
        return jnp.where(slot == index, dot(vol_ref[depth], pick), 0.0)

    for tile in range(3):
        planes = ((0, depths - 1), (0, 1)) if tile == 2 else (range(1 + SLOTS * tile, 1 + SLOTS * (tile + 1)), range(SLOTS))
        total = None
        for depth, index in zip(*planes):
            term = piece(depth, index)
            total = term if total is None else total + term
        packed = total.astype(jnp.bfloat16)
        side_ref[tile] = packed
        top_corner_ref[tile] = packed[:SIDE]
        bottom_corner_ref[tile] = packed[rows - SIDE :]
    top_ref[...] = vol_ref[:, :SIDE, :]
    bottom_ref[...] = vol_ref[:, rows - SIDE :, :]


def moments(grad_i, grad_x, grad_z):
    terms = (
        grad_i * grad_i,
        grad_x * grad_x,
        grad_z * grad_z,
        grad_i * grad_x,
        grad_i * grad_z,
        grad_x * grad_z,
    )
    return [term.astype(jnp.bfloat16) for term in terms]


def main_kernel(
    tables, vol_ref, side_ref, next_ref, last_ref, next_corner_ref, last_corner_ref, table_ref,
    dip_i_ref, dip_x_ref, plan_ref,
    pad_ref, halo_ref, lines_ref, smooth_ref, diff_h_ref, lined_h_ref, lined_a_ref, lined_b_ref,
    out_i_ref, out_x_ref, out_p_ref, sems,
):
    depths, rows, cols = vol_ref.shape
    count = depths - 2
    padded = rows + 2 * SIDE
    x = lax.axis_index("xl")
    il = lax.axis_index("il")
    last = lax.axis_size("il") - 1

    pad_ref[:, :rows, :] = vol_ref[...]
    pad_ref[:, rows : rows + SIDE, :] = next_ref[...]
    pad_ref[:, rows + SIDE :, :] = last_ref[...]
    for tile in range(3):
        lanes = slice(128 * tile, 128 * (tile + 1))
        halo_ref[:rows, lanes] = side_ref[tile]
        halo_ref[rows : rows + SIDE, lanes] = next_corner_ref[tile]
        halo_ref[rows + SIDE :, lanes] = last_corner_ref[tile]

    column = lax.broadcasted_iota(jnp.int32, (rows, padded), 1)
    inside = (column < rows) | ((column < rows + SIDE) & (il < last)) | ((column >= rows + SIDE) & (il > 0))
    lines_ref[...] = jnp.where(inside, tables.load(table_ref, "lines").astype(jnp.float32), 0.0).astype(jnp.bfloat16)

    def by_side(name):
        zero = tables.load(table_ref, name + "0").astype(jnp.float32)
        return jnp.where(x == 0, zero, tables.load(table_ref, name + "1").astype(jnp.float32))

    slot_row = lax.div(lax.broadcasted_iota(jnp.int32, (128, cols), 0), SIDE)
    smooth_h, diff_h = by_side("smooth_h"), by_side("diff_h")
    for index in range(SLOTS):
        smooth_ref[index, :cols, :] = tables.load(table_ref, "smooth_x")
        smooth_ref[index, cols:, :] = jnp.where(slot_row == index, smooth_h, 0.0).astype(jnp.bfloat16)
        diff_h_ref[index] = jnp.where(slot_row == index, diff_h, 0.0).astype(jnp.bfloat16)

    diff_i = tables.load(table_ref, "diff_i")
    diff_x = tables.load(table_ref, "diff_x")
    edge = by_side("edge").astype(jnp.bfloat16)
    slot_lane = lax.div(lax.broadcasted_iota(jnp.int32, (padded, 128), 1), SIDE)
    for group in range(2):
        both = dot(halo_ref[...], tables.load(table_ref, f"halo{group}"))
        grad_z, grad_x = both[:, :128], both[:, 128:]
        for index in range(SLOTS):
            near = dot(pad_ref[SLOTS * group + index + 1], edge)
            grad_x = grad_x + jnp.where(slot_lane == index, near, 0.0)
        grad_i = dot(diff_i, halo_ref[:, 128 * group : 128 * (group + 1)])
        for comp, term in enumerate(moments(grad_i, grad_x, grad_z)):
            lined_h_ref[group, rows * comp : rows * (comp + 1), :] = dot(lines_ref[...], term).astype(jnp.bfloat16)

    def stage_lines(z, lined_ref):
        group, index = lax.div(z, SLOTS), lax.rem(z, SLOTS)
        centre = pad_ref[z + 1]
        grad_i = dot(diff_i, centre)
        grad_x = dot(centre, diff_x) + dot(
            halo_ref[:, pl.ds(pl.multiple_of(128 * group, 128), 128)], diff_h_ref[index]
        )
        grad_z = pad_ref[z + 2].astype(jnp.float32) - pad_ref[z].astype(jnp.float32)
        lined_ref[:, cols:] = lined_h_ref[group]
        for comp, term in enumerate(moments(grad_i, grad_x, grad_z)):
            lined_ref[rows * comp : rows * (comp + 1), :cols] = dot(lines_ref[...], term).astype(jnp.bfloat16)

    def copies(z):
        pairs = ((out_i_ref, dip_i_ref), (out_x_ref, dip_x_ref), (out_p_ref, plan_ref))
        return [pltpu.make_async_copy(src.at[z], dst.at[z], sems.at[z, n]) for n, (src, dst) in enumerate(pairs)]

    def stage_attributes(z, lined_ref):
        weights = smooth_ref[lax.rem(z, SLOTS)]
        a, b, c, d, e, f = [dot(lined_ref[rows * comp : rows * (comp + 1), :], weights) for comp in range(6)]
        low = c + 1e-6
        inverse = -1.0 / low
        out_i_ref[z] = e * inverse
        out_x_ref[z] = f * inverse
        spread = (a - b) * (a - c) + (b - c) * (b - c) + 3.0 * (d * d + e * e + f * f)
        out_p_ref[z] = jnp.sqrt(spread) / (a + b + low)
        for copy in copies(z):
            copy.start()

    stage_lines(0, lined_a_ref)

    def pair(k, carry):
        z = 2 * k
        stage_lines(z + 1, lined_b_ref)
        stage_attributes(z, lined_a_ref)
        stage_lines(jnp.minimum(z + 2, count - 1), lined_a_ref)
        stage_attributes(z + 1, lined_b_ref)
        return carry

    lax.fori_loop(0, count // 2, pair, 0)
    for z in range(count):
        for copy in copies(z):
            copy.wait()


def body(volume):
    depths, rows, cols = volume.shape
    il, xl = lax.axis_size("il"), lax.axis_size("xl")
    assert xl == 2 and depths == 2 * SLOTS + 2 and cols == 256
    bf16 = jnp.bfloat16
    whole = pl.BlockSpec(memory_space=pltpu.VMEM)
    side, top, bottom, top_corner, bottom_corner = pl.pallas_call(
        side_kernel,
        out_shape=(
            jax.ShapeDtypeStruct((3, rows, 128), bf16),
            jax.ShapeDtypeStruct((depths, SIDE, cols), bf16),
            jax.ShapeDtypeStruct((depths, SIDE, cols), bf16),
            jax.ShapeDtypeStruct((3, SIDE, 128), bf16),
            jax.ShapeDtypeStruct((3, SIDE, 128), bf16),
        ),
        in_specs=[whole],
        out_specs=(whole,) * 5,
        compiler_params=pltpu.CompilerParams(vmem_limit_bytes=32 << 20),
        name="side_kernel",
    )(volume)

    up = [(i, i + 1) for i in range(il - 1)]
    down = [(i + 1, i) for i in range(il - 1)]
    swap = [(0, 1), (1, 0)]

    def crossed(pairs):
        return [(s * 2 + x, t * 2 + 1 - x) for s, t in pairs for x in range(2)]

    last_rows = lax.ppermute(bottom, "il", up)
    next_rows = lax.ppermute(top, "il", down)
    side_in = lax.ppermute(side, "xl", swap)
    last_corner = lax.ppermute(bottom_corner, ("il", "xl"), crossed(up))
    next_corner = lax.ppermute(top_corner, ("il", "xl"), crossed(down))

    tables = Tables(rows, cols)
    count, padded = depths - 2, rows + 2 * SIDE
    out = jax.ShapeDtypeStruct((count, rows, cols), jnp.float32)
    anywhere = pl.BlockSpec(memory_space=pl.ANY)
    return pl.pallas_call(
        lambda *refs: main_kernel(tables, *refs),
        out_shape=(out,) * 3,
        in_specs=[whole] * 7,
        out_specs=(anywhere,) * 3,
        scratch_shapes=[
            pltpu.VMEM((depths, padded, cols), bf16),
            pltpu.VMEM((padded, 384), bf16),
            pltpu.VMEM((rows, padded), bf16),
            pltpu.VMEM((SLOTS, cols + 128, cols), bf16),
            pltpu.VMEM((SLOTS, 128, cols), bf16),
            pltpu.VMEM((2, 6 * rows, 128), bf16),
            pltpu.VMEM((6 * rows, cols + 128), bf16),
            pltpu.VMEM((6 * rows, cols + 128), bf16),
            pltpu.VMEM((count, rows, cols), jnp.float32),
            pltpu.VMEM((count, rows, cols), jnp.float32),
            pltpu.VMEM((count, rows, cols), jnp.float32),
            pltpu.SemaphoreType.DMA((count, 3)),
        ],
        compiler_params=pltpu.CompilerParams(vmem_limit_bytes=48 << 20),
        name="main_kernel",
    )(volume, side_in, next_rows, last_rows, next_corner, last_corner, jnp.asarray(tables.table))


def solution(mesh):
    spec = P(None, ("parts", "il"), "xl")
    return jax.shard_map(body, mesh=mesh, in_specs=(spec,), out_specs=(spec,) * 3, check_vma=False)
```

time: 445 us -> 35 us (0.08)
  the two profiles are of different devices: /device:TPU:0 before, /device:TPU:11 now
where the time goes in v1:
time: 35 us; the launch traced here: 34.7 us
  Pallas kernels  13.7 us (39%)
  starting transfers between devices  12.4 us (35%)
  waiting for transfers between devices  3.96 us (11%)
  local copies, waits for them, and re-layouts  3.85 us (11%)
  between operations  0.7 us (2%)
    pallas_call x1, Pallas kernels, body(): pl.pallas_call(lambda *refs: main_kernel(tables, *refs), out_shape=(out,)...  13.3 us
    ppermute x1, waiting for transfers between devices, body(): last_corner = lax.ppermute(bottom_corner, ('il', 'xl'), crossed(up))  3.95 us
    unnamed x6, local copies, waits for them, and re-layouts  3.85 us
    ppermute x1, starting transfers between devices, body(): next_corner = lax.ppermute(top_corner, ('il', 'xl'), crossed(down))  3.83 us
    ppermute x1, starting transfers between devices, body(): next_rows = lax.ppermute(top, 'il', down)  3.03 us
    ppermute x1, starting transfers between devices, body(): last_rows = lax.ppermute(bottom, 'il', up)  2.25 us
    ppermute x1, starting transfers between devices, body(): last_corner = lax.ppermute(bottom_corner, ('il', 'xl'), crossed(up))  2.03 us
    ppermute x1, starting transfers between devices, body(): side_in = lax.ppermute(side, 'xl', swap)  1.3 us
  transfers between devices with their start and end apart: 5, of which 1 were waited for; matrix products, arithmetic and copies ran while one was open for 0% of the time, Pallas kernels for 0%

profile of v1, /device:TPU:11, one launch (start us, length us, event | category | flops | bytes accessed | tf_op | source)
XLA Modules:
  0.0 34.7 jit_solution(14945781239943612701)
XLA Ops:
  0.6 0.0 copy-start
  0.6 1.3 %copy-done = bf16[18,128,256]{2,1,0:T(8,128)(2,1)S(1)} copy-done((bf16[18,128,256]{2,1,0:T(8,128)(2,1)S(1)}, bf16[18,128,256]{2,1,0:T(8,128)(2,1)}, u32[]{:S(2)}) %copy-start) | copy-done | bytes 1179672
  1.9 0.5 %side_kernel.1 = (bf16[3,128,128]{2,1,0:T(8,128)(2,1)S(1)}, bf16[18,16,256]{2,1,0:T(8,128)(2,1)S(1)}, bf16[18,16,256]{2,1,0:T(8,128)(2,1)S(1)}, bf16[3,16,128]{2,1,0:T(8,128)(2,1)S(1)}, bf16[3,16,128]{2,1,0:T(8,128)(2,1)S(1)}) custom-call(bf16[18,128,256]{2,1,0:T(8,128)(2,1)S(1)} %copy-done), custom_call_target="tpu_custom_call" | custom-call | tf_op jit(solution)/shard_map/side_kernel/pallas_call | solution.py:221
  2.4 3.0 %collective-permute-start.1 = (bf16[18,16,256]{2,1,0:T(8,128)(2,1)S(1)}, bf16[18,16,256]{2,1,0:T(8,128)(2,1)S(1)}, u32[]{:S(2)}, u32[]{:S(2)}) collective-permute-start(bf16[18,16,256]{2,1,0:T(8,128)(2,1)S(1)} %get-tuple-element.9), channel_id=1, source_target_pairs={{2,0},{4,2},{6,4},{8,6},{10,8},{12,10},{14,12},{3,1},{5,3},{7,5},{... | collective-permute-start | bytes 442376 | tf_op jit(solution)/shard_map/ppermute | solution.py:244
  5.4 2.2 %collective-permute-start.2 = (bf16[18,16,256]{2,1,0:T(8,128)(2,1)S(1)}, bf16[18,16,256]{2,1,0:T(8,128)(2,1)S(1)}, u32[]{:S(2)}, u32[]{:S(2)}) collective-permute-start(bf16[18,16,256]{2,1,0:T(8,128)(2,1)S(1)} %get-tuple-element.10), channel_id=1, source_target_pairs={{0,2},{2,4},{4,6},{6,8},{8,10},{10,12},{12,14},{1,3},{3,5},{5,7},{... | collective-permute-start | bytes 442376 | tf_op jit(solution)/shard_map/ppermute | solution.py:243
  7.7 1.3 %collective-permute-start = (bf16[3,128,128]{2,1,0:T(8,128)(2,1)S(1)}, bf16[3,128,128]{2,1,0:T(8,128)(2,1)S(1)}, u32[]{:S(2)}, u32[]{:S(2)}) collective-permute-start(bf16[3,128,128]{2,1,0:T(8,128)(2,1)S(1)} %get-tuple-element.8), channel_id=1, source_target_pairs={{0,1},{1,0},{2,3},{3,2},{4,5},{5,4},{6,7},{7,6},{8,9},{9,8},{10,11... | collective-permute-start | bytes 294920 | tf_op jit(solution)/shard_map/ppermute | solution.py:245
  9.0 3.8 %collective-permute-start.3 = (bf16[3,16,128]{2,1,0:T(8,128)(2,1)S(1)}, bf16[3,16,128]{2,1,0:T(8,128)(2,1)S(1)}, u32[]{:S(2)}, u32[]{:S(2)}) collective-permute-start(bf16[3,16,128]{2,1,0:T(8,128)(2,1)S(1)} %get-tuple-element.11), channel_id=1, source_target_pairs={{2,1},{3,0},{4,3},{5,2},{6,5},{7,4},{8,7},{9,6},{10,9},{11,8},{12,... | collective-permute-start | bytes 36872 | tf_op jit(solution)/shard_map/ppermute | solution.py:247
  12.8 2.0 %collective-permute-start.4 = (bf16[3,16,128]{2,1,0:T(8,128)(2,1)S(1)}, bf16[3,16,128]{2,1,0:T(8,128)(2,1)S(1)}, u32[]{:S(2)}, u32[]{:S(2)}) collective-permute-start(bf16[3,16,128]{2,1,0:T(8,128)(2,1)S(1)} %get-tuple-element.12), channel_id=1, source_target_pairs={{0,3},{1,2},{2,5},{3,4},{4,7},{5,6},{6,9},{7,8},{8,11},{9,10},{10,... | collective-permute-start | bytes 36872 | tf_op jit(solution)/shard_map/ppermute | solution.py:246
  14.9 0.0 collective-permute-done.3.refs_4_
  14.9 4.0 %collective-permute-done.4.refs_5_ = bf16[3,16,128]{2,1,0:T(8,128)(2,1)S(1)} collective-permute-done((bf16[3,16,128]{2,1,0:T(8,128)(2,1)S(1)}, bf16[3,16,128]{2,1,0:T(8,128)(2,1)S(1)}, u32[]{:S(2)}, u32[]{:S(2)}) %collective-permute-start.4) | collective-permute-done | bytes 12320 | tf_op jit(solution)/shard_map/ppermute | solution.py:246
  18.8 0.0 collective-permute-done.refs_1_
  18.8 0.0 collective-permute-done.1.refs_2_
  18.8 0.0 collective-permute-done.2.refs_3_
  18.8 0.0 copy-start.1
  18.8 1.3 %copy-done.1 = bf16[18,128,256]{2,1,0:T(8,128)(2,1)S(1)} copy-done((bf16[18,128,256]{2,1,0:T(8,128)(2,1)S(1)}, bf16[18,128,256]{2,1,0:T(8,128)(2,1)}, u32[]{:S(2)}) %copy-start.1) | copy-done | bytes 1179672
  20.1 0.0 copy-start.2
  20.1 1.3 %copy-done.2 = bf16[2592,256]{1,0:T(8,128)(2,1)S(1)} copy-done((bf16[2592,256]{1,0:T(8,128)(2,1)S(1)}, bf16[2592,256]{1,0:T(8,128)(2,1)}, u32[]{:S(2)}) %copy-start.2) | copy-done | bytes 1327128
  21.4 13.3 %main_kernel.1 = (f32[16,128,256]{2,1,0:T(8,128)}, f32[16,128,256]{2,1,0:T(8,128)}, f32[16,128,256]{2,1,0:T(8,128)}) custom-call(bf16[18,128,256]{2,1,0:T(8,128)(2,1)S(1)} %copy-done.1, bf16[3,128,128]{2,1,0:T(8,128)(2,1)S(1)} %collective-permute-done.refs_1_, bf16[18,16,256]{2,1,0:T(8,128)(2,1)S(1)} %collective-permute-done.1.refs_2_, ...), custom_call_target="tpu_custom_call" | custom-call | tf_op jit(solution)/shard_map/main_kernel/pallas_call | solution.py:253
Async XLA Ops:
  0.6 1.3 %copy-start = (bf16[18,128,256]{2,1,0:T(8,128)(2,1)S(1)}, bf16[18,128,256]{2,1,0:T(8,128)(2,1)}, u32[]{:S(2)}) copy-start(bf16[18,128,256]{2,1,0:T(8,128)(2,1)} %refs_0_.1) | copy-start | bytes 3538948
  2.4 16.4 %collective-permute-start.1 = (bf16[18,16,256]{2,1,0:T(8,128)(2,1)S(1)}, bf16[18,16,256]{2,1,0:T(8,128)(2,1)S(1)}, u32[]{:S(2)}, u32[]{:S(2)}) collective-permute-start(bf16[18,16,256]{2,1,0:T(8,128)(2,1)S(1)} %get-tuple-element.9), channel_id=1, source_target_pairs={{2,0},{4,2},{6,4},{8,6},{10,8},{12,10},{14,12},{3,1},{5,3},{7,5},{... | collective-permute-start | bytes 442376 | tf_op jit(solution)/shard_map/ppermute | solution.py:244
  5.4 13.4 %collective-permute-start.2 = (bf16[18,16,256]{2,1,0:T(8,128)(2,1)S(1)}, bf16[18,16,256]{2,1,0:T(8,128)(2,1)S(1)}, u32[]{:S(2)}, u32[]{:S(2)}) collective-permute-start(bf16[18,16,256]{2,1,0:T(8,128)(2,1)S(1)} %get-tuple-element.10), channel_id=1, source_target_pairs={{0,2},{2,4},{4,6},{6,8},{8,10},{10,12},{12,14},{1,3},{3,5},{5,7},{... | collective-permute-start | bytes 442376 | tf_op jit(solution)/shard_map/ppermute | solution.py:243
  7.7 11.1 %collective-permute-start = (bf16[3,128,128]{2,1,0:T(8,128)(2,1)S(1)}, bf16[3,128,128]{2,1,0:T(8,128)(2,1)S(1)}, u32[]{:S(2)}, u32[]{:S(2)}) collective-permute-start(bf16[3,128,128]{2,1,0:T(8,128)(2,1)S(1)} %get-tuple-element.8), channel_id=1, source_target_pairs={{0,1},{1,0},{2,3},{3,2},{4,5},{5,4},{6,7},{7,6},{8,9},{9,8},{10,11... | collective-permute-start | bytes 294920 | tf_op jit(solution)/shard_map/ppermute | solution.py:245
  9.0 5.9 %collective-permute-start.3 = (bf16[3,16,128]{2,1,0:T(8,128)(2,1)S(1)}, bf16[3,16,128]{2,1,0:T(8,128)(2,1)S(1)}, u32[]{:S(2)}, u32[]{:S(2)}) collective-permute-start(bf16[3,16,128]{2,1,0:T(8,128)(2,1)S(1)} %get-tuple-element.11), channel_id=1, source_target_pairs={{2,1},{3,0},{4,3},{5,2},{6,5},{7,4},{8,7},{9,6},{10,9},{11,8},{12,... | collective-permute-start | bytes 36872 | tf_op jit(solution)/shard_map/ppermute | solution.py:247
  12.8 6.0 %collective-permute-start.4 = (bf16[3,16,128]{2,1,0:T(8,128)(2,1)S(1)}, bf16[3,16,128]{2,1,0:T(8,128)(2,1)S(1)}, u32[]{:S(2)}, u32[]{:S(2)}) collective-permute-start(bf16[3,16,128]{2,1,0:T(8,128)(2,1)S(1)} %get-tuple-element.12), channel_id=1, source_target_pairs={{0,3},{1,2},{2,5},{3,4},{4,7},{5,6},{6,9},{7,8},{8,11},{9,10},{10,... | collective-permute-start | bytes 36872 | tf_op jit(solution)/shard_map/ppermute | solution.py:246
  18.8 1.3 %copy-start.1 = (bf16[18,128,256]{2,1,0:T(8,128)(2,1)S(1)}, bf16[18,128,256]{2,1,0:T(8,128)(2,1)}, u32[]{:S(2)}) copy-start(bf16[18,128,256]{2,1,0:T(8,128)(2,1)} %refs_0_.1) | copy-start | bytes 3538948
  20.1 1.3 %copy-start.2 = (bf16[2592,256]{1,0:T(8,128)(2,1)S(1)}, bf16[2592,256]{1,0:T(8,128)(2,1)}, u32[]{:S(2)}) copy-start(bf16[2592,256]{1,0:T(8,128)(2,1)} %constant.2.clone.refs_6_) | copy-start | bytes 3981316

commit v2 on v0

v2 whole, which is shorter than its diff:
```python
import jax
import jax.numpy as jnp
import ml_dtypes
import numpy as np
from jax import lax
from jax.experimental import pallas as pl
from jax.experimental.pallas import tpu as pltpu
from jax.sharding import PartitionSpec as P

RADIUS = 9
REACH = RADIUS + 1
SIDE = 16
SLOTS = 8
TILES = 3
EDGE = 16
OWN = 2
FAR = -1000
WHOLE = pl.BlockSpec(memory_space=pltpu.VMEM)
IN_HBM = pl.BlockSpec(memory_space=pltpu.HBM)


def filter_taps():
    offsets = np.arange(2 * RADIUS + 1).astype(np.float32)
    sigma = np.float32(RADIUS / 3.0)
    shape = np.exp(np.float32(-0.5) * ((offsets - RADIUS) / sigma) ** 2)
    return (shape / np.sum(shape, dtype=np.float32)).astype(ml_dtypes.bfloat16).astype(np.float32)


def iota(shape, dim):
    return lax.broadcasted_iota(jnp.int32, shape, dim)


def band(source, target, scale=1.0):
    offset = jnp.abs(source - target)
    weights = jnp.zeros(offset.shape, jnp.float32)
    for distance, tap in enumerate(filter_taps()[RADIUS:]):
        weights = jnp.where(offset == distance, jnp.float32(scale * tap), weights)
    return weights


def difference(source, target):
    offset = source - target
    return jnp.where(offset == 1, 1.0, jnp.where(offset == -1, -1.0, 0.0)).astype(jnp.float32)


def dot(left, right):
    return jnp.dot(left, right, preferred_element_type=jnp.float32)


def halo_plane(lane, tile, depths):
    slot = lax.div(lane, SIDE)
    rest = jnp.where(slot == 0, 0, jnp.where(slot == 1, depths - 1, FAR))
    return jnp.where(tile < 2, 1 + SLOTS * tile + slot, rest)


def halo_column(lane, x, cols):
    place = lax.rem(lane, SIDE)
    return jnp.where(x == 0, cols - OWN + place, place - (SIDE - OWN))


def edge_position(index, rows):
    first = index < EDGE
    previous = index - 2 * EDGE - REACH
    following = rows + index - 3 * EDGE
    outer = jnp.where(index < 2 * EDGE + REACH, previous, jnp.where(index < 3 * EDGE, FAR + 2 * index, following))
    outer = jnp.where(index >= 3 * EDGE + REACH, FAR + 2 * index, outer)
    return jnp.where(first, index, jnp.where(index < 2 * EDGE, rows - 2 * EDGE + index, outer))


def pack_kernel(
    hbm_ref, vol_ref, send_ref, own_ref, lines_ref, diff_i_ref, diff_x_ref, smooth_ref, halo_ref, lines_e_ref, diff_e_ref, sem
):
    depths, rows, cols = vol_ref.shape
    load = pltpu.make_async_copy(hbm_ref, vol_ref, sem)
    load.start()
    x, il, last = lax.axis_index("xl"), lax.axis_index("il"), lax.axis_size("il") - 1
    bf16 = jnp.bfloat16

    target, source = iota((rows, rows), 0), iota((rows, rows), 1)
    inner = (source > 0) & (source < rows - 1)
    lines_ref[...] = jnp.where(inner, band(source, target, 0.25), 0.0).astype(bf16)
    diff_i_ref[...] = difference(source, target).astype(bf16)
    target, source = iota((2 * EDGE, 4 * EDGE), 0), iota((2 * EDGE, 4 * EDGE), 1)
    source_at, target_at = edge_position(source, rows), edge_position(target, rows)
    use = (source_at == 0) | (source_at == rows - 1)
    use = use | ((source_at < 0) & (il > 0)) | ((source_at >= rows) & (il < last))
    lines_e_ref[...] = jnp.where(use, band(source_at, target_at, 0.25), 0.0).astype(bf16)
    target, source = iota((4 * EDGE, 4 * EDGE), 0), iota((4 * EDGE, 4 * EDGE), 1)
    diff_e_ref[...] = difference(edge_position(source, rows), edge_position(target, rows)).astype(bf16)

    source, target = iota((cols, cols), 0), iota((cols, cols), 1)
    diff_x_ref[...] = difference(source, target).astype(bf16)
    moved = source == jnp.where(x == 0, cols - 1, 0)
    smooth_own = jnp.where(moved, 0.0, band(source, target)).astype(bf16)
    lane, target = iota((128, cols), 0), iota((128, cols), 1)
    place = lax.rem(lane, SIDE)
    repeated = place == jnp.where(x == 0, 0, SIDE - 1)
    smooth_halo = jnp.where(repeated, 0.0, band(halo_column(lane, x, cols), target))
    for index in range(SLOTS):
        smooth_ref[index, :cols, :] = smooth_own
        smooth_ref[index, cols:, :] = jnp.where(lax.div(lane, SIDE) == index, smooth_halo, 0.0).astype(bf16)

    source, target = iota((128, 128), 0), iota((128, 128), 1)
    same = lax.rem(source, SIDE) == lax.rem(target, SIDE)
    across = difference(lax.rem(source, SIDE), lax.rem(target, SIDE))
    for group in range(2):
        centre = halo_plane(target, group, depths)
        for tile in range(TILES):
            plane = halo_plane(source, tile, depths)
            part = slice(128 * tile, 128 * (tile + 1))
            halo_ref[group, part, :128] = jnp.where(same, difference(plane, centre), 0.0).astype(bf16)
            halo_ref[group, part, 128:] = jnp.where(plane == centre, across, 0.0).astype(bf16)

    source, lane = iota((cols, 256), 0), iota((cols, 256), 1)
    place = lax.rem(lane, SIDE)
    low, high = place < SIDE - OWN, place >= OWN
    sent = jnp.where(x == 0, jnp.where(low, cols - (SIDE - OWN) + place, FAR), jnp.where(high, place - OWN, FAR))
    low, high = place < OWN, place >= SIDE - OWN
    kept = jnp.where(x == 0, jnp.where(low, cols - OWN + place, FAR), jnp.where(high, place - (SIDE - OWN), FAR))
    pick = jnp.where(source == jnp.where(lane < 128, sent, kept), 1.0, 0.0).astype(bf16)
    slot = lax.div(lax.rem(iota((rows, 256), 1), 128), SIDE)

    load.wait()
    for tile in range(TILES):
        if tile < 2:
            planes = [(1 + SLOTS * tile + index, index) for index in range(SLOTS)]
        else:
            planes = [(0, 0), (depths - 1, 1)]
        packed = jnp.zeros((rows, 256), jnp.float32)
        for plane, index in planes:
            packed = jnp.where(slot == index, dot(vol_ref[plane], pick), packed)
        packed = packed.astype(bf16)
        send_ref[tile] = packed[:, :128]
        own_ref[tile] = packed[:, 128:]


def rows_kernel(vol_ref, own_ref, side_ref, halo_ref, first_ref, second_ref, packed_ref):
    depths, rows, cols = vol_ref.shape
    even = lax.rem(lax.axis_index("il"), 2) == 0

    def put(row, top, bottom):
        top, bottom = top[:REACH], bottom[EDGE - REACH :]
        lanes = top.shape[1]
        packed_ref[0, row : row + REACH, :lanes] = jnp.where(even, bottom, top)
        packed_ref[1, row : row + REACH, :lanes] = jnp.where(even, top, bottom)

    packed_ref[:, depths * REACH :, :] = jnp.zeros_like(packed_ref[:, depths * REACH :, :])
    for depth in range(depths):
        top = vol_ref[depth, :EDGE, :].astype(jnp.float32)
        bottom = vol_ref[depth, rows - EDGE :, :].astype(jnp.float32)
        put(REACH * depth, top, bottom)
    tiles = []
    for tile in range(TILES):
        merged = own_ref[tile].astype(jnp.float32) + side_ref[tile].astype(jnp.float32)
        halo_ref[:, 128 * tile : 128 * (tile + 1)] = merged.astype(jnp.bfloat16)
        tiles.append((merged[:EDGE], merged[rows - EDGE :]))
    tops = jnp.concatenate([tiles[0][0], tiles[1][0]], axis=1)
    bottoms = jnp.concatenate([tiles[0][1], tiles[1][1]], axis=1)
    put(REACH * depths, tops, bottoms)
    put(REACH * (depths + 1), *tiles[2])
    first_ref[...] = packed_ref[0].astype(jnp.bfloat16)
    second_ref[...] = packed_ref[1].astype(jnp.bfloat16)


def moments(grad_i, grad_x, grad_z):
    terms = (
        grad_i * grad_i,
        grad_x * grad_x,
        grad_z * grad_z,
        grad_i * grad_x,
        grad_i * grad_z,
        grad_x * grad_z,
    )
    return [term.astype(jnp.bfloat16) for term in terms]


def own_lines(start, count, vol_ref, lines_ref, diff_i_ref, diff_x_ref, inner_ref, part_ref):
    rows = vol_ref.shape[1]

    def step(k, carry):
        z = start + k
        centre = vol_ref[z + 1]
        grad_i = dot(diff_i_ref[...], centre)
        grad_x = dot(centre, diff_x_ref[...])
        grad_z = vol_ref[z + 2].astype(jnp.float32) - vol_ref[z].astype(jnp.float32)
        for comp, term in enumerate(moments(grad_i, grad_x, grad_z)):
            summed = dot(lines_ref[...], term)
            inner_ref[k, comp] = summed[EDGE : rows - EDGE].astype(jnp.bfloat16)
            part_ref[k, comp, :EDGE] = summed[:EDGE]
            part_ref[k, comp, EDGE:] = summed[rows - EDGE :]
        return carry

    lax.fori_loop(0, count, step, 0, unroll=2)


def lines_kernel(start, count, vol_ref, lines_ref, diff_i_ref, diff_x_ref, inner_ref, part_ref):
    own_lines(start, count, vol_ref, lines_ref, diff_i_ref, diff_x_ref, inner_ref, part_ref)


def lines_halo_kernel(
    start, count, vol_ref, lines_ref, diff_i_ref, diff_x_ref, halo_ref, diff_h_ref, inner_ref, part_ref, part_h_ref
):
    for group in range(2):
        both = dot(halo_ref[...], diff_h_ref[group])
        grad_i = dot(diff_i_ref[...], halo_ref[:, 128 * group : 128 * (group + 1)])
        for comp, term in enumerate(moments(grad_i, both[:, 128:], both[:, :128])):
            part_h_ref[group, comp] = dot(lines_ref[...], term)
    own_lines(start, count, vol_ref, lines_ref, diff_i_ref, diff_x_ref, inner_ref, part_ref)


def final_kernel(
    vol_ref, halo_ref, first_ref, second_ref, inner_a_ref, part_a_ref, inner_b_ref, part_b_ref, part_h_ref,
    smooth_ref, diff_x_ref, diff_h_ref, lines_e_ref, diff_e_ref,
    dip_i_ref, dip_x_ref, plan_ref,
    packed_ref, block_ref, block_h_ref, lined_h_ref, edge_a_ref, edge_b_ref,
    out_i_ref, out_x_ref, out_p_ref, sems,
):
    depths, rows, cols = vol_ref.shape
    count, half = depths - 2, inner_a_ref.shape[0]
    even = lax.rem(lax.axis_index("il"), 2) == 0
    bf16 = jnp.bfloat16

    first, second = first_ref[...].astype(jnp.float32), second_ref[...].astype(jnp.float32)
    packed_ref[0] = jnp.where(even, second, first)
    packed_ref[1] = jnp.where(even, first, second)
    for depth in range(depths):
        block_ref[depth, :EDGE] = vol_ref[depth, :EDGE]
        block_ref[depth, EDGE : 2 * EDGE] = vol_ref[depth, rows - EDGE :]
        for side in range(2):
            at = EDGE * (2 + side)
            block_ref[depth, at : at + EDGE] = packed_ref[side, REACH * depth : REACH * depth + EDGE].astype(bf16)
    block_h_ref[:EDGE] = halo_ref[:EDGE]
    block_h_ref[EDGE : 2 * EDGE] = halo_ref[rows - EDGE :]
    for side in range(2):
        at, row = EDGE * (2 + side), REACH * depths
        block_h_ref[at : at + EDGE, :256] = packed_ref[side, row : row + EDGE].astype(bf16)
        block_h_ref[at : at + EDGE, 256:] = packed_ref[side, row + REACH : row + REACH + EDGE, :128].astype(bf16)

    for group in range(2):
        both = dot(block_h_ref[...], diff_h_ref[group])
        grad_i = dot(diff_e_ref[...], block_h_ref[:, 128 * group : 128 * (group + 1)])
        for comp, term in enumerate(moments(grad_i, both[:, 128:], both[:, :128])):
            outer = dot(lines_e_ref[...], term)
            lined_h_ref[group, comp, :EDGE] = (part_h_ref[group, comp, :EDGE] + outer[:EDGE]).astype(bf16)
            lined_h_ref[group, comp, EDGE : rows - EDGE] = part_h_ref[group, comp, EDGE : rows - EDGE].astype(bf16)
            lined_h_ref[group, comp, rows - EDGE :] = (part_h_ref[group, comp, rows - EDGE :] + outer[EDGE:]).astype(bf16)

    def copies(z):
        pairs = ((out_i_ref, dip_i_ref), (out_x_ref, dip_x_ref), (out_p_ref, plan_ref))
        return [pltpu.make_async_copy(src.at[z], dst.at[z], sems.at[z, n]) for n, (src, dst) in enumerate(pairs)]

    def run(group, inner_ref, part_ref):
        def stage_edge(k, edge_ref):
            z = half * group + k
            centre = block_ref[z + 1]
            grad_i = dot(diff_e_ref[...], centre)
            grad_x = dot(centre, diff_x_ref[...])
            grad_z = block_ref[z + 2].astype(jnp.float32) - block_ref[z].astype(jnp.float32)
            for comp, term in enumerate(moments(grad_i, grad_x, grad_z)):
                edge_ref[comp] = (part_ref[k, comp] + dot(lines_e_ref[...], term)).astype(bf16)

        def stage_attributes(k, edge_ref):
            z = half * group + k
            weights = smooth_ref[k]

            def smoothed(comp):
                own = jnp.concatenate([edge_ref[comp, :EDGE], inner_ref[k, comp], edge_ref[comp, EDGE:]], axis=0)
                return dot(jnp.concatenate([own, lined_h_ref[group, comp]], axis=1), weights)

            a, b, c, d, e, f = [smoothed(comp) for comp in range(6)]
            low = c + 1e-6
            inverse = -1.0 / low
            out_i_ref[z] = e * inverse
            out_x_ref[z] = f * inverse
            spread = (a - b) * (a - c) + (b - c) * (b - c) + 3.0 * (d * d + e * e + f * f)
            out_p_ref[z] = jnp.sqrt(spread) / (a + b + low)
            for copy in copies(z):
                copy.start()

        stage_edge(0, edge_a_ref)

        def pair(pair_index, carry):
            k = 2 * pair_index
            stage_edge(k + 1, edge_b_ref)
            stage_attributes(k, edge_a_ref)
            stage_edge(jnp.minimum(k + 2, half - 1), edge_a_ref)
            stage_attributes(k + 1, edge_b_ref)
            return carry

        lax.fori_loop(0, half // 2, pair, 0)

    run(0, inner_a_ref, part_a_ref)
    run(1, inner_b_ref, part_b_ref)
    for z in range(count):
        for copy in copies(z):
            copy.wait()


def call(name, kernel, outs, scratch, operands, in_specs=None, out_specs=None, flops=0, limit=16):
    return pl.pallas_call(
        kernel,
        out_shape=tuple(jax.ShapeDtypeStruct(*out) for out in outs),
        in_specs=in_specs or [WHOLE] * len(operands),
        out_specs=out_specs or (WHOLE,) * len(outs),
        scratch_shapes=scratch,
        compiler_params=pltpu.CompilerParams(vmem_limit_bytes=limit << 20),
        name=name,
        cost_estimate=pl.CostEstimate(flops=flops, bytes_accessed=0, transcendentals=0),
    )(*operands)


def body(volume):
    depths, rows, cols = volume.shape
    il, xl = lax.axis_size("il"), lax.axis_size("xl")
    count = depths - 2
    assert xl == 2 and il % 2 == 0 and count == 2 * SLOTS and cols == 256
    bf16, f32 = jnp.bfloat16, jnp.float32
    packed_rows = -(-REACH * (depths + 2) // 16) * 16

    vol, send, own, lines, diff_i, diff_x, smooth, diff_h, lines_e, diff_e = call(
        "pack_kernel",
        pack_kernel,
        [
            (volume.shape, bf16),
            ((TILES, rows, 128), bf16),
            ((TILES, rows, 128), bf16),
            ((rows, rows), bf16),
            ((rows, rows), bf16),
            ((cols, cols), bf16),
            ((SLOTS, cols + 128, cols), bf16),
            ((2, 128 * TILES, 256), bf16),
            ((2 * EDGE, 4 * EDGE), bf16),
            ((4 * EDGE, 4 * EDGE), bf16),
        ],
        [pltpu.SemaphoreType.DMA],
        [volume],
        in_specs=[IN_HBM],
    )
    side = lax.ppermute(send, "xl", [(0, 1), (1, 0)])

    def own_outs(half):
        return [((half, 6, rows - 2 * EDGE, cols), bf16), ((half, 6, 2 * EDGE, cols), f32)]

    half = count // 2
    work = half * 1024 * 2 * 256 * 256
    inner_a, part_a = call(
        "lines_kernel",
        lambda *refs: lines_kernel(0, half, *refs),
        own_outs(half),
        [],
        [vol, lines, diff_i, diff_x],
        flops=work,
    )
    halo, first, second = call(
        "rows_kernel",
        rows_kernel,
        [((rows, 128 * TILES), bf16), ((packed_rows, cols), bf16), ((packed_rows, cols), bf16)],
        [pltpu.VMEM((2, packed_rows, cols), f32)],
        [vol, own, side],
    )
    one = [(i, i ^ 1) for i in range(il)]
    two = [pair for i in range(1, il - 1, 2) for pair in ((i, i + 1), (i + 1, i))]
    first_in = lax.ppermute(first, "il", one)
    second_in = lax.ppermute(second, "il", two)
    inner_b, part_b, part_h = call(
        "lines_halo_kernel",
        lambda *refs: lines_halo_kernel(half, half, *refs),
        own_outs(half) + [((2, 6, rows, 128), f32)],
        [],
        [vol, lines, diff_i, diff_x, halo, diff_h],
        flops=work,
    )
    return call(
        "final_kernel",
        final_kernel,
        [((count, rows, cols), f32)] * 3,
        [
            pltpu.VMEM((2, packed_rows, cols), f32),
            pltpu.VMEM((depths, 4 * EDGE, cols), bf16),
            pltpu.VMEM((4 * EDGE, 128 * TILES), bf16),
            pltpu.VMEM((2, 6, rows, 128), bf16),
            pltpu.VMEM((6, 2 * EDGE, cols), bf16),
            pltpu.VMEM((6, 2 * EDGE, cols), bf16),
            pltpu.VMEM((count, rows, cols), f32),
            pltpu.VMEM((count, rows, cols), f32),
            pltpu.VMEM((count, rows, cols), f32),
            pltpu.SemaphoreType.DMA((count, 3)),
        ],
        [vol, halo, first_in, second_in, inner_a, part_a, inner_b, part_b, part_h, smooth, diff_x, diff_h, lines_e, diff_e],
        out_specs=(IN_HBM,) * 3,
        flops=count * 2048 * 2 * 256 * 256,
        limit=24,
    )


def solution(mesh):
    spec = P(None, ("parts", "il"), "xl")
    return jax.shard_map(body, mesh=mesh, in_specs=(spec,), out_specs=(spec,) * 3, check_vma=False)
```

time: 445 us -> 26.5 us (0.06)
  the two profiles are of different devices: /device:TPU:0 before, /device:TPU:12 now
where the time goes in v2:
time: 26.5 us; the launch traced here: 26.4 us
  Pallas kernels  18 us (68%)
  starting transfers between devices  5.08 us (19%)
  waiting for transfers between devices  1.29 us (5%)
  local copies, waits for them, and re-layouts  1.26 us (5%)
  between operations  0.7 us (3%)
    pallas_call x5, Pallas kernels, call(): pl.pallas_call(kernel, out_shape=tuple((jax.ShapeDtypeStruct(*out) for ou...  18 us
    ppermute x1, starting transfers between devices, body(): second_in = lax.ppermute(second, 'il', two)  4.43 us
    ppermute x1, waiting for transfers between devices, body(): side = lax.ppermute(send, 'xl', [(0, 1), (1, 0)])  1.29 us
    unnamed x2, local copies, waits for them, and re-layouts  1.26 us
    ppermute x1, starting transfers between devices, body(): first_in = lax.ppermute(first, 'il', one)  0.58 us
  transfers between devices with their start and end apart: 3, of which 1 were waited for; matrix products, arithmetic and copies ran while one was open for 0% of the time, Pallas kernels for 23%

profile of v2, /device:TPU:12, one launch (start us, length us, event | category | flops | bytes accessed | tf_op | source)
XLA Modules:
  0.0 26.4 jit_solution(846758988264117405)
XLA Ops:
  0.6 0.0 copy-start
  0.6 1.3 %copy-done = bf16[18,128,256]{2,1,0:T(8,128)(2,1)S(1)} copy-done((bf16[18,128,256]{2,1,0:T(8,128)(2,1)S(1)}, bf16[18,128,256]{2,1,0:T(8,128)(2,1)}, u32[]{:S(2)}) %copy-start) | copy-done | bytes 1179672
  1.9 1.3 %pack_kernel.1 = (bf16[18,128,256]{2,1,0:T(8,128)(2,1)S(1)}, bf16[3,128,128]{2,1,0:T(8,128)(2,1)S(1)}, bf16[3,128,128]{2,1,0:T(8,128)(2,1)S(1)}, bf16[128,128]{1...) custom-call(bf16[18,128,256]{2,1,0:T(8,128)(2,1)S(1)} %copy-done), custom_call_target="tpu_custom_call" | custom-call | tf_op jit(solution)/shard_map/pack_kernel/pallas_call | solution.py:300
  3.2 0.1 collective-permute-start
  3.3 1.3 %collective-permute-done.side_ref = bf16[3,128,128]{2,1,0:T(8,128)(2,1)S(1)} collective-permute-done((bf16[3,128,128]{2,1,0:T(8,128)(2,1)S(1)}, bf16[3,128,128]{2,1,0:T(8,128)(2,1)S(1)}, u32[]{:S(2)}, u32[]{:S(2)}) %collective-permute-start) | collective-permute-done | bytes 98336 | tf_op jit(solution)/shard_map/ppermute | solution.py:339
  4.6 0.1 rows_kernel.1
  4.8 0.6 %collective-permute-start.1 = (bf16[208,256]{1,0:T(8,128)(2,1)S(1)}, bf16[208,256]{1,0:T(8,128)(2,1)S(1)}, u32[]{:S(2)}, u32[]{:S(2)}) collective-permute-start(bf16[208,256]{1,0:T(8,128)(2,1)S(1)} %get-tuple-element.25), channel_id=1, source_target_pairs={{0,2},{2,0},{4,6},{6,4},{8,10},{10,8},{12,14},{14,12},{1,3},{3,1},... | collective-permute-start | bytes 319496 | tf_op jit(solution)/shard_map/ppermute | solution.py:363
  5.3 4.4 %collective-permute-start.2 = (bf16[208,256]{1,0:T(8,128)(2,1)S(1)}, bf16[208,256]{1,0:T(8,128)(2,1)S(1)}, u32[]{:S(2)}, u32[]{:S(2)}) collective-permute-start(bf16[208,256]{1,0:T(8,128)(2,1)S(1)} %get-tuple-element.26), channel_id=1, source_target_pairs={{2,4},{4,2},{6,8},{8,6},{10,12},{12,10},{3,5},{5,3},{7,9},{9,7},{1... | collective-permute-start | bytes 319496 | tf_op jit(solution)/shard_map/ppermute | solution.py:364
  9.8 2.7 %lines_kernel.1 = (bf16[8,6,96,256]{3,2,1,0:T(8,128)(2,1)S(1)}, f32[8,6,32,256]{3,2,1,0:T(8,128)S(1)}) custom-call(bf16[18,128,256]{2,1,0:T(8,128)(2,1)S(1)} %get-tuple-element.21.vol_ref.refs_0_, bf16[128,128]{1,0:T(8,128)(2,1)S(1)} %get-tuple-element.27.refs_1_, bf16[128,128]{1,0:T(8,128)(2,1)S(1)} %get-tuple-element.28.refs_2_, ...), custom_call_target="tpu_custom_call" | custom-call | flops 1073741824 | tf_op jit(solution)/shard_map/lines_kernel/pallas_call | solution.py:300
  12.5 3.3 %lines_halo_kernel.1 = (bf16[8,6,96,256]{3,2,1,0:T(8,128)(2,1)S(1)}, f32[8,6,32,256]{3,2,1,0:T(8,128)S(1)}, f32[2,6,128,128]{3,2,1,0:T(8,128)S(1)}) custom-call(bf16[18,128,256]{2,1,0:T(8,128)(2,1)S(1)} %get-tuple-element.21.vol_ref.refs_0_, bf16[128,128]{1,0:T(8,128)(2,1)S(1)} %get-tuple-element.27.refs_1_, bf16[128,128]{1,0:T(8,128)(2,1)S(1)} %get-tuple-element.28.refs_2_, ...), custom_call_target="tpu_custom_call" | custom-call | flops 1073741824 | tf_op jit(solution)/shard_map/lines_halo_kernel/pallas_call | solution.py:300
  15.8 0.0 collective-permute-done.1.first_ref
  15.8 0.0 collective-permute-done.2.second_ref
  15.8 10.5 %final_kernel.1 = (f32[16,128,256]{2,1,0:T(8,128)}, f32[16,128,256]{2,1,0:T(8,128)}, f32[16,128,256]{2,1,0:T(8,128)}) custom-call(bf16[18,128,256]{2,1,0:T(8,128)(2,1)S(1)} %get-tuple-element.21.vol_ref.refs_0_, bf16[128,384]{1,0:T(8,128)(2,1)S(1)} %get-tuple-element.24.refs_4_.halo_ref, bf16[208,256]{1,0:T(8,128)(2,1)S(1)} %collective-permute-done.1.first_ref, ...), custom_call_target="tpu_custom_call" | custom-call | flops 4294967296 | tf_op jit(solution)/shard_map/final_kernel/pallas_call | solution.py:300
Async XLA Ops:
  0.6 1.3 %copy-start = (bf16[18,128,256]{2,1,0:T(8,128)(2,1)S(1)}, bf16[18,128,256]{2,1,0:T(8,128)(2,1)}, u32[]{:S(2)}) copy-start(bf16[18,128,256]{2,1,0:T(8,128)(2,1)} %hbm_ref.1) | copy-start | bytes 3538948
  3.2 1.4 %collective-permute-start = (bf16[3,128,128]{2,1,0:T(8,128)(2,1)S(1)}, bf16[3,128,128]{2,1,0:T(8,128)(2,1)S(1)}, u32[]{:S(2)}, u32[]{:S(2)}) collective-permute-start(bf16[3,128,128]{2,1,0:T(8,128)(2,1)S(1)} %get-tuple-element.23), channel_id=1, source_target_pairs={{0,1},{1,0},{2,3},{3,2},{4,5},{5,4},{6,7},{7,6},{8,9},{9,8},{10,11... | collective-permute-start | bytes 294920 | tf_op jit(solution)/shard_map/ppermute | solution.py:339
  4.8 11.1 %collective-permute-start.1 = (bf16[208,256]{1,0:T(8,128)(2,1)S(1)}, bf16[208,256]{1,0:T(8,128)(2,1)S(1)}, u32[]{:S(2)}, u32[]{:S(2)}) collective-permute-start(bf16[208,256]{1,0:T(8,128)(2,1)S(1)} %get-tuple-element.25), channel_id=1, source_target_pairs={{0,2},{2,0},{4,6},{6,4},{8,10},{10,8},{12,14},{14,12},{1,3},{3,1},... | collective-permute-start | bytes 319496 | tf_op jit(solution)/shard_map/ppermute | solution.py:363
  5.3 10.5 %collective-permute-start.2 = (bf16[208,256]{1,0:T(8,128)(2,1)S(1)}, bf16[208,256]{1,0:T(8,128)(2,1)S(1)}, u32[]{:S(2)}, u32[]{:S(2)}) collective-permute-start(bf16[208,256]{1,0:T(8,128)(2,1)S(1)} %get-tuple-element.26), channel_id=1, source_target_pairs={{2,4},{4,2},{6,8},{8,6},{10,12},{12,10},{3,5},{5,3},{7,9},{9,7},{1... | collective-permute-start | bytes 319496 | tf_op jit(solution)/shard_map/ppermute | solution.py:364

commit v3 on v2

--- a/solution.py
+++ b/solution.py
@@ -14,6 +14,7 @@
 TILES = 3
 EDGE = 16
 OWN = 2
+TINY = float(np.finfo(np.float32).tiny)
 FAR = -1000
 WHOLE = pl.BlockSpec(memory_space=pltpu.VMEM)
 IN_HBM = pl.BlockSpec(memory_space=pltpu.HBM)
@@ -45,6 +46,11 @@
 
 def dot(left, right):
     return jnp.dot(left, right, preferred_element_type=jnp.float32)
+
+
+def reciprocal(value):
+    guess = pl.reciprocal(value, approx=True)
+    return guess * (2.0 - value * guess)
 
 
 def halo_plane(lane, tile, depths):
@@ -67,12 +73,8 @@
     return jnp.where(first, index, jnp.where(index < 2 * EDGE, rows - 2 * EDGE + index, outer))
 
 
-def pack_kernel(
-    hbm_ref, vol_ref, send_ref, own_ref, lines_ref, diff_i_ref, diff_x_ref, smooth_ref, halo_ref, lines_e_ref, diff_e_ref, sem
-):
-    depths, rows, cols = vol_ref.shape
-    load = pltpu.make_async_copy(hbm_ref, vol_ref, sem)
-    load.start()
+def tables_kernel(depths, lines_ref, diff_i_ref, diff_x_ref, smooth_ref, halo_ref, lines_e_ref, diff_e_ref, pick_ref):
+    rows, cols = lines_ref.shape[0], diff_x_ref.shape[0]
     x, il, last = lax.axis_index("xl"), lax.axis_index("il"), lax.axis_size("il") - 1
     bf16 = jnp.bfloat16
 
@@ -117,10 +119,13 @@
     sent = jnp.where(x == 0, jnp.where(low, cols - (SIDE - OWN) + place, FAR), jnp.where(high, place - OWN, FAR))
     low, high = place < OWN, place >= SIDE - OWN
     kept = jnp.where(x == 0, jnp.where(low, cols - OWN + place, FAR), jnp.where(high, place - (SIDE - OWN), FAR))
-    pick = jnp.where(source == jnp.where(lane < 128, sent, kept), 1.0, 0.0).astype(bf16)
+    pick_ref[...] = jnp.where(source == jnp.where(lane < 128, sent, kept), 1.0, 0.0).astype(bf16)
+
+
+def pack_kernel(vol_ref, pick_ref, copy_ref, send_ref, own_ref):
+    depths, rows, cols = vol_ref.shape
     slot = lax.div(lax.rem(iota((rows, 256), 1), 128), SIDE)
-
-    load.wait()
+    copy_ref[...] = vol_ref[...]
     for tile in range(TILES):
         if tile < 2:
             planes = [(1 + SLOTS * tile + index, index) for index in range(SLOTS)]
@@ -128,13 +133,13 @@
             planes = [(0, 0), (depths - 1, 1)]
         packed = jnp.zeros((rows, 256), jnp.float32)
         for plane, index in planes:
-            packed = jnp.where(slot == index, dot(vol_ref[plane], pick), packed)
-        packed = packed.astype(bf16)
+            packed = jnp.where(slot == index, dot(vol_ref[plane], pick_ref[...]), packed)
+        packed = packed.astype(jnp.bfloat16)
         send_ref[tile] = packed[:, :128]
         own_ref[tile] = packed[:, 128:]
 
 
-def rows_kernel(vol_ref, own_ref, side_ref, halo_ref, first_ref, second_ref, packed_ref):
+def rows_kernel(vol_ref, own_ref, side_ref, after_ref, halo_ref, first_ref, second_ref, packed_ref):
     depths, rows, cols = vol_ref.shape
     even = lax.rem(lax.axis_index("il"), 2) == 0
 
@@ -174,38 +179,52 @@
     return [term.astype(jnp.bfloat16) for term in terms]
 
 
-def own_lines(start, count, vol_ref, lines_ref, diff_i_ref, diff_x_ref, inner_ref, part_ref):
+def own_lines(start, count, vol_ref, lines_ref, diff_i_ref, diff_x_ref, inner_ref, part_ref, even_ref, odd_ref):
     rows = vol_ref.shape[1]
 
-    def step(k, carry):
+    def stage_moments(k, moments_ref):
         z = start + k
         centre = vol_ref[z + 1]
         grad_i = dot(diff_i_ref[...], centre)
         grad_x = dot(centre, diff_x_ref[...])
         grad_z = vol_ref[z + 2].astype(jnp.float32) - vol_ref[z].astype(jnp.float32)
         for comp, term in enumerate(moments(grad_i, grad_x, grad_z)):
-            summed = dot(lines_ref[...], term)
+            moments_ref[comp] = term
+
+    def stage_lines(k, moments_ref):
+        for comp in range(6):
+            summed = dot(lines_ref[...], moments_ref[comp])
             inner_ref[k, comp] = summed[EDGE : rows - EDGE].astype(jnp.bfloat16)
             part_ref[k, comp, :EDGE] = summed[:EDGE]
             part_ref[k, comp, EDGE:] = summed[rows - EDGE :]
+
+    stage_moments(0, even_ref)
+
+    def pair(index, carry):
+        k = 2 * index
+        stage_moments(k + 1, odd_ref)
+        stage_lines(k, even_ref)
+        stage_moments(jnp.minimum(k + 2, count - 1), even_ref)
+        stage_lines(k + 1, odd_ref)
         return carry
 
-    lax.fori_loop(0, count, step, 0, unroll=2)
-
-
-def lines_kernel(start, count, vol_ref, lines_ref, diff_i_ref, diff_x_ref, inner_ref, part_ref):
-    own_lines(start, count, vol_ref, lines_ref, diff_i_ref, diff_x_ref, inner_ref, part_ref)
+    lax.fori_loop(0, count // 2, pair, 0)
+
+
+def lines_kernel(start, count, *refs):
+    own_lines(start, count, *refs)
 
 
 def lines_halo_kernel(
-    start, count, vol_ref, lines_ref, diff_i_ref, diff_x_ref, halo_ref, diff_h_ref, inner_ref, part_ref, part_h_ref
+    start, count, vol_ref, lines_ref, diff_i_ref, diff_x_ref, halo_ref, diff_h_ref, inner_ref, part_ref, part_h_ref,
+    even_ref, odd_ref,
 ):
     for group in range(2):
         both = dot(halo_ref[...], diff_h_ref[group])
         grad_i = dot(diff_i_ref[...], halo_ref[:, 128 * group : 128 * (group + 1)])
         for comp, term in enumerate(moments(grad_i, both[:, 128:], both[:, :128])):
             part_h_ref[group, comp] = dot(lines_ref[...], term)
-    own_lines(start, count, vol_ref, lines_ref, diff_i_ref, diff_x_ref, inner_ref, part_ref)
+    own_lines(start, count, vol_ref, lines_ref, diff_i_ref, diff_x_ref, inner_ref, part_ref, even_ref, odd_ref)
 
 
 def final_kernel(
@@ -269,11 +288,12 @@
 
             a, b, c, d, e, f = [smoothed(comp) for comp in range(6)]
             low = c + 1e-6
-            inverse = -1.0 / low
-            out_i_ref[z] = e * inverse
-            out_x_ref[z] = f * inverse
+            inverse = reciprocal(low)
+            out_i_ref[z] = -e * inverse
+            out_x_ref[z] = -f * inverse
             spread = (a - b) * (a - c) + (b - c) * (b - c) + 3.0 * (d * d + e * e + f * f)
-            out_p_ref[z] = jnp.sqrt(spread) / (a + b + low)
+            root = spread * lax.rsqrt(jnp.maximum(spread, TINY))
+            out_p_ref[z] = root * reciprocal(a + b + low)
             for copy in copies(z):
                 copy.start()
 
@@ -315,15 +335,14 @@
     count = depths - 2
     assert xl == 2 and il % 2 == 0 and count == 2 * SLOTS and cols == 256
     bf16, f32 = jnp.bfloat16, jnp.float32
+    half = count // 2
+    work = half * 1024 * 2 * 256 * 256
     packed_rows = -(-REACH * (depths + 2) // 16) * 16
 
-    vol, send, own, lines, diff_i, diff_x, smooth, diff_h, lines_e, diff_e = call(
-        "pack_kernel",
-        pack_kernel,
+    lines, diff_i, diff_x, smooth, diff_h, lines_e, diff_e, pick = call(
+        "tables_kernel",
+        lambda *refs: tables_kernel(depths, *refs),
         [
-            (volume.shape, bf16),
-            ((TILES, rows, 128), bf16),
-            ((TILES, rows, 128), bf16),
             ((rows, rows), bf16),
             ((rows, rows), bf16),
             ((cols, cols), bf16),
@@ -331,23 +350,24 @@
             ((2, 128 * TILES, 256), bf16),
             ((2 * EDGE, 4 * EDGE), bf16),
             ((4 * EDGE, 4 * EDGE), bf16),
+            ((cols, 256), bf16),
         ],
-        [pltpu.SemaphoreType.DMA],
-        [volume],
-        in_specs=[IN_HBM],
-    )
+        [],
+        [],
+        flops=work,
+    )
+    halo_tile = ((TILES, rows, 128), bf16)
+    vol, send, own = call("pack_kernel", pack_kernel, [(volume.shape, bf16), halo_tile, halo_tile], [], [volume, pick])
     side = lax.ppermute(send, "xl", [(0, 1), (1, 0)])
 
     def own_outs(half):
         return [((half, 6, rows - 2 * EDGE, cols), bf16), ((half, 6, 2 * EDGE, cols), f32)]
 
-    half = count // 2
-    work = half * 1024 * 2 * 256 * 256
     inner_a, part_a = call(
         "lines_kernel",
         lambda *refs: lines_kernel(0, half, *refs),
         own_outs(half),
-        [],
+        [pltpu.VMEM((6, rows, cols), bf16)] * 2,
         [vol, lines, diff_i, diff_x],
         flops=work,
     )
@@ -356,7 +376,8 @@
         rows_kernel,
         [((rows, 128 * TILES), bf16), ((packed_rows, cols), bf16), ((packed_rows, cols), bf16)],
         [pltpu.VMEM((2, packed_rows, cols), f32)],
-        [vol, own, side],
+        [vol, own, side, part_a],
+        in_specs=[WHOLE] * 3 + [pl.BlockSpec(memory_space=pl.ANY)],
     )
     one = [(i, i ^ 1) for i in range(il)]
     two = [pair for i in range(1, il - 1, 2) for pair in ((i, i + 1), (i + 1, i))]
@@ -366,7 +387,7 @@
         "lines_halo_kernel",
         lambda *refs: lines_halo_kernel(half, half, *refs),
         own_outs(half) + [((2, 6, rows, 128), f32)],
-        [],
+        [pltpu.VMEM((6, rows, cols), bf16)] * 2,
         [vol, lines, diff_i, diff_x, halo, diff_h],
         flops=work,
     )

time: 26.5 us -> 24.8 us (0.936)
  the two profiles are of different devices: /device:TPU:12 before, /device:TPU:10 now
where the time goes in v3:
time: 24.8 us; the launch traced here: 24.6 us
  Pallas kernels  16.1 us (65%)
  starting transfers between devices  3.93 us (16%)
  waiting for transfers between devices  3.14 us (13%)
  local copies, waits for them, and re-layouts  0.71 us (3%)
  between operations  0.71 us (3%)
    pallas_call x6, Pallas kernels, call(): pl.pallas_call(kernel, out_shape=tuple((jax.ShapeDtypeStruct(*out) for ou...  16.1 us
    ppermute x1, waiting for transfers between devices, body(): second_in = lax.ppermute(second, 'il', two)  3.14 us
    ppermute x1, starting transfers between devices, body(): second_in = lax.ppermute(second, 'il', two)  2.29 us
    ppermute x1, starting transfers between devices, body(): first_in = lax.ppermute(first, 'il', one)  1.57 us
    unnamed x2, local copies, waits for them, and re-layouts  0.71 us
  transfers between devices with their start and end apart: 3, of which 1 were waited for; matrix products, arithmetic and copies ran while one was open for 0% of the time, Pallas kernels for 18%

profile of v3, /device:TPU:10, one launch (start us, length us, event | category | flops | bytes accessed | tf_op | source)
XLA Modules:
  0.0 24.6 jit_solution(1288000034893296833)
XLA Ops:
  0.6 0.0 copy-start
  0.6 0.5 %tables_kernel.1 = (bf16[128,128]{1,0:T(8,128)(2,1)S(1)}, bf16[128,128]{1,0:T(8,128)(2,1)S(1)}, bf16[256,256]{1,0:T(8,128)(2,1)S(1)}, bf16[8,384,256]{2,1,0:T(8,...) custom-call(), custom_call_target="tpu_custom_call" | custom-call | flops 1073741824 | tf_op jit(solution)/shard_map/tables_kernel/pallas_call | solution.py:320
  1.2 0.7 %copy-done = bf16[18,128,256]{2,1,0:T(8,128)(2,1)S(1)} copy-done((bf16[18,128,256]{2,1,0:T(8,128)(2,1)S(1)}, bf16[18,128,256]{2,1,0:T(8,128)(2,1)}, u32[]{:S(2)}) %copy-start) | copy-done | bytes 1179672
  1.9 0.6 %pack_kernel.1 = (bf16[18,128,256]{2,1,0:T(8,128)(2,1)S(1)}, bf16[3,128,128]{2,1,0:T(8,128)(2,1)S(1)}, bf16[3,128,128]{2,1,0:T(8,128)(2,1)S(1)}) custom-call(bf16[18,128,256]{2,1,0:T(8,128)(2,1)S(1)} %copy-done, bf16[256,256]{1,0:T(8,128)(2,1)S(1)} %get-tuple-element.22.pick_ref), custom_call_target="tpu_custom_call" | custom-call | tf_op jit(solution)/shard_map/pack_kernel/pallas_call | solution.py:320
  2.5 0.1 collective-permute-start
  2.5 1.9 %lines_kernel.1 = (bf16[8,6,96,256]{3,2,1,0:T(8,128)(2,1)S(1)}, f32[8,6,32,256]{3,2,1,0:T(8,128)S(1)}) custom-call(bf16[18,128,256]{2,1,0:T(8,128)(2,1)S(1)} %get-tuple-element.23.refs_0_.vol_ref, bf16[128,128]{1,0:T(8,128)(2,1)S(1)} %get-tuple-element.26.refs_1_, bf16[128,128]{1,0:T(8,128)(2,1)S(1)} %get-tuple-element.27.refs_2_, ...), custom_call_target="tpu_custom_call" | custom-call | flops 1073741824 | tf_op jit(solution)/shard_map/lines_kernel/pallas_call | solution.py:320
  4.5 0.0 collective-permute-done.side_ref
  4.5 0.2 rows_kernel.1
  4.6 1.6 %collective-permute-start.1 = (bf16[208,256]{1,0:T(8,128)(2,1)S(1)}, bf16[208,256]{1,0:T(8,128)(2,1)S(1)}, u32[]{:S(2)}, u32[]{:S(2)}) collective-permute-start(bf16[208,256]{1,0:T(8,128)(2,1)S(1)} %get-tuple-element.31), channel_id=1, source_target_pairs={{0,2},{2,0},{4,6},{6,4},{8,10},{10,8},{12,14},{14,12},{1,3},{3,1},... | collective-permute-start | bytes 319496 | tf_op jit(solution)/shard_map/ppermute | solution.py:384
  6.2 2.3 %collective-permute-start.2 = (bf16[208,256]{1,0:T(8,128)(2,1)S(1)}, bf16[208,256]{1,0:T(8,128)(2,1)S(1)}, u32[]{:S(2)}, u32[]{:S(2)}) collective-permute-start(bf16[208,256]{1,0:T(8,128)(2,1)S(1)} %get-tuple-element.32), channel_id=1, source_target_pairs={{2,4},{4,2},{6,8},{8,6},{10,12},{12,10},{3,5},{5,3},{7,9},{9,7},{1... | collective-permute-start | bytes 319496 | tf_op jit(solution)/shard_map/ppermute | solution.py:385
  8.5 2.4 %lines_halo_kernel.1 = (bf16[8,6,96,256]{3,2,1,0:T(8,128)(2,1)S(1)}, f32[8,6,32,256]{3,2,1,0:T(8,128)S(1)}, f32[2,6,128,128]{3,2,1,0:T(8,128)S(1)}) custom-call(bf16[18,128,256]{2,1,0:T(8,128)(2,1)S(1)} %get-tuple-element.23.refs_0_.vol_ref, bf16[128,128]{1,0:T(8,128)(2,1)S(1)} %get-tuple-element.26.refs_1_, bf16[128,128]{1,0:T(8,128)(2,1)S(1)} %get-tuple-element.27.refs_2_, ...), custom_call_target="tpu_custom_call" | custom-call | flops 1073741824 | tf_op jit(solution)/shard_map/lines_halo_kernel/pallas_call | solution.py:320
  11.0 0.0 collective-permute-done.1.first_ref
  11.0 3.1 %collective-permute-done.2.second_ref = bf16[208,256]{1,0:T(8,128)(2,1)S(1)} collective-permute-done((bf16[208,256]{1,0:T(8,128)(2,1)S(1)}, bf16[208,256]{1,0:T(8,128)(2,1)S(1)}, u32[]{:S(2)}, u32[]{:S(2)}) %collective-permute-start.2) | collective-permute-done | bytes 106528 | tf_op jit(solution)/shard_map/ppermute | solution.py:385
  14.1 10.5 %final_kernel.1 = (f32[16,128,256]{2,1,0:T(8,128)}, f32[16,128,256]{2,1,0:T(8,128)}, f32[16,128,256]{2,1,0:T(8,128)}) custom-call(bf16[18,128,256]{2,1,0:T(8,128)(2,1)S(1)} %get-tuple-element.23.refs_0_.vol_ref, bf16[128,384]{1,0:T(8,128)(2,1)S(1)} %get-tuple-element.30.refs_4_.halo_ref, bf16[208,256]{1,0:T(8,128)(2,1)S(1)} %collective-permute-done.1.first_ref, ...), custom_call_target="tpu_custom_call" | custom-call | flops 4294967296 | tf_op jit(solution)/shard_map/final_kernel/pallas_call | solution.py:320
Async XLA Ops:
  0.6 1.3 %copy-start = (bf16[18,128,256]{2,1,0:T(8,128)(2,1)S(1)}, bf16[18,128,256]{2,1,0:T(8,128)(2,1)}, u32[]{:S(2)}) copy-start(bf16[18,128,256]{2,1,0:T(8,128)(2,1)} %vol_ref.1) | copy-start | bytes 3538948
  2.5 2.0 %collective-permute-start = (bf16[3,128,128]{2,1,0:T(8,128)(2,1)S(1)}, bf16[3,128,128]{2,1,0:T(8,128)(2,1)S(1)}, u32[]{:S(2)}, u32[]{:S(2)}) collective-permute-start(bf16[3,128,128]{2,1,0:T(8,128)(2,1)S(1)} %get-tuple-element.25), channel_id=1, source_target_pairs={{0,1},{1,0},{2,3},{3,2},{4,5},{5,4},{6,7},{7,6},{8,9},{9,8},{10,11... | collective-permute-start | bytes 294920 | tf_op jit(solution)/shard_map/ppermute | solution.py:361
  4.6 6.3 %collective-permute-start.1 = (bf16[208,256]{1,0:T(8,128)(2,1)S(1)}, bf16[208,256]{1,0:T(8,128)(2,1)S(1)}, u32[]{:S(2)}, u32[]{:S(2)}) collective-permute-start(bf16[208,256]{1,0:T(8,128)(2,1)S(1)} %get-tuple-element.31), channel_id=1, source_target_pairs={{0,2},{2,0},{4,6},{6,4},{8,10},{10,8},{12,14},{14,12},{1,3},{3,1},... | collective-permute-start | bytes 319496 | tf_op jit(solution)/shard_map/ppermute | solution.py:384
  6.2 7.9 %collective-permute-start.2 = (bf16[208,256]{1,0:T(8,128)(2,1)S(1)}, bf16[208,256]{1,0:T(8,128)(2,1)S(1)}, u32[]{:S(2)}, u32[]{:S(2)}) collective-permute-start(bf16[208,256]{1,0:T(8,128)(2,1)S(1)} %get-tuple-element.32), channel_id=1, source_target_pairs={{2,4},{4,2},{6,8},{8,6},{10,12},{12,10},{3,5},{5,3},{7,9},{9,7},{1... | collective-permute-start | bytes 319496 | tf_op jit(solution)/shard_map/ppermute | solution.py:385

commit v4 on v3

--- a/solution.py
+++ b/solution.py
@@ -179,6 +179,14 @@
     return [term.astype(jnp.bfloat16) for term in terms]
 
 
+def store_chunks(summed, comp, inner_ref, part_ref):
+    chunks = summed.shape[0] // EDGE
+    for chunk in range(1, chunks - 1):
+        inner_ref[chunk - 1, comp] = summed[EDGE * chunk : EDGE * (chunk + 1)].astype(jnp.bfloat16)
+    part_ref[0, comp] = summed[:EDGE]
+    part_ref[1, comp] = summed[EDGE * (chunks - 1) :]
+
+
 def own_lines(start, count, vol_ref, lines_ref, diff_i_ref, diff_x_ref, inner_ref, part_ref, even_ref, odd_ref):
     rows = vol_ref.shape[1]
 
@@ -194,9 +202,7 @@
     def stage_lines(k, moments_ref):
         for comp in range(6):
             summed = dot(lines_ref[...], moments_ref[comp])
-            inner_ref[k, comp] = summed[EDGE : rows - EDGE].astype(jnp.bfloat16)
-            part_ref[k, comp, :EDGE] = summed[:EDGE]
-            part_ref[k, comp, EDGE:] = summed[rows - EDGE :]
+            store_chunks(summed, comp, inner_ref.at[k], part_ref.at[k])
 
     stage_moments(0, even_ref)
 
@@ -216,32 +222,85 @@
 
 
 def lines_halo_kernel(
-    start, count, vol_ref, lines_ref, diff_i_ref, diff_x_ref, halo_ref, diff_h_ref, inner_ref, part_ref, part_h_ref,
-    even_ref, odd_ref,
+    start, count, vol_ref, lines_ref, diff_i_ref, diff_x_ref, halo_ref, diff_h_ref, rows_ref,
+    inner_ref, part_ref, inner_h_ref, part_h_ref, rows_out_ref, even_ref, odd_ref,
 ):
+    rows_out_ref[...] = rows_ref[...]
     for group in range(2):
         both = dot(halo_ref[...], diff_h_ref[group])
         grad_i = dot(diff_i_ref[...], halo_ref[:, 128 * group : 128 * (group + 1)])
         for comp, term in enumerate(moments(grad_i, both[:, 128:], both[:, :128])):
-            part_h_ref[group, comp] = dot(lines_ref[...], term)
+            store_chunks(dot(lines_ref[...], term), comp, inner_h_ref.at[group], part_h_ref.at[group])
     own_lines(start, count, vol_ref, lines_ref, diff_i_ref, diff_x_ref, inner_ref, part_ref, even_ref, odd_ref)
 
 
+def attributes(own, halo, weights, store):
+    own = own.reshape(-1, own.shape[-1])
+    halo = halo.reshape(-1, halo.shape[-1])
+    tensor = dot(jnp.concatenate([own, halo], axis=1), weights)
+    for chunk in range(tensor.shape[0] // (6 * EDGE)):
+        base = 6 * EDGE * chunk
+        a, b, c, d, e, f = [tensor[base + EDGE * comp : base + EDGE * (comp + 1)] for comp in range(6)]
+        low = c + 1e-6
+        inverse = reciprocal(low)
+        spread = (a - b) * (a - c) + (b - c) * (b - c) + 3.0 * (d * d + e * e + f * f)
+        root = spread * lax.rsqrt(jnp.maximum(spread, TINY))
+        store(chunk, (-e * inverse, -f * inverse, root * reciprocal(a + b + low)))
+
+
+def inner_kernel(inner_a_ref, inner_b_ref, inner_h_ref, smooth_ref, dip_i_ref, dip_x_ref, plan_ref, out_ref, sems):
+    half, chunks = inner_a_ref.shape[:2]
+    inner = EDGE * chunks
+    targets = (dip_i_ref, dip_x_ref, plan_ref)
+
+    def copies(pair):
+        return [
+            pltpu.make_async_copy(
+                out_ref.at[n, pl.ds(half * group + 2 * pair, 2)],
+                target.at[pl.ds(half * group + 2 * pair, 2), pl.ds(EDGE, inner)],
+                sems.at[pair, group, n],
+            )
+            for group in range(2)
+            for n, target in enumerate(targets)
+        ]
+
+    def step(pair, carry):
+        for parity in range(2):
+            k = 2 * pair + parity
+
+            def store(chunk, values):
+                group, row = chunk // chunks, EDGE * (chunk % chunks)
+                for n, value in enumerate(values):
+                    out_ref[n, half * group + k, row : row + EDGE] = value
+
+            own = jnp.concatenate([inner_a_ref[k], inner_b_ref[k]], axis=0)
+            attributes(own, inner_h_ref[...], smooth_ref[k], store)
+        for copy in copies(pair):
+            copy.start()
+        return carry
+
+    lax.fori_loop(0, half // 2, step, 0)
+    for pair in range(half // 2):
+        for copy in copies(pair):
+            copy.wait()
+
+
 def final_kernel(
-    vol_ref, halo_ref, first_ref, second_ref, inner_a_ref, part_a_ref, inner_b_ref, part_b_ref, part_h_ref,
-    smooth_ref, diff_x_ref, diff_h_ref, lines_e_ref, diff_e_ref,
+    vol_ref, halo_ref, first_ref, second_ref, part_a_ref, part_b_ref, part_h_ref,
+    smooth_ref, diff_x_ref, diff_h_ref, lines_e_ref, diff_e_ref, inner_i_ref, inner_x_ref, inner_p_ref,
     dip_i_ref, dip_x_ref, plan_ref,
-    packed_ref, block_ref, block_h_ref, lined_h_ref, edge_a_ref, edge_b_ref,
-    out_i_ref, out_x_ref, out_p_ref, sems,
+    packed_ref, block_ref, block_h_ref, lined_h_ref, even_ref, odd_ref, out_ref, sems,
 ):
     depths, rows, cols = vol_ref.shape
-    count, half = depths - 2, inner_a_ref.shape[0]
-    even = lax.rem(lax.axis_index("il"), 2) == 0
+    half = part_a_ref.shape[0]
+    parts = (part_a_ref, part_b_ref)
+    targets = (dip_i_ref, dip_x_ref, plan_ref)
+    is_even = lax.rem(lax.axis_index("il"), 2) == 0
     bf16 = jnp.bfloat16
 
     first, second = first_ref[...].astype(jnp.float32), second_ref[...].astype(jnp.float32)
-    packed_ref[0] = jnp.where(even, second, first)
-    packed_ref[1] = jnp.where(even, first, second)
+    packed_ref[0] = jnp.where(is_even, second, first)
+    packed_ref[1] = jnp.where(is_even, first, second)
     for depth in range(depths):
         block_ref[depth, :EDGE] = vol_ref[depth, :EDGE]
         block_ref[depth, EDGE : 2 * EDGE] = vol_ref[depth, rows - EDGE :]
@@ -260,63 +319,62 @@
         grad_i = dot(diff_e_ref[...], block_h_ref[:, 128 * group : 128 * (group + 1)])
         for comp, term in enumerate(moments(grad_i, both[:, 128:], both[:, :128])):
             outer = dot(lines_e_ref[...], term)
-            lined_h_ref[group, comp, :EDGE] = (part_h_ref[group, comp, :EDGE] + outer[:EDGE]).astype(bf16)
-            lined_h_ref[group, comp, EDGE : rows - EDGE] = part_h_ref[group, comp, EDGE : rows - EDGE].astype(bf16)
-            lined_h_ref[group, comp, rows - EDGE :] = (part_h_ref[group, comp, rows - EDGE :] + outer[EDGE:]).astype(bf16)
-
-    def copies(z):
-        pairs = ((out_i_ref, dip_i_ref), (out_x_ref, dip_x_ref), (out_p_ref, plan_ref))
-        return [pltpu.make_async_copy(src.at[z], dst.at[z], sems.at[z, n]) for n, (src, dst) in enumerate(pairs)]
-
-    def run(group, inner_ref, part_ref):
-        def stage_edge(k, edge_ref):
+            for end in range(2):
+                summed = part_h_ref[group, end, comp] + outer[EDGE * end : EDGE * (end + 1)]
+                lined_h_ref[group, end, comp] = summed.astype(bf16)
+
+    def stage_edge(k, edge_ref):
+        for group in range(2):
             z = half * group + k
             centre = block_ref[z + 1]
             grad_i = dot(diff_e_ref[...], centre)
             grad_x = dot(centre, diff_x_ref[...])
             grad_z = block_ref[z + 2].astype(jnp.float32) - block_ref[z].astype(jnp.float32)
             for comp, term in enumerate(moments(grad_i, grad_x, grad_z)):
-                edge_ref[comp] = (part_ref[k, comp] + dot(lines_e_ref[...], term)).astype(bf16)
-
-        def stage_attributes(k, edge_ref):
-            z = half * group + k
-            weights = smooth_ref[k]
-
-            def smoothed(comp):
-                own = jnp.concatenate([edge_ref[comp, :EDGE], inner_ref[k, comp], edge_ref[comp, EDGE:]], axis=0)
-                return dot(jnp.concatenate([own, lined_h_ref[group, comp]], axis=1), weights)
-
-            a, b, c, d, e, f = [smoothed(comp) for comp in range(6)]
-            low = c + 1e-6
-            inverse = reciprocal(low)
-            out_i_ref[z] = -e * inverse
-            out_x_ref[z] = -f * inverse
-            spread = (a - b) * (a - c) + (b - c) * (b - c) + 3.0 * (d * d + e * e + f * f)
-            root = spread * lax.rsqrt(jnp.maximum(spread, TINY))
-            out_p_ref[z] = root * reciprocal(a + b + low)
-            for copy in copies(z):
-                copy.start()
-
-        stage_edge(0, edge_a_ref)
-
-        def pair(pair_index, carry):
-            k = 2 * pair_index
-            stage_edge(k + 1, edge_b_ref)
-            stage_attributes(k, edge_a_ref)
-            stage_edge(jnp.minimum(k + 2, half - 1), edge_a_ref)
-            stage_attributes(k + 1, edge_b_ref)
-            return carry
-
-        lax.fori_loop(0, half // 2, pair, 0)
-
-    run(0, inner_a_ref, part_a_ref)
-    run(1, inner_b_ref, part_b_ref)
-    for z in range(count):
-        for copy in copies(z):
+                outer = dot(lines_e_ref[...], term)
+                for end in range(2):
+                    summed = parts[group][k, end, comp] + outer[EDGE * end : EDGE * (end + 1)]
+                    edge_ref[group, end, comp] = summed.astype(bf16)
+
+    def stage_attributes(k, edge_ref):
+        def store(chunk, values):
+            group, end = chunk // 2, chunk % 2
+            for n, value in enumerate(values):
+                out_ref[n, end, half * group + k] = value
+
+        attributes(edge_ref[...], lined_h_ref[...], smooth_ref[k], store)
+
+    def copies(pair):
+        return [
+            pltpu.make_async_copy(
+                out_ref.at[n, end, pl.ds(half * group + 2 * pair, 2)],
+                target.at[pl.ds(half * group + 2 * pair, 2), pl.ds((rows - EDGE) * end, EDGE)],
+                sems.at[pair, group, end, n],
+            )
+            for group in range(2)
+            for end in range(2)
+            for n, target in enumerate(targets)
+        ]
+
+    stage_edge(0, even_ref)
+
+    def step(pair, carry):
+        k = 2 * pair
+        stage_edge(k + 1, odd_ref)
+        stage_attributes(k, even_ref)
+        stage_edge(jnp.minimum(k + 2, half - 1), even_ref)
+        stage_attributes(k + 1, odd_ref)
+        for copy in copies(pair):
+            copy.start()
+        return carry
+
+    lax.fori_loop(0, half // 2, step, 0)
+    for pair in range(half // 2):
+        for copy in copies(pair):
             copy.wait()
 
 
-def call(name, kernel, outs, scratch, operands, in_specs=None, out_specs=None, flops=0, limit=16):
+def call(name, kernel, outs, scratch, operands, in_specs=None, out_specs=None, flops=0, limit=16, aliases={}):
     return pl.pallas_call(
         kernel,
         out_shape=tuple(jax.ShapeDtypeStruct(*out) for out in outs),
@@ -325,6 +383,7 @@
         scratch_shapes=scratch,
         compiler_params=pltpu.CompilerParams(vmem_limit_bytes=limit << 20),
         name=name,
+        input_output_aliases=aliases,
         cost_estimate=pl.CostEstimate(flops=flops, bytes_accessed=0, transcendentals=0),
     )(*operands)
 
@@ -360,13 +419,15 @@
     vol, send, own = call("pack_kernel", pack_kernel, [(volume.shape, bf16), halo_tile, halo_tile], [], [volume, pick])
     side = lax.ppermute(send, "xl", [(0, 1), (1, 0)])
 
-    def own_outs(half):
-        return [((half, 6, rows - 2 * EDGE, cols), bf16), ((half, 6, 2 * EDGE, cols), f32)]
+    chunks = rows // EDGE - 2
+
+    def own_outs(count, lanes):
+        return [((count, chunks, 6, EDGE, lanes), bf16), ((count, 2, 6, EDGE, lanes), f32)]
 
     inner_a, part_a = call(
         "lines_kernel",
         lambda *refs: lines_kernel(0, half, *refs),
-        own_outs(half),
+        own_outs(half, cols),
         [pltpu.VMEM((6, rows, cols), bf16)] * 2,
         [vol, lines, diff_i, diff_x],
         flops=work,
@@ -382,35 +443,45 @@
     one = [(i, i ^ 1) for i in range(il)]
     two = [pair for i in range(1, il - 1, 2) for pair in ((i, i + 1), (i + 1, i))]
     first_in = lax.ppermute(first, "il", one)
-    second_in = lax.ppermute(second, "il", two)
-    inner_b, part_b, part_h = call(
+    inner_b, part_b, inner_h, part_h, second = call(
         "lines_halo_kernel",
         lambda *refs: lines_halo_kernel(half, half, *refs),
-        own_outs(half) + [((2, 6, rows, 128), f32)],
+        own_outs(half, cols) + own_outs(2, 128) + [((packed_rows, cols), bf16)],
         [pltpu.VMEM((6, rows, cols), bf16)] * 2,
-        [vol, lines, diff_i, diff_x, halo, diff_h],
+        [vol, lines, diff_i, diff_x, halo, diff_h, second],
         flops=work,
     )
+    second_in = lax.ppermute(second, "il", two)
+    outs = [((count, rows, cols), f32)] * 3
+    inner_outs = call(
+        "inner_kernel",
+        inner_kernel,
+        outs,
+        [pltpu.VMEM((3, count, rows - 2 * EDGE, cols), f32), pltpu.SemaphoreType.DMA((half // 2, 2, 3))],
+        [inner_a, inner_b, inner_h, smooth],
+        out_specs=(IN_HBM,) * 3,
+        flops=3 * work,
+    )
+    operands = [vol, halo, first_in, second_in, part_a, part_b, part_h, smooth, diff_x, diff_h, lines_e, diff_e]
     return call(
         "final_kernel",
         final_kernel,
-        [((count, rows, cols), f32)] * 3,
+        outs,
         [
             pltpu.VMEM((2, packed_rows, cols), f32),
             pltpu.VMEM((depths, 4 * EDGE, cols), bf16),
             pltpu.VMEM((4 * EDGE, 128 * TILES), bf16),
-            pltpu.VMEM((2, 6, rows, 128), bf16),
-            pltpu.VMEM((6, 2 * EDGE, cols), bf16),
-            pltpu.VMEM((6, 2 * EDGE, cols), bf16),
-            pltpu.VMEM((count, rows, cols), f32),
-            pltpu.VMEM((count, rows, cols), f32),
-            pltpu.VMEM((count, rows, cols), f32),
-            pltpu.SemaphoreType.DMA((count, 3)),
+            pltpu.VMEM((2, 2, 6, EDGE, 128), bf16),
+            pltpu.VMEM((2, 2, 6, EDGE, cols), bf16),
+            pltpu.VMEM((2, 2, 6, EDGE, cols), bf16),
+            pltpu.VMEM((3, 2, count, EDGE, cols), f32),
+            pltpu.SemaphoreType.DMA((half // 2, 2, 2, 3)),
         ],
-        [vol, halo, first_in, second_in, inner_a, part_a, inner_b, part_b, part_h, smooth, diff_x, diff_h, lines_e, diff_e],
+        operands + list(inner_outs),
+        in_specs=[WHOLE] * len(operands) + [IN_HBM] * 3,
         out_specs=(IN_HBM,) * 3,
-        flops=count * 2048 * 2 * 256 * 256,
-        limit=24,
+        flops=work,
+        aliases={len(operands) + n: n for n in range(3)},
     )
 
 

time: 24.8 us -> 23.5 us (0.948)
  the two profiles are of different devices: /device:TPU:10 before, /device:TPU:5 now
where the time goes in v4:
time: 23.5 us; the launch traced here: 23.4 us
  Pallas kernels  16.7 us (71%)
  starting transfers between devices  5.19 us (22%)
  between operations  0.72 us (3%)
  local copies, waits for them, and re-layouts  0.71 us (3%)
    pallas_call x7, Pallas kernels, call(): pl.pallas_call(kernel, out_shape=tuple((jax.ShapeDtypeStruct(*out) for ou...  16.7 us
    ppermute x1, starting transfers between devices, body(): second_in = lax.ppermute(second, 'il', two)  4.38 us
    ppermute x1, starting transfers between devices, body(): side = lax.ppermute(send, 'xl', [(0, 1), (1, 0)])  0.74 us
    unnamed x2, local copies, waits for them, and re-layouts  0.71 us
  transfers between devices with their start and end apart: 3, of which 0 were waited for; matrix products, arithmetic and copies ran while one was open for 0% of the time, Pallas kernels for 40%

profile of v4, /device:TPU:5, one launch (start us, length us, event | category | flops | bytes accessed | tf_op | source)
XLA Modules:
  0.0 23.4 jit_solution(4353247032368977051)
XLA Ops:
  0.6 0.0 copy-start
  0.6 0.5 %tables_kernel.1 = (bf16[128,128]{1,0:T(8,128)(2,1)S(1)}, bf16[128,128]{1,0:T(8,128)(2,1)S(1)}, bf16[256,256]{1,0:T(8,128)(2,1)S(1)}, bf16[8,384,256]{2,1,0:T(8,...) custom-call(), custom_call_target="tpu_custom_call" | custom-call | flops 1073741824 | tf_op jit(solution)/shard_map/tables_kernel/pallas_call | solution.py:378
  1.2 0.7 %copy-done = bf16[18,128,256]{2,1,0:T(8,128)(2,1)S(1)} copy-done((bf16[18,128,256]{2,1,0:T(8,128)(2,1)S(1)}, bf16[18,128,256]{2,1,0:T(8,128)(2,1)}, u32[]{:S(2)}) %copy-start) | copy-done | bytes 1179672
  1.9 0.5 %pack_kernel.1 = (bf16[18,128,256]{2,1,0:T(8,128)(2,1)S(1)}, bf16[3,128,128]{2,1,0:T(8,128)(2,1)S(1)}, bf16[3,128,128]{2,1,0:T(8,128)(2,1)S(1)}) custom-call(bf16[18,128,256]{2,1,0:T(8,128)(2,1)S(1)} %copy-done, bf16[256,256]{1,0:T(8,128)(2,1)S(1)} %get-tuple-element.27.pick_ref), custom_call_target="tpu_custom_call" | custom-call | tf_op jit(solution)/shard_map/pack_kernel/pallas_call | solution.py:378
  2.4 0.7 %collective-permute-start = (bf16[3,128,128]{2,1,0:T(8,128)(2,1)S(1)}, bf16[3,128,128]{2,1,0:T(8,128)(2,1)S(1)}, u32[]{:S(2)}, u32[]{:S(2)}) collective-permute-start(bf16[3,128,128]{2,1,0:T(8,128)(2,1)S(1)} %get-tuple-element.30), channel_id=1, source_target_pairs={{0,1},{1,0},{2,3},{3,2},{4,5},{5,4},{6,7},{7,6},{8,9},{9,8},{10,11... | collective-permute-start | bytes 294920 | tf_op jit(solution)/shard_map/ppermute | solution.py:420
  3.2 1.9 %lines_kernel.1 = (bf16[8,6,6,16,256]{4,3,2,1,0:T(8,128)(2,1)S(1)}, f32[8,2,6,16,256]{4,3,2,1,0:T(8,128)S(1)}) custom-call(bf16[18,128,256]{2,1,0:T(8,128)(2,1)S(1)} %get-tuple-element.28.refs_0_.vol_ref, bf16[128,128]{1,0:T(8,128)(2,1)S(1)} %get-tuple-element.31.refs_1_, bf16[128,128]{1,0:T(8,128)(2,1)S(1)} %get-tuple-element.32.refs_2_, ...), custom_call_target="tpu_custom_call" | custom-call | flops 1073741824 | tf_op jit(solution)/shard_map/lines_kernel/pallas_call | solution.py:378
  5.1 0.0 collective-permute-done.side_ref
  5.1 0.2 rows_kernel.1
  5.3 0.1 collective-permute-start.1
  5.3 2.4 %lines_halo_kernel.1 = (bf16[8,6,6,16,256]{4,3,2,1,0:T(8,128)(2,1)S(1)}, f32[8,2,6,16,256]{4,3,2,1,0:T(8,128)S(1)}, bf16[2,6,6,16,128]{4,3,2,1,0:T(8,128)(2,1)S(...) custom-call(bf16[18,128,256]{2,1,0:T(8,128)(2,1)S(1)} %get-tuple-element.28.refs_0_.vol_ref, ...), custom_call_target="tpu_custom_call" | custom-call | flops 1073741824 | tf_op jit(solution)/shard_map/lines_halo_kernel/pallas_call | solution.py:378
  7.8 4.4 %collective-permute-start.2 = (bf16[208,256]{1,0:T(8,128)(2,1)S(1)}, bf16[208,256]{1,0:T(8,128)(2,1)S(1)}, u32[]{:S(2)}, u32[]{:S(2)}) collective-permute-start(bf16[208,256]{1,0:T(8,128)(2,1)S(1)} %get-tuple-element.39), channel_id=1, source_target_pairs={{2,4},{4,2},{6,8},{8,6},{10,12},{12,10},{3,5},{5,3},{7,9},{9,7},{1... | collective-permute-start | bytes 319496 | tf_op jit(solution)/shard_map/ppermute | solution.py:454
  12.2 4.9 %inner_kernel.1 = (f32[16,128,256]{2,1,0:T(8,128)}, f32[16,128,256]{2,1,0:T(8,128)}, f32[16,128,256]{2,1,0:T(8,128)}) custom-call(bf16[8,6,6,16,256]{4,3,2,1,0:T(8,128)(2,1)S(1)} %get-tuple-element.45.inner_a_ref, bf16[8,6,6,16,256]{4,3,2,1,0:T(8,128)(2,1)S(1)} %get-tuple-element.46.inner_b_ref, ...), custom_call_target="tpu_custom_call" | custom-call | flops 3221225472 | tf_op jit(solution)/shard_map/inner_kernel/pallas_call | solution.py:378
  17.1 0.0 collective-permute-done.1.first_ref
  17.1 0.0 collective-permute-done.2.second_ref
  17.1 6.2 %final_kernel.1 = (f32[16,128,256]{2,1,0:T(8,128)}, f32[16,128,256]{2,1,0:T(8,128)}, f32[16,128,256]{2,1,0:T(8,128)}) custom-call(bf16[18,128,256]{2,1,0:T(8,128)(2,1)S(1)} %get-tuple-element.28.refs_0_.vol_ref, bf16[128,384]{1,0:T(8,128)(2,1)S(1)} %get-tuple-element.35.refs_4_.halo_ref, ...), custom_call_target="tpu_custom_call", output_to_operand_aliasing={{0}: (12, {}), {1}: (13, {}), {2}: (14, {})} | custom-call | flops 1073741824 | tf_op jit(solution)/shard_map/final_kernel/pallas_call | solution.py:378
Async XLA Ops:
  0.6 1.3 %copy-start = (bf16[18,128,256]{2,1,0:T(8,128)(2,1)S(1)}, bf16[18,128,256]{2,1,0:T(8,128)(2,1)}, u32[]{:S(2)}) copy-start(bf16[18,128,256]{2,1,0:T(8,128)(2,1)} %vol_ref.1) | copy-start | bytes 3538948
  2.4 2.7 %collective-permute-start = (bf16[3,128,128]{2,1,0:T(8,128)(2,1)S(1)}, bf16[3,128,128]{2,1,0:T(8,128)(2,1)S(1)}, u32[]{:S(2)}, u32[]{:S(2)}) collective-permute-start(bf16[3,128,128]{2,1,0:T(8,128)(2,1)S(1)} %get-tuple-element.30), channel_id=1, source_target_pairs={{0,1},{1,0},{2,3},{3,2},{4,5},{5,4},{6,7},{7,6},{8,9},{9,8},{10,11... | collective-permute-start | bytes 294920 | tf_op jit(solution)/shard_map/ppermute | solution.py:420
  5.3 11.8 %collective-permute-start.1 = (bf16[208,256]{1,0:T(8,128)(2,1)S(1)}, bf16[208,256]{1,0:T(8,128)(2,1)S(1)}, u32[]{:S(2)}, u32[]{:S(2)}) collective-permute-start(bf16[208,256]{1,0:T(8,128)(2,1)S(1)} %get-tuple-element.36), channel_id=1, source_target_pairs={{0,2},{2,0},{4,6},{6,4},{8,10},{10,8},{12,14},{14,12},{1,3},{3,1},... | collective-permute-start | bytes 319496 | tf_op jit(solution)/shard_map/ppermute | solution.py:445
  7.8 9.3 %collective-permute-start.2 = (bf16[208,256]{1,0:T(8,128)(2,1)S(1)}, bf16[208,256]{1,0:T(8,128)(2,1)S(1)}, u32[]{:S(2)}, u32[]{:S(2)}) collective-permute-start(bf16[208,256]{1,0:T(8,128)(2,1)S(1)} %get-tuple-element.39), channel_id=1, source_target_pairs={{2,4},{4,2},{6,8},{8,6},{10,12},{12,10},{3,5},{5,3},{7,9},{9,7},{1... | collective-permute-start | bytes 319496 | tf_op jit(solution)/shard_map/ppermute | solution.py:454

commit v5 on v4

v5 whole, which is shorter than its diff:
```python
import jax
import jax.numpy as jnp
import ml_dtypes
import numpy as np
from jax import lax
from jax.experimental import pallas as pl
from jax.experimental.pallas import tpu as pltpu
from jax.sharding import PartitionSpec as P

RADIUS = 9
REACH = RADIUS + 1
SIDE = 16
SLOTS = 8
TILES = 3
EDGE = 16
OWN = 2
TINY = float(np.finfo(np.float32).tiny)
FAR = -1000
WHOLE = pl.BlockSpec(memory_space=pltpu.VMEM)
IN_HBM = pl.BlockSpec(memory_space=pltpu.HBM)


def filter_taps():
    offsets = np.arange(2 * RADIUS + 1).astype(np.float32)
    sigma = np.float32(RADIUS / 3.0)
    shape = np.exp(np.float32(-0.5) * ((offsets - RADIUS) / sigma) ** 2)
    return (shape / np.sum(shape, dtype=np.float32)).astype(ml_dtypes.bfloat16).astype(np.float32)


def iota(shape, dim):
    return lax.broadcasted_iota(jnp.int32, shape, dim)


def band(source, target, scale=1.0):
    offset = jnp.abs(source - target)
    weights = jnp.zeros(offset.shape, jnp.float32)
    for distance, tap in enumerate(filter_taps()[RADIUS:]):
        weights = jnp.where(offset == distance, jnp.float32(scale * tap), weights)
    return weights


def difference(source, target):
    offset = source - target
    return jnp.where(offset == 1, 1.0, jnp.where(offset == -1, -1.0, 0.0)).astype(jnp.float32)


def dot(left, right):
    return jnp.dot(left, right, preferred_element_type=jnp.float32)


def reciprocal(value):
    guess = pl.reciprocal(value, approx=True)
    return guess * (2.0 - value * guess)


def halo_plane(lane, tile, depths):
    slot = lax.div(lane, SIDE)
    rest = jnp.where(slot == 0, 0, jnp.where(slot == 1, depths - 1, FAR))
    return jnp.where(tile < 2, 1 + SLOTS * tile + slot, rest)


def halo_column(lane, x, cols):
    place = lax.rem(lane, SIDE)
    return jnp.where(x == 0, cols - OWN + place, place - (SIDE - OWN))


def low_end(exchange):
    even = lax.rem(lax.axis_index("il"), 2) == 0
    return jnp.logical_not(even) if exchange == 0 else even


def tables_kernel(depths, lines_ref, diff_i_ref, diff_x_ref, smooth_ref, pack_h_ref, diff_h_ref, lines_e_ref, diff_e_ref, pick_ref):
    rows, cols = lines_ref.shape[0], diff_x_ref.shape[0]
    x, il, last = lax.axis_index("xl"), lax.axis_index("il"), lax.axis_size("il") - 1
    bf16 = jnp.bfloat16

    target, source = iota((rows, rows), 0), iota((rows, rows), 1)
    inner = (source > 0) & (source < rows - 1)
    lines_ref[...] = jnp.where(inner, band(source, target, 0.25), 0.0).astype(bf16)
    diff_i_ref[...] = difference(source, target).astype(bf16)
    span = EDGE * (depths - 2)
    target, source = iota((span, span), 0), iota((span, span), 1)
    depth = lax.div(source, EDGE) == lax.div(target, EDGE)
    target, source = lax.rem(target, EDGE), lax.rem(source, EDGE)
    diff_e_ref[...] = jnp.where(depth, difference(source, target), 0.0).astype(bf16)
    for exchange in range(2):
        low = low_end(exchange)
        source_at = jnp.where(low, source - REACH, rows - (EDGE - REACH) + source)
        target_at = jnp.where(low, target, rows - EDGE + target)
        first = jnp.where(low & (il > 0), -rows, 0)
        final = jnp.where(jnp.logical_not(low) & (il < last), 2 * rows, rows - 1)
        use = depth & (source_at >= first) & (source_at <= final) & ((source_at <= 0) | (source_at >= rows - 1))
        lines_e_ref[exchange] = jnp.where(use, band(source_at, target_at, 0.25), 0.0).astype(bf16)

    source, target = iota((cols, cols), 0), iota((cols, cols), 1)
    diff_x_ref[...] = difference(source, target).astype(bf16)
    moved = source == jnp.where(x == 0, cols - 1, 0)
    column = lax.rem(target + 128 * x, cols)
    smooth_ref[...] = jnp.where(moved, 0.0, band(source, column)).astype(bf16)
    source, target = iota((256, 256), 0), iota((256, 256), 1)
    place = lax.rem(source, SIDE)
    use = (lax.div(source, SIDE) == lax.div(target, SIDE)) & (place != jnp.where(x == 0, 0, SIDE - 1))
    column = jnp.where(x == 0, cols - SIDE, 0) + lax.rem(target, SIDE)
    pack_h_ref[...] = jnp.where(use, band(halo_column(place, x, cols), column), 0.0).astype(bf16)

    source, target = iota((128, 128), 0), iota((128, 128), 1)
    same = lax.rem(source, SIDE) == lax.rem(target, SIDE)
    across = difference(lax.rem(source, SIDE), lax.rem(target, SIDE))
    for group in range(2):
        centre = halo_plane(target, group, depths)
        for tile in range(TILES):
            plane = halo_plane(source, tile, depths)
            part, out = slice(128 * tile, 128 * (tile + 1)), 128 * group
            diff_h_ref[part, out : out + 128] = jnp.where(same, difference(plane, centre), 0.0).astype(bf16)
            diff_h_ref[part, 256 + out : 384 + out] = jnp.where(plane == centre, across, 0.0).astype(bf16)

    source, lane = iota((cols, 256), 0), iota((cols, 256), 1)
    place = lax.rem(lane, SIDE)
    low, high = place < SIDE - OWN, place >= OWN
    sent = jnp.where(x == 0, jnp.where(low, cols - (SIDE - OWN) + place, FAR), jnp.where(high, place - OWN, FAR))
    low, high = place < OWN, place >= SIDE - OWN
    kept = jnp.where(x == 0, jnp.where(low, cols - OWN + place, FAR), jnp.where(high, place - (SIDE - OWN), FAR))
    pick_ref[...] = jnp.where(source == jnp.where(lane < 128, sent, kept), 1.0, 0.0).astype(bf16)


def pack_kernel(vol_ref, pick_ref, copy_ref, send_ref, own_ref):
    depths, rows, cols = vol_ref.shape
    slot = lax.div(lax.rem(iota((rows, 256), 1), 128), SIDE)
    copy_ref[...] = vol_ref[...]
    for tile in range(TILES):
        if tile < 2:
            planes = [(1 + SLOTS * tile + index, index) for index in range(SLOTS)]
        else:
            planes = [(0, 0), (depths - 1, 1)]
        packed = jnp.zeros((rows, 256), jnp.float32)
        for plane, index in planes:
            packed = jnp.where(slot == index, dot(vol_ref[plane], pick_ref[...]), packed)
        packed = packed.astype(jnp.bfloat16)
        send_ref[tile] = packed[:, :128]
        own_ref[tile] = packed[:, 128:]


def rows_kernel(vol_ref, own_ref, side_ref, halo_ref, first_ref, second_ref, packed_ref):
    depths, rows, cols = vol_ref.shape
    even = lax.rem(lax.axis_index("il"), 2) == 0

    def put(row, top, bottom):
        top, bottom = top[:REACH], bottom[EDGE - REACH :]
        lanes = top.shape[1]
        packed_ref[0, row : row + REACH, :lanes] = jnp.where(even, bottom, top)
        packed_ref[1, row : row + REACH, :lanes] = jnp.where(even, top, bottom)

    packed_ref[:, depths * REACH :, :] = jnp.zeros_like(packed_ref[:, depths * REACH :, :])
    for depth in range(depths):
        top = vol_ref[depth, :EDGE, :].astype(jnp.float32)
        bottom = vol_ref[depth, rows - EDGE :, :].astype(jnp.float32)
        put(REACH * depth, top, bottom)
    tiles = []
    for tile in range(TILES):
        merged = own_ref[tile].astype(jnp.float32) + side_ref[tile].astype(jnp.float32)
        halo_ref[:, 128 * tile : 128 * (tile + 1)] = merged.astype(jnp.bfloat16)
        tiles.append((merged[:EDGE], merged[rows - EDGE :]))
    tops = jnp.concatenate([tiles[0][0], tiles[1][0]], axis=1)
    bottoms = jnp.concatenate([tiles[0][1], tiles[1][1]], axis=1)
    put(REACH * depths, tops, bottoms)
    put(REACH * (depths + 1), *tiles[2])
    first_ref[...] = packed_ref[0].astype(jnp.bfloat16)
    second_ref[...] = packed_ref[1].astype(jnp.bfloat16)


def moments(grad_i, grad_x, grad_z):
    terms = (
        grad_i * grad_i,
        grad_x * grad_x,
        grad_z * grad_z,
        grad_i * grad_x,
        grad_i * grad_z,
        grad_x * grad_z,
    )
    return [term.astype(jnp.bfloat16) for term in terms]


def store_chunks(summed, comp, inner_ref, part_ref):
    chunks = summed.shape[0] // EDGE
    for chunk in range(1, chunks - 1):
        inner_ref[chunk - 1, comp] = summed[EDGE * chunk : EDGE * (chunk + 1)].astype(jnp.bfloat16)
    part_ref[0, comp] = summed[:EDGE]
    part_ref[1, comp] = summed[EDGE * (chunks - 1) :]


def lines_kernel(
    vol_ref, halo_ref, rows_ref, lines_ref, diff_i_ref, diff_x_ref, diff_h_ref,
    inner_ref, part_ref, inner_h_ref, part_h_ref, rows_out_ref, even_ref, odd_ref,
):
    depths, rows, cols = vol_ref.shape
    count = depths - 2
    rows_out_ref[...] = rows_ref[...]
    both = dot(halo_ref[...], diff_h_ref[...])
    grad_i = dot(diff_i_ref[...], halo_ref[:, :256])
    for comp, term in enumerate(moments(grad_i, both[:, 256:], both[:, :256])):
        store_chunks(dot(lines_ref[...], term), comp, inner_h_ref, part_h_ref)

    def stage_moments(z, moments_ref):
        centre = vol_ref[pl.ds(z + 1, 2)]
        across = dot(centre.reshape(2 * rows, cols), diff_x_ref[...])
        for k in range(2):
            grad_i = dot(diff_i_ref[...], centre[k])
            grad_x = across[rows * k : rows * (k + 1)]
            grad_z = vol_ref[z + k + 2].astype(jnp.float32) - vol_ref[z + k].astype(jnp.float32)
            for comp, term in enumerate(moments(grad_i, grad_x, grad_z)):
                moments_ref[k, comp] = term

    def stage_lines(z, moments_ref):
        for k in range(2):
            for comp in range(6):
                store_chunks(dot(lines_ref[...], moments_ref[k, comp]), comp, inner_ref.at[z + k], part_ref.at[:, :, z + k])

    stage_moments(0, even_ref)

    def step(index, carry):
        z = 4 * index
        stage_moments(z + 2, odd_ref)
        stage_lines(z, even_ref)
        stage_moments(jnp.minimum(z + 4, count - 2), even_ref)
        stage_lines(z + 2, odd_ref)
        return carry

    lax.fori_loop(0, count // 4, step, 0)


def attributes(own, border, smooth_ref, store):
    x = lax.axis_index("xl")
    tensor = dot(own, smooth_ref[...])
    halves = (tensor[:, :128], tensor[:, 128:] + border)
    lanes = (pl.multiple_of(128 * x, 128), pl.multiple_of(128 - 128 * x, 128))
    for chunk in range(own.shape[0] // (6 * EDGE)):
        base = 6 * EDGE * chunk
        for half, lane in zip(halves, lanes):
            a, b, c, d, e, f = [half[base + EDGE * comp : base + EDGE * (comp + 1)] for comp in range(6)]
            low = c + 1e-6
            inverse = reciprocal(low)
            spread = (a - b) * (a - c) + (b - c) * (b - c) + 3.0 * (d * d + e * e + f * f)
            root = spread * lax.rsqrt(jnp.maximum(spread, TINY))
            store(chunk, pl.ds(lane, 128), (-e * inverse, -f * inverse, root * reciprocal(a + b + low)))


def border_of(packed, slot):
    base = jnp.where(lax.axis_index("xl") == 0, 128 - SIDE, 0)
    moved = pltpu.roll(packed, lax.rem(base - SIDE * slot + 128, 128), 1)
    return jnp.where(lax.div(iota(packed.shape, 1), SIDE) == lax.div(base, SIDE), moved, 0.0)


def inner_kernel(inner_ref, inner_h_ref, smooth_ref, pack_h_ref, dip_i_ref, dip_x_ref, plan_ref, border_ref, out_ref, sems):
    count, chunks = inner_ref.shape[:2]
    half, inner = count // 2, EDGE * chunks
    targets = (dip_i_ref, dip_x_ref, plan_ref)
    border_ref[...] = dot(inner_h_ref[...].reshape(6 * inner, 256), pack_h_ref[...])

    def copies(pair):
        return [
            pltpu.make_async_copy(
                out_ref.at[n, pl.ds(half * group + 2 * pair, 2)],
                target.at[pl.ds(half * group + 2 * pair, 2), pl.ds(EDGE, inner)],
                sems.at[pair, group, n],
            )
            for group in range(2)
            for n, target in enumerate(targets)
        ]

    def step(pair, carry):
        for parity in range(2):
            k = 2 * pair + parity
            for group in range(2):

                def store(chunk, lanes, values):
                    for n, value in enumerate(values):
                        out_ref[n, half * group + k, EDGE * chunk : EDGE * (chunk + 1), lanes] = value

                border = border_of(border_ref[:, 128 * group : 128 * (group + 1)], k)
                attributes(inner_ref[half * group + k].reshape(6 * inner, 256), border, smooth_ref, store)
        for copy in copies(pair):
            copy.start()
        return carry

    lax.fori_loop(0, half // 2, step, 0)
    for pair in range(half // 2):
        for copy in copies(pair):
            copy.wait()


def end_kernel(
    exchange, vol_ref, halo_ref, rows_ref, part_ref, part_h_ref,
    smooth_ref, pack_h_ref, diff_x_ref, diff_h_ref, lines_e_ref, diff_e_ref, in_i_ref, in_x_ref, in_p_ref,
    dip_i_ref, dip_x_ref, plan_ref,
    packed_ref, block_ref, block_h_ref, border_ref, edge_ref, out_ref, sems,
):
    depths, rows, cols = vol_ref.shape
    count, half = depths - 2, (depths - 2) // 2
    bf16, f32 = jnp.bfloat16, jnp.float32
    low = low_end(exchange)
    end = jnp.where(low, 0, 1)
    start = pl.multiple_of(jnp.where(low, 0, rows - EDGE), EDGE)
    targets = (dip_i_ref, dip_x_ref, plan_ref)

    packed_ref[:8] = jnp.zeros_like(packed_ref[:8])
    packed_ref[8:] = rows_ref[...].astype(f32)

    def joined(row, own):
        lanes = own.shape[1]
        before = packed_ref[8 + row : 8 + row + EDGE, :lanes]
        after = packed_ref[8 + row - (EDGE - REACH) : 8 + row + REACH, :lanes]
        own = own.astype(f32)
        place = iota(own.shape, 0)
        first = jnp.where(place < REACH, before, pltpu.roll(own, REACH, 0))
        second = jnp.where(place < EDGE - REACH, pltpu.roll(own, EDGE - REACH, 0), after)
        return jnp.where(low, first, second).astype(bf16)

    for depth in range(depths):
        block_ref[depth] = joined(REACH * depth, vol_ref[depth, pl.ds(start, EDGE)])
    own_h = halo_ref[pl.ds(start, EDGE)]
    block_h_ref[:, :256] = joined(REACH * depths, own_h[:, :256])
    block_h_ref[:, 256:] = joined(REACH * (depths + 1), own_h[:, 256:])

    both = dot(block_h_ref[...], diff_h_ref[...])
    grad_i = dot(diff_e_ref[:EDGE, :EDGE], block_h_ref[:, :256])
    lined_h = []
    for comp, term in enumerate(moments(grad_i, both[:, 256:], both[:, :256])):
        summed = part_h_ref[end, comp] + dot(lines_e_ref[exchange, :EDGE, :EDGE], term)
        lined_h.append(summed.astype(bf16))
    border_ref[...] = dot(jnp.concatenate(lined_h, axis=0), pack_h_ref[...])

    centre = block_ref[1 : count + 1].reshape(count * EDGE, cols)
    grad_i = dot(diff_e_ref[...], centre)
    grad_x = dot(centre, diff_x_ref[...])
    grad_z = block_ref[2:].astype(f32) - block_ref[:count].astype(f32)
    for comp, term in enumerate(moments(grad_i, grad_x, grad_z.reshape(count * EDGE, cols))):
        outer = dot(lines_e_ref[exchange], term)
        summed = part_ref[end, comp] + outer.reshape(count, EDGE, cols)
        edge_ref[:, comp] = summed.astype(bf16)

    def copies(pair):
        return [
            pltpu.make_async_copy(
                out_ref.at[n, pl.ds(half * group + 2 * pair, 2)],
                target.at[pl.ds(half * group + 2 * pair, 2), pl.ds(start, EDGE)],
                sems.at[pair, group, n],
            )
            for group in range(2)
            for n, target in enumerate(targets)
        ]

    def step(pair, carry):
        own, border, places = [], [], []
        for group in range(2):
            for parity in range(2):
                k = 2 * pair + parity
                places.append(half * group + k)
                own.append(edge_ref[half * group + k].reshape(6 * EDGE, cols))
                border.append(border_of(border_ref[:, 128 * group : 128 * (group + 1)], k))

        def store(chunk, lanes, values):
            for n, value in enumerate(values):
                out_ref[n, places[chunk], :, lanes] = value

        attributes(jnp.concatenate(own, axis=0), jnp.concatenate(border, axis=0), smooth_ref, store)
        for copy in copies(pair):
            copy.start()
        return carry

    lax.fori_loop(0, half // 2, step, 0)
    for pair in range(half // 2):
        for copy in copies(pair):
            copy.wait()


def call(name, kernel, outs, scratch, operands, in_specs=None, out_specs=None, flops=0, limit=16, aliases={}):
    return pl.pallas_call(
        kernel,
        out_shape=tuple(jax.ShapeDtypeStruct(*out) for out in outs),
        in_specs=in_specs or [WHOLE] * len(operands),
        out_specs=out_specs or (WHOLE,) * len(outs),
        scratch_shapes=scratch,
        compiler_params=pltpu.CompilerParams(vmem_limit_bytes=limit << 20),
        name=name,
        input_output_aliases=aliases,
        cost_estimate=pl.CostEstimate(flops=flops, bytes_accessed=0, transcendentals=0),
    )(*operands)


def body(volume):
    depths, rows, cols = volume.shape
    il, xl = lax.axis_size("il"), lax.axis_size("xl")
    count = depths - 2
    assert xl == 2 and il % 2 == 0 and count == 2 * SLOTS and cols == 256
    bf16, f32 = jnp.bfloat16, jnp.float32
    half = count // 2
    work = half * 1024 * 2 * 256 * 256
    packed_rows = -(-REACH * (depths + 2) // 16) * 16

    span = EDGE * count
    lines, diff_i, diff_x, smooth, pack_h, diff_h, lines_e, diff_e, pick = call(
        "tables_kernel",
        lambda *refs: tables_kernel(depths, *refs),
        [
            ((rows, rows), bf16),
            ((rows, rows), bf16),
            ((cols, cols), bf16),
            ((cols, cols), bf16),
            ((256, 256), bf16),
            ((128 * TILES, 512), bf16),
            ((2, span, span), bf16),
            ((span, span), bf16),
            ((cols, 256), bf16),
        ],
        [],
        [],
        flops=work,
    )
    halo_tile = ((TILES, rows, 128), bf16)
    vol, send, own = call("pack_kernel", pack_kernel, [(volume.shape, bf16), halo_tile, halo_tile], [], [volume, pick])
    side = lax.ppermute(send, "xl", [(0, 1), (1, 0)])
    packed = ((packed_rows, cols), bf16)
    halo, first, second = call(
        "rows_kernel",
        rows_kernel,
        [((rows, 128 * TILES), bf16), packed, packed],
        [pltpu.VMEM((2, packed_rows, cols), f32)],
        [vol, own, side],
    )
    one = [(i, i ^ 1) for i in range(il)]
    two = [pair for i in range(1, il - 1, 2) for pair in ((i, i + 1), (i + 1, i))]
    second_in = lax.ppermute(second, "il", two)
    chunks = rows // EDGE - 2
    inner, part, inner_h, part_h, first = call(
        "lines_kernel",
        lines_kernel,
        [
            ((count, chunks, 6, EDGE, cols), bf16),
            ((2, 6, count, EDGE, cols), f32),
            ((chunks, 6, EDGE, 256), bf16),
            ((2, 6, EDGE, 256), f32),
            packed,
        ],
        [pltpu.VMEM((2, 6, rows, cols), bf16)] * 2,
        [vol, halo, first, lines, diff_i, diff_x, diff_h],
        flops=2 * work,
    )
    first_in = lax.ppermute(first, "il", one)
    shapes = [((count, rows, cols), f32)] * 3
    sems = pltpu.SemaphoreType.DMA((half // 2, 2, 3))
    outs = call(
        "inner_kernel",
        inner_kernel,
        shapes,
        [pltpu.VMEM((6 * EDGE * chunks, 256), f32), pltpu.VMEM((3, count, EDGE * chunks, cols), f32), sems],
        [inner, inner_h, smooth, pack_h],
        out_specs=(IN_HBM,) * 3,
        flops=2 * work,
    )
    tables = [smooth, pack_h, diff_x, diff_h, lines_e, diff_e]
    for exchange, received in ((1, second_in), (0, first_in)):
        operands = [vol, halo, received, part, part_h, *tables]
        outs = call(
            "end_kernel",
            lambda *refs, exchange=exchange: end_kernel(exchange, *refs),
            shapes,
            [
                pltpu.VMEM((8 + packed_rows, cols), f32),
                pltpu.VMEM((depths, EDGE, cols), bf16),
                pltpu.VMEM((EDGE, 128 * TILES), bf16),
                pltpu.VMEM((6 * EDGE, 256), f32),
                pltpu.VMEM((count, 6, EDGE, cols), bf16),
                pltpu.VMEM((3, count, EDGE, cols), f32),
                sems,
            ],
            operands + list(outs),
            in_specs=[WHOLE] * len(operands) + [IN_HBM] * 3,
            out_specs=(IN_HBM,) * 3,
            flops=work,
            aliases={len(operands) + n: n for n in range(3)},
        )
    return outs


def solution(mesh):
    spec = P(None, ("parts", "il"), "xl")
    return jax.shard_map(body, mesh=mesh, in_specs=(spec,), out_specs=(spec,) * 3, check_vma=False)
```

time: 23.5 us -> 24.3 us (1.034)
  the two profiles are of different devices: /device:TPU:5 before, /device:TPU:0 now
where the time goes in v5:
time: 24.3 us; the launch traced here: 24.2 us
  Pallas kernels  15.3 us (63%)
  starting transfers between devices  6.87 us (28%)
  waiting for transfers between devices  0.95 us (4%)
  between operations  0.71 us (3%)
  local copies, waits for them, and re-layouts  0.31 us (1%)
    pallas_call x7, Pallas kernels, call(): pl.pallas_call(kernel, out_shape=tuple((jax.ShapeDtypeStruct(*out) for ou...  15.3 us
    ppermute x1, starting transfers between devices, body(): first_in = lax.ppermute(first, 'il', one)  5.69 us
    ppermute x1, waiting for transfers between devices, body(): side = lax.ppermute(send, 'xl', [(0, 1), (1, 0)])  0.94 us
    ppermute x1, starting transfers between devices, body(): second_in = lax.ppermute(second, 'il', two)  0.67 us
    ppermute x1, starting transfers between devices, body(): side = lax.ppermute(send, 'xl', [(0, 1), (1, 0)])  0.52 us
  transfers between devices with their start and end apart: 3, of which 1 were waited for; matrix products, arithmetic and copies ran while one was open for 0% of the time, Pallas kernels for 45%

profile of v5, /device:TPU:0, one launch (start us, length us, event | category | flops | bytes accessed | tf_op | source)
XLA Modules:
  0.0 24.2 jit_solution(14735834562968536913)
XLA Ops:
  0.6 0.0 copy-start
  0.6 1.0 %tables_kernel.1 = (bf16[128,128]{1,0:T(8,128)(2,1)S(1)}, bf16[128,128]{1,0:T(8,128)(2,1)S(1)}, bf16[256,256]{1,0:T(8,128)(2,1)S(1)}, bf16[256,256]{1,0:T(8,128)...) custom-call(), custom_call_target="tpu_custom_call" | custom-call | flops 1073741824 | tf_op jit(solution)/shard_map/tables_kernel/pallas_call | solution.py:377
  1.6 0.3 %copy-done = bf16[18,128,256]{2,1,0:T(8,128)(2,1)S(1)} copy-done((bf16[18,128,256]{2,1,0:T(8,128)(2,1)S(1)}, bf16[18,128,256]{2,1,0:T(8,128)(2,1)}, u32[]{:S(2)}) %copy-start) | copy-done | bytes 1179672
  1.9 0.5 %pack_kernel.1 = (bf16[18,128,256]{2,1,0:T(8,128)(2,1)S(1)}, bf16[3,128,128]{2,1,0:T(8,128)(2,1)S(1)}, bf16[3,128,128]{2,1,0:T(8,128)(2,1)S(1)}) custom-call(bf16[18,128,256]{2,1,0:T(8,128)(2,1)S(1)} %copy-done, bf16[256,256]{1,0:T(8,128)(2,1)S(1)} %get-tuple-element.29.pick_ref), custom_call_target="tpu_custom_call" | custom-call | tf_op jit(solution)/shard_map/pack_kernel/pallas_call | solution.py:377
  2.4 0.5 %collective-permute-start = (bf16[3,128,128]{2,1,0:T(8,128)(2,1)S(1)}, bf16[3,128,128]{2,1,0:T(8,128)(2,1)S(1)}, u32[]{:S(2)}, u32[]{:S(2)}) collective-permute-start(bf16[3,128,128]{2,1,0:T(8,128)(2,1)S(1)} %get-tuple-element.32), channel_id=1, source_target_pairs={{0,1},{1,0},{2,3},{3,2},{4,5},{5,4},{6,7},{7,6},{8,9},{9,8},{10,11... | collective-permute-start | bytes 294920 | tf_op jit(solution)/shard_map/ppermute | solution.py:421
  3.0 0.9 %collective-permute-done.side_ref = bf16[3,128,128]{2,1,0:T(8,128)(2,1)S(1)} collective-permute-done((bf16[3,128,128]{2,1,0:T(8,128)(2,1)S(1)}, bf16[3,128,128]{2,1,0:T(8,128)(2,1)S(1)}, u32[]{:S(2)}, u32[]{:S(2)}) %collective-permute-start) | collective-permute-done | bytes 98336 | tf_op jit(solution)/shard_map/ppermute | solution.py:421
  3.9 0.1 rows_kernel.1
  4.0 0.7 %collective-permute-start.2 = (bf16[208,256]{1,0:T(8,128)(2,1)S(1)}, bf16[208,256]{1,0:T(8,128)(2,1)S(1)}, u32[]{:S(2)}, u32[]{:S(2)}) collective-permute-start(bf16[208,256]{1,0:T(8,128)(2,1)S(1)} %get-tuple-element.46), channel_id=1, source_target_pairs={{2,4},{4,2},{6,8},{8,6},{10,12},{12,10},{3,5},{5,3},{7,9},{9,7},{1... | collective-permute-start | bytes 319496 | tf_op jit(solution)/shard_map/ppermute | solution.py:432
  4.7 3.4 %lines_kernel.1 = (bf16[16,6,6,16,256]{4,3,2,1,0:T(8,128)(2,1)S(1)}, f32[2,6,16,16,256]{4,3,2,1,0:T(8,128)S(1)}, bf16[6,6,16,256]{3,2,1,0:T(8,128)(2,1)S(1)}, f3...) custom-call(bf16[18,128,256]{2,1,0:T(8,128)(2,1)S(1)} %get-tuple-element.30.vol_ref.refs_0_, ...), custom_call_target="tpu_custom_call" | custom-call | flops 2147483648 | tf_op jit(solution)/shard_map/lines_kernel/pallas_call | solution.py:377
  8.2 5.7 %collective-permute-start.1 = (bf16[208,256]{1,0:T(8,128)(2,1)S(1)}, bf16[208,256]{1,0:T(8,128)(2,1)S(1)}, u32[]{:S(2)}, u32[]{:S(2)}) collective-permute-start(bf16[208,256]{1,0:T(8,128)(2,1)S(1)} %get-tuple-element.39), channel_id=1, source_target_pairs={{0,2},{2,0},{4,6},{6,4},{8,10},{10,8},{12,14},{14,12},{1,3},{3,1},... | collective-permute-start | bytes 319496 | tf_op jit(solution)/shard_map/ppermute | solution.py:448
  13.9 4.6 %inner_kernel.1 = (f32[16,128,256]{2,1,0:T(8,128)}, f32[16,128,256]{2,1,0:T(8,128)}, f32[16,128,256]{2,1,0:T(8,128)}) custom-call(bf16[16,6,6,16,256]{4,3,2,1,0:T(8,128)(2,1)S(1)} %get-tuple-element.47.inner_ref, bf16[6,6,16,256]{3,2,1,0:T(8,128)(2,1)S(1)} %get-tuple-element.48.inner_h_ref, bf16[256,256]{1,0:T(8,128)(2,1)S(1)} %get-tuple-element.42.smooth_ref.refs_5_, ...), custom_call_target="tpu_custom_call" | custom-call | flops 2147483648 | tf_op jit(solution)/shard_map/inner_kernel/pallas_call | solution.py:377
  18.4 0.0 collective-permute-done.2.refs_2_
  18.4 2.8 %end_kernel.2 = (f32[16,128,256]{2,1,0:T(8,128)}, f32[16,128,256]{2,1,0:T(8,128)}, f32[16,128,256]{2,1,0:T(8,128)}) custom-call(bf16[18,128,256]{2,1,0:T(8,128)(2,1)S(1)} %get-tuple-element.30.vol_ref.refs_0_, bf16[128,384]{1,0:T(8,128)(2,1)S(1)} %get-tuple-element.33.halo_ref.refs_1_, ...), custom_call_target="tpu_custom_call", output_to_operand_aliasing={{0}: (11, {}), {1}: (12, {}), {2}: (13, {})} | custom-call | flops 1073741824 | tf_op jit(solution)/shard_map/end_kernel/pallas_call | solution.py:377
  21.3 0.0 collective-permute-done.1.refs_2_
  21.3 2.8 %end_kernel.3 = (f32[16,128,256]{2,1,0:T(8,128)}, f32[16,128,256]{2,1,0:T(8,128)}, f32[16,128,256]{2,1,0:T(8,128)}) custom-call(bf16[18,128,256]{2,1,0:T(8,128)(2,1)S(1)} %get-tuple-element.30.vol_ref.refs_0_, bf16[128,384]{1,0:T(8,128)(2,1)S(1)} %get-tuple-element.33.halo_ref.refs_1_, ...), custom_call_target="tpu_custom_call", output_to_operand_aliasing={{0}: (11, {}), {1}: (12, {}), {2}: (13, {})} | custom-call | flops 1073741824 | tf_op jit(solution)/shard_map/end_kernel/pallas_call | solution.py:377
Async XLA Ops:
  0.6 1.3 %copy-start = (bf16[18,128,256]{2,1,0:T(8,128)(2,1)S(1)}, bf16[18,128,256]{2,1,0:T(8,128)(2,1)}, u32[]{:S(2)}) copy-start(bf16[18,128,256]{2,1,0:T(8,128)(2,1)} %vol_ref.1) | copy-start | bytes 3538948
  2.4 1.5 %collective-permute-start = (bf16[3,128,128]{2,1,0:T(8,128)(2,1)S(1)}, bf16[3,128,128]{2,1,0:T(8,128)(2,1)S(1)}, u32[]{:S(2)}, u32[]{:S(2)}) collective-permute-start(bf16[3,128,128]{2,1,0:T(8,128)(2,1)S(1)} %get-tuple-element.32), channel_id=1, source_target_pairs={{0,1},{1,0},{2,3},{3,2},{4,5},{5,4},{6,7},{7,6},{8,9},{9,8},{10,11... | collective-permute-start | bytes 294920 | tf_op jit(solution)/shard_map/ppermute | solution.py:421
  4.0 14.4 %collective-permute-start.2 = (bf16[208,256]{1,0:T(8,128)(2,1)S(1)}, bf16[208,256]{1,0:T(8,128)(2,1)S(1)}, u32[]{:S(2)}, u32[]{:S(2)}) collective-permute-start(bf16[208,256]{1,0:T(8,128)(2,1)S(1)} %get-tuple-element.46), channel_id=1, source_target_pairs={{2,4},{4,2},{6,8},{8,6},{10,12},{12,10},{3,5},{5,3},{7,9},{9,7},{1... | collective-permute-start | bytes 319496 | tf_op jit(solution)/shard_map/ppermute | solution.py:432
  8.2 13.1 %collective-permute-start.1 = (bf16[208,256]{1,0:T(8,128)(2,1)S(1)}, bf16[208,256]{1,0:T(8,128)(2,1)S(1)}, u32[]{:S(2)}, u32[]{:S(2)}) collective-permute-start(bf16[208,256]{1,0:T(8,128)(2,1)S(1)} %get-tuple-element.39), channel_id=1, source_target_pairs={{0,2},{2,0},{4,6},{6,4},{8,10},{10,8},{12,14},{14,12},{1,3},{3,1},... | collective-permute-start | bytes 319496 | tf_op jit(solution)/shard_map/ppermute | solution.py:448

commit v6 on v5

--- a/solution.py
+++ b/solution.py
@@ -15,9 +15,11 @@
 EDGE = 16
 OWN = 2
 TINY = float(np.finfo(np.float32).tiny)
+HEAD = 4
 FAR = -1000
 WHOLE = pl.BlockSpec(memory_space=pltpu.VMEM)
 IN_HBM = pl.BlockSpec(memory_space=pltpu.HBM)
+ANYWHERE = pl.BlockSpec(memory_space=pl.ANY)
 
 
 def filter_taps():
@@ -140,7 +142,7 @@
         own_ref[tile] = packed[:, 128:]
 
 
-def rows_kernel(vol_ref, own_ref, side_ref, halo_ref, first_ref, second_ref, packed_ref):
+def rows_kernel(vol_ref, own_ref, side_ref, after_ref, halo_ref, ends_ref, packed_ref):
     depths, rows, cols = vol_ref.shape
     even = lax.rem(lax.axis_index("il"), 2) == 0
 
@@ -164,8 +166,11 @@
     bottoms = jnp.concatenate([tiles[0][1], tiles[1][1]], axis=1)
     put(REACH * depths, tops, bottoms)
     put(REACH * (depths + 1), *tiles[2])
-    first_ref[...] = packed_ref[0].astype(jnp.bfloat16)
-    second_ref[...] = packed_ref[1].astype(jnp.bfloat16)
+    ends_ref[...] = packed_ref[...].astype(jnp.bfloat16)
+
+
+def relay_kernel(ends_ref, after_ref, out_ref):
+    out_ref[...] = ends_ref[1]
 
 
 def moments(grad_i, grad_x, grad_z):
@@ -188,17 +193,24 @@
     part_ref[1, comp] = summed[EDGE * (chunks - 1) :]
 
 
-def lines_kernel(
-    vol_ref, halo_ref, rows_ref, lines_ref, diff_i_ref, diff_x_ref, diff_h_ref,
-    inner_ref, part_ref, inner_h_ref, part_h_ref, rows_out_ref, even_ref, odd_ref,
+def lines_kernel(vol_ref, lines_ref, diff_i_ref, diff_x_ref, inner_ref, part_ref, even_ref, odd_ref):
+    own_lines(0, HEAD, vol_ref, lines_ref, diff_i_ref, diff_x_ref, inner_ref, part_ref, even_ref, odd_ref)
+
+
+def more_lines_kernel(
+    vol_ref, halo_ref, lines_ref, diff_i_ref, diff_x_ref, diff_h_ref, inner_in_ref, part_in_ref,
+    inner_ref, part_ref, inner_h_ref, part_h_ref, even_ref, odd_ref,
 ):
-    depths, rows, cols = vol_ref.shape
-    count = depths - 2
-    rows_out_ref[...] = rows_ref[...]
     both = dot(halo_ref[...], diff_h_ref[...])
     grad_i = dot(diff_i_ref[...], halo_ref[:, :256])
     for comp, term in enumerate(moments(grad_i, both[:, 256:], both[:, :256])):
         store_chunks(dot(lines_ref[...], term), comp, inner_h_ref, part_h_ref)
+    stop = vol_ref.shape[0] - 2
+    own_lines(HEAD, stop, vol_ref, lines_ref, diff_i_ref, diff_x_ref, inner_ref, part_ref, even_ref, odd_ref)
+
+
+def own_lines(first, stop, vol_ref, lines_ref, diff_i_ref, diff_x_ref, inner_ref, part_ref, even_ref, odd_ref):
+    depths, rows, cols = vol_ref.shape
 
     def stage_moments(z, moments_ref):
         centre = vol_ref[pl.ds(z + 1, 2)]
@@ -215,17 +227,17 @@
             for comp in range(6):
                 store_chunks(dot(lines_ref[...], moments_ref[k, comp]), comp, inner_ref.at[z + k], part_ref.at[:, :, z + k])
 
-    stage_moments(0, even_ref)
+    stage_moments(first, even_ref)
 
     def step(index, carry):
-        z = 4 * index
+        z = first + 4 * index
         stage_moments(z + 2, odd_ref)
         stage_lines(z, even_ref)
-        stage_moments(jnp.minimum(z + 4, count - 2), even_ref)
+        stage_moments(jnp.minimum(z + 4, stop - 2), even_ref)
         stage_lines(z + 2, odd_ref)
         return carry
 
-    lax.fori_loop(0, count // 4, step, 0)
+    lax.fori_loop(0, (stop - first) // 4, step, 0)
 
 
 def attributes(own, border, smooth_ref, store):
@@ -250,60 +262,51 @@
     return jnp.where(lax.div(iota(packed.shape, 1), SIDE) == lax.div(base, SIDE), moved, 0.0)
 
 
-def inner_kernel(inner_ref, inner_h_ref, smooth_ref, pack_h_ref, dip_i_ref, dip_x_ref, plan_ref, border_ref, out_ref, sems):
+def inner_kernel(inner_ref, inner_h_ref, smooth_ref, pack_h_ref, out_ref, border_ref):
     count, chunks = inner_ref.shape[:2]
     half, inner = count // 2, EDGE * chunks
-    targets = (dip_i_ref, dip_x_ref, plan_ref)
     border_ref[...] = dot(inner_h_ref[...].reshape(6 * inner, 256), pack_h_ref[...])
 
-    def copies(pair):
-        return [
-            pltpu.make_async_copy(
-                out_ref.at[n, pl.ds(half * group + 2 * pair, 2)],
-                target.at[pl.ds(half * group + 2 * pair, 2), pl.ds(EDGE, inner)],
-                sems.at[pair, group, n],
-            )
-            for group in range(2)
-            for n, target in enumerate(targets)
-        ]
-
-    def step(pair, carry):
-        for parity in range(2):
-            k = 2 * pair + parity
-            for group in range(2):
-
-                def store(chunk, lanes, values):
-                    for n, value in enumerate(values):
-                        out_ref[n, half * group + k, EDGE * chunk : EDGE * (chunk + 1), lanes] = value
-
-                border = border_of(border_ref[:, 128 * group : 128 * (group + 1)], k)
-                attributes(inner_ref[half * group + k].reshape(6 * inner, 256), border, smooth_ref, store)
-        for copy in copies(pair):
-            copy.start()
+    def step(k, carry):
+        for group in range(2):
+
+            def store(chunk, lanes, values):
+                for n, value in enumerate(values):
+                    out_ref[n, half * group + k, EDGE * chunk : EDGE * (chunk + 1), lanes] = value
+
+            border = border_of(border_ref[:, 128 * group : 128 * (group + 1)], k)
+            attributes(inner_ref[half * group + k].reshape(6 * inner, 256), border, smooth_ref, store)
         return carry
 
-    lax.fori_loop(0, half // 2, step, 0)
-    for pair in range(half // 2):
-        for copy in copies(pair):
-            copy.wait()
+    lax.fori_loop(0, half, step, 0, unroll=2)
 
 
 def end_kernel(
     exchange, vol_ref, halo_ref, rows_ref, part_ref, part_h_ref,
-    smooth_ref, pack_h_ref, diff_x_ref, diff_h_ref, lines_e_ref, diff_e_ref, in_i_ref, in_x_ref, in_p_ref,
-    dip_i_ref, dip_x_ref, plan_ref,
-    packed_ref, block_ref, block_h_ref, border_ref, edge_ref, out_ref, sems,
+    smooth_ref, pack_h_ref, diff_x_ref, diff_h_ref, lines_e_ref, diff_e_ref, done_ref, *refs,
 ):
+    last = exchange == 1
+    targets, refs = (refs[3:6], refs[6:]) if last else (refs[:3], refs[3:])
+    if last:
+        packed_ref, block_ref, block_h_ref, border_ref, edge_ref, out_ref, done_sems, sems = refs
+    else:
+        out_ref, packed_ref, block_ref, block_h_ref, border_ref, edge_ref, done_sems = refs
     depths, rows, cols = vol_ref.shape
     count, half = depths - 2, (depths - 2) // 2
     bf16, f32 = jnp.bfloat16, jnp.float32
     low = low_end(exchange)
     end = jnp.where(low, 0, 1)
     start = pl.multiple_of(jnp.where(low, 0, rows - EDGE), EDGE)
-    targets = (dip_i_ref, dip_x_ref, plan_ref)
+    done_start = pl.multiple_of(jnp.where(low, rows - EDGE, 0), EDGE) if last else EDGE
+    finished = [
+        pltpu.make_async_copy(done_ref.at[n], target.at[:, pl.ds(done_start, done_ref.shape[2])], done_sems.at[n])
+        for n, target in enumerate(targets)
+    ]
+    for copy in finished:
+        copy.start()
 
     packed_ref[:8] = jnp.zeros_like(packed_ref[:8])
-    packed_ref[8:] = rows_ref[...].astype(f32)
+    packed_ref[8:] = (rows_ref[...] if last else rows_ref[0]).astype(f32)
 
     def joined(row, own):
         lanes = own.shape[1]
@@ -338,18 +341,8 @@
         summed = part_ref[end, comp] + outer.reshape(count, EDGE, cols)
         edge_ref[:, comp] = summed.astype(bf16)
 
-    def copies(pair):
-        return [
-            pltpu.make_async_copy(
-                out_ref.at[n, pl.ds(half * group + 2 * pair, 2)],
-                target.at[pl.ds(half * group + 2 * pair, 2), pl.ds(start, EDGE)],
-                sems.at[pair, group, n],
-            )
-            for group in range(2)
-            for n, target in enumerate(targets)
-        ]
-
-    def step(pair, carry):
+    copies = []
+    for pair in range(half // 2):
         own, border, places = [], [], []
         for group in range(2):
             for parity in range(2):
@@ -363,14 +356,17 @@
                 out_ref[n, places[chunk], :, lanes] = value
 
         attributes(jnp.concatenate(own, axis=0), jnp.concatenate(border, axis=0), smooth_ref, store)
-        for copy in copies(pair):
-            copy.start()
-        return carry
-
-    lax.fori_loop(0, half // 2, step, 0)
-    for pair in range(half // 2):
-        for copy in copies(pair):
-            copy.wait()
+        if last:
+            for group in range(2):
+                depth = pl.ds(half * group + 2 * pair, 2)
+                for n, target in enumerate(targets):
+                    copy = pltpu.make_async_copy(
+                        out_ref.at[n, depth], target.at[depth, pl.ds(start, EDGE)], sems.at[pair, group, n]
+                    )
+                    copy.start()
+                    copies.append(copy)
+    for copy in finished + copies:
+        copy.wait()
 
 
 def call(name, kernel, outs, scratch, operands, in_specs=None, out_specs=None, flops=0, limit=16, aliases={}):
@@ -419,67 +415,75 @@
     halo_tile = ((TILES, rows, 128), bf16)
     vol, send, own = call("pack_kernel", pack_kernel, [(volume.shape, bf16), halo_tile, halo_tile], [], [volume, pick])
     side = lax.ppermute(send, "xl", [(0, 1), (1, 0)])
-    packed = ((packed_rows, cols), bf16)
-    halo, first, second = call(
+    chunks = rows // EDGE - 2
+    lined = [((count, chunks, 6, EDGE, cols), bf16), ((2, 6, count, EDGE, cols), f32)]
+    moment_slots = [pltpu.VMEM((2, 6, rows, cols), bf16)] * 2
+    inner, part = call("lines_kernel", lines_kernel, lined, moment_slots, [vol, lines, diff_i, diff_x], flops=work // 4)
+    halo, ends = call(
         "rows_kernel",
         rows_kernel,
-        [((rows, 128 * TILES), bf16), packed, packed],
+        [((rows, 128 * TILES), bf16), ((2, packed_rows, cols), bf16)],
         [pltpu.VMEM((2, packed_rows, cols), f32)],
-        [vol, own, side],
-    )
-    one = [(i, i ^ 1) for i in range(il)]
-    two = [pair for i in range(1, il - 1, 2) for pair in ((i, i + 1), (i + 1, i))]
-    second_in = lax.ppermute(second, "il", two)
-    chunks = rows // EDGE - 2
-    inner, part, inner_h, part_h, first = call(
-        "lines_kernel",
-        lines_kernel,
-        [
-            ((count, chunks, 6, EDGE, cols), bf16),
-            ((2, 6, count, EDGE, cols), f32),
-            ((chunks, 6, EDGE, 256), bf16),
-            ((2, 6, EDGE, 256), f32),
-            packed,
-        ],
-        [pltpu.VMEM((2, 6, rows, cols), bf16)] * 2,
-        [vol, halo, first, lines, diff_i, diff_x, diff_h],
+        [vol, own, side, part],
+        in_specs=[WHOLE] * 3 + [ANYWHERE],
+    )
+    ends_in = lax.ppermute(ends, "il", [(i, i ^ 1) for i in range(il)])
+    operands = [vol, halo, lines, diff_i, diff_x, diff_h, inner, part]
+    inner, part, inner_h, part_h = call(
+        "more_lines_kernel",
+        more_lines_kernel,
+        lined + [((chunks, 6, EDGE, 256), bf16), ((2, 6, EDGE, 256), f32)],
+        moment_slots,
+        operands,
         flops=2 * work,
-    )
-    first_in = lax.ppermute(first, "il", one)
-    shapes = [((count, rows, cols), f32)] * 3
-    sems = pltpu.SemaphoreType.DMA((half // 2, 2, 3))
-    outs = call(
+        aliases={len(operands) - 2 + n: n for n in range(2)},
+    )
+    (done,) = call(
         "inner_kernel",
         inner_kernel,
-        shapes,
-        [pltpu.VMEM((6 * EDGE * chunks, 256), f32), pltpu.VMEM((3, count, EDGE * chunks, cols), f32), sems],
+        [((3, count, EDGE * chunks, cols), f32)],
+        [pltpu.VMEM((6 * EDGE * chunks, 256), f32)],
         [inner, inner_h, smooth, pack_h],
+        flops=2 * work,
+    )
+    (relayed,) = call(
+        "relay_kernel", relay_kernel, [((packed_rows, cols), bf16)], [], [ends_in, done], in_specs=[WHOLE, ANYWHERE]
+    )
+    onward = [(i, i + 2) for i in range(0, il - 2, 2)] + [(i, i - 2) for i in range(3, il, 2)]
+    relayed_in = lax.ppermute(relayed, "il", onward)
+
+    outs = [((count, rows, cols), f32)] * 3
+    end_rows = (3, count, EDGE, cols)
+    tables = [smooth, pack_h, diff_x, diff_h, lines_e, diff_e]
+    scratch = [
+        pltpu.VMEM((8 + packed_rows, cols), f32),
+        pltpu.VMEM((depths, EDGE, cols), bf16),
+        pltpu.VMEM((EDGE, 128 * TILES), bf16),
+        pltpu.VMEM((6 * EDGE, 256), f32),
+        pltpu.VMEM((count, 6, EDGE, cols), bf16),
+    ]
+    sems = pltpu.SemaphoreType.DMA((3,))
+    *outs_in, done = call(
+        "near_end_kernel",
+        lambda *refs: end_kernel(0, *refs),
+        outs + [(end_rows, f32)],
+        scratch + [sems],
+        [vol, halo, ends_in, part, part_h, *tables, done],
+        out_specs=(IN_HBM,) * 3 + (WHOLE,),
+        flops=work,
+    )
+    operands = [vol, halo, relayed_in, part, part_h, *tables, done]
+    return call(
+        "far_end_kernel",
+        lambda *refs: end_kernel(1, *refs),
+        outs,
+        scratch + [pltpu.VMEM(end_rows, f32), sems, pltpu.SemaphoreType.DMA((half // 2, 2, 3))],
+        operands + outs_in,
+        in_specs=[WHOLE] * len(operands) + [IN_HBM] * 3,
         out_specs=(IN_HBM,) * 3,
-        flops=2 * work,
-    )
-    tables = [smooth, pack_h, diff_x, diff_h, lines_e, diff_e]
-    for exchange, received in ((1, second_in), (0, first_in)):
-        operands = [vol, halo, received, part, part_h, *tables]
-        outs = call(
-            "end_kernel",
-            lambda *refs, exchange=exchange: end_kernel(exchange, *refs),
-            shapes,
-            [
-                pltpu.VMEM((8 + packed_rows, cols), f32),
-                pltpu.VMEM((depths, EDGE, cols), bf16),
-                pltpu.VMEM((EDGE, 128 * TILES), bf16),
-                pltpu.VMEM((6 * EDGE, 256), f32),
-                pltpu.VMEM((count, 6, EDGE, cols), bf16),
-                pltpu.VMEM((3, count, EDGE, cols), f32),
-                sems,
-            ],
-            operands + list(outs),
-            in_specs=[WHOLE] * len(operands) + [IN_HBM] * 3,
-            out_specs=(IN_HBM,) * 3,
-            flops=work,
-            aliases={len(operands) + n: n for n in range(3)},
-        )
-    return outs
+        flops=work,
+        aliases={len(operands) + n: n for n in range(3)},
+    )
 
 
 def solution(mesh):

time: 24.3 us -> 22 us (0.905)
  Pallas kernels: 15.3 us -> 13.8 us
  waiting for transfers between devices: 0.95 us -> 0.07 us
    pallas_call x7 -> x9, Pallas kernels: 15.3 us -> 13.8 us  [call(): pl.pallas_call(kernel, out_shape=tuple((jax.ShapeDtypeStruct(*out) for ou...]
    ppermute x1, waiting for transfers between devices: 0.94 us -> 0.06 us  [body(): side = lax.ppermute(send, 'xl', [(0, 1), (1, 0)])]
where the time goes in v6:
time: 22 us; the launch traced here: 21.8 us
  Pallas kernels  13.8 us (63%)
  starting transfers between devices  6.94 us (32%)
  between operations  0.72 us (3%)
  local copies, waits for them, and re-layouts  0.31 us (1%)
    pallas_call x9, Pallas kernels, call(): pl.pallas_call(kernel, out_shape=tuple((jax.ShapeDtypeStruct(*out) for ou...  13.8 us
    ppermute x1, starting transfers between devices, body(): relayed_in = lax.ppermute(relayed, 'il', onward)  3.49 us
    ppermute x1, starting transfers between devices, body(): ends_in = lax.ppermute(ends, 'il', [(i, i ^ 1) for i in range(il)])  2.94 us
    ppermute x1, starting transfers between devices, body(): side = lax.ppermute(send, 'xl', [(0, 1), (1, 0)])  0.52 us
  transfers between devices with their start and end apart: 3, of which 1 were waited for; matrix products, arithmetic and copies ran while one was open for 0% of the time, Pallas kernels for 45%

profile of v6, /device:TPU:0, one launch (start us, length us, event | category | flops | bytes accessed | tf_op | source)
XLA Modules:
  0.0 21.8 jit_solution(2364527754708587145)
XLA Ops:
  0.6 0.0 copy-start
  0.6 1.0 %tables_kernel.1 = (bf16[128,128]{1,0:T(8,128)(2,1)S(1)}, bf16[128,128]{1,0:T(8,128)(2,1)S(1)}, bf16[256,256]{1,0:T(8,128)(2,1)S(1)}, bf16[256,256]{1,0:T(8,128)...) custom-call(), custom_call_target="tpu_custom_call" | custom-call | flops 1073741824 | tf_op jit(solution)/shard_map/tables_kernel/pallas_call | solution.py:373
  1.6 0.3 %copy-done = bf16[18,128,256]{2,1,0:T(8,128)(2,1)S(1)} copy-done((bf16[18,128,256]{2,1,0:T(8,128)(2,1)S(1)}, bf16[18,128,256]{2,1,0:T(8,128)(2,1)}, u32[]{:S(2)}) %copy-start) | copy-done | bytes 1179672
  1.9 0.5 %pack_kernel.1 = (bf16[18,128,256]{2,1,0:T(8,128)(2,1)S(1)}, bf16[3,128,128]{2,1,0:T(8,128)(2,1)S(1)}, bf16[3,128,128]{2,1,0:T(8,128)(2,1)S(1)}) custom-call(bf16[18,128,256]{2,1,0:T(8,128)(2,1)S(1)} %copy-done, bf16[256,256]{1,0:T(8,128)(2,1)S(1)} %get-tuple-element.27.pick_ref), custom_call_target="tpu_custom_call" | custom-call | tf_op jit(solution)/shard_map/pack_kernel/pallas_call | solution.py:373
  2.4 0.5 %collective-permute-start = (bf16[3,128,128]{2,1,0:T(8,128)(2,1)S(1)}, bf16[3,128,128]{2,1,0:T(8,128)(2,1)S(1)}, u32[]{:S(2)}, u32[]{:S(2)}) collective-permute-start(bf16[3,128,128]{2,1,0:T(8,128)(2,1)S(1)} %get-tuple-element.30), channel_id=1, source_target_pairs={{0,1},{1,0},{2,3},{3,2},{4,5},{5,4},{6,7},{7,6},{8,9},{9,8},{10,11... | collective-permute-start | bytes 294920 | tf_op jit(solution)/shard_map/ppermute | solution.py:417
  3.0 0.9 %lines_kernel.1 = (bf16[16,6,6,16,256]{4,3,2,1,0:T(8,128)(2,1)S(1)}, f32[2,6,16,16,256]{4,3,2,1,0:T(8,128)S(1)}) custom-call(bf16[18,128,256]{2,1,0:T(8,128)(2,1)S(1)} %get-tuple-element.28.vol_ref.refs_0_, bf16[128,128]{1,0:T(8,128)(2,1)S(1)} %get-tuple-element.31.lines_ref, bf16[128,128]{1,0:T(8,128)(2,1)S(1)} %get-tuple-element.32.diff_i_ref, ...), custom_call_target="tpu_custom_call" | custom-call | flops 268435456 | tf_op jit(solution)/shard_map/lines_kernel/pallas_call | solution.py:373
  3.8 0.1 collective-permute-done.side_ref
  3.9 0.1 rows_kernel.1
  4.0 2.9 %collective-permute-start.1 = (bf16[2,208,256]{2,1,0:T(8,128)(2,1)S(1)}, bf16[2,208,256]{2,1,0:T(8,128)(2,1)S(1)}, u32[]{:S(2)}, u32[]{:S(2)}) collective-permute-start(bf16[2,208,256]{2,1,0:T(8,128)(2,1)S(1)} %get-tuple-element.36), channel_id=1, source_target_pairs={{0,2},{2,0},{4,6},{6,4},{8,10},{10,8},{12,14},{14,12},{1,3},{3,1},... | collective-permute-start | bytes 638984 | tf_op jit(solution)/shard_map/ppermute | solution.py:430
  7.0 2.8 %more_lines_kernel.1 = (bf16[16,6,6,16,256]{4,3,2,1,0:T(8,128)(2,1)S(1)}, f32[2,6,16,16,256]{4,3,2,1,0:T(8,128)S(1)}, bf16[6,6,16,256]{3,2,1,0:T(8,128)(2,1)S(1)}, f32[2,6,16,256]{3,2,1,0:T(8,128)S(1)}) custom-call(bf16[18,128,256]{2,1,0:T(8,128)(2,1)S(1)} %get-tuple-element.28.vol_ref.refs_0_, ...), custom_call_target="tpu_custom_call", output_to_operand_aliasing={{0}: (6, {}), {1}: (7, {})} | custom-call | flops 2147483648 | tf_op jit(solution)/shard_map/more_lines_kernel/pallas_call | solution.py:373
  9.8 3.4 %inner_kernel.1.after_ref.refs_11_ = f32[3,16,96,256]{3,2,1,0:T(8,128)S(1)} custom-call(bf16[16,6,6,16,256]{4,3,2,1,0:T(8,128)(2,1)S(1)} %get-tuple-element.39.inner_ref, bf16[6,6,16,256]{3,2,1,0:T(8,128)(2,1)S(1)} %get-tuple-element.40.inner_h_ref, bf16[256,256]{1,0:T(8,128)(2,1)S(1)} %get-tuple-element.41.smooth_ref.refs_5_, ...), custom_call_target="tpu_custom_call" | custom-call | flops 2147483648 | tf_op jit(solution)/shard_map/inner_kernel/pallas_call | solution.py:373
  13.1 0.0 collective-permute-done.1.ends_ref.refs_2_
  13.2 3.5 %collective-permute-start.2 = (bf16[208,256]{1,0:T(8,128)(2,1)S(1)}, bf16[208,256]{1,0:T(8,128)(2,1)S(1)}, u32[]{:S(2)}, u32[]{:S(2)}) collective-permute-start(bf16[208,256]{1,0:T(8,128)(2,1)S(1)} %relay_kernel.1), channel_id=1, source_target_pairs={{0,4},{4,8},{8,12},{6,2},{10,6},{14,10},{1,5},{5,9},{9,13},{7,3},{... | collective-permute-start | bytes 319496 | tf_op jit(solution)/shard_map/ppermute | solution.py:453
  16.7 2.9 %near_end_kernel.1 = (f32[16,128,256]{2,1,0:T(8,128)}, f32[16,128,256]{2,1,0:T(8,128)}, f32[16,128,256]{2,1,0:T(8,128)}, f32[3,16,16,256]{3,2,1,0:T(8,128)S(1)}) custom-call(bf16[18,128,256]{2,1,0:T(8,128)(2,1)S(1)} %get-tuple-element.28.vol_ref.refs_0_, bf16[128,384]{1,0:T(8,128)(2,1)S(1)} %get-tuple-element.35.halo_ref.refs_1_, ...), custom_call_target="tpu_custom_call" | custom-call | flops 1073741824 | tf_op jit(solution)/shard_map/near_end_kernel/pallas_call | solution.py:373
  19.5 0.0 collective-permute-done.2.refs_2_
  19.6 2.3 %far_end_kernel.1 = (f32[16,128,256]{2,1,0:T(8,128)}, f32[16,128,256]{2,1,0:T(8,128)}, f32[16,128,256]{2,1,0:T(8,128)}) custom-call(bf16[18,128,256]{2,1,0:T(8,128)(2,1)S(1)} %get-tuple-element.28.vol_ref.refs_0_, bf16[128,384]{1,0:T(8,128)(2,1)S(1)} %get-tuple-element.35.halo_ref.refs_1_, ...), custom_call_target="tpu_custom_call", output_to_operand_aliasing={{0}: (12, {}), {1}: (13, {}), {2}: (14, {})} | custom-call | flops 1073741824 | tf_op jit(solution)/shard_map/far_end_kernel/pallas_call | solution.py:373
  (1 shorter events, 0.0 us)
Async XLA Ops:
  0.6 1.3 %copy-start = (bf16[18,128,256]{2,1,0:T(8,128)(2,1)S(1)}, bf16[18,128,256]{2,1,0:T(8,128)(2,1)}, u32[]{:S(2)}) copy-start(bf16[18,128,256]{2,1,0:T(8,128)(2,1)} %vol_ref.1) | copy-start | bytes 3538948
  2.4 1.5 %collective-permute-start = (bf16[3,128,128]{2,1,0:T(8,128)(2,1)S(1)}, bf16[3,128,128]{2,1,0:T(8,128)(2,1)S(1)}, u32[]{:S(2)}, u32[]{:S(2)}) collective-permute-start(bf16[3,128,128]{2,1,0:T(8,128)(2,1)S(1)} %get-tuple-element.30), channel_id=1, source_target_pairs={{0,1},{1,0},{2,3},{3,2},{4,5},{5,4},{6,7},{7,6},{8,9},{9,8},{10,11... | collective-permute-start | bytes 294920 | tf_op jit(solution)/shard_map/ppermute | solution.py:417
  4.0 9.1 %collective-permute-start.1 = (bf16[2,208,256]{2,1,0:T(8,128)(2,1)S(1)}, bf16[2,208,256]{2,1,0:T(8,128)(2,1)S(1)}, u32[]{:S(2)}, u32[]{:S(2)}) collective-permute-start(bf16[2,208,256]{2,1,0:T(8,128)(2,1)S(1)} %get-tuple-element.36), channel_id=1, source_target_pairs={{0,2},{2,0},{4,6},{6,4},{8,10},{10,8},{12,14},{14,12},{1,3},{3,1},... | collective-permute-start | bytes 638984 | tf_op jit(solution)/shard_map/ppermute | solution.py:430
  13.2 6.4 %collective-permute-start.2 = (bf16[208,256]{1,0:T(8,128)(2,1)S(1)}, bf16[208,256]{1,0:T(8,128)(2,1)S(1)}, u32[]{:S(2)}, u32[]{:S(2)}) collective-permute-start(bf16[208,256]{1,0:T(8,128)(2,1)S(1)} %relay_kernel.1), channel_id=1, source_target_pairs={{0,4},{4,8},{8,12},{6,2},{10,6},{14,10},{1,5},{5,9},{9,13},{7,3},{... | collective-permute-start | bytes 319496 | tf_op jit(solution)/shard_map/ppermute | solution.py:453

commit v7 on v6

--- a/solution.py
+++ b/solution.py
@@ -16,6 +16,7 @@
 OWN = 2
 TINY = float(np.finfo(np.float32).tiny)
 HEAD = 4
+PART = 4
 FAR = -1000
 WHOLE = pl.BlockSpec(memory_space=pltpu.VMEM)
 IN_HBM = pl.BlockSpec(memory_space=pltpu.HBM)
@@ -129,6 +130,7 @@
     depths, rows, cols = vol_ref.shape
     slot = lax.div(lax.rem(iota((rows, 256), 1), 128), SIDE)
     copy_ref[...] = vol_ref[...]
+    picked = dot(vol_ref[...].reshape(depths * rows, cols), pick_ref[...])
     for tile in range(TILES):
         if tile < 2:
             planes = [(1 + SLOTS * tile + index, index) for index in range(SLOTS)]
@@ -136,7 +138,7 @@
             planes = [(0, 0), (depths - 1, 1)]
         packed = jnp.zeros((rows, 256), jnp.float32)
         for plane, index in planes:
-            packed = jnp.where(slot == index, dot(vol_ref[plane], pick_ref[...]), packed)
+            packed = jnp.where(slot == index, picked[rows * plane : rows * (plane + 1)], packed)
         packed = packed.astype(jnp.bfloat16)
         send_ref[tile] = packed[:, :128]
         own_ref[tile] = packed[:, 128:]
@@ -262,23 +264,52 @@
     return jnp.where(lax.div(iota(packed.shape, 1), SIDE) == lax.div(base, SIDE), moved, 0.0)
 
 
-def inner_kernel(inner_ref, inner_h_ref, smooth_ref, pack_h_ref, out_ref, border_ref):
+def inner_kernel(
+    inner_ref, inner_h_ref, smooth_ref, pack_h_ref, dip_i_ref, dip_x_ref, plan_ref, later_ref, border_ref, out_ref, sems
+):
     count, chunks = inner_ref.shape[:2]
     half, inner = count // 2, EDGE * chunks
+    targets = (dip_i_ref, dip_x_ref, plan_ref)
     border_ref[...] = dot(inner_h_ref[...].reshape(6 * inner, 256), pack_h_ref[...])
 
-    def step(k, carry):
+    def finish(k, target_ref):
         for group in range(2):
 
             def store(chunk, lanes, values):
                 for n, value in enumerate(values):
-                    out_ref[n, half * group + k, EDGE * chunk : EDGE * (chunk + 1), lanes] = value
+                    target_ref[n, group, k % (half // 2), EDGE * chunk : EDGE * (chunk + 1), lanes] = value
 
             border = border_of(border_ref[:, 128 * group : 128 * (group + 1)], k)
             attributes(inner_ref[half * group + k].reshape(6 * inner, 256), border, smooth_ref, store)
+
+    def copies(pair):
+        return [
+            pltpu.make_async_copy(
+                out_ref.at[n, group, pl.ds(2 * pair, 2)],
+                target.at[pl.ds(half * group + 2 * pair, 2), pl.ds(EDGE, inner)],
+                sems.at[pair, group, n],
+            )
+            for group in range(2)
+            for n, target in enumerate(targets)
+        ]
+
+    def first(pair, carry):
+        finish(2 * pair, out_ref)
+        finish(2 * pair + 1, out_ref)
+        for copy in copies(pair):
+            copy.start()
         return carry
 
-    lax.fori_loop(0, half, step, 0, unroll=2)
+    def second(pair, carry):
+        finish(2 * pair, later_ref)
+        finish(2 * pair + 1, later_ref)
+        return carry
+
+    lax.fori_loop(0, half // 4, first, 0)
+    lax.fori_loop(half // 4, half // 2, second, 0)
+    for pair in range(half // 4):
+        for copy in copies(pair):
+            copy.wait()
 
 
 def end_kernel(
@@ -286,7 +317,7 @@
     smooth_ref, pack_h_ref, diff_x_ref, diff_h_ref, lines_e_ref, diff_e_ref, done_ref, *refs,
 ):
     last = exchange == 1
-    targets, refs = (refs[3:6], refs[6:]) if last else (refs[:3], refs[3:])
+    targets, refs = refs[3:6], refs[6:]
     if last:
         packed_ref, block_ref, block_h_ref, border_ref, edge_ref, out_ref, done_sems, sems = refs
     else:
@@ -297,16 +328,27 @@
     low = low_end(exchange)
     end = jnp.where(low, 0, 1)
     start = pl.multiple_of(jnp.where(low, 0, rows - EDGE), EDGE)
-    done_start = pl.multiple_of(jnp.where(low, rows - EDGE, 0), EDGE) if last else EDGE
-    finished = [
-        pltpu.make_async_copy(done_ref.at[n], target.at[:, pl.ds(done_start, done_ref.shape[2])], done_sems.at[n])
-        for n, target in enumerate(targets)
-    ]
+    other = pl.multiple_of(jnp.where(low, rows - EDGE, 0), EDGE)
+    finished = []
+    for n, target in enumerate(targets):
+        for group in range(2):
+            if last:
+                source = done_ref.at[n, pl.ds(half * group, half)]
+                place = target.at[pl.ds(half * group, half), pl.ds(other, EDGE)]
+            else:
+                source = done_ref.at[n, group]
+                place = target.at[pl.ds(half * group + half // 2, half // 2), pl.ds(EDGE, rows - 2 * EDGE)]
+            finished.append(pltpu.make_async_copy(source, place, done_sems.at[n, group]))
     for copy in finished:
         copy.start()
 
     packed_ref[:8] = jnp.zeros_like(packed_ref[:8])
-    packed_ref[8:] = (rows_ref[...] if last else rows_ref[0]).astype(f32)
+    if last:
+        il = lax.axis_index("il")
+        outside = (low & (il == 0)) | (jnp.logical_not(low) & (il == lax.axis_size("il") - 1))
+        packed_ref[8:] = jnp.where(outside, 0.0, rows_ref[...].astype(f32))
+    else:
+        packed_ref[8:] = rows_ref[0].astype(f32)
 
     def joined(row, own):
         lanes = own.shape[1]
@@ -342,11 +384,11 @@
         edge_ref[:, comp] = summed.astype(bf16)
 
     copies = []
-    for pair in range(half // 2):
+    for pair in range(half // PART):
         own, border, places = [], [], []
         for group in range(2):
-            for parity in range(2):
-                k = 2 * pair + parity
+            for parity in range(PART):
+                k = PART * pair + parity
                 places.append(half * group + k)
                 own.append(edge_ref[half * group + k].reshape(6 * EDGE, cols))
                 border.append(border_of(border_ref[:, 128 * group : 128 * (group + 1)], k))
@@ -358,7 +400,7 @@
         attributes(jnp.concatenate(own, axis=0), jnp.concatenate(border, axis=0), smooth_ref, store)
         if last:
             for group in range(2):
-                depth = pl.ds(half * group + 2 * pair, 2)
+                depth = pl.ds(half * group + PART * pair, PART)
                 for n, target in enumerate(targets):
                     copy = pltpu.make_async_copy(
                         out_ref.at[n, depth], target.at[depth, pl.ds(start, EDGE)], sems.at[pair, group, n]
@@ -438,21 +480,28 @@
         flops=2 * work,
         aliases={len(operands) - 2 + n: n for n in range(2)},
     )
-    (done,) = call(
+    outs = [((count, rows, cols), f32)] * 3
+    saved = (3, 2, half // 2, EDGE * chunks, cols)
+    *outs_in, done = call(
         "inner_kernel",
         inner_kernel,
-        [((3, count, EDGE * chunks, cols), f32)],
-        [pltpu.VMEM((6 * EDGE * chunks, 256), f32)],
+        outs + [(saved, f32)],
+        [
+            pltpu.VMEM((6 * EDGE * chunks, 256), f32),
+            pltpu.VMEM(saved, f32),
+            pltpu.SemaphoreType.DMA((half // 4, 2, 3)),
+        ],
         [inner, inner_h, smooth, pack_h],
+        out_specs=(IN_HBM,) * 3 + (WHOLE,),
         flops=2 * work,
     )
     (relayed,) = call(
         "relay_kernel", relay_kernel, [((packed_rows, cols), bf16)], [], [ends_in, done], in_specs=[WHOLE, ANYWHERE]
     )
-    onward = [(i, i + 2) for i in range(0, il - 2, 2)] + [(i, i - 2) for i in range(3, il, 2)]
+    onward = [(i, i + 2) for i in range(0, il - 2, 2)] + [(il - 2, il - 1)]
+    onward += [(i, i - 2) for i in range(3, il, 2)] + [(1, 0)]
     relayed_in = lax.ppermute(relayed, "il", onward)
 
-    outs = [((count, rows, cols), f32)] * 3
     end_rows = (3, count, EDGE, cols)
     tables = [smooth, pack_h, diff_x, diff_h, lines_e, diff_e]
     scratch = [
@@ -462,22 +511,25 @@
         pltpu.VMEM((6 * EDGE, 256), f32),
         pltpu.VMEM((count, 6, EDGE, cols), bf16),
     ]
-    sems = pltpu.SemaphoreType.DMA((3,))
+    sems = pltpu.SemaphoreType.DMA((3, 2))
+    operands = [vol, halo, ends_in, part, part_h, *tables, done]
     *outs_in, done = call(
         "near_end_kernel",
         lambda *refs: end_kernel(0, *refs),
         outs + [(end_rows, f32)],
         scratch + [sems],
-        [vol, halo, ends_in, part, part_h, *tables, done],
+        operands + outs_in,
+        in_specs=[WHOLE] * len(operands) + [IN_HBM] * 3,
         out_specs=(IN_HBM,) * 3 + (WHOLE,),
         flops=work,
+        aliases={len(operands) + n: n for n in range(3)},
     )
     operands = [vol, halo, relayed_in, part, part_h, *tables, done]
     return call(
         "far_end_kernel",
         lambda *refs: end_kernel(1, *refs),
         outs,
-        scratch + [pltpu.VMEM(end_rows, f32), sems, pltpu.SemaphoreType.DMA((half // 2, 2, 3))],
+        scratch + [pltpu.VMEM(end_rows, f32), sems, pltpu.SemaphoreType.DMA((half // PART, 2, 3))],
         operands + outs_in,
         in_specs=[WHOLE] * len(operands) + [IN_HBM] * 3,
         out_specs=(IN_HBM,) * 3,

time: 22 us -> 20.4 us (0.927)
  starting transfers between devices: 6.94 us -> 5.1 us
  waiting for transfers between devices: 0.07 us -> 1.01 us
  Pallas kernels: 13.8 us -> 13.2 us
    ppermute x1, starting transfers between devices: 3.49 us -> 1.65 us  [body(): relayed_in = lax.ppermute(relayed, 'il', onward)]
    ppermute x1, waiting for transfers between devices: 0.01 us -> 0.93 us  [body(): relayed_in = lax.ppermute(relayed, 'il', onward)]
    pallas_call x9, Pallas kernels: 13.8 us -> 13.2 us  [call(): pl.pallas_call(kernel, out_shape=tuple((jax.ShapeDtypeStruct(*out) for ou...]
  transfers between devices with their start and end apart: 3 -> 3, of which waited for: 1 -> 2; matrix products, arithmetic and copies ran while one was open for 0% -> 0% of each run, Pallas kernels for 45% -> 46%
where the time goes in v7:
time: 20.4 us; the launch traced here: 20.3 us
  Pallas kernels  13.2 us (65%)
  starting transfers between devices  5.1 us (25%)
  waiting for transfers between devices  1.01 us (5%)
  between operations  0.71 us (3%)
  local copies, waits for them, and re-layouts  0.31 us (2%)
    pallas_call x9, Pallas kernels, call(): pl.pallas_call(kernel, out_shape=tuple((jax.ShapeDtypeStruct(*out) for ou...  13.2 us
    ppermute x1, starting transfers between devices, body(): ends_in = lax.ppermute(ends, 'il', [(i, i ^ 1) for i in range(il)])  2.94 us
    ppermute x1, starting transfers between devices, body(): relayed_in = lax.ppermute(relayed, 'il', onward)  1.65 us
    ppermute x1, waiting for transfers between devices, body(): relayed_in = lax.ppermute(relayed, 'il', onward)  0.93 us
    ppermute x1, starting transfers between devices, body(): side = lax.ppermute(send, 'xl', [(0, 1), (1, 0)])  0.52 us
  transfers between devices with their start and end apart: 3, of which 2 were waited for; matrix products, arithmetic and copies ran while one was open for 0% of the time, Pallas kernels for 46%

profile of v7, /device:TPU:0, one launch (start us, length us, event | category | flops | bytes accessed | tf_op | source)
XLA Modules:
  0.0 20.3 jit_solution(9599200618620720097)
XLA Ops:
  0.6 0.0 copy-start
  0.6 1.0 %tables_kernel.1 = (bf16[128,128]{1,0:T(8,128)(2,1)S(1)}, bf16[128,128]{1,0:T(8,128)(2,1)S(1)}, bf16[256,256]{1,0:T(8,128)(2,1)S(1)}, bf16[256,256]{1,0:T(8,128)...) custom-call(), custom_call_target="tpu_custom_call" | custom-call | flops 1073741824 | tf_op jit(solution)/shard_map/tables_kernel/pallas_call | solution.py:415
  1.6 0.3 %copy-done = bf16[18,128,256]{2,1,0:T(8,128)(2,1)S(1)} copy-done((bf16[18,128,256]{2,1,0:T(8,128)(2,1)S(1)}, bf16[18,128,256]{2,1,0:T(8,128)(2,1)}, u32[]{:S(2)}) %copy-start) | copy-done | bytes 1179672
  1.9 0.5 %pack_kernel.1 = (bf16[18,128,256]{2,1,0:T(8,128)(2,1)S(1)}, bf16[3,128,128]{2,1,0:T(8,128)(2,1)S(1)}, bf16[3,128,128]{2,1,0:T(8,128)(2,1)S(1)}) custom-call(bf16[18,128,256]{2,1,0:T(8,128)(2,1)S(1)} %copy-done, bf16[256,256]{1,0:T(8,128)(2,1)S(1)} %get-tuple-element.31.pick_ref), custom_call_target="tpu_custom_call" | custom-call | tf_op jit(solution)/shard_map/pack_kernel/pallas_call | solution.py:415
  2.4 0.5 %collective-permute-start = (bf16[3,128,128]{2,1,0:T(8,128)(2,1)S(1)}, bf16[3,128,128]{2,1,0:T(8,128)(2,1)S(1)}, u32[]{:S(2)}, u32[]{:S(2)}) collective-permute-start(bf16[3,128,128]{2,1,0:T(8,128)(2,1)S(1)} %get-tuple-element.34), channel_id=1, source_target_pairs={{0,1},{1,0},{2,3},{3,2},{4,5},{5,4},{6,7},{7,6},{8,9},{9,8},{10,11... | collective-permute-start | bytes 294920 | tf_op jit(solution)/shard_map/ppermute | solution.py:459
  2.9 0.9 %lines_kernel.1 = (bf16[16,6,6,16,256]{4,3,2,1,0:T(8,128)(2,1)S(1)}, f32[2,6,16,16,256]{4,3,2,1,0:T(8,128)S(1)}) custom-call(bf16[18,128,256]{2,1,0:T(8,128)(2,1)S(1)} %get-tuple-element.32.vol_ref.refs_0_, bf16[128,128]{1,0:T(8,128)(2,1)S(1)} %get-tuple-element.35.lines_ref, bf16[128,128]{1,0:T(8,128)(2,1)S(1)} %get-tuple-element.36.diff_i_ref, ...), custom_call_target="tpu_custom_call" | custom-call | flops 268435456 | tf_op jit(solution)/shard_map/lines_kernel/pallas_call | solution.py:415
  3.8 0.1 collective-permute-done.side_ref
  3.9 0.1 rows_kernel.1
  4.0 2.9 %collective-permute-start.1 = (bf16[2,208,256]{2,1,0:T(8,128)(2,1)S(1)}, bf16[2,208,256]{2,1,0:T(8,128)(2,1)S(1)}, u32[]{:S(2)}, u32[]{:S(2)}) collective-permute-start(bf16[2,208,256]{2,1,0:T(8,128)(2,1)S(1)} %get-tuple-element.40), channel_id=1, source_target_pairs={{0,2},{2,0},{4,6},{6,4},{8,10},{10,8},{12,14},{14,12},{1,3},{3,1},... | collective-permute-start | bytes 638984 | tf_op jit(solution)/shard_map/ppermute | solution.py:472
  7.0 2.7 %more_lines_kernel.1 = (bf16[16,6,6,16,256]{4,3,2,1,0:T(8,128)(2,1)S(1)}, f32[2,6,16,16,256]{4,3,2,1,0:T(8,128)S(1)}, bf16[6,6,16,256]{3,2,1,0:T(8,128)(2,1)S(1)}, f32[2,6,16,256]{3,2,1,0:T(8,128)S(1)}) custom-call(bf16[18,128,256]{2,1,0:T(8,128)(2,1)S(1)} %get-tuple-element.32.vol_ref.refs_0_, ...), custom_call_target="tpu_custom_call", output_to_operand_aliasing={{0}: (6, {}), {1}: (7, {})} | custom-call | flops 2147483648 | tf_op jit(solution)/shard_map/more_lines_kernel/pallas_call | solution.py:415
  9.7 3.5 %inner_kernel.1 = (f32[16,128,256]{2,1,0:T(8,128)}, f32[16,128,256]{2,1,0:T(8,128)}, f32[16,128,256]{2,1,0:T(8,128)}, f32[3,2,4,96,256]{4,3,2,1,0:T(8,128)S(1)}) custom-call(bf16[16,6,6,16,256]{4,3,2,1,0:T(8,128)(2,1)S(1)} %get-tuple-element.43.inner_ref, bf16[6,6,16,256]{3,2,1,0:T(8,128)(2,1)S(1)} %get-tuple-element.44.inner_h_ref, ...), custom_call_target="tpu_custom_call" | custom-call | flops 2147483648 | tf_op jit(solution)/shard_map/inner_kernel/pallas_call | solution.py:415
  13.1 0.0 collective-permute-done.1.ends_ref.refs_2_
  13.2 1.6 %collective-permute-start.2 = (bf16[208,256]{1,0:T(8,128)(2,1)S(1)}, bf16[208,256]{1,0:T(8,128)(2,1)S(1)}, u32[]{:S(2)}, u32[]{:S(2)}) collective-permute-start(bf16[208,256]{1,0:T(8,128)(2,1)S(1)} %relay_kernel.1), channel_id=1, source_target_pairs={{0,4},{4,8},{8,12},{12,14},{6,2},{10,6},{14,10},{2,0},{1,5},{5,9},... | collective-permute-start | bytes 319496 | tf_op jit(solution)/shard_map/ppermute | solution.py:503
  14.8 2.2 %near_end_kernel.1 = (f32[16,128,256]{2,1,0:T(8,128)}, f32[16,128,256]{2,1,0:T(8,128)}, f32[16,128,256]{2,1,0:T(8,128)}, f32[3,16,16,256]{3,2,1,0:T(8,128)S(1)}) custom-call(bf16[18,128,256]{2,1,0:T(8,128)(2,1)S(1)} %get-tuple-element.32.vol_ref.refs_0_, ...), custom_call_target="tpu_custom_call", output_to_operand_aliasing={{0}: (12, {}), {1}: (13, {}), {2}: (14, {})} | custom-call | flops 1073741824 | tf_op jit(solution)/shard_map/near_end_kernel/pallas_call | solution.py:415
  17.1 0.9 %collective-permute-done.2.refs_2_ = bf16[208,256]{1,0:T(8,128)(2,1)S(1)} collective-permute-done((bf16[208,256]{1,0:T(8,128)(2,1)S(1)}, bf16[208,256]{1,0:T(8,128)(2,1)S(1)}, u32[]{:S(2)}, u32[]{:S(2)}) %collective-permute-start.2) | collective-permute-done | bytes 106528 | tf_op jit(solution)/shard_map/ppermute | solution.py:503
  18.0 2.3 %far_end_kernel.1 = (f32[16,128,256]{2,1,0:T(8,128)}, f32[16,128,256]{2,1,0:T(8,128)}, f32[16,128,256]{2,1,0:T(8,128)}) custom-call(bf16[18,128,256]{2,1,0:T(8,128)(2,1)S(1)} %get-tuple-element.32.vol_ref.refs_0_, bf16[128,384]{1,0:T(8,128)(2,1)S(1)} %get-tuple-element.39.halo_ref.refs_1_, ...), custom_call_target="tpu_custom_call", output_to_operand_aliasing={{0}: (12, {}), {1}: (13, {}), {2}: (14, {})} | custom-call | flops 1073741824 | tf_op jit(solution)/shard_map/far_end_kernel/pallas_call | solution.py:415
  (1 shorter events, 0.0 us)
Async XLA Ops:
  0.6 1.3 %copy-start = (bf16[18,128,256]{2,1,0:T(8,128)(2,1)S(1)}, bf16[18,128,256]{2,1,0:T(8,128)(2,1)}, u32[]{:S(2)}) copy-start(bf16[18,128,256]{2,1,0:T(8,128)(2,1)} %vol_ref.1) | copy-start | bytes 3538948
  2.4 1.5 %collective-permute-start = (bf16[3,128,128]{2,1,0:T(8,128)(2,1)S(1)}, bf16[3,128,128]{2,1,0:T(8,128)(2,1)S(1)}, u32[]{:S(2)}, u32[]{:S(2)}) collective-permute-start(bf16[3,128,128]{2,1,0:T(8,128)(2,1)S(1)} %get-tuple-element.34), channel_id=1, source_target_pairs={{0,1},{1,0},{2,3},{3,2},{4,5},{5,4},{6,7},{7,6},{8,9},{9,8},{10,11... | collective-permute-start | bytes 294920 | tf_op jit(solution)/shard_map/ppermute | solution.py:459
  4.0 9.1 %collective-permute-start.1 = (bf16[2,208,256]{2,1,0:T(8,128)(2,1)S(1)}, bf16[2,208,256]{2,1,0:T(8,128)(2,1)S(1)}, u32[]{:S(2)}, u32[]{:S(2)}) collective-permute-start(bf16[2,208,256]{2,1,0:T(8,128)(2,1)S(1)} %get-tuple-element.40), channel_id=1, source_target_pairs={{0,2},{2,0},{4,6},{6,4},{8,10},{10,8},{12,14},{14,12},{1,3},{3,1},... | collective-permute-start | bytes 638984 | tf_op jit(solution)/shard_map/ppermute | solution.py:472
  13.2 4.8 %collective-permute-start.2 = (bf16[208,256]{1,0:T(8,128)(2,1)S(1)}, bf16[208,256]{1,0:T(8,128)(2,1)S(1)}, u32[]{:S(2)}, u32[]{:S(2)}) collective-permute-start(bf16[208,256]{1,0:T(8,128)(2,1)S(1)} %relay_kernel.1), channel_id=1, source_target_pairs={{0,4},{4,8},{8,12},{12,14},{6,2},{10,6},{14,10},{2,0},{1,5},{5,9},... | collective-permute-start | bytes 319496 | tf_op jit(solution)/shard_map/ppermute | solution.py:503

commit v8 on v6

--- a/solution.py
+++ b/solution.py
@@ -15,7 +15,8 @@
 EDGE = 16
 OWN = 2
 TINY = float(np.finfo(np.float32).tiny)
-HEAD = 4
+HEAD = 2
+AHEAD = 2
 FAR = -1000
 WHOLE = pl.BlockSpec(memory_space=pltpu.VMEM)
 IN_HBM = pl.BlockSpec(memory_space=pltpu.HBM)
@@ -129,6 +130,7 @@
     depths, rows, cols = vol_ref.shape
     slot = lax.div(lax.rem(iota((rows, 256), 1), 128), SIDE)
     copy_ref[...] = vol_ref[...]
+    picked = dot(vol_ref[...].reshape(depths * rows, cols), pick_ref[...])
     for tile in range(TILES):
         if tile < 2:
             planes = [(1 + SLOTS * tile + index, index) for index in range(SLOTS)]
@@ -136,13 +138,13 @@
             planes = [(0, 0), (depths - 1, 1)]
         packed = jnp.zeros((rows, 256), jnp.float32)
         for plane, index in planes:
-            packed = jnp.where(slot == index, dot(vol_ref[plane], pick_ref[...]), packed)
+            packed = jnp.where(slot == index, picked[rows * plane : rows * (plane + 1)], packed)
         packed = packed.astype(jnp.bfloat16)
         send_ref[tile] = packed[:, :128]
         own_ref[tile] = packed[:, 128:]
 
 
-def rows_kernel(vol_ref, own_ref, side_ref, after_ref, halo_ref, ends_ref, packed_ref):
+def rows_kernel(vol_ref, own_ref, side_ref, after_ref, halo_ref, near_ref, far_ref, packed_ref):
     depths, rows, cols = vol_ref.shape
     even = lax.rem(lax.axis_index("il"), 2) == 0
 
@@ -166,11 +168,12 @@
     bottoms = jnp.concatenate([tiles[0][1], tiles[1][1]], axis=1)
     put(REACH * depths, tops, bottoms)
     put(REACH * (depths + 1), *tiles[2])
-    ends_ref[...] = packed_ref[...].astype(jnp.bfloat16)
-
-
-def relay_kernel(ends_ref, after_ref, out_ref):
-    out_ref[...] = ends_ref[1]
+    near_ref[...] = packed_ref[0].astype(jnp.bfloat16)
+    far_ref[...] = packed_ref[1].astype(jnp.bfloat16)
+
+
+def relay_kernel(rows_ref, after_ref, out_ref):
+    out_ref[...] = rows_ref[...]
 
 
 def moments(grad_i, grad_x, grad_z):
@@ -193,51 +196,30 @@
     part_ref[1, comp] = summed[EDGE * (chunks - 1) :]
 
 
+def make_moments(pair, vol_ref, diff_i_ref, diff_x_ref, moments_ref):
+    depths, rows, cols = vol_ref.shape
+    planes = [vol_ref[2 * pair + k] for k in range(4)]
+    across = dot(jnp.concatenate(planes[1:3], axis=0), diff_x_ref[...])
+    for k in range(2):
+        grad_i = dot(diff_i_ref[...], planes[k + 1])
+        grad_x = across[rows * k : rows * (k + 1)]
+        grad_z = planes[k + 2].astype(jnp.float32) - planes[k].astype(jnp.float32)
+        for comp, term in enumerate(moments(grad_i, grad_x, grad_z)):
+            moments_ref[k, comp] = term
+
+
+def make_lines(pair, lines_ref, moments_ref, inner_ref, part_ref):
+    for k in range(2):
+        z = 2 * pair + k
+        for comp in range(6):
+            store_chunks(dot(lines_ref[...], moments_ref[k, comp]), comp, inner_ref.at[z], part_ref.at[:, :, z])
+
+
 def lines_kernel(vol_ref, lines_ref, diff_i_ref, diff_x_ref, inner_ref, part_ref, even_ref, odd_ref):
-    own_lines(0, HEAD, vol_ref, lines_ref, diff_i_ref, diff_x_ref, inner_ref, part_ref, even_ref, odd_ref)
-
-
-def more_lines_kernel(
-    vol_ref, halo_ref, lines_ref, diff_i_ref, diff_x_ref, diff_h_ref, inner_in_ref, part_in_ref,
-    inner_ref, part_ref, inner_h_ref, part_h_ref, even_ref, odd_ref,
-):
-    both = dot(halo_ref[...], diff_h_ref[...])
-    grad_i = dot(diff_i_ref[...], halo_ref[:, :256])
-    for comp, term in enumerate(moments(grad_i, both[:, 256:], both[:, :256])):
-        store_chunks(dot(lines_ref[...], term), comp, inner_h_ref, part_h_ref)
-    stop = vol_ref.shape[0] - 2
-    own_lines(HEAD, stop, vol_ref, lines_ref, diff_i_ref, diff_x_ref, inner_ref, part_ref, even_ref, odd_ref)
-
-
-def own_lines(first, stop, vol_ref, lines_ref, diff_i_ref, diff_x_ref, inner_ref, part_ref, even_ref, odd_ref):
-    depths, rows, cols = vol_ref.shape
-
-    def stage_moments(z, moments_ref):
-        centre = vol_ref[pl.ds(z + 1, 2)]
-        across = dot(centre.reshape(2 * rows, cols), diff_x_ref[...])
-        for k in range(2):
-            grad_i = dot(diff_i_ref[...], centre[k])
-            grad_x = across[rows * k : rows * (k + 1)]
-            grad_z = vol_ref[z + k + 2].astype(jnp.float32) - vol_ref[z + k].astype(jnp.float32)
-            for comp, term in enumerate(moments(grad_i, grad_x, grad_z)):
-                moments_ref[k, comp] = term
-
-    def stage_lines(z, moments_ref):
-        for k in range(2):
-            for comp in range(6):
-                store_chunks(dot(lines_ref[...], moments_ref[k, comp]), comp, inner_ref.at[z + k], part_ref.at[:, :, z + k])
-
-    stage_moments(first, even_ref)
-
-    def step(index, carry):
-        z = first + 4 * index
-        stage_moments(z + 2, odd_ref)
-        stage_lines(z, even_ref)
-        stage_moments(jnp.minimum(z + 4, stop - 2), even_ref)
-        stage_lines(z + 2, odd_ref)
-        return carry
-
-    lax.fori_loop(0, (stop - first) // 4, step, 0)
+    slots = (even_ref, odd_ref)
+    for pair in range(HEAD):
+        make_moments(pair, vol_ref, diff_i_ref, diff_x_ref, slots[pair % 2])
+        make_lines(pair, lines_ref, slots[pair % 2], inner_ref, part_ref)
 
 
 def attributes(own, border, smooth_ref, store):
@@ -262,23 +244,67 @@
     return jnp.where(lax.div(iota(packed.shape, 1), SIDE) == lax.div(base, SIDE), moved, 0.0)
 
 
-def inner_kernel(inner_ref, inner_h_ref, smooth_ref, pack_h_ref, out_ref, border_ref):
+def own_kernel(
+    stage, vol_ref, lines_ref, diff_i_ref, diff_x_ref, smooth_ref, halo_ref, diff_h_ref, pack_h_ref,
+    inner_in_ref, part_in_ref, *refs,
+):
+    if stage == 0:
+        inner_ref, part_ref, *targets, later_ref, part_h_ref, border_ref, even_ref, odd_ref, out_ref, sems = refs
+        both = dot(halo_ref[...], diff_h_ref[...])
+        grad_i = dot(diff_i_ref[...], halo_ref[:, :256])
+        lined_h = [[] for chunk in range(inner_ref.shape[1])]
+        for comp, term in enumerate(moments(grad_i, both[:, 256:], both[:, :256])):
+            summed = dot(lines_ref[...], term)
+            for chunk, parts in enumerate(lined_h):
+                parts.append(summed[EDGE * (chunk + 1) : EDGE * (chunk + 2)].astype(jnp.bfloat16))
+            part_h_ref[0, comp] = summed[:EDGE]
+            part_h_ref[1, comp] = summed[EDGE * (len(lined_h) + 1) :]
+        border_ref[...] = dot(jnp.concatenate(sum(lined_h, []), axis=0), pack_h_ref[...])
+        finished = []
+    else:
+        border_ref, done_ref, *refs = refs
+        inner_ref, part_ref, *targets, later_ref, even_ref, odd_ref, out_ref, sems, done_sems = refs[3:]
+        finished = []
     count, chunks = inner_ref.shape[:2]
-    half, inner = count // 2, EDGE * chunks
-    border_ref[...] = dot(inner_h_ref[...].reshape(6 * inner, 256), pack_h_ref[...])
-
-    def step(k, carry):
-        for group in range(2):
+    pairs, inner = count // 4, EDGE * chunks
+    slots = (even_ref, odd_ref)
+
+    def place(target, pair):
+        return target.at[pl.ds(2 * pair, 2), pl.ds(EDGE, inner)]
+
+    if stage == 1:
+        for n, target in enumerate(targets):
+            finished.append(pltpu.make_async_copy(done_ref.at[n], place(target, pairs - 1), done_sems.at[n]))
+            finished[-1].start()
+
+    ahead = list(range(HEAD, pairs + AHEAD) if stage == 0 else range(pairs + AHEAD, 2 * pairs))
+    for step in range(pairs):
+        pair = pairs * stage + step
+        todo = ahead[step : step + 1]
+        for q in todo:
+            make_moments(q, vol_ref, diff_i_ref, diff_x_ref, slots[q % 2])
+        for k in range(2):
+            z = 2 * pair + k
 
             def store(chunk, lanes, values):
+                rows = slice(EDGE * chunk, EDGE * (chunk + 1))
                 for n, value in enumerate(values):
-                    out_ref[n, half * group + k, EDGE * chunk : EDGE * (chunk + 1), lanes] = value
-
-            border = border_of(border_ref[:, 128 * group : 128 * (group + 1)], k)
-            attributes(inner_ref[half * group + k].reshape(6 * inner, 256), border, smooth_ref, store)
-        return carry
-
-    lax.fori_loop(0, half, step, 0, unroll=2)
+                    if step == pairs - 1:
+                        later_ref[n, k, rows, lanes] = value
+                    else:
+                        out_ref[n, 2 * step + k, rows, lanes] = value
+
+            border = border_of(border_ref[:, 128 * stage : 128 * (stage + 1)], z % SLOTS)
+            attributes(inner_ref[z].reshape(6 * inner, 256), border, smooth_ref, store)
+        for q in todo:
+            make_lines(q, lines_ref, slots[q % 2], inner_ref, part_ref)
+        if step < pairs - 1:
+            for n, target in enumerate(targets):
+                source = out_ref.at[n, pl.ds(2 * step, 2)]
+                finished.append(pltpu.make_async_copy(source, place(target, pair), sems.at[step, n]))
+                finished[-1].start()
+    for copy in finished:
+        copy.wait()
 
 
 def end_kernel(
@@ -286,7 +312,7 @@
     smooth_ref, pack_h_ref, diff_x_ref, diff_h_ref, lines_e_ref, diff_e_ref, done_ref, *refs,
 ):
     last = exchange == 1
-    targets, refs = (refs[3:6], refs[6:]) if last else (refs[:3], refs[3:])
+    targets, refs = refs[3:6], refs[6:]
     if last:
         packed_ref, block_ref, block_h_ref, border_ref, edge_ref, out_ref, done_sems, sems = refs
     else:
@@ -297,16 +323,24 @@
     low = low_end(exchange)
     end = jnp.where(low, 0, 1)
     start = pl.multiple_of(jnp.where(low, 0, rows - EDGE), EDGE)
-    done_start = pl.multiple_of(jnp.where(low, rows - EDGE, 0), EDGE) if last else EDGE
-    finished = [
-        pltpu.make_async_copy(done_ref.at[n], target.at[:, pl.ds(done_start, done_ref.shape[2])], done_sems.at[n])
-        for n, target in enumerate(targets)
-    ]
+    other = pl.multiple_of(jnp.where(low, rows - EDGE, 0), EDGE)
+    finished = []
+    for n, target in enumerate(targets):
+        if last:
+            place = target.at[:, pl.ds(other, EDGE)]
+        else:
+            place = target.at[pl.ds(count - 2, 2), pl.ds(EDGE, rows - 2 * EDGE)]
+        finished.append(pltpu.make_async_copy(done_ref.at[n], place, done_sems.at[n]))
     for copy in finished:
         copy.start()
 
     packed_ref[:8] = jnp.zeros_like(packed_ref[:8])
-    packed_ref[8:] = (rows_ref[...] if last else rows_ref[0]).astype(f32)
+    if last:
+        il = lax.axis_index("il")
+        outside = (low & (il == 0)) | (jnp.logical_not(low) & (il == lax.axis_size("il") - 1))
+        packed_ref[8:] = jnp.where(outside, 0.0, rows_ref[...].astype(f32))
+    else:
+        packed_ref[8:] = rows_ref[...].astype(f32)
 
     def joined(row, own):
         lanes = own.shape[1]
@@ -332,39 +366,34 @@
         lined_h.append(summed.astype(bf16))
     border_ref[...] = dot(jnp.concatenate(lined_h, axis=0), pack_h_ref[...])
 
-    centre = block_ref[1 : count + 1].reshape(count * EDGE, cols)
-    grad_i = dot(diff_e_ref[...], centre)
-    grad_x = dot(centre, diff_x_ref[...])
-    grad_z = block_ref[2:].astype(f32) - block_ref[:count].astype(f32)
-    for comp, term in enumerate(moments(grad_i, grad_x, grad_z.reshape(count * EDGE, cols))):
-        outer = dot(lines_e_ref[exchange], term)
-        summed = part_ref[end, comp] + outer.reshape(count, EDGE, cols)
-        edge_ref[:, comp] = summed.astype(bf16)
-
+    span = EDGE * half
     copies = []
-    for pair in range(half // 2):
-        own, border, places = [], [], []
-        for group in range(2):
-            for parity in range(2):
-                k = 2 * pair + parity
-                places.append(half * group + k)
-                own.append(edge_ref[half * group + k].reshape(6 * EDGE, cols))
-                border.append(border_of(border_ref[:, 128 * group : 128 * (group + 1)], k))
+    for group in range(2):
+        first = half * group
+        centre = block_ref[first + 1 : first + half + 1].reshape(span, cols)
+        grad_i = dot(diff_e_ref[:span, :span], centre)
+        grad_x = dot(centre, diff_x_ref[...])
+        grad_z = block_ref[first + 2 : first + half + 2].astype(f32) - block_ref[first : first + half].astype(f32)
+        for comp, term in enumerate(moments(grad_i, grad_x, grad_z.reshape(span, cols))):
+            outer = dot(lines_e_ref[exchange, :span, :span], term)
+            summed = part_ref[end, comp, first : first + half] + outer.reshape(half, EDGE, cols)
+            edge_ref[first : first + half, comp] = summed.astype(bf16)
+    for group in range(2):
+        first = half * group
+        border = [border_of(border_ref[:, 128 * group : 128 * (group + 1)], k) for k in range(half)]
 
         def store(chunk, lanes, values):
             for n, value in enumerate(values):
-                out_ref[n, places[chunk], :, lanes] = value
-
-        attributes(jnp.concatenate(own, axis=0), jnp.concatenate(border, axis=0), smooth_ref, store)
+                out_ref[n, first + chunk, :, lanes] = value
+
+        own = edge_ref[first : first + half].reshape(6 * span, cols)
+        attributes(own, jnp.concatenate(border, axis=0), smooth_ref, store)
         if last:
-            for group in range(2):
-                depth = pl.ds(half * group + 2 * pair, 2)
-                for n, target in enumerate(targets):
-                    copy = pltpu.make_async_copy(
-                        out_ref.at[n, depth], target.at[depth, pl.ds(start, EDGE)], sems.at[pair, group, n]
-                    )
-                    copy.start()
-                    copies.append(copy)
+            depth = pl.ds(first, half)
+            for n, target in enumerate(targets):
+                copy = pltpu.make_async_copy(out_ref.at[n, depth], target.at[depth, pl.ds(start, EDGE)], sems.at[group, n])
+                copy.start()
+                copies.append(copy)
     for copy in finished + copies:
         copy.wait()
 
@@ -419,40 +448,51 @@
     lined = [((count, chunks, 6, EDGE, cols), bf16), ((2, 6, count, EDGE, cols), f32)]
     moment_slots = [pltpu.VMEM((2, 6, rows, cols), bf16)] * 2
     inner, part = call("lines_kernel", lines_kernel, lined, moment_slots, [vol, lines, diff_i, diff_x], flops=work // 4)
-    halo, ends = call(
+    packed = ((packed_rows, cols), bf16)
+    halo, near, far = call(
         "rows_kernel",
         rows_kernel,
-        [((rows, 128 * TILES), bf16), ((2, packed_rows, cols), bf16)],
+        [((rows, 128 * TILES), bf16), packed, packed],
         [pltpu.VMEM((2, packed_rows, cols), f32)],
         [vol, own, side, part],
         in_specs=[WHOLE] * 3 + [ANYWHERE],
     )
-    ends_in = lax.ppermute(ends, "il", [(i, i ^ 1) for i in range(il)])
-    operands = [vol, halo, lines, diff_i, diff_x, diff_h, inner, part]
-    inner, part, inner_h, part_h = call(
-        "more_lines_kernel",
-        more_lines_kernel,
-        lined + [((chunks, 6, EDGE, 256), bf16), ((2, 6, EDGE, 256), f32)],
-        moment_slots,
-        operands,
-        flops=2 * work,
-        aliases={len(operands) - 2 + n: n for n in range(2)},
-    )
-    (done,) = call(
-        "inner_kernel",
-        inner_kernel,
-        [((3, count, EDGE * chunks, cols), f32)],
-        [pltpu.VMEM((6 * EDGE * chunks, 256), f32)],
-        [inner, inner_h, smooth, pack_h],
-        flops=2 * work,
-    )
-    (relayed,) = call(
-        "relay_kernel", relay_kernel, [((packed_rows, cols), bf16)], [], [ends_in, done], in_specs=[WHOLE, ANYWHERE]
-    )
-    onward = [(i, i + 2) for i in range(0, il - 2, 2)] + [(i, i - 2) for i in range(3, il, 2)]
+    swap = [(i, i ^ 1) for i in range(il)]
+    onward = [(i, i + 2) for i in range(0, il - 2, 2)] + [(il - 2, il - 1)]
+    onward += [(i, i - 2) for i in range(3, il, 2)] + [(1, 0)]
+    far_in = lax.ppermute(far, "il", swap)
+    near_in = lax.ppermute(near, "il", swap)
+
+    outs = [((count, rows, cols), f32)] * 3
+    saved = ((3, 2, EDGE * chunks, cols), f32)
+    border = ((6 * EDGE * chunks, 256), f32)
+    ready = [((3, count // 2 - 2, EDGE * chunks, cols), f32)]
+    own_scratch = moment_slots + [pltpu.VMEM(*ready[0]), pltpu.SemaphoreType.DMA((count // 4 - 1, 3))]
+    shared = [vol, lines, diff_i, diff_x, smooth, halo, diff_h, pack_h]
+    inner, part, *outs_in, done, part_h, border = call(
+        "first_own_kernel",
+        lambda *refs: own_kernel(0, *refs),
+        lined + outs + [saved, ((2, 6, EDGE, 256), f32), border],
+        own_scratch,
+        shared + [inner, part],
+        out_specs=(WHOLE,) * 2 + (IN_HBM,) * 3 + (WHOLE,) * 3,
+        flops=3 * work,
+        aliases={len(shared) + n: n for n in range(2)},
+    )
+    (relayed,) = call("relay_kernel", relay_kernel, [packed], [], [far_in, done], in_specs=[WHOLE, ANYWHERE])
     relayed_in = lax.ppermute(relayed, "il", onward)
-
-    outs = [((count, rows, cols), f32)] * 3
+    inner, part, *outs_in, done = call(
+        "second_own_kernel",
+        lambda *refs: own_kernel(1, *refs),
+        lined + outs + [saved],
+        own_scratch + [pltpu.SemaphoreType.DMA((3,))],
+        shared + [inner, part, border, done] + outs_in,
+        in_specs=[WHOLE] * (len(shared) + 4) + [IN_HBM] * 3,
+        out_specs=(WHOLE,) * 2 + (IN_HBM,) * 3 + (WHOLE,),
+        flops=3 * work,
+        aliases={len(shared): 0, len(shared) + 1: 1} | {len(shared) + 4 + n: 2 + n for n in range(3)},
+    )
+
     end_rows = (3, count, EDGE, cols)
     tables = [smooth, pack_h, diff_x, diff_h, lines_e, diff_e]
     scratch = [
@@ -463,21 +503,24 @@
         pltpu.VMEM((count, 6, EDGE, cols), bf16),
     ]
     sems = pltpu.SemaphoreType.DMA((3,))
+    operands = [vol, halo, near_in, part, part_h, *tables, done]
     *outs_in, done = call(
         "near_end_kernel",
         lambda *refs: end_kernel(0, *refs),
         outs + [(end_rows, f32)],
         scratch + [sems],
-        [vol, halo, ends_in, part, part_h, *tables, done],
+        operands + outs_in,
+        in_specs=[WHOLE] * len(operands) + [IN_HBM] * 3,
         out_specs=(IN_HBM,) * 3 + (WHOLE,),
         flops=work,
+        aliases={len(operands) + n: n for n in range(3)},
     )
     operands = [vol, halo, relayed_in, part, part_h, *tables, done]
     return call(
         "far_end_kernel",
         lambda *refs: end_kernel(1, *refs),
         outs,
-        scratch + [pltpu.VMEM(end_rows, f32), sems, pltpu.SemaphoreType.DMA((half // 2, 2, 3))],
+        scratch + [pltpu.VMEM(end_rows, f32), sems, pltpu.SemaphoreType.DMA((2, 3))],
         operands + outs_in,
         in_specs=[WHOLE] * len(operands) + [IN_HBM] * 3,
         out_specs=(IN_HBM,) * 3,

time: 22 us -> 19.5 us (0.89)
  starting transfers between devices: 6.94 us -> 5.59 us
  Pallas kernels: 13.8 us -> 12.7 us
    ppermute x1, starting transfers between devices: 3.49 us -> 2.06 us  [body(): relayed_in = lax.ppermute(relayed, 'il', onward)]
    pallas_call x9, Pallas kernels: 13.8 us -> 12.7 us  [call(): pl.pallas_call(kernel, out_shape=tuple((jax.ShapeDtypeStruct(*out) for ou...]
    ppermute x1 -> x2, starting transfers between devices: 2.94 us -> 3.02 us  [the longest x1 2.94 us: body(): far_in = lax.ppermute(far, 'il', swap)]
  transfers between devices with their start and end apart: 3 -> 4, of which waited for: 1 -> 0; matrix products, arithmetic and copies ran while one was open for 0% -> 0% of each run, Pallas kernels for 45% -> 46%
where the time goes in v8:
time: 19.5 us; the launch traced here: 19.3 us
  Pallas kernels  12.7 us (65%)
  starting transfers between devices  5.59 us (29%)
  between operations  0.72 us (4%)
  local copies, waits for them, and re-layouts  0.31 us (2%)
    pallas_call x9, Pallas kernels, call(): pl.pallas_call(kernel, out_shape=tuple((jax.ShapeDtypeStruct(*out) for ou...  12.7 us
    ppermute x1, starting transfers between devices, body(): far_in = lax.ppermute(far, 'il', swap)  2.94 us
    ppermute x1, starting transfers between devices, body(): relayed_in = lax.ppermute(relayed, 'il', onward)  2.06 us
    ppermute x1, starting transfers between devices, body(): side = lax.ppermute(send, 'xl', [(0, 1), (1, 0)])  0.52 us
  transfers between devices with their start and end apart: 4, of which 0 were waited for; matrix products, arithmetic and copies ran while one was open for 0% of the time, Pallas kernels for 46%

profile of v8, /device:TPU:0, one launch (start us, length us, event | category | flops | bytes accessed | tf_op | source)
XLA Modules:
  0.0 19.3 jit_solution(6474803249254009987)
XLA Ops:
  0.6 0.0 copy-start
  0.6 1.0 %tables_kernel.1 = (bf16[128,128]{1,0:T(8,128)(2,1)S(1)}, bf16[128,128]{1,0:T(8,128)(2,1)S(1)}, bf16[256,256]{1,0:T(8,128)(2,1)S(1)}, bf16[256,256]{1,0:T(8,128)...) custom-call(), custom_call_target="tpu_custom_call" | custom-call | flops 1073741824 | tf_op jit(solution)/shard_map/tables_kernel/pallas_call | solution.py:402
  1.6 0.3 %copy-done = bf16[18,128,256]{2,1,0:T(8,128)(2,1)S(1)} copy-done((bf16[18,128,256]{2,1,0:T(8,128)(2,1)S(1)}, bf16[18,128,256]{2,1,0:T(8,128)(2,1)}, u32[]{:S(2)}) %copy-start) | copy-done | bytes 1179672
  1.9 0.5 %pack_kernel.1 = (bf16[18,128,256]{2,1,0:T(8,128)(2,1)S(1)}, bf16[3,128,128]{2,1,0:T(8,128)(2,1)S(1)}, bf16[3,128,128]{2,1,0:T(8,128)(2,1)S(1)}) custom-call(bf16[18,128,256]{2,1,0:T(8,128)(2,1)S(1)} %copy-done, bf16[256,256]{1,0:T(8,128)(2,1)S(1)} %get-tuple-element.37.pick_ref), custom_call_target="tpu_custom_call" | custom-call | tf_op jit(solution)/shard_map/pack_kernel/pallas_call | solution.py:402
  2.4 0.5 %collective-permute-start = (bf16[3,128,128]{2,1,0:T(8,128)(2,1)S(1)}, bf16[3,128,128]{2,1,0:T(8,128)(2,1)S(1)}, u32[]{:S(2)}, u32[]{:S(2)}) collective-permute-start(bf16[3,128,128]{2,1,0:T(8,128)(2,1)S(1)} %get-tuple-element.40), channel_id=1, source_target_pairs={{0,1},{1,0},{2,3},{3,2},{4,5},{5,4},{6,7},{7,6},{8,9},{9,8},{10,11... | collective-permute-start | bytes 294920 | tf_op jit(solution)/shard_map/ppermute | solution.py:446
  2.9 0.9 %lines_kernel.1 = (bf16[16,6,6,16,256]{4,3,2,1,0:T(8,128)(2,1)S(1)}, f32[2,6,16,16,256]{4,3,2,1,0:T(8,128)S(1)}) custom-call(bf16[18,128,256]{2,1,0:T(8,128)(2,1)S(1)} %get-tuple-element.38.vol_ref.refs_0_, bf16[128,128]{1,0:T(8,128)(2,1)S(1)} %get-tuple-element.41.lines_ref.refs_1_, bf16[128,128]{1,0:T(8,128)(2,1)S(1)} %get-tuple-element.42.diff_i_ref.refs_2_, ...), custom_call_target="tpu_custom_call" | custom-call | flops 268435456 | tf_op jit(solution)/shard_map/lines_kernel/pallas_call | solution.py:402
  3.9 0.0 collective-permute-done.side_ref
  3.9 0.2 rows_kernel.1
  4.0 2.9 %collective-permute-start.1 = (bf16[208,256]{1,0:T(8,128)(2,1)S(1)}, bf16[208,256]{1,0:T(8,128)(2,1)S(1)}, u32[]{:S(2)}, u32[]{:S(2)}) collective-permute-start(bf16[208,256]{1,0:T(8,128)(2,1)S(1)} %get-tuple-element.46), channel_id=1, source_target_pairs={{0,2},{2,0},{4,6},{6,4},{8,10},{10,8},{12,14},{14,12},{1,3},{3,1},... | collective-permute-start | bytes 319496 | tf_op jit(solution)/shard_map/ppermute | solution.py:463
  7.0 0.1 collective-permute-start.3
  7.1 3.8 %first_own_kernel.1 = (bf16[16,6,6,16,256]{4,3,2,1,0:T(8,128)(2,1)S(1)}, f32[2,6,16,16,256]{4,3,2,1,0:T(8,128)S(1)}, f32[16,128,256]{2,1,0:T(8,128)}, f32[16,128...) custom-call(bf16[18,128,256]{2,1,0:T(8,128)(2,1)S(1)} %get-tuple-ele, ...), custom_call_target="tpu_custom_call", output_to_operand_aliasing={{0}: (8, {}), {1}: (9, {})} | custom-call | flops 3221225472 | tf_op jit(solution)/shard_map/first_own_kernel/pallas_call | solution.py:402
  10.8 0.0 collective-permute-done.1.rows_ref
  10.9 2.1 %collective-permute-start.2 = (bf16[208,256]{1,0:T(8,128)(2,1)S(1)}, bf16[208,256]{1,0:T(8,128)(2,1)S(1)}, u32[]{:S(2)}, u32[]{:S(2)}) collective-permute-start(bf16[208,256]{1,0:T(8,128)(2,1)S(1)} %relay_kernel.1), channel_id=1, source_target_pairs={{0,4},{4,8},{8,12},{12,14},{6,2},{10,6},{14,10},{2,0},{1,5},{5,9},... | collective-permute-start | bytes 319496 | tf_op jit(solution)/shard_map/ppermute | solution.py:483
  12.9 2.6 %second_own_kernel.1 = (bf16[16,6,6,16,256]{4,3,2,1,0:T(8,128)(2,1)S(1)}, f32[2,6,16,16,256]{4,3,2,1,0:T(8,128)S(1)}, f32[16,128,256]{2,1,0:T(8,128)}, f32[16,12...) custom-call(bf16[18,128,256]{2,1,0:T(8,128)(2,1)S(1)} %get-tuple-ele, ...), custom_call_target="tpu_custom_call", output_to_operand_aliasing={{0}: (8, {}), {1}: (9, {}), {2}: (12, {}), {3}: (13, {}), {... | custom-call | flops 3221225472 | tf_op jit(solution)/shard_map/second_own_kernel/pallas_call | solution.py:402
  15.6 0.0 collective-permute-done.3.refs_2_
  15.6 1.6 %near_end_kernel.1 = (f32[16,128,256]{2,1,0:T(8,128)}, f32[16,128,256]{2,1,0:T(8,128)}, f32[16,128,256]{2,1,0:T(8,128)}, f32[3,16,16,256]{3,2,1,0:T(8,128)S(1)}) custom-call(bf16[18,128,256]{2,1,0:T(8,128)(2,1)S(1)} %get-tuple-element.38.vol_ref.refs_0_, ...), custom_call_target="tpu_custom_call", output_to_operand_aliasing={{0}: (12, {}), {1}: (13, {}), {2}: (14, {})} | custom-call | flops 1073741824 | tf_op jit(solution)/shard_map/near_end_kernel/pallas_call | solution.py:402
  17.2 0.0 collective-permute-done.2.refs_2_
  17.2 2.2 %far_end_kernel.1 = (f32[16,128,256]{2,1,0:T(8,128)}, f32[16,128,256]{2,1,0:T(8,128)}, f32[16,128,256]{2,1,0:T(8,128)}) custom-call(bf16[18,128,256]{2,1,0:T(8,128)(2,1)S(1)} %get-tuple-element.38.vol_ref.refs_0_, bf16[128,384]{1,0:T(8,128)(2,1)S(1)} %get-tuple-element.45.refs_5_.refs_1_, ...), custom_call_target="tpu_custom_call", output_to_operand_aliasing={{0}: (12, {}), {1}: (13, {}), {2}: (14, {})} | custom-call | flops 1073741824 | tf_op jit(solution)/shard_map/far_end_kernel/pallas_call | solution.py:402
  (1 shorter events, 0.0 us)
Async XLA Ops:
  0.6 1.3 %copy-start = (bf16[18,128,256]{2,1,0:T(8,128)(2,1)S(1)}, bf16[18,128,256]{2,1,0:T(8,128)(2,1)}, u32[]{:S(2)}) copy-start(bf16[18,128,256]{2,1,0:T(8,128)(2,1)} %vol_ref.1) | copy-start | bytes 3538948
  2.4 1.5 %collective-permute-start = (bf16[3,128,128]{2,1,0:T(8,128)(2,1)S(1)}, bf16[3,128,128]{2,1,0:T(8,128)(2,1)S(1)}, u32[]{:S(2)}, u32[]{:S(2)}) collective-permute-start(bf16[3,128,128]{2,1,0:T(8,128)(2,1)S(1)} %get-tuple-element.40), channel_id=1, source_target_pairs={{0,1},{1,0},{2,3},{3,2},{4,5},{5,4},{6,7},{7,6},{8,9},{9,8},{10,11... | collective-permute-start | bytes 294920 | tf_op jit(solution)/shard_map/ppermute | solution.py:446
  4.0 6.8 %collective-permute-start.1 = (bf16[208,256]{1,0:T(8,128)(2,1)S(1)}, bf16[208,256]{1,0:T(8,128)(2,1)S(1)}, u32[]{:S(2)}, u32[]{:S(2)}) collective-permute-start(bf16[208,256]{1,0:T(8,128)(2,1)S(1)} %get-tuple-element.46), channel_id=1, source_target_pairs={{0,2},{2,0},{4,6},{6,4},{8,10},{10,8},{12,14},{14,12},{1,3},{3,1},... | collective-permute-start | bytes 319496 | tf_op jit(solution)/shard_map/ppermute | solution.py:463
  7.0 8.6 %collective-permute-start.3 = (bf16[208,256]{1,0:T(8,128)(2,1)S(1)}, bf16[208,256]{1,0:T(8,128)(2,1)S(1)}, u32[]{:S(2)}, u32[]{:S(2)}) collective-permute-start(bf16[208,256]{1,0:T(8,128)(2,1)S(1)} %get-tuple-element.62), channel_id=1, source_target_pairs={{0,2},{2,0},{4,6},{6,4},{8,10},{10,8},{12,14},{14,12},{1,3},{3,1},... | collective-permute-start | bytes 319496 | tf_op jit(solution)/shard_map/ppermute | solution.py:464
  10.9 6.3 %collective-permute-start.2 = (bf16[208,256]{1,0:T(8,128)(2,1)S(1)}, bf16[208,256]{1,0:T(8,128)(2,1)S(1)}, u32[]{:S(2)}, u32[]{:S(2)}) collective-permute-start(bf16[208,256]{1,0:T(8,128)(2,1)S(1)} %relay_kernel.1), channel_id=1, source_target_pairs={{0,4},{4,8},{8,12},{12,14},{6,2},{10,6},{14,10},{2,0},{1,5},{5,9},... | collective-permute-start | bytes 319496 | tf_op jit(solution)/shard_map/ppermute | solution.py:483

commit v9 on v8

--- a/solution.py
+++ b/solution.py
@@ -72,7 +72,7 @@
     return jnp.logical_not(even) if exchange == 0 else even
 
 
-def tables_kernel(depths, lines_ref, diff_i_ref, diff_x_ref, smooth_ref, pack_h_ref, diff_h_ref, lines_e_ref, diff_e_ref, pick_ref):
+def tables_kernel(depths, lines_ref, diff_i_ref, diff_x_ref, smooth_ref, pack_h_ref, diff_h_ref, lines_e_ref, diff_e_ref, pick_ref, mask_ref):
     rows, cols = lines_ref.shape[0], diff_x_ref.shape[0]
     x, il, last = lax.axis_index("xl"), lax.axis_index("il"), lax.axis_size("il") - 1
     bf16 = jnp.bfloat16
@@ -124,6 +124,9 @@
     low, high = place < OWN, place >= SIDE - OWN
     kept = jnp.where(x == 0, jnp.where(low, cols - OWN + place, FAR), jnp.where(high, place - (SIDE - OWN), FAR))
     pick_ref[...] = jnp.where(source == jnp.where(lane < 128, sent, kept), 1.0, 0.0).astype(bf16)
+    lane = iota((8, 128), 1)
+    border = jnp.where(x == 0, lane - (128 - SIDE), lane)
+    mask_ref[...] = jnp.where((border >= 0) & (border < SIDE), 1.0, 0.0)
 
 
 def pack_kernel(vol_ref, pick_ref, copy_ref, send_ref, own_ref):
@@ -232,20 +235,21 @@
         for half, lane in zip(halves, lanes):
             a, b, c, d, e, f = [half[base + EDGE * comp : base + EDGE * (comp + 1)] for comp in range(6)]
             low = c + 1e-6
-            inverse = reciprocal(low)
+            guess = pl.reciprocal(low, approx=True)
+            inverse = guess * (low * guess - 2.0)
             spread = (a - b) * (a - c) + (b - c) * (b - c) + 3.0 * (d * d + e * e + f * f)
             root = spread * lax.rsqrt(jnp.maximum(spread, TINY))
-            store(chunk, pl.ds(lane, 128), (-e * inverse, -f * inverse, root * reciprocal(a + b + low)))
-
-
-def border_of(packed, slot):
+            store(chunk, pl.ds(lane, 128), (e * inverse, f * inverse, root * reciprocal(a + b + low)))
+
+
+def border_of(packed, slot, mask_ref):
     base = jnp.where(lax.axis_index("xl") == 0, 128 - SIDE, 0)
     moved = pltpu.roll(packed, lax.rem(base - SIDE * slot + 128, 128), 1)
-    return jnp.where(lax.div(iota(packed.shape, 1), SIDE) == lax.div(base, SIDE), moved, 0.0)
+    return (moved.reshape(-1, 8, 128) * mask_ref[...]).reshape(packed.shape)
 
 
 def own_kernel(
-    stage, vol_ref, lines_ref, diff_i_ref, diff_x_ref, smooth_ref, halo_ref, diff_h_ref, pack_h_ref,
+    stage, vol_ref, lines_ref, diff_i_ref, diff_x_ref, smooth_ref, halo_ref, diff_h_ref, pack_h_ref, mask_ref,
     inner_in_ref, part_in_ref, *refs,
 ):
     if stage == 0:
@@ -294,7 +298,7 @@
                     else:
                         out_ref[n, 2 * step + k, rows, lanes] = value
 
-            border = border_of(border_ref[:, 128 * stage : 128 * (stage + 1)], z % SLOTS)
+            border = border_of(border_ref[:, 128 * stage : 128 * (stage + 1)], z % SLOTS, mask_ref)
             attributes(inner_ref[z].reshape(6 * inner, 256), border, smooth_ref, store)
         for q in todo:
             make_lines(q, lines_ref, slots[q % 2], inner_ref, part_ref)
@@ -309,7 +313,7 @@
 
 def end_kernel(
     exchange, vol_ref, halo_ref, rows_ref, part_ref, part_h_ref,
-    smooth_ref, pack_h_ref, diff_x_ref, diff_h_ref, lines_e_ref, diff_e_ref, done_ref, *refs,
+    smooth_ref, pack_h_ref, diff_x_ref, diff_h_ref, lines_e_ref, diff_e_ref, mask_ref, done_ref, *refs,
 ):
     last = exchange == 1
     targets, refs = refs[3:6], refs[6:]
@@ -380,7 +384,7 @@
             edge_ref[first : first + half, comp] = summed.astype(bf16)
     for group in range(2):
         first = half * group
-        border = [border_of(border_ref[:, 128 * group : 128 * (group + 1)], k) for k in range(half)]
+        border = [border_of(border_ref[:, 128 * group : 128 * (group + 1)], k, mask_ref) for k in range(half)]
 
         def store(chunk, lanes, values):
             for n, value in enumerate(values):
@@ -423,7 +427,7 @@
     packed_rows = -(-REACH * (depths + 2) // 16) * 16
 
     span = EDGE * count
-    lines, diff_i, diff_x, smooth, pack_h, diff_h, lines_e, diff_e, pick = call(
+    lines, diff_i, diff_x, smooth, pack_h, diff_h, lines_e, diff_e, pick, mask = call(
         "tables_kernel",
         lambda *refs: tables_kernel(depths, *refs),
         [
@@ -436,6 +440,7 @@
             ((2, span, span), bf16),
             ((span, span), bf16),
             ((cols, 256), bf16),
+            ((8, 128), f32),
         ],
         [],
         [],
@@ -468,7 +473,7 @@
     border = ((6 * EDGE * chunks, 256), f32)
     ready = [((3, count // 2 - 2, EDGE * chunks, cols), f32)]
     own_scratch = moment_slots + [pltpu.VMEM(*ready[0]), pltpu.SemaphoreType.DMA((count // 4 - 1, 3))]
-    shared = [vol, lines, diff_i, diff_x, smooth, halo, diff_h, pack_h]
+    shared = [vol, lines, diff_i, diff_x, smooth, halo, diff_h, pack_h, mask]
     inner, part, *outs_in, done, part_h, border = call(
         "first_own_kernel",
         lambda *refs: own_kernel(0, *refs),
@@ -494,7 +499,7 @@
     )
 
     end_rows = (3, count, EDGE, cols)
-    tables = [smooth, pack_h, diff_x, diff_h, lines_e, diff_e]
+    tables = [smooth, pack_h, diff_x, diff_h, lines_e, diff_e, mask]
     scratch = [
         pltpu.VMEM((8 + packed_rows, cols), f32),
         pltpu.VMEM((depths, EDGE, cols), bf16),

time: 19.5 us -> 19.6 us (level)
  no operation moved by 1% of the time
where the time goes in v9:
time: 19.6 us; the launch traced here: 19.4 us
  Pallas kernels  12.8 us (65%)
  starting transfers between devices  5.58 us (28%)
  between operations  0.72 us (4%)
  local copies, waits for them, and re-layouts  0.31 us (2%)
    pallas_call x9, Pallas kernels, call(): pl.pallas_call(kernel, out_shape=tuple((jax.ShapeDtypeStruct(*out) for ou...  12.8 us
    ppermute x1, starting transfers between devices, body(): far_in = lax.ppermute(far, 'il', swap)  2.94 us
    ppermute x1, starting transfers between devices, body(): relayed_in = lax.ppermute(relayed, 'il', onward)  2.05 us
    ppermute x1, starting transfers between devices, body(): side = lax.ppermute(send, 'xl', [(0, 1), (1, 0)])  0.52 us
  transfers between devices with their start and end apart: 4, of which 0 were waited for; matrix products, arithmetic and copies ran while one was open for 0% of the time, Pallas kernels for 46%

profile of v9, /device:TPU:0, one launch (start us, length us, event | category | flops | bytes accessed | tf_op | source)
XLA Modules:
  0.0 19.4 jit_solution(16992628552839234954)
XLA Ops:
  0.6 0.0 copy-start
  0.6 1.0 %tables_kernel.1 = (bf16[128,128]{1,0:T(8,128)(2,1)S(1)}, bf16[128,128]{1,0:T(8,128)(2,1)S(1)}, bf16[256,256]{1,0:T(8,128)(2,1)S(1)}, bf16[256,256]{1,0:T(8,128)...) custom-call(), custom_call_target="tpu_custom_call" | custom-call | flops 1073741824 | tf_op jit(solution)/shard_map/tables_kernel/pallas_call | solution.py:406
  1.6 0.3 %copy-done = bf16[18,128,256]{2,1,0:T(8,128)(2,1)S(1)} copy-done((bf16[18,128,256]{2,1,0:T(8,128)(2,1)S(1)}, bf16[18,128,256]{2,1,0:T(8,128)(2,1)}, u32[]{:S(2)}) %copy-start) | copy-done | bytes 1179672
  1.9 0.5 %pack_kernel.1 = (bf16[18,128,256]{2,1,0:T(8,128)(2,1)S(1)}, bf16[3,128,128]{2,1,0:T(8,128)(2,1)S(1)}, bf16[3,128,128]{2,1,0:T(8,128)(2,1)S(1)}) custom-call(bf16[18,128,256]{2,1,0:T(8,128)(2,1)S(1)} %copy-done, bf16[256,256]{1,0:T(8,128)(2,1)S(1)} %get-tuple-element.38.pick_ref), custom_call_target="tpu_custom_call" | custom-call | tf_op jit(solution)/shard_map/pack_kernel/pallas_call | solution.py:406
  2.4 0.5 %collective-permute-start = (bf16[3,128,128]{2,1,0:T(8,128)(2,1)S(1)}, bf16[3,128,128]{2,1,0:T(8,128)(2,1)S(1)}, u32[]{:S(2)}, u32[]{:S(2)}) collective-permute-start(bf16[3,128,128]{2,1,0:T(8,128)(2,1)S(1)} %get-tuple-element.41), channel_id=1, source_target_pairs={{0,1},{1,0},{2,3},{3,2},{4,5},{5,4},{6,7},{7,6},{8,9},{9,8},{10,11... | collective-permute-start | bytes 294920 | tf_op jit(solution)/shard_map/ppermute | solution.py:451
  2.9 0.9 %lines_kernel.1 = (bf16[16,6,6,16,256]{4,3,2,1,0:T(8,128)(2,1)S(1)}, f32[2,6,16,16,256]{4,3,2,1,0:T(8,128)S(1)}) custom-call(bf16[18,128,256]{2,1,0:T(8,128)(2,1)S(1)} %get-tuple-element.39.vol_ref.refs_0_, bf16[128,128]{1,0:T(8,128)(2,1)S(1)} %get-tuple-element.42.lines_ref.refs_1_, bf16[128,128]{1,0:T(8,128)(2,1)S(1)} %get-tuple-element.43.diff_i_ref.refs_2_, ...), custom_call_target="tpu_custom_call" | custom-call | flops 268435456 | tf_op jit(solution)/shard_map/lines_kernel/pallas_call | solution.py:406
  3.9 0.0 collective-permute-done.side_ref
  3.9 0.1 rows_kernel.1
  4.0 2.9 %collective-permute-start.1 = (bf16[208,256]{1,0:T(8,128)(2,1)S(1)}, bf16[208,256]{1,0:T(8,128)(2,1)S(1)}, u32[]{:S(2)}, u32[]{:S(2)}) collective-permute-start(bf16[208,256]{1,0:T(8,128)(2,1)S(1)} %get-tuple-element.47), channel_id=1, source_target_pairs={{0,2},{2,0},{4,6},{6,4},{8,10},{10,8},{12,14},{14,12},{1,3},{3,1},... | collective-permute-start | bytes 319496 | tf_op jit(solution)/shard_map/ppermute | solution.py:468
  7.0 0.1 collective-permute-start.3
  7.1 3.9 %first_own_kernel.1 = (bf16[16,6,6,16,256]{4,3,2,1,0:T(8,128)(2,1)S(1)}, f32[2,6,16,16,256]{4,3,2,1,0:T(8,128)S(1)}, f32[16,128,256]{2,1,0:T(8,128)}, f32[16,128...) custom-call(bf16[18,128,256]{2,1,0:T(8,128)(2,1)S(1)} %get-tuple-ele, ...), custom_call_target="tpu_custom_call", output_to_operand_aliasing={{0}: (9, {}), {1}: (10, {})} | custom-call | flops 3221225472 | tf_op jit(solution)/shard_map/first_own_kernel/pallas_call | solution.py:406
  11.0 0.0 collective-permute-done.1.rows_ref
  11.0 2.0 %collective-permute-start.2 = (bf16[208,256]{1,0:T(8,128)(2,1)S(1)}, bf16[208,256]{1,0:T(8,128)(2,1)S(1)}, u32[]{:S(2)}, u32[]{:S(2)}) collective-permute-start(bf16[208,256]{1,0:T(8,128)(2,1)S(1)} %relay_kernel.1), channel_id=1, source_target_pairs={{0,4},{4,8},{8,12},{12,14},{6,2},{10,6},{14,10},{2,0},{1,5},{5,9},... | collective-permute-start | bytes 319496 | tf_op jit(solution)/shard_map/ppermute | solution.py:488
  13.0 2.6 %second_own_kernel.1 = (bf16[16,6,6,16,256]{4,3,2,1,0:T(8,128)(2,1)S(1)}, f32[2,6,16,16,256]{4,3,2,1,0:T(8,128)S(1)}, f32[16,128,256]{2,1,0:T(8,128)}, f32[16,12...) custom-call(bf16[18,128,256]{2,1,0:T(8,128)(2,1)S(1)} %get-tuple-ele, ...), custom_call_target="tpu_custom_call", output_to_operand_aliasing={{0}: (9, {}), {1}: (10, {}), {2}: (13, {}), {3}: (14, {}), ... | custom-call | flops 3221225472 | tf_op jit(solution)/shard_map/second_own_kernel/pallas_call | solution.py:406
  15.7 0.0 collective-permute-done.3.refs_2_
  15.7 1.6 %near_end_kernel.1 = (f32[16,128,256]{2,1,0:T(8,128)}, f32[16,128,256]{2,1,0:T(8,128)}, f32[16,128,256]{2,1,0:T(8,128)}, f32[3,16,16,256]{3,2,1,0:T(8,128)S(1)}) custom-call(bf16[18,128,256]{2,1,0:T(8,128)(2,1)S(1)} %get-tuple-element.39.vol_ref.refs_0_, ...), custom_call_target="tpu_custom_call", output_to_operand_aliasing={{0}: (13, {}), {1}: (14, {}), {2}: (15, {})} | custom-call | flops 1073741824 | tf_op jit(solution)/shard_map/near_end_kernel/pallas_call | solution.py:406
  17.2 0.0 collective-permute-done.2.refs_2_
  17.3 2.2 %far_end_kernel.1 = (f32[16,128,256]{2,1,0:T(8,128)}, f32[16,128,256]{2,1,0:T(8,128)}, f32[16,128,256]{2,1,0:T(8,128)}) custom-call(bf16[18,128,256]{2,1,0:T(8,128)(2,1)S(1)} %get-tuple-element.39.vol_ref.refs_0_, bf16[128,384]{1,0:T(8,128)(2,1)S(1)} %get-tuple-element.46.refs_5_.refs_1_, ...), custom_call_target="tpu_custom_call", output_to_operand_aliasing={{0}: (13, {}), {1}: (14, {}), {2}: (15, {})} | custom-call | flops 1073741824 | tf_op jit(solution)/shard_map/far_end_kernel/pallas_call | solution.py:406
  (1 shorter events, 0.0 us)
Async XLA Ops:
  0.6 1.3 %copy-start = (bf16[18,128,256]{2,1,0:T(8,128)(2,1)S(1)}, bf16[18,128,256]{2,1,0:T(8,128)(2,1)}, u32[]{:S(2)}) copy-start(bf16[18,128,256]{2,1,0:T(8,128)(2,1)} %vol_ref.1) | copy-start | bytes 3538948
  2.4 1.5 %collective-permute-start = (bf16[3,128,128]{2,1,0:T(8,128)(2,1)S(1)}, bf16[3,128,128]{2,1,0:T(8,128)(2,1)S(1)}, u32[]{:S(2)}, u32[]{:S(2)}) collective-permute-start(bf16[3,128,128]{2,1,0:T(8,128)(2,1)S(1)} %get-tuple-element.41), channel_id=1, source_target_pairs={{0,1},{1,0},{2,3},{3,2},{4,5},{5,4},{6,7},{7,6},{8,9},{9,8},{10,11... | collective-permute-start | bytes 294920 | tf_op jit(solution)/shard_map/ppermute | solution.py:451
  4.0 6.9 %collective-permute-start.1 = (bf16[208,256]{1,0:T(8,128)(2,1)S(1)}, bf16[208,256]{1,0:T(8,128)(2,1)S(1)}, u32[]{:S(2)}, u32[]{:S(2)}) collective-permute-start(bf16[208,256]{1,0:T(8,128)(2,1)S(1)} %get-tuple-element.47), channel_id=1, source_target_pairs={{0,2},{2,0},{4,6},{6,4},{8,10},{10,8},{12,14},{14,12},{1,3},{3,1},... | collective-permute-start | bytes 319496 | tf_op jit(solution)/shard_map/ppermute | solution.py:468
  7.0 8.7 %collective-permute-start.3 = (bf16[208,256]{1,0:T(8,128)(2,1)S(1)}, bf16[208,256]{1,0:T(8,128)(2,1)S(1)}, u32[]{:S(2)}, u32[]{:S(2)}) collective-permute-start(bf16[208,256]{1,0:T(8,128)(2,1)S(1)} %get-tuple-element.64), channel_id=1, source_target_pairs={{0,2},{2,0},{4,6},{6,4},{8,10},{10,8},{12,14},{14,12},{1,3},{3,1},... | collective-permute-start | bytes 319496 | tf_op jit(solution)/shard_map/ppermute | solution.py:469
  11.0 6.3 %collective-permute-start.2 = (bf16[208,256]{1,0:T(8,128)(2,1)S(1)}, bf16[208,256]{1,0:T(8,128)(2,1)S(1)}, u32[]{:S(2)}, u32[]{:S(2)}) collective-permute-start(bf16[208,256]{1,0:T(8,128)(2,1)S(1)} %relay_kernel.1), channel_id=1, source_target_pairs={{0,4},{4,8},{8,12},{12,14},{6,2},{10,6},{14,10},{2,0},{1,5},{5,9},... | collective-permute-start | bytes 319496 | tf_op jit(solution)/shard_map/ppermute | solution.py:488

commit v10 on v9

--- a/solution.py
+++ b/solution.py
@@ -211,35 +211,35 @@
             moments_ref[k, comp] = term
 
 
-def make_lines(pair, lines_ref, moments_ref, inner_ref, part_ref):
-    for k in range(2):
-        z = 2 * pair + k
-        for comp in range(6):
-            store_chunks(dot(lines_ref[...], moments_ref[k, comp]), comp, inner_ref.at[z], part_ref.at[:, :, z])
+def make_lines(z, comp, lines_ref, moments_ref, inner_ref, part_ref):
+    store_chunks(dot(lines_ref[...], moments_ref[z % 2, comp]), comp, inner_ref.at[z], part_ref.at[:, :, z])
 
 
 def lines_kernel(vol_ref, lines_ref, diff_i_ref, diff_x_ref, inner_ref, part_ref, even_ref, odd_ref):
     slots = (even_ref, odd_ref)
     for pair in range(HEAD):
         make_moments(pair, vol_ref, diff_i_ref, diff_x_ref, slots[pair % 2])
-        make_lines(pair, lines_ref, slots[pair % 2], inner_ref, part_ref)
-
-
-def attributes(own, border, smooth_ref, store):
+        for k in range(2):
+            for comp in range(6):
+                make_lines(2 * pair + k, comp, lines_ref, slots[pair % 2], inner_ref, part_ref)
+
+
+def tensor_of(own, smooth_ref, tensor_ref):
+    tensor_ref[...] = dot(own.reshape(-1, own.shape[-1]), smooth_ref[...])
+
+
+def attributes(tensor, border, store):
     x = lax.axis_index("xl")
-    tensor = dot(own, smooth_ref[...])
     halves = (tensor[:, :128], tensor[:, 128:] + border)
     lanes = (pl.multiple_of(128 * x, 128), pl.multiple_of(128 - 128 * x, 128))
-    for chunk in range(own.shape[0] // (6 * EDGE)):
-        base = 6 * EDGE * chunk
-        for half, lane in zip(halves, lanes):
-            a, b, c, d, e, f = [half[base + EDGE * comp : base + EDGE * (comp + 1)] for comp in range(6)]
-            low = c + 1e-6
-            guess = pl.reciprocal(low, approx=True)
-            inverse = guess * (low * guess - 2.0)
-            spread = (a - b) * (a - c) + (b - c) * (b - c) + 3.0 * (d * d + e * e + f * f)
-            root = spread * lax.rsqrt(jnp.maximum(spread, TINY))
-            store(chunk, pl.ds(lane, 128), (e * inverse, f * inverse, root * reciprocal(a + b + low)))
+    for half, lane in zip(halves, lanes):
+        a, b, c, d, e, f = [half[EDGE * comp : EDGE * (comp + 1)] for comp in range(6)]
+        low = c + 1e-6
+        guess = pl.reciprocal(low, approx=True)
+        inverse = guess * (low * guess - 2.0)
+        spread = (a - b) * (a - c) + (b - c) * (b - c) + 3.0 * (d * d + e * e + f * f)
+        root = spread * lax.rsqrt(jnp.maximum(spread, TINY))
+        store(pl.ds(lane, 128), (e * inverse, f * inverse, root * reciprocal(a + b + low)))
 
 
 def border_of(packed, slot, mask_ref):
@@ -253,7 +253,7 @@
     inner_in_ref, part_in_ref, *refs,
 ):
     if stage == 0:
-        inner_ref, part_ref, *targets, later_ref, part_h_ref, border_ref, even_ref, odd_ref, out_ref, sems = refs
+        inner_ref, part_ref, *targets, later_ref, part_h_ref, border_ref, even_ref, odd_ref, tensor_ref, out_ref, sems = refs
         both = dot(halo_ref[...], diff_h_ref[...])
         grad_i = dot(diff_i_ref[...], halo_ref[:, :256])
         lined_h = [[] for chunk in range(inner_ref.shape[1])]
@@ -267,7 +267,7 @@
         finished = []
     else:
         border_ref, done_ref, *refs = refs
-        inner_ref, part_ref, *targets, later_ref, even_ref, odd_ref, out_ref, sems, done_sems = refs[3:]
+        inner_ref, part_ref, *targets, later_ref, even_ref, odd_ref, tensor_ref, out_ref, sems, done_sems = refs[3:]
         finished = []
     count, chunks = inner_ref.shape[:2]
     pairs, inner = count // 4, EDGE * chunks
@@ -281,31 +281,35 @@
             finished.append(pltpu.make_async_copy(done_ref.at[n], place(target, pairs - 1), done_sems.at[n]))
             finished[-1].start()
 
-    ahead = list(range(HEAD, pairs + AHEAD) if stage == 0 else range(pairs + AHEAD, 2 * pairs))
-    for step in range(pairs):
-        pair = pairs * stage + step
-        todo = ahead[step : step + 1]
-        for q in todo:
-            make_moments(q, vol_ref, diff_i_ref, diff_x_ref, slots[q % 2])
-        for k in range(2):
-            z = 2 * pair + k
-
-            def store(chunk, lanes, values):
-                rows = slice(EDGE * chunk, EDGE * (chunk + 1))
+    half = count // 2
+    ahead = range(2 * HEAD, half + 2 * AHEAD) if stage == 0 else range(half + 2 * AHEAD, count)
+    tensor_of(inner_ref[half * stage], smooth_ref, tensor_ref.at[0])
+    for step in range(half):
+        z = half * stage + step
+        later = ahead[step] if step < len(ahead) else None
+        if later is not None and later % 2 == 0:
+            make_moments(later // 2, vol_ref, diff_i_ref, diff_x_ref, slots[later // 2 % 2])
+        if step < half - 1:
+            tensor_of(inner_ref[z + 1], smooth_ref, tensor_ref.at[(step + 1) % 2])
+        for chunk in range(chunks):
+            rows = slice(EDGE * chunk, EDGE * (chunk + 1))
+            part = slice(6 * EDGE * chunk, 6 * EDGE * (chunk + 1))
+
+            def store(lanes, values):
                 for n, value in enumerate(values):
-                    if step == pairs - 1:
-                        later_ref[n, k, rows, lanes] = value
+                    if step >= half - 2:
+                        later_ref[n, step % 2, rows, lanes] = value
                     else:
-                        out_ref[n, 2 * step + k, rows, lanes] = value
-
-            border = border_of(border_ref[:, 128 * stage : 128 * (stage + 1)], z % SLOTS, mask_ref)
-            attributes(inner_ref[z].reshape(6 * inner, 256), border, smooth_ref, store)
-        for q in todo:
-            make_lines(q, lines_ref, slots[q % 2], inner_ref, part_ref)
-        if step < pairs - 1:
+                        out_ref[n, step, rows, lanes] = value
+
+            border = border_of(border_ref[part, 128 * stage : 128 * (stage + 1)], z % SLOTS, mask_ref)
+            attributes(tensor_ref[step % 2, part], border, store)
+            if later is not None:
+                make_lines(later, chunk, lines_ref, slots[later // 2 % 2], inner_ref, part_ref)
+        if step % 2 == 1 and step < half - 2:
             for n, target in enumerate(targets):
-                source = out_ref.at[n, pl.ds(2 * step, 2)]
-                finished.append(pltpu.make_async_copy(source, place(target, pair), sems.at[step, n]))
+                source = out_ref.at[n, pl.ds(step - 1, 2)]
+                finished.append(pltpu.make_async_copy(source, place(target, z // 2), sems.at[step // 2, n]))
                 finished[-1].start()
     for copy in finished:
         copy.wait()
@@ -318,9 +322,9 @@
     last = exchange == 1
     targets, refs = refs[3:6], refs[6:]
     if last:
-        packed_ref, block_ref, block_h_ref, border_ref, edge_ref, out_ref, done_sems, sems = refs
+        packed_ref, block_ref, block_h_ref, border_ref, edge_ref, tensor_ref, out_ref, done_sems, sems = refs
     else:
-        out_ref, packed_ref, block_ref, block_h_ref, border_ref, edge_ref, done_sems = refs
+        out_ref, packed_ref, block_ref, block_h_ref, border_ref, edge_ref, tensor_ref, done_sems = refs
     depths, rows, cols = vol_ref.shape
     count, half = depths - 2, (depths - 2) // 2
     bf16, f32 = jnp.bfloat16, jnp.float32
@@ -372,32 +376,50 @@
 
     span = EDGE * half
     copies = []
-    for group in range(2):
+    def make_block_moments(group):
         first = half * group
         centre = block_ref[first + 1 : first + half + 1].reshape(span, cols)
         grad_i = dot(diff_e_ref[:span, :span], centre)
         grad_x = dot(centre, diff_x_ref[...])
         grad_z = block_ref[first + 2 : first + half + 2].astype(f32) - block_ref[first : first + half].astype(f32)
-        for comp, term in enumerate(moments(grad_i, grad_x, grad_z.reshape(span, cols))):
-            outer = dot(lines_e_ref[exchange, :span, :span], term)
-            summed = part_ref[end, comp, first : first + half] + outer.reshape(half, EDGE, cols)
-            edge_ref[first : first + half, comp] = summed.astype(bf16)
-    for group in range(2):
+        return moments(grad_i, grad_x, grad_z.reshape(span, cols))
+
+    def make_edge(group, comp, term):
         first = half * group
-        border = [border_of(border_ref[:, 128 * group : 128 * (group + 1)], k, mask_ref) for k in range(half)]
-
-        def store(chunk, lanes, values):
+        outer = dot(lines_e_ref[exchange, :span, :span], term)
+        summed = part_ref[end, comp, first : first + half] + outer.reshape(half, EDGE, cols)
+        edge_ref[first : first + half, comp] = summed.astype(bf16)
+
+    def finish(group, k):
+        def store(lanes, values):
             for n, value in enumerate(values):
-                out_ref[n, first + chunk, :, lanes] = value
-
-        own = edge_ref[first : first + half].reshape(6 * span, cols)
-        attributes(own, jnp.concatenate(border, axis=0), smooth_ref, store)
-        if last:
-            depth = pl.ds(first, half)
-            for n, target in enumerate(targets):
-                copy = pltpu.make_async_copy(out_ref.at[n, depth], target.at[depth, pl.ds(start, EDGE)], sems.at[group, n])
-                copy.start()
-                copies.append(copy)
+                out_ref[n, half * group + k, :, lanes] = value
+
+        border = border_of(border_ref[:, 128 * group : 128 * (group + 1)], k, mask_ref)
+        attributes(tensor_ref[group, 6 * EDGE * k : 6 * EDGE * (k + 1)], border, store)
+
+    def send(group):
+        depth = pl.ds(half * group, half)
+        for n, target in enumerate(targets):
+            copy = pltpu.make_async_copy(out_ref.at[n, depth], target.at[depth, pl.ds(start, EDGE)], sems.at[group, n])
+            copy.start()
+            copies.append(copy)
+
+    for comp, term in enumerate(make_block_moments(0)):
+        make_edge(0, comp, term)
+    later = make_block_moments(1)
+    tensor_of(edge_ref[:half], smooth_ref, tensor_ref.at[0])
+    for k in range(half):
+        if k < 6:
+            make_edge(1, k, later[k])
+        finish(0, k)
+    if last:
+        send(0)
+    tensor_of(edge_ref[half:], smooth_ref, tensor_ref.at[1])
+    for k in range(half):
+        finish(1, k)
+    if last:
+        send(1)
     for copy in finished + copies:
         copy.wait()
 
@@ -420,7 +442,7 @@
     depths, rows, cols = volume.shape
     il, xl = lax.axis_size("il"), lax.axis_size("xl")
     count = depths - 2
-    assert xl == 2 and il % 2 == 0 and count == 2 * SLOTS and cols == 256
+    assert xl == 2 and il % 2 == 0 and count == 2 * SLOTS and rows == 128 and cols == 256
     bf16, f32 = jnp.bfloat16, jnp.float32
     half = count // 2
     work = half * 1024 * 2 * 256 * 256
@@ -472,7 +494,7 @@
     saved = ((3, 2, EDGE * chunks, cols), f32)
     border = ((6 * EDGE * chunks, 256), f32)
     ready = [((3, count // 2 - 2, EDGE * chunks, cols), f32)]
-    own_scratch = moment_slots + [pltpu.VMEM(*ready[0]), pltpu.SemaphoreType.DMA((count // 4 - 1, 3))]
+    own_scratch = moment_slots + [pltpu.VMEM((2, 6 * EDGE * chunks, cols), f32), pltpu.VMEM(*ready[0]), pltpu.SemaphoreType.DMA((count // 4 - 1, 3))]
     shared = [vol, lines, diff_i, diff_x, smooth, halo, diff_h, pack_h, mask]
     inner, part, *outs_in, done, part_h, border = call(
         "first_own_kernel",
@@ -506,6 +528,7 @@
         pltpu.VMEM((EDGE, 128 * TILES), bf16),
         pltpu.VMEM((6 * EDGE, 256), f32),
         pltpu.VMEM((count, 6, EDGE, cols), bf16),
+        pltpu.VMEM((2, half * 6 * EDGE, cols), f32),
     ]
     sems = pltpu.SemaphoreType.DMA((3,))
     operands = [vol, halo, near_in, part, part_h, *tables, done]

time: 19.6 us -> 19.7 us (level)
  transfers between devices with their start and end apart: 4 -> 4, of which waited for: 0 -> 0; matrix products, arithmetic and copies ran while one was open for 0% -> 0% of each run, Pallas kernels for 46% -> 47%
where the time goes in v10:
time: 19.7 us; the launch traced here: 19.5 us
  Pallas kernels  12.9 us (65%)
  starting transfers between devices  5.58 us (28%)
  between operations  0.72 us (4%)
  local copies, waits for them, and re-layouts  0.31 us (2%)
    pallas_call x9, Pallas kernels, call(): pl.pallas_call(kernel, out_shape=tuple((jax.ShapeDtypeStruct(*out) for ou...  12.9 us
    ppermute x1, starting transfers between devices, body(): far_in = lax.ppermute(far, 'il', swap)  2.94 us
    ppermute x1, starting transfers between devices, body(): relayed_in = lax.ppermute(relayed, 'il', onward)  2.05 us
    ppermute x1, starting transfers between devices, body(): side = lax.ppermute(send, 'xl', [(0, 1), (1, 0)])  0.52 us
  transfers between devices with their start and end apart: 4, of which 0 were waited for; matrix products, arithmetic and copies ran while one was open for 0% of the time, Pallas kernels for 47%

profile of v10, /device:TPU:0, one launch (start us, length us, event | category | flops | bytes accessed | tf_op | source)
XLA Modules:
  0.0 19.5 jit_solution(17422516114144303814)
XLA Ops:
  0.6 0.0 copy-start
  0.6 1.0 %tables_kernel.1 = (bf16[128,128]{1,0:T(8,128)(2,1)S(1)}, bf16[128,128]{1,0:T(8,128)(2,1)S(1)}, bf16[256,256]{1,0:T(8,128)(2,1)S(1)}, bf16[256,256]{1,0:T(8,128)...) custom-call(), custom_call_target="tpu_custom_call" | custom-call | flops 1073741824 | tf_op jit(solution)/shard_map/tables_kernel/pallas_call | solution.py:428
  1.6 0.3 %copy-done = bf16[18,128,256]{2,1,0:T(8,128)(2,1)S(1)} copy-done((bf16[18,128,256]{2,1,0:T(8,128)(2,1)S(1)}, bf16[18,128,256]{2,1,0:T(8,128)(2,1)}, u32[]{:S(2)}) %copy-start) | copy-done | bytes 1179672
  1.9 0.5 %pack_kernel.1 = (bf16[18,128,256]{2,1,0:T(8,128)(2,1)S(1)}, bf16[3,128,128]{2,1,0:T(8,128)(2,1)S(1)}, bf16[3,128,128]{2,1,0:T(8,128)(2,1)S(1)}) custom-call(bf16[18,128,256]{2,1,0:T(8,128)(2,1)S(1)} %copy-done, bf16[256,256]{1,0:T(8,128)(2,1)S(1)} %get-tuple-element.38.pick_ref), custom_call_target="tpu_custom_call" | custom-call | tf_op jit(solution)/shard_map/pack_kernel/pallas_call | solution.py:428
  2.4 0.5 %collective-permute-start = (bf16[3,128,128]{2,1,0:T(8,128)(2,1)S(1)}, bf16[3,128,128]{2,1,0:T(8,128)(2,1)S(1)}, u32[]{:S(2)}, u32[]{:S(2)}) collective-permute-start(bf16[3,128,128]{2,1,0:T(8,128)(2,1)S(1)} %get-tuple-element.41), channel_id=1, source_target_pairs={{0,1},{1,0},{2,3},{3,2},{4,5},{5,4},{6,7},{7,6},{8,9},{9,8},{10,11... | collective-permute-start | bytes 294920 | tf_op jit(solution)/shard_map/ppermute | solution.py:473
  2.9 0.9 %lines_kernel.1 = (bf16[16,6,6,16,256]{4,3,2,1,0:T(8,128)(2,1)S(1)}, f32[2,6,16,16,256]{4,3,2,1,0:T(8,128)S(1)}) custom-call(bf16[18,128,256]{2,1,0:T(8,128)(2,1)S(1)} %get-tuple-element.39.vol_ref.refs_0_, bf16[128,128]{1,0:T(8,128)(2,1)S(1)} %get-tuple-element.42.lines_ref.refs_1_, bf16[128,128]{1,0:T(8,128)(2,1)S(1)} %get-tuple-element.43.diff_i_ref.refs_2_, ...), custom_call_target="tpu_custom_call" | custom-call | flops 268435456 | tf_op jit(solution)/shard_map/lines_kernel/pallas_call | solution.py:428
  3.9 0.0 collective-permute-done.side_ref
  3.9 0.1 rows_kernel.1
  4.0 2.9 %collective-permute-start.1 = (bf16[208,256]{1,0:T(8,128)(2,1)S(1)}, bf16[208,256]{1,0:T(8,128)(2,1)S(1)}, u32[]{:S(2)}, u32[]{:S(2)}) collective-permute-start(bf16[208,256]{1,0:T(8,128)(2,1)S(1)} %get-tuple-element.47), channel_id=1, source_target_pairs={{0,2},{2,0},{4,6},{6,4},{8,10},{10,8},{12,14},{14,12},{1,3},{3,1},... | collective-permute-start | bytes 319496 | tf_op jit(solution)/shard_map/ppermute | solution.py:490
  7.0 0.1 collective-permute-start.3
  7.1 3.8 %first_own_kernel.1 = (bf16[16,6,6,16,256]{4,3,2,1,0:T(8,128)(2,1)S(1)}, f32[2,6,16,16,256]{4,3,2,1,0:T(8,128)S(1)}, f32[16,128,256]{2,1,0:T(8,128)}, f32[16,128...) custom-call(bf16[18,128,256]{2,1,0:T(8,128)(2,1)S(1)} %get-tuple-ele, ...), custom_call_target="tpu_custom_call", output_to_operand_aliasing={{0}: (9, {}), {1}: (10, {})} | custom-call | flops 3221225472 | tf_op jit(solution)/shard_map/first_own_kernel/pallas_call | solution.py:428
  10.8 0.0 collective-permute-done.1.rows_ref
  10.9 2.1 %collective-permute-start.2 = (bf16[208,256]{1,0:T(8,128)(2,1)S(1)}, bf16[208,256]{1,0:T(8,128)(2,1)S(1)}, u32[]{:S(2)}, u32[]{:S(2)}) collective-permute-start(bf16[208,256]{1,0:T(8,128)(2,1)S(1)} %relay_kernel.1), channel_id=1, source_target_pairs={{0,4},{4,8},{8,12},{12,14},{6,2},{10,6},{14,10},{2,0},{1,5},{5,9},... | collective-permute-start | bytes 319496 | tf_op jit(solution)/shard_map/ppermute | solution.py:510
  12.9 2.6 %second_own_kernel.1 = (bf16[16,6,6,16,256]{4,3,2,1,0:T(8,128)(2,1)S(1)}, f32[2,6,16,16,256]{4,3,2,1,0:T(8,128)S(1)}, f32[16,128,256]{2,1,0:T(8,128)}, f32[16,12...) custom-call(bf16[18,128,256]{2,1,0:T(8,128)(2,1)S(1)} %get-tuple-ele, ...), custom_call_target="tpu_custom_call", output_to_operand_aliasing={{0}: (9, {}), {1}: (10, {}), {2}: (13, {}), {3}: (14, {}), ... | custom-call | flops 3221225472 | tf_op jit(solution)/shard_map/second_own_kernel/pallas_call | solution.py:428
  15.5 0.0 collective-permute-done.3.refs_2_
  15.5 1.8 %near_end_kernel.1 = (f32[16,128,256]{2,1,0:T(8,128)}, f32[16,128,256]{2,1,0:T(8,128)}, f32[16,128,256]{2,1,0:T(8,128)}, f32[3,16,16,256]{3,2,1,0:T(8,128)S(1)}) custom-call(bf16[18,128,256]{2,1,0:T(8,128)(2,1)S(1)} %get-tuple-element.39.vol_ref.refs_0_, ...), custom_call_target="tpu_custom_call", output_to_operand_aliasing={{0}: (13, {}), {1}: (14, {}), {2}: (15, {})} | custom-call | flops 1073741824 | tf_op jit(solution)/shard_map/near_end_kernel/pallas_call | solution.py:428
  17.3 0.0 collective-permute-done.2.refs_2_
  17.3 2.2 %far_end_kernel.1 = (f32[16,128,256]{2,1,0:T(8,128)}, f32[16,128,256]{2,1,0:T(8,128)}, f32[16,128,256]{2,1,0:T(8,128)}) custom-call(bf16[18,128,256]{2,1,0:T(8,128)(2,1)S(1)} %get-tuple-element.39.vol_ref.refs_0_, bf16[128,384]{1,0:T(8,128)(2,1)S(1)} %get-tuple-element.46.refs_5_.refs_1_, ...), custom_call_target="tpu_custom_call", output_to_operand_aliasing={{0}: (13, {}), {1}: (14, {}), {2}: (15, {})} | custom-call | flops 1073741824 | tf_op jit(solution)/shard_map/far_end_kernel/pallas_call | solution.py:428
  (1 shorter events, 0.0 us)
Async XLA Ops:
  0.6 1.3 %copy-start = (bf16[18,128,256]{2,1,0:T(8,128)(2,1)S(1)}, bf16[18,128,256]{2,1,0:T(8,128)(2,1)}, u32[]{:S(2)}) copy-start(bf16[18,128,256]{2,1,0:T(8,128)(2,1)} %vol_ref.1) | copy-start | bytes 3538948
  2.4 1.5 %collective-permute-start = (bf16[3,128,128]{2,1,0:T(8,128)(2,1)S(1)}, bf16[3,128,128]{2,1,0:T(8,128)(2,1)S(1)}, u32[]{:S(2)}, u32[]{:S(2)}) collective-permute-start(bf16[3,128,128]{2,1,0:T(8,128)(2,1)S(1)} %get-tuple-element.41), channel_id=1, source_target_pairs={{0,1},{1,0},{2,3},{3,2},{4,5},{5,4},{6,7},{7,6},{8,9},{9,8},{10,11... | collective-permute-start | bytes 294920 | tf_op jit(solution)/shard_map/ppermute | solution.py:473
  4.0 6.8 %collective-permute-start.1 = (bf16[208,256]{1,0:T(8,128)(2,1)S(1)}, bf16[208,256]{1,0:T(8,128)(2,1)S(1)}, u32[]{:S(2)}, u32[]{:S(2)}) collective-permute-start(bf16[208,256]{1,0:T(8,128)(2,1)S(1)} %get-tuple-element.47), channel_id=1, source_target_pairs={{0,2},{2,0},{4,6},{6,4},{8,10},{10,8},{12,14},{14,12},{1,3},{3,1},... | collective-permute-start | bytes 319496 | tf_op jit(solution)/shard_map/ppermute | solution.py:490
  7.0 8.5 %collective-permute-start.3 = (bf16[208,256]{1,0:T(8,128)(2,1)S(1)}, bf16[208,256]{1,0:T(8,128)(2,1)S(1)}, u32[]{:S(2)}, u32[]{:S(2)}) collective-permute-start(bf16[208,256]{1,0:T(8,128)(2,1)S(1)} %get-tuple-element.64), channel_id=1, source_target_pairs={{0,2},{2,0},{4,6},{6,4},{8,10},{10,8},{12,14},{14,12},{1,3},{3,1},... | collective-permute-start | bytes 319496 | tf_op jit(solution)/shard_map/ppermute | solution.py:491
  10.9 6.5 %collective-permute-start.2 = (bf16[208,256]{1,0:T(8,128)(2,1)S(1)}, bf16[208,256]{1,0:T(8,128)(2,1)S(1)}, u32[]{:S(2)}, u32[]{:S(2)}) collective-permute-start(bf16[208,256]{1,0:T(8,128)(2,1)S(1)} %relay_kernel.1), channel_id=1, source_target_pairs={{0,4},{4,8},{8,12},{12,14},{6,2},{10,6},{14,10},{2,0},{1,5},{5,9},... | collective-permute-start | bytes 319496 | tf_op jit(solution)/shard_map/ppermute | solution.py:510

commit v11 on v10

--- a/solution.py
+++ b/solution.py
@@ -72,8 +72,8 @@
     return jnp.logical_not(even) if exchange == 0 else even
 
 
-def tables_kernel(depths, lines_ref, diff_i_ref, diff_x_ref, smooth_ref, pack_h_ref, diff_h_ref, lines_e_ref, diff_e_ref, pick_ref, mask_ref):
-    rows, cols = lines_ref.shape[0], diff_x_ref.shape[0]
+def tables_kernel(depths, lines_ref, diff_i_ref, smooth_ref, pack_h_ref, diff_h_ref, lines_e_ref, diff_e_ref, pick_ref, mask_ref):
+    rows, cols = lines_ref.shape[0], smooth_ref.shape[0]
     x, il, last = lax.axis_index("xl"), lax.axis_index("il"), lax.axis_size("il") - 1
     bf16 = jnp.bfloat16
 
@@ -81,11 +81,11 @@
     inner = (source > 0) & (source < rows - 1)
     lines_ref[...] = jnp.where(inner, band(source, target, 0.25), 0.0).astype(bf16)
     diff_i_ref[...] = difference(source, target).astype(bf16)
-    span = EDGE * (depths - 2)
+    span = EDGE * SLOTS
     target, source = iota((span, span), 0), iota((span, span), 1)
     depth = lax.div(source, EDGE) == lax.div(target, EDGE)
     target, source = lax.rem(target, EDGE), lax.rem(source, EDGE)
-    diff_e_ref[...] = jnp.where(depth, difference(source, target), 0.0).astype(bf16)
+    diff_e_ref[...] = difference(source, target)[:EDGE, :EDGE].astype(bf16)
     for exchange in range(2):
         low = low_end(exchange)
         source_at = jnp.where(low, source - REACH, rows - (EDGE - REACH) + source)
@@ -96,7 +96,6 @@
         lines_e_ref[exchange] = jnp.where(use, band(source_at, target_at, 0.25), 0.0).astype(bf16)
 
     source, target = iota((cols, cols), 0), iota((cols, cols), 1)
-    diff_x_ref[...] = difference(source, target).astype(bf16)
     moved = source == jnp.where(x == 0, cols - 1, 0)
     column = lax.rem(target + 128 * x, cols)
     smooth_ref[...] = jnp.where(moved, 0.0, band(source, column)).astype(bf16)
@@ -126,7 +125,9 @@
     pick_ref[...] = jnp.where(source == jnp.where(lane < 128, sent, kept), 1.0, 0.0).astype(bf16)
     lane = iota((8, 128), 1)
     border = jnp.where(x == 0, lane - (128 - SIDE), lane)
-    mask_ref[...] = jnp.where((border >= 0) & (border < SIDE), 1.0, 0.0)
+    mask_ref[0] = jnp.where((border >= 0) & (border < SIDE), 1.0, 0.0)
+    mask_ref[1] = jnp.where(lane > 0, 1.0, 0.0)
+    mask_ref[2] = jnp.where(lane < 127, 1.0, 0.0)
 
 
 def pack_kernel(vol_ref, pick_ref, copy_ref, send_ref, own_ref):
@@ -199,15 +200,19 @@
     part_ref[1, comp] = summed[EDGE * (chunks - 1) :]
 
 
-def make_moments(pair, vol_ref, diff_i_ref, diff_x_ref, moments_ref):
-    depths, rows, cols = vol_ref.shape
-    planes = [vol_ref[2 * pair + k] for k in range(4)]
-    across = dot(jnp.concatenate(planes[1:3], axis=0), diff_x_ref[...])
+def gradients(before, centre, after, mask_ref):
+    rows, cols = centre.shape
+    left, right = pltpu.roll(centre, 1, 1), pltpu.roll(centre, cols - 1, 1)
+    left_0 = (left[:, :128].reshape(-1, 8, 128) * mask_ref[1]).reshape(rows, 128)
+    right_1 = (right[:, cols - 128 :].reshape(-1, 8, 128) * mask_ref[2]).reshape(rows, 128)
+    grad_x = jnp.concatenate([right[:, : cols - 128] - left_0, right_1 - left[:, 128:]], axis=1)
+    return pltpu.roll(centre, rows - 1, 0) - pltpu.roll(centre, 1, 0), grad_x, after - before
+
+
+def make_moments(pair, vol_ref, mask_ref, moments_ref):
+    planes = [vol_ref[2 * pair + k].astype(jnp.float32) for k in range(4)]
     for k in range(2):
-        grad_i = dot(diff_i_ref[...], planes[k + 1])
-        grad_x = across[rows * k : rows * (k + 1)]
-        grad_z = planes[k + 2].astype(jnp.float32) - planes[k].astype(jnp.float32)
-        for comp, term in enumerate(moments(grad_i, grad_x, grad_z)):
+        for comp, term in enumerate(moments(*gradients(*planes[k : k + 3], mask_ref))):
             moments_ref[k, comp] = term
 
 
@@ -215,10 +220,10 @@
     store_chunks(dot(lines_ref[...], moments_ref[z % 2, comp]), comp, inner_ref.at[z], part_ref.at[:, :, z])
 
 
-def lines_kernel(vol_ref, lines_ref, diff_i_ref, diff_x_ref, inner_ref, part_ref, even_ref, odd_ref):
+def lines_kernel(vol_ref, lines_ref, mask_ref, inner_ref, part_ref, even_ref, odd_ref):
     slots = (even_ref, odd_ref)
     for pair in range(HEAD):
-        make_moments(pair, vol_ref, diff_i_ref, diff_x_ref, slots[pair % 2])
+        make_moments(pair, vol_ref, mask_ref, slots[pair % 2])
         for k in range(2):
             for comp in range(6):
                 make_lines(2 * pair + k, comp, lines_ref, slots[pair % 2], inner_ref, part_ref)
@@ -245,11 +250,11 @@
 def border_of(packed, slot, mask_ref):
     base = jnp.where(lax.axis_index("xl") == 0, 128 - SIDE, 0)
     moved = pltpu.roll(packed, lax.rem(base - SIDE * slot + 128, 128), 1)
-    return (moved.reshape(-1, 8, 128) * mask_ref[...]).reshape(packed.shape)
+    return (moved.reshape(-1, 8, 128) * mask_ref[0]).reshape(packed.shape)
 
 
 def own_kernel(
-    stage, vol_ref, lines_ref, diff_i_ref, diff_x_ref, smooth_ref, halo_ref, diff_h_ref, pack_h_ref, mask_ref,
+    stage, vol_ref, lines_ref, diff_i_ref, smooth_ref, halo_ref, diff_h_ref, pack_h_ref, mask_ref,
     inner_in_ref, part_in_ref, *refs,
 ):
     if stage == 0:
@@ -288,7 +293,7 @@
         z = half * stage + step
         later = ahead[step] if step < len(ahead) else None
         if later is not None and later % 2 == 0:
-            make_moments(later // 2, vol_ref, diff_i_ref, diff_x_ref, slots[later // 2 % 2])
+            make_moments(later // 2, vol_ref, mask_ref, slots[later // 2 % 2])
         if step < half - 1:
             tensor_of(inner_ref[z + 1], smooth_ref, tensor_ref.at[(step + 1) % 2])
         for chunk in range(chunks):
@@ -317,7 +322,7 @@
 
 def end_kernel(
     exchange, vol_ref, halo_ref, rows_ref, part_ref, part_h_ref,
-    smooth_ref, pack_h_ref, diff_x_ref, diff_h_ref, lines_e_ref, diff_e_ref, mask_ref, done_ref, *refs,
+    smooth_ref, pack_h_ref, diff_h_ref, lines_e_ref, diff_e_ref, mask_ref, done_ref, *refs,
 ):
     last = exchange == 1
     targets, refs = refs[3:6], refs[6:]
@@ -367,7 +372,7 @@
     block_h_ref[:, 256:] = joined(REACH * (depths + 1), own_h[:, 256:])
 
     both = dot(block_h_ref[...], diff_h_ref[...])
-    grad_i = dot(diff_e_ref[:EDGE, :EDGE], block_h_ref[:, :256])
+    grad_i = dot(diff_e_ref[...], block_h_ref[:, :256])
     lined_h = []
     for comp, term in enumerate(moments(grad_i, both[:, 256:], both[:, :256])):
         summed = part_h_ref[end, comp] + dot(lines_e_ref[exchange, :EDGE, :EDGE], term)
@@ -378,11 +383,8 @@
     copies = []
     def make_block_moments(group):
         first = half * group
-        centre = block_ref[first + 1 : first + half + 1].reshape(span, cols)
-        grad_i = dot(diff_e_ref[:span, :span], centre)
-        grad_x = dot(centre, diff_x_ref[...])
-        grad_z = block_ref[first + 2 : first + half + 2].astype(f32) - block_ref[first : first + half].astype(f32)
-        return moments(grad_i, grad_x, grad_z.reshape(span, cols))
+        planes = [block_ref[first + k : first + half + k].astype(f32).reshape(span, cols) for k in range(3)]
+        return moments(*gradients(*planes, mask_ref))
 
     def make_edge(group, comp, term):
         first = half * group
@@ -448,21 +450,20 @@
     work = half * 1024 * 2 * 256 * 256
     packed_rows = -(-REACH * (depths + 2) // 16) * 16
 
-    span = EDGE * count
-    lines, diff_i, diff_x, smooth, pack_h, diff_h, lines_e, diff_e, pick, mask = call(
+    span = EDGE * SLOTS
+    lines, diff_i, smooth, pack_h, diff_h, lines_e, diff_e, pick, mask = call(
         "tables_kernel",
         lambda *refs: tables_kernel(depths, *refs),
         [
             ((rows, rows), bf16),
             ((rows, rows), bf16),
             ((cols, cols), bf16),
-            ((cols, cols), bf16),
             ((256, 256), bf16),
             ((128 * TILES, 512), bf16),
             ((2, span, span), bf16),
-            ((span, span), bf16),
+            ((EDGE, EDGE), bf16),
             ((cols, 256), bf16),
-            ((8, 128), f32),
+            ((3, 8, 128), f32),
         ],
         [],
         [],
@@ -474,7 +475,7 @@
     chunks = rows // EDGE - 2
     lined = [((count, chunks, 6, EDGE, cols), bf16), ((2, 6, count, EDGE, cols), f32)]
     moment_slots = [pltpu.VMEM((2, 6, rows, cols), bf16)] * 2
-    inner, part = call("lines_kernel", lines_kernel, lined, moment_slots, [vol, lines, diff_i, diff_x], flops=work // 4)
+    inner, part = call("lines_kernel", lines_kernel, lined, moment_slots, [vol, lines, mask], flops=work // 4)
     packed = ((packed_rows, cols), bf16)
     halo, near, far = call(
         "rows_kernel",
@@ -495,7 +496,7 @@
     border = ((6 * EDGE * chunks, 256), f32)
     ready = [((3, count // 2 - 2, EDGE * chunks, cols), f32)]
     own_scratch = moment_slots + [pltpu.VMEM((2, 6 * EDGE * chunks, cols), f32), pltpu.VMEM(*ready[0]), pltpu.SemaphoreType.DMA((count // 4 - 1, 3))]
-    shared = [vol, lines, diff_i, diff_x, smooth, halo, diff_h, pack_h, mask]
+    shared = [vol, lines, diff_i, smooth, halo, diff_h, pack_h, mask]
     inner, part, *outs_in, done, part_h, border = call(
         "first_own_kernel",
         lambda *refs: own_kernel(0, *refs),
@@ -521,7 +522,7 @@
     )
 
     end_rows = (3, count, EDGE, cols)
-    tables = [smooth, pack_h, diff_x, diff_h, lines_e, diff_e, mask]
+    tables = [smooth, pack_h, diff_h, lines_e, diff_e, mask]
     scratch = [
         pltpu.VMEM((8 + packed_rows, cols), f32),
         pltpu.VMEM((depths, EDGE, cols), bf16),

time: 19.7 us -> 19.7 us (level)
  Pallas kernels: 12.9 us -> 12.3 us
  waiting for transfers between devices: 0.03 us -> 0.29 us
  local copies, waits for them, and re-layouts: 0.31 us -> 0.52 us
    pallas_call x9, Pallas kernels: 12.9 us -> 12.3 us  [call(): pl.pallas_call(kernel, out_shape=tuple((jax.ShapeDtypeStruct(*out) for ou...]
    ppermute x1, waiting for transfers between devices: 0.03 us -> 0.25 us  [body(): side = lax.ppermute(send, 'xl', [(0, 1), (1, 0)])]
    unnamed x2, local copies, waits for them, and re-layouts: 0.31 us -> 0.52 us
  transfers between devices with their start and end apart: 4 -> 4, of which waited for: 0 -> 1; matrix products, arithmetic and copies ran while one was open for 0% -> 0% of each run, Pallas kernels for 47% -> 45%
where the time goes in v11:
time: 19.7 us; the launch traced here: 19.5 us
  Pallas kernels  12.3 us (62%)
  starting transfers between devices  5.7 us (29%)
  between operations  0.71 us (4%)
  local copies, waits for them, and re-layouts  0.52 us (3%)
  waiting for transfers between devices  0.29 us (1%)
    pallas_call x9, Pallas kernels, call(): pl.pallas_call(kernel, out_shape=tuple((jax.ShapeDtypeStruct(*out) for ou...  12.3 us
    ppermute x1, starting transfers between devices, body(): far_in = lax.ppermute(far, 'il', swap)  2.94 us
    ppermute x1, starting transfers between devices, body(): relayed_in = lax.ppermute(relayed, 'il', onward)  2.17 us
    ppermute x1, starting transfers between devices, body(): side = lax.ppermute(send, 'xl', [(0, 1), (1, 0)])  0.52 us
    unnamed x2, local copies, waits for them, and re-layouts  0.52 us
  transfers between devices with their start and end apart: 4, of which 1 were waited for; matrix products, arithmetic and copies ran while one was open for 0% of the time, Pallas kernels for 45%

profile of v11, /device:TPU:0, one launch (start us, length us, event | category | flops | bytes accessed | tf_op | source)
XLA Modules:
  0.0 19.5 jit_solution(16555487560531912679)
XLA Ops:
  0.6 0.0 copy-start
  0.6 0.7 %tables_kernel.1 = (bf16[128,128]{1,0:T(8,128)(2,1)S(1)}, bf16[128,128]{1,0:T(8,128)(2,1)S(1)}, bf16[256,256]{1,0:T(8,128)(2,1)S(1)}, bf16[256,256]{1,0:T(8,128)...) custom-call(), custom_call_target="tpu_custom_call" | custom-call | flops 1073741824 | tf_op jit(solution)/shard_map/tables_kernel/pallas_call | solution.py:430
  1.4 0.5 %copy-done = bf16[18,128,256]{2,1,0:T(8,128)(2,1)S(1)} copy-done((bf16[18,128,256]{2,1,0:T(8,128)(2,1)S(1)}, bf16[18,128,256]{2,1,0:T(8,128)(2,1)}, u32[]{:S(2)}) %copy-start) | copy-done | bytes 1179672
  1.9 0.5 %pack_kernel.1 = (bf16[18,128,256]{2,1,0:T(8,128)(2,1)S(1)}, bf16[3,128,128]{2,1,0:T(8,128)(2,1)S(1)}, bf16[3,128,128]{2,1,0:T(8,128)(2,1)S(1)}) custom-call(bf16[18,128,256]{2,1,0:T(8,128)(2,1)S(1)} %copy-done, bf16[256,256]{1,0:T(8,128)(2,1)S(1)} %get-tuple-element.37.pick_ref), custom_call_target="tpu_custom_call" | custom-call | tf_op jit(solution)/shard_map/pack_kernel/pallas_call | solution.py:430
  2.4 0.5 %collective-permute-start = (bf16[3,128,128]{2,1,0:T(8,128)(2,1)S(1)}, bf16[3,128,128]{2,1,0:T(8,128)(2,1)S(1)}, u32[]{:S(2)}, u32[]{:S(2)}) collective-permute-start(bf16[3,128,128]{2,1,0:T(8,128)(2,1)S(1)} %get-tuple-element.40), channel_id=1, source_target_pairs={{0,1},{1,0},{2,3},{3,2},{4,5},{5,4},{6,7},{7,6},{8,9},{9,8},{10,11... | collective-permute-start | bytes 294920 | tf_op jit(solution)/shard_map/ppermute | solution.py:474
  2.9 0.7 %lines_kernel.1 = (bf16[16,6,6,16,256]{4,3,2,1,0:T(8,128)(2,1)S(1)}, f32[2,6,16,16,256]{4,3,2,1,0:T(8,128)S(1)}) custom-call(bf16[18,128,256]{2,1,0:T(8,128)(2,1)S(1)} %get-tuple-element.38.vol_ref.refs_0_, bf16[128,128]{1,0:T(8,128)(2,1)S(1)} %get-tuple-element.41.lines_ref.refs_1_, f32[3,8,128]{2,1,0:T(8,128)S(1)} %get-tuple-element.42.mask_ref.refs_7_.refs_10_), custom_call_target="tpu_custom_call" | custom-call | flops 268435456 | tf_op jit(solution)/shard_map/lines_kernel/pallas_call | solution.py:430
  3.6 0.2 %collective-permute-done.side_ref = bf16[3,128,128]{2,1,0:T(8,128)(2,1)S(1)} collective-permute-done((bf16[3,128,128]{2,1,0:T(8,128)(2,1)S(1)}, bf16[3,128,128]{2,1,0:T(8,128)(2,1)S(1)}, u32[]{:S(2)}, u32[]{:S(2)}) %collective-permute-start) | collective-permute-done | bytes 98336 | tf_op jit(solution)/shard_map/ppermute | solution.py:474
  3.9 0.1 rows_kernel.1
  4.0 2.9 %collective-permute-start.1 = (bf16[208,256]{1,0:T(8,128)(2,1)S(1)}, bf16[208,256]{1,0:T(8,128)(2,1)S(1)}, u32[]{:S(2)}, u32[]{:S(2)}) collective-permute-start(bf16[208,256]{1,0:T(8,128)(2,1)S(1)} %get-tuple-element.45), channel_id=1, source_target_pairs={{0,2},{2,0},{4,6},{6,4},{8,10},{10,8},{12,14},{14,12},{1,3},{3,1},... | collective-permute-start | bytes 319496 | tf_op jit(solution)/shard_map/ppermute | solution.py:491
  7.0 0.1 collective-permute-start.3
  7.1 3.6 %first_own_kernel.1 = (bf16[16,6,6,16,256]{4,3,2,1,0:T(8,128)(2,1)S(1)}, f32[2,6,16,16,256]{4,3,2,1,0:T(8,128)S(1)}, f32[16,128,256]{2,1,0:T(8,128)}, f32[16,128...) custom-call(bf16[18,128,256]{2,1,0:T(8,128)(2,1)S(1)} %get-tuple-ele, ...), custom_call_target="tpu_custom_call", output_to_operand_aliasing={{0}: (8, {}), {1}: (9, {})} | custom-call | flops 3221225472 | tf_op jit(solution)/shard_map/first_own_kernel/pallas_call | solution.py:430
  10.7 0.0 collective-permute-done.1.rows_ref
  10.7 2.2 %collective-permute-start.2 = (bf16[208,256]{1,0:T(8,128)(2,1)S(1)}, bf16[208,256]{1,0:T(8,128)(2,1)S(1)}, u32[]{:S(2)}, u32[]{:S(2)}) collective-permute-start(bf16[208,256]{1,0:T(8,128)(2,1)S(1)} %relay_kernel.1), channel_id=1, source_target_pairs={{0,4},{4,8},{8,12},{12,14},{6,2},{10,6},{14,10},{2,0},{1,5},{5,9},... | collective-permute-start | bytes 319496 | tf_op jit(solution)/shard_map/ppermute | solution.py:511
  12.9 2.6 %second_own_kernel.1 = (bf16[16,6,6,16,256]{4,3,2,1,0:T(8,128)(2,1)S(1)}, f32[2,6,16,16,256]{4,3,2,1,0:T(8,128)S(1)}, f32[16,128,256]{2,1,0:T(8,128)}, f32[16,12...) custom-call(bf16[18,128,256]{2,1,0:T(8,128)(2,1)S(1)} %get-tuple-ele, ...), custom_call_target="tpu_custom_call", output_to_operand_aliasing={{0}: (8, {}), {1}: (9, {}), {2}: (12, {}), {3}: (13, {}), {... | custom-call | flops 3221225472 | tf_op jit(solution)/shard_map/second_own_kernel/pallas_call | solution.py:430
  15.5 0.0 collective-permute-done.3.refs_2_
  15.5 1.8 %near_end_kernel.1 = (f32[16,128,256]{2,1,0:T(8,128)}, f32[16,128,256]{2,1,0:T(8,128)}, f32[16,128,256]{2,1,0:T(8,128)}, f32[3,16,16,256]{3,2,1,0:T(8,128)S(1)}) custom-call(bf16[18,128,256]{2,1,0:T(8,128)(2,1)S(1)} %get-tuple-element.38.vol_ref.refs_0_, ...), custom_call_target="tpu_custom_call", output_to_operand_aliasing={{0}: (12, {}), {1}: (13, {}), {2}: (14, {})} | custom-call | flops 1073741824 | tf_op jit(solution)/shard_map/near_end_kernel/pallas_call | solution.py:430
  17.3 0.0 collective-permute-done.2.refs_2_
  17.3 2.2 %far_end_kernel.1 = (f32[16,128,256]{2,1,0:T(8,128)}, f32[16,128,256]{2,1,0:T(8,128)}, f32[16,128,256]{2,1,0:T(8,128)}) custom-call(bf16[18,128,256]{2,1,0:T(8,128)(2,1)S(1)} %get-tuple-element.38.vol_ref.refs_0_, bf16[128,384]{1,0:T(8,128)(2,1)S(1)} %get-tuple-element.44.refs_4_.refs_1_, ...), custom_call_target="tpu_custom_call", output_to_operand_aliasing={{0}: (12, {}), {1}: (13, {}), {2}: (14, {})} | custom-call | flops 1073741824 | tf_op jit(solution)/shard_map/far_end_kernel/pallas_call | solution.py:430
  (1 shorter events, 0.0 us)
Async XLA Ops:
  0.6 1.3 %copy-start = (bf16[18,128,256]{2,1,0:T(8,128)(2,1)S(1)}, bf16[18,128,256]{2,1,0:T(8,128)(2,1)}, u32[]{:S(2)}) copy-start(bf16[18,128,256]{2,1,0:T(8,128)(2,1)} %vol_ref.1) | copy-start | bytes 3538948
  2.4 1.5 %collective-permute-start = (bf16[3,128,128]{2,1,0:T(8,128)(2,1)S(1)}, bf16[3,128,128]{2,1,0:T(8,128)(2,1)S(1)}, u32[]{:S(2)}, u32[]{:S(2)}) collective-permute-start(bf16[3,128,128]{2,1,0:T(8,128)(2,1)S(1)} %get-tuple-element.40), channel_id=1, source_target_pairs={{0,1},{1,0},{2,3},{3,2},{4,5},{5,4},{6,7},{7,6},{8,9},{9,8},{10,11... | collective-permute-start | bytes 294920 | tf_op jit(solution)/shard_map/ppermute | solution.py:474
  4.0 6.7 %collective-permute-start.1 = (bf16[208,256]{1,0:T(8,128)(2,1)S(1)}, bf16[208,256]{1,0:T(8,128)(2,1)S(1)}, u32[]{:S(2)}, u32[]{:S(2)}) collective-permute-start(bf16[208,256]{1,0:T(8,128)(2,1)S(1)} %get-tuple-element.45), channel_id=1, source_target_pairs={{0,2},{2,0},{4,6},{6,4},{8,10},{10,8},{12,14},{14,12},{1,3},{3,1},... | collective-permute-start | bytes 319496 | tf_op jit(solution)/shard_map/ppermute | solution.py:491
  7.0 8.6 %collective-permute-start.3 = (bf16[208,256]{1,0:T(8,128)(2,1)S(1)}, bf16[208,256]{1,0:T(8,128)(2,1)S(1)}, u32[]{:S(2)}, u32[]{:S(2)}) collective-permute-start(bf16[208,256]{1,0:T(8,128)(2,1)S(1)} %get-tuple-element.62), channel_id=1, source_target_pairs={{0,2},{2,0},{4,6},{6,4},{8,10},{10,8},{12,14},{14,12},{1,3},{3,1},... | collective-permute-start | bytes 319496 | tf_op jit(solution)/shard_map/ppermute | solution.py:492
  10.7 6.6 %collective-permute-start.2 = (bf16[208,256]{1,0:T(8,128)(2,1)S(1)}, bf16[208,256]{1,0:T(8,128)(2,1)S(1)}, u32[]{:S(2)}, u32[]{:S(2)}) collective-permute-start(bf16[208,256]{1,0:T(8,128)(2,1)S(1)} %relay_kernel.1), channel_id=1, source_target_pairs={{0,4},{4,8},{8,12},{12,14},{6,2},{10,6},{14,10},{2,0},{1,5},{5,9},... | collective-permute-start | bytes 319496 | tf_op jit(solution)/shard_map/ppermute | solution.py:511

commit v12 on v11

--- a/solution.py
+++ b/solution.py
@@ -16,7 +16,6 @@
 OWN = 2
 TINY = float(np.finfo(np.float32).tiny)
 HEAD = 2
-AHEAD = 2
 FAR = -1000
 WHOLE = pl.BlockSpec(memory_space=pltpu.VMEM)
 IN_HBM = pl.BlockSpec(memory_space=pltpu.HBM)
@@ -216,17 +215,20 @@
             moments_ref[k, comp] = term
 
 
-def make_lines(z, comp, lines_ref, moments_ref, inner_ref, part_ref):
-    store_chunks(dot(lines_ref[...], moments_ref[z % 2, comp]), comp, inner_ref.at[z], part_ref.at[:, :, z])
-
-
-def lines_kernel(vol_ref, lines_ref, mask_ref, inner_ref, part_ref, even_ref, odd_ref):
-    slots = (even_ref, odd_ref)
-    for pair in range(HEAD):
-        make_moments(pair, vol_ref, mask_ref, slots[pair % 2])
+def make_lines(pair, k, comp, lines_ref, moments_ref, inner_ref, part_ref):
+    z = 2 * pair + k
+    store_chunks(dot(lines_ref[...], moments_ref[k, comp]), comp, inner_ref.at[z], part_ref.at[:, :, z])
+
+
+def lines_kernel(vol_ref, lines_ref, mask_ref, inner_ref, part_ref, moments_ref):
+    def step(pair, carry):
+        make_moments(pair, vol_ref, mask_ref, moments_ref)
         for k in range(2):
             for comp in range(6):
-                make_lines(2 * pair + k, comp, lines_ref, slots[pair % 2], inner_ref, part_ref)
+                make_lines(pair, k, comp, lines_ref, moments_ref, inner_ref, part_ref)
+        return carry
+
+    lax.fori_loop(0, HEAD, step, 0)
 
 
 def tensor_of(own, smooth_ref, tensor_ref):
@@ -258,7 +260,7 @@
     inner_in_ref, part_in_ref, *refs,
 ):
     if stage == 0:
-        inner_ref, part_ref, *targets, later_ref, part_h_ref, border_ref, even_ref, odd_ref, tensor_ref, out_ref, sems = refs
+        inner_ref, part_ref, *targets, out_ref, part_h_ref, border_ref, moments_ref, tensor_ref, sems = refs
         both = dot(halo_ref[...], diff_h_ref[...])
         grad_i = dot(diff_i_ref[...], halo_ref[:, :256])
         lined_h = [[] for chunk in range(inner_ref.shape[1])]
@@ -269,53 +271,70 @@
             part_h_ref[0, comp] = summed[:EDGE]
             part_h_ref[1, comp] = summed[EDGE * (len(lined_h) + 1) :]
         border_ref[...] = dot(jnp.concatenate(sum(lined_h, []), axis=0), pack_h_ref[...])
-        finished = []
     else:
         border_ref, done_ref, *refs = refs
-        inner_ref, part_ref, *targets, later_ref, even_ref, odd_ref, tensor_ref, out_ref, sems, done_sems = refs[3:]
-        finished = []
+        inner_ref, part_ref, *targets, out_ref, moments_ref, tensor_ref, sems, done_sems = refs[3:]
     count, chunks = inner_ref.shape[:2]
     pairs, inner = count // 4, EDGE * chunks
-    slots = (even_ref, odd_ref)
-
-    def place(target, pair):
-        return target.at[pl.ds(2 * pair, 2), pl.ds(EDGE, inner)]
-
+    origin = pairs * stage
+
+    def copies(source_ref, step, pair, sem):
+        rows = pl.ds(EDGE, inner)
+        return [
+            pltpu.make_async_copy(source_ref.at[n, pl.ds(2 * step, 2)], target.at[pl.ds(2 * pair, 2), rows], sem.at[n])
+            for n, target in enumerate(targets)
+        ]
+
+    finished = []
     if stage == 1:
-        for n, target in enumerate(targets):
-            finished.append(pltpu.make_async_copy(done_ref.at[n], place(target, pairs - 1), done_sems.at[n]))
-            finished[-1].start()
-
-    half = count // 2
-    ahead = range(2 * HEAD, half + 2 * AHEAD) if stage == 0 else range(half + 2 * AHEAD, count)
-    tensor_of(inner_ref[half * stage], smooth_ref, tensor_ref.at[0])
-    for step in range(half):
-        z = half * stage + step
-        later = ahead[step] if step < len(ahead) else None
-        if later is not None and later % 2 == 0:
-            make_moments(later // 2, vol_ref, mask_ref, slots[later // 2 % 2])
-        if step < half - 1:
-            tensor_of(inner_ref[z + 1], smooth_ref, tensor_ref.at[(step + 1) % 2])
-        for chunk in range(chunks):
-            rows = slice(EDGE * chunk, EDGE * (chunk + 1))
-            part = slice(6 * EDGE * chunk, 6 * EDGE * (chunk + 1))
-
-            def store(lanes, values):
-                for n, value in enumerate(values):
-                    if step >= half - 2:
-                        later_ref[n, step % 2, rows, lanes] = value
-                    else:
-                        out_ref[n, step, rows, lanes] = value
-
-            border = border_of(border_ref[part, 128 * stage : 128 * (stage + 1)], z % SLOTS, mask_ref)
-            attributes(tensor_ref[step % 2, part], border, store)
-            if later is not None:
-                make_lines(later, chunk, lines_ref, slots[later // 2 % 2], inner_ref, part_ref)
-        if step % 2 == 1 and step < half - 2:
-            for n, target in enumerate(targets):
-                source = out_ref.at[n, pl.ds(step - 1, 2)]
-                finished.append(pltpu.make_async_copy(source, place(target, z // 2), sems.at[step // 2, n]))
-                finished[-1].start()
+        finished += copies(done_ref, pairs - 1, pairs - 1, done_sems)
+        for copy in finished:
+            copy.start()
+
+    def make_tensors(pair):
+        for k in range(2):
+            tensor_of(inner_ref[2 * pair + k], smooth_ref, tensor_ref.at[k])
+
+    def run(first, stop, ahead):
+        def step(index, carry):
+            pair = origin + index
+            for k in range(2):
+                slot = lax.rem(2 * pair + k, SLOTS)
+                for chunk in range(chunks):
+                    rows = slice(EDGE * chunk, EDGE * (chunk + 1))
+                    part = slice(6 * EDGE * chunk, 6 * EDGE * (chunk + 1))
+
+                    def store(lanes, values):
+                        for n, value in enumerate(values):
+                            out_ref[n, 2 * index + k, rows, lanes] = value
+
+                    border = border_of(border_ref[part, 128 * stage : 128 * (stage + 1)], slot, mask_ref)
+                    attributes(tensor_ref[k, part], border, store)
+                    if ahead:
+                        make_lines(pair + ahead, k, chunk, lines_ref, moments_ref, inner_ref, part_ref)
+            make_tensors(jnp.minimum(pair + 1, 2 * pairs - 1))
+            if ahead:
+                make_moments(jnp.minimum(pair + ahead + 1, 2 * pairs - 1), vol_ref, mask_ref, moments_ref)
+
+            @pl.when(index < pairs - 1)
+            def _():
+                for copy in copies(out_ref, index, pair, sems.at[index]):
+                    copy.start()
+
+            return carry
+
+        lax.fori_loop(first, stop, step, 0)
+
+    make_tensors(origin)
+    if stage == 0:
+        make_moments(HEAD, vol_ref, mask_ref, moments_ref)
+        run(0, pairs, HEAD)
+    else:
+        make_moments(pairs + HEAD, vol_ref, mask_ref, moments_ref)
+        run(0, pairs - HEAD, HEAD)
+        run(pairs - HEAD, pairs, 0)
+    for step in range(pairs - 1):
+        finished += copies(out_ref, step, origin + step, sems.at[step])
     for copy in finished:
         copy.wait()
 
@@ -340,10 +359,11 @@
     finished = []
     for n, target in enumerate(targets):
         if last:
-            place = target.at[:, pl.ds(other, EDGE)]
+            copy = pltpu.make_async_copy(done_ref.at[n], target.at[:, pl.ds(other, EDGE)], done_sems.at[n])
         else:
             place = target.at[pl.ds(count - 2, 2), pl.ds(EDGE, rows - 2 * EDGE)]
-        finished.append(pltpu.make_async_copy(done_ref.at[n], place, done_sems.at[n]))
+            copy = pltpu.make_async_copy(done_ref.at[n, pl.ds(half - 2, 2)], place, done_sems.at[n])
+        finished.append(copy)
     for copy in finished:
         copy.start()
 
@@ -407,21 +427,15 @@
             copy.start()
             copies.append(copy)
 
-    for comp, term in enumerate(make_block_moments(0)):
-        make_edge(0, comp, term)
-    later = make_block_moments(1)
-    tensor_of(edge_ref[:half], smooth_ref, tensor_ref.at[0])
-    for k in range(half):
-        if k < 6:
-            make_edge(1, k, later[k])
-        finish(0, k)
-    if last:
-        send(0)
-    tensor_of(edge_ref[half:], smooth_ref, tensor_ref.at[1])
-    for k in range(half):
-        finish(1, k)
-    if last:
-        send(1)
+    for group in range(2):
+        for comp, term in enumerate(make_block_moments(group)):
+            make_edge(group, comp, term)
+    for group in range(2):
+        tensor_of(edge_ref[half * group : half * (group + 1)], smooth_ref, tensor_ref.at[group])
+        for k in range(half):
+            finish(group, k)
+        if last:
+            send(group)
     for copy in finished + copies:
         copy.wait()
 
@@ -474,7 +488,7 @@
     side = lax.ppermute(send, "xl", [(0, 1), (1, 0)])
     chunks = rows // EDGE - 2
     lined = [((count, chunks, 6, EDGE, cols), bf16), ((2, 6, count, EDGE, cols), f32)]
-    moment_slots = [pltpu.VMEM((2, 6, rows, cols), bf16)] * 2
+    moment_slots = [pltpu.VMEM((2, 6, rows, cols), bf16)]
     inner, part = call("lines_kernel", lines_kernel, lined, moment_slots, [vol, lines, mask], flops=work // 4)
     packed = ((packed_rows, cols), bf16)
     halo, near, far = call(
@@ -492,10 +506,9 @@
     near_in = lax.ppermute(near, "il", swap)
 
     outs = [((count, rows, cols), f32)] * 3
-    saved = ((3, 2, EDGE * chunks, cols), f32)
+    saved = ((3, half, EDGE * chunks, cols), f32)
     border = ((6 * EDGE * chunks, 256), f32)
-    ready = [((3, count // 2 - 2, EDGE * chunks, cols), f32)]
-    own_scratch = moment_slots + [pltpu.VMEM((2, 6 * EDGE * chunks, cols), f32), pltpu.VMEM(*ready[0]), pltpu.SemaphoreType.DMA((count // 4 - 1, 3))]
+    own_scratch = moment_slots + [pltpu.VMEM((2, 6 * EDGE * chunks, cols), f32), pltpu.SemaphoreType.DMA((half // 2 - 1, 3))]
     shared = [vol, lines, diff_i, smooth, halo, diff_h, pack_h, mask]
     inner, part, *outs_in, done, part_h, border = call(
         "first_own_kernel",

time: 19.7 us -> 20.6 us (1.046)
  Pallas kernels: 12.3 us -> 13.6 us
  waiting for transfers between devices: 0.29 us -> 0.06 us
    pallas_call x9, Pallas kernels: 12.3 us -> 13.6 us  [call(): pl.pallas_call(kernel, out_shape=tuple((jax.ShapeDtypeStruct(*out) for ou...]
  transfers between devices with their start and end apart: 4 -> 4, of which waited for: 1 -> 1; matrix products, arithmetic and copies ran while one was open for 0% -> 0% of each run, Pallas kernels for 45% -> 50%
where the time goes in v12:
time: 20.6 us; the launch traced here: 20.4 us
  Pallas kernels  13.6 us (66%)
  starting transfers between devices  5.58 us (27%)
  between operations  0.72 us (3%)
  local copies, waits for them, and re-layouts  0.52 us (3%)
    pallas_call x9, Pallas kernels, call(): pl.pallas_call(kernel, out_shape=tuple((jax.ShapeDtypeStruct(*out) for ou...  13.6 us
    ppermute x1, starting transfers between devices, body(): far_in = lax.ppermute(far, 'il', swap)  2.93 us
    ppermute x1, starting transfers between devices, body(): relayed_in = lax.ppermute(relayed, 'il', onward)  2.05 us
    ppermute x1, starting transfers between devices, body(): side = lax.ppermute(send, 'xl', [(0, 1), (1, 0)])  0.52 us
    unnamed x2, local copies, waits for them, and re-layouts  0.52 us
  transfers between devices with their start and end apart: 4, of which 1 were waited for; matrix products, arithmetic and copies ran while one was open for 0% of the time, Pallas kernels for 50%

profile of v12, /device:TPU:0, one launch (start us, length us, event | category | flops | bytes accessed | tf_op | source)
XLA Modules:
  0.0 20.4 jit_solution(18294793442193388560)
XLA Ops:
  0.6 0.0 copy-start
  0.6 0.7 %tables_kernel.1 = (bf16[128,128]{1,0:T(8,128)(2,1)S(1)}, bf16[128,128]{1,0:T(8,128)(2,1)S(1)}, bf16[256,256]{1,0:T(8,128)(2,1)S(1)}, bf16[256,256]{1,0:T(8,128)...) custom-call(), custom_call_target="tpu_custom_call" | custom-call | flops 1073741824 | tf_op jit(solution)/shard_map/tables_kernel/pallas_call | solution.py:444
  1.4 0.5 %copy-done = bf16[18,128,256]{2,1,0:T(8,128)(2,1)S(1)} copy-done((bf16[18,128,256]{2,1,0:T(8,128)(2,1)S(1)}, bf16[18,128,256]{2,1,0:T(8,128)(2,1)}, u32[]{:S(2)}) %copy-start) | copy-done | bytes 1179672
  1.9 0.5 %pack_kernel.1 = (bf16[18,128,256]{2,1,0:T(8,128)(2,1)S(1)}, bf16[3,128,128]{2,1,0:T(8,128)(2,1)S(1)}, bf16[3,128,128]{2,1,0:T(8,128)(2,1)S(1)}) custom-call(bf16[18,128,256]{2,1,0:T(8,128)(2,1)S(1)} %copy-done, bf16[256,256]{1,0:T(8,128)(2,1)S(1)} %get-tuple-element.37.pick_ref), custom_call_target="tpu_custom_call" | custom-call | tf_op jit(solution)/shard_map/pack_kernel/pallas_call | solution.py:444
  2.4 0.5 %collective-permute-start = (bf16[3,128,128]{2,1,0:T(8,128)(2,1)S(1)}, bf16[3,128,128]{2,1,0:T(8,128)(2,1)S(1)}, u32[]{:S(2)}, u32[]{:S(2)}) collective-permute-start(bf16[3,128,128]{2,1,0:T(8,128)(2,1)S(1)} %get-tuple-element.40), channel_id=1, source_target_pairs={{0,1},{1,0},{2,3},{3,2},{4,5},{5,4},{6,7},{7,6},{8,9},{9,8},{10,11... | collective-permute-start | bytes 294920 | tf_op jit(solution)/shard_map/ppermute | solution.py:488
  2.9 0.9 %lines_kernel.1 = (bf16[16,6,6,16,256]{4,3,2,1,0:T(8,128)(2,1)S(1)}, f32[2,6,16,16,256]{4,3,2,1,0:T(8,128)S(1)}) custom-call(bf16[18,128,256]{2,1,0:T(8,128)(2,1)S(1)} %get-tuple-element.38.vol_ref.refs_0_, bf16[128,128]{1,0:T(8,128)(2,1)S(1)} %get-tuple-element.41.lines_ref.refs_1_, f32[3,8,128]{2,1,0:T(8,128)S(1)} %get-tuple-element.42.mask_ref.refs_7_.refs_10_), custom_call_target="tpu_custom_call" | custom-call | flops 268435456 | tf_op jit(solution)/shard_map/lines_kernel/pallas_call | solution.py:444
  3.8 0.1 collective-permute-done.side_ref
  3.9 0.1 rows_kernel.1
  4.0 2.9 %collective-permute-start.1 = (bf16[208,256]{1,0:T(8,128)(2,1)S(1)}, bf16[208,256]{1,0:T(8,128)(2,1)S(1)}, u32[]{:S(2)}, u32[]{:S(2)}) collective-permute-start(bf16[208,256]{1,0:T(8,128)(2,1)S(1)} %get-tuple-element.45), channel_id=1, source_target_pairs={{0,2},{2,0},{4,6},{6,4},{8,10},{10,8},{12,14},{14,12},{1,3},{3,1},... | collective-permute-start | bytes 319496 | tf_op jit(solution)/shard_map/ppermute | solution.py:505
  7.0 0.1 collective-permute-start.3
  7.1 4.4 %first_own_kernel.1 = (bf16[16,6,6,16,256]{4,3,2,1,0:T(8,128)(2,1)S(1)}, f32[2,6,16,16,256]{4,3,2,1,0:T(8,128)S(1)}, f32[16,128,256]{2,1,0:T(8,128)}, f32[16,128...) custom-call(bf16[18,128,256]{2,1,0:T(8,128)(2,1)S(1)} %get-tuple-ele, ...), custom_call_target="tpu_custom_call", output_to_operand_aliasing={{0}: (8, {}), {1}: (9, {})} | custom-call | flops 3221225472 | tf_op jit(solution)/shard_map/first_own_kernel/pallas_call | solution.py:444
  11.4 0.0 collective-permute-done.1.rows_ref
  11.5 2.1 %collective-permute-start.2 = (bf16[208,256]{1,0:T(8,128)(2,1)S(1)}, bf16[208,256]{1,0:T(8,128)(2,1)S(1)}, u32[]{:S(2)}, u32[]{:S(2)}) collective-permute-start(bf16[208,256]{1,0:T(8,128)(2,1)S(1)} %relay_kernel.1), channel_id=1, source_target_pairs={{0,4},{4,8},{8,12},{12,14},{6,2},{10,6},{14,10},{2,0},{1,5},{5,9},... | collective-permute-start | bytes 319496 | tf_op jit(solution)/shard_map/ppermute | solution.py:524
  13.5 3.4 %second_own_kernel.1 = (bf16[16,6,6,16,256]{4,3,2,1,0:T(8,128)(2,1)S(1)}, f32[2,6,16,16,256]{4,3,2,1,0:T(8,128)S(1)}, f32[16,128,256]{2,1,0:T(8,128)}, f32[16,12...) custom-call(bf16[18,128,256]{2,1,0:T(8,128)(2,1)S(1)} %get-tuple-ele, ...), custom_call_target="tpu_custom_call", output_to_operand_aliasing={{0}: (8, {}), {1}: (9, {}), {2}: (12, {}), {3}: (13, {}), {... | custom-call | flops 3221225472 | tf_op jit(solution)/shard_map/second_own_kernel/pallas_call | solution.py:444
  16.9 0.0 collective-permute-done.3.refs_2_
  16.9 1.6 %near_end_kernel.1 = (f32[16,128,256]{2,1,0:T(8,128)}, f32[16,128,256]{2,1,0:T(8,128)}, f32[16,128,256]{2,1,0:T(8,128)}, f32[3,16,16,256]{3,2,1,0:T(8,128)S(1)}) custom-call(bf16[18,128,256]{2,1,0:T(8,128)(2,1)S(1)} %get-tuple-element.38.vol_ref.refs_0_, ...), custom_call_target="tpu_custom_call", output_to_operand_aliasing={{0}: (12, {}), {1}: (13, {}), {2}: (14, {})} | custom-call | flops 1073741824 | tf_op jit(solution)/shard_map/near_end_kernel/pallas_call | solution.py:444
  18.5 0.0 collective-permute-done.2.refs_2_
  18.5 2.0 %far_end_kernel.1 = (f32[16,128,256]{2,1,0:T(8,128)}, f32[16,128,256]{2,1,0:T(8,128)}, f32[16,128,256]{2,1,0:T(8,128)}) custom-call(bf16[18,128,256]{2,1,0:T(8,128)(2,1)S(1)} %get-tuple-element.38.vol_ref.refs_0_, bf16[128,384]{1,0:T(8,128)(2,1)S(1)} %get-tuple-element.44.refs_4_.refs_1_, ...), custom_call_target="tpu_custom_call", output_to_operand_aliasing={{0}: (12, {}), {1}: (13, {}), {2}: (14, {})} | custom-call | flops 1073741824 | tf_op jit(solution)/shard_map/far_end_kernel/pallas_call | solution.py:444
  (1 shorter events, 0.0 us)
Async XLA Ops:
  0.6 1.3 %copy-start = (bf16[18,128,256]{2,1,0:T(8,128)(2,1)S(1)}, bf16[18,128,256]{2,1,0:T(8,128)(2,1)}, u32[]{:S(2)}) copy-start(bf16[18,128,256]{2,1,0:T(8,128)(2,1)} %vol_ref.1) | copy-start | bytes 3538948
  2.4 1.5 %collective-permute-start = (bf16[3,128,128]{2,1,0:T(8,128)(2,1)S(1)}, bf16[3,128,128]{2,1,0:T(8,128)(2,1)S(1)}, u32[]{:S(2)}, u32[]{:S(2)}) collective-permute-start(bf16[3,128,128]{2,1,0:T(8,128)(2,1)S(1)} %get-tuple-element.40), channel_id=1, source_target_pairs={{0,1},{1,0},{2,3},{3,2},{4,5},{5,4},{6,7},{7,6},{8,9},{9,8},{10,11... | collective-permute-start | bytes 294920 | tf_op jit(solution)/shard_map/ppermute | solution.py:488
  4.0 7.4 %collective-permute-start.1 = (bf16[208,256]{1,0:T(8,128)(2,1)S(1)}, bf16[208,256]{1,0:T(8,128)(2,1)S(1)}, u32[]{:S(2)}, u32[]{:S(2)}) collective-permute-start(bf16[208,256]{1,0:T(8,128)(2,1)S(1)} %get-tuple-element.45), channel_id=1, source_target_pairs={{0,2},{2,0},{4,6},{6,4},{8,10},{10,8},{12,14},{14,12},{1,3},{3,1},... | collective-permute-start | bytes 319496 | tf_op jit(solution)/shard_map/ppermute | solution.py:505
  7.0 9.9 %collective-permute-start.3 = (bf16[208,256]{1,0:T(8,128)(2,1)S(1)}, bf16[208,256]{1,0:T(8,128)(2,1)S(1)}, u32[]{:S(2)}, u32[]{:S(2)}) collective-permute-start(bf16[208,256]{1,0:T(8,128)(2,1)S(1)} %get-tuple-element.62), channel_id=1, source_target_pairs={{0,2},{2,0},{4,6},{6,4},{8,10},{10,8},{12,14},{14,12},{1,3},{3,1},... | collective-permute-start | bytes 319496 | tf_op jit(solution)/shard_map/ppermute | solution.py:506
  11.5 7.0 %collective-permute-start.2 = (bf16[208,256]{1,0:T(8,128)(2,1)S(1)}, bf16[208,256]{1,0:T(8,128)(2,1)S(1)}, u32[]{:S(2)}, u32[]{:S(2)}) collective-permute-start(bf16[208,256]{1,0:T(8,128)(2,1)S(1)} %relay_kernel.1), channel_id=1, source_target_pairs={{0,4},{4,8},{8,12},{12,14},{6,2},{10,6},{14,10},{2,0},{1,5},{5,9},... | collective-permute-start | bytes 319496 | tf_op jit(solution)/shard_map/ppermute | solution.py:524

commit v13 on v10

--- a/solution.py
+++ b/solution.py
@@ -51,11 +51,6 @@
     return jnp.dot(left, right, preferred_element_type=jnp.float32)
 
 
-def reciprocal(value):
-    guess = pl.reciprocal(value, approx=True)
-    return guess * (2.0 - value * guess)
-
-
 def halo_plane(lane, tile, depths):
     slot = lax.div(lane, SIDE)
     rest = jnp.where(slot == 0, 0, jnp.where(slot == 1, depths - 1, FAR))
@@ -72,7 +67,7 @@
     return jnp.logical_not(even) if exchange == 0 else even
 
 
-def tables_kernel(depths, lines_ref, diff_i_ref, diff_x_ref, smooth_ref, pack_h_ref, diff_h_ref, lines_e_ref, diff_e_ref, pick_ref, mask_ref):
+def tables_kernel(depths, lines_ref, diff_i_ref, diff_x_ref, diff_z_ref, smooth_ref, pack_h_ref, diff_h_ref, lines_e_ref, diff_e_ref, pick_ref, mask_ref):
     rows, cols = lines_ref.shape[0], diff_x_ref.shape[0]
     x, il, last = lax.axis_index("xl"), lax.axis_index("il"), lax.axis_size("il") - 1
     bf16 = jnp.bfloat16
@@ -81,7 +76,9 @@
     inner = (source > 0) & (source < rows - 1)
     lines_ref[...] = jnp.where(inner, band(source, target, 0.25), 0.0).astype(bf16)
     diff_i_ref[...] = difference(source, target).astype(bf16)
-    span = EDGE * (depths - 2)
+    target, source = iota((rows, 2 * rows), 0), iota((rows, 2 * rows), 1)
+    diff_z_ref[...] = jnp.where(source == target + rows, 1.0, jnp.where(source == target, -1.0, 0.0)).astype(bf16)
+    span = EDGE * SLOTS
     target, source = iota((span, span), 0), iota((span, span), 1)
     depth = lax.div(source, EDGE) == lax.div(target, EDGE)
     target, source = lax.rem(target, EDGE), lax.rem(source, EDGE)
@@ -199,14 +196,14 @@
     part_ref[1, comp] = summed[EDGE * (chunks - 1) :]
 
 
-def make_moments(pair, vol_ref, diff_i_ref, diff_x_ref, moments_ref):
-    depths, rows, cols = vol_ref.shape
+def make_moments(pair, vol_ref, diff_i_ref, diff_x_ref, diff_z_ref, moments_ref):
+    rows = vol_ref.shape[1]
     planes = [vol_ref[2 * pair + k] for k in range(4)]
     across = dot(jnp.concatenate(planes[1:3], axis=0), diff_x_ref[...])
     for k in range(2):
         grad_i = dot(diff_i_ref[...], planes[k + 1])
         grad_x = across[rows * k : rows * (k + 1)]
-        grad_z = planes[k + 2].astype(jnp.float32) - planes[k].astype(jnp.float32)
+        grad_z = dot(diff_z_ref[...], jnp.concatenate([planes[k], planes[k + 2]], axis=0))
         for comp, term in enumerate(moments(grad_i, grad_x, grad_z)):
             moments_ref[k, comp] = term
 
@@ -215,10 +212,10 @@
     store_chunks(dot(lines_ref[...], moments_ref[z % 2, comp]), comp, inner_ref.at[z], part_ref.at[:, :, z])
 
 
-def lines_kernel(vol_ref, lines_ref, diff_i_ref, diff_x_ref, inner_ref, part_ref, even_ref, odd_ref):
+def lines_kernel(vol_ref, lines_ref, diff_i_ref, diff_x_ref, diff_z_ref, inner_ref, part_ref, even_ref, odd_ref):
     slots = (even_ref, odd_ref)
     for pair in range(HEAD):
-        make_moments(pair, vol_ref, diff_i_ref, diff_x_ref, slots[pair % 2])
+        make_moments(pair, vol_ref, diff_i_ref, diff_x_ref, diff_z_ref, slots[pair % 2])
         for k in range(2):
             for comp in range(6):
                 make_lines(2 * pair + k, comp, lines_ref, slots[pair % 2], inner_ref, part_ref)
@@ -234,12 +231,11 @@
     lanes = (pl.multiple_of(128 * x, 128), pl.multiple_of(128 - 128 * x, 128))
     for half, lane in zip(halves, lanes):
         a, b, c, d, e, f = [half[EDGE * comp : EDGE * (comp + 1)] for comp in range(6)]
-        low = c + 1e-6
-        guess = pl.reciprocal(low, approx=True)
-        inverse = guess * (low * guess - 2.0)
+        low = -1e-6 - c
+        inverse = pl.reciprocal(low, approx=True)
         spread = (a - b) * (a - c) + (b - c) * (b - c) + 3.0 * (d * d + e * e + f * f)
         root = spread * lax.rsqrt(jnp.maximum(spread, TINY))
-        store(pl.ds(lane, 128), (e * inverse, f * inverse, root * reciprocal(a + b + low)))
+        store(pl.ds(lane, 128), (e * inverse, f * inverse, root * pl.reciprocal(a + b - low, approx=True)))
 
 
 def border_of(packed, slot, mask_ref):
@@ -249,7 +245,7 @@
 
 
 def own_kernel(
-    stage, vol_ref, lines_ref, diff_i_ref, diff_x_ref, smooth_ref, halo_ref, diff_h_ref, pack_h_ref, mask_ref,
+    stage, vol_ref, lines_ref, diff_i_ref, diff_x_ref, diff_z_ref, smooth_ref, halo_ref, diff_h_ref, pack_h_ref, mask_ref,
     inner_in_ref, part_in_ref, *refs,
 ):
     if stage == 0:
@@ -288,7 +284,7 @@
         z = half * stage + step
         later = ahead[step] if step < len(ahead) else None
         if later is not None and later % 2 == 0:
-            make_moments(later // 2, vol_ref, diff_i_ref, diff_x_ref, slots[later // 2 % 2])
+            make_moments(later // 2, vol_ref, diff_i_ref, diff_x_ref, diff_z_ref, slots[later // 2 % 2])
         if step < half - 1:
             tensor_of(inner_ref[z + 1], smooth_ref, tensor_ref.at[(step + 1) % 2])
         for chunk in range(chunks):
@@ -317,7 +313,7 @@
 
 def end_kernel(
     exchange, vol_ref, halo_ref, rows_ref, part_ref, part_h_ref,
-    smooth_ref, pack_h_ref, diff_x_ref, diff_h_ref, lines_e_ref, diff_e_ref, mask_ref, done_ref, *refs,
+    smooth_ref, pack_h_ref, diff_x_ref, diff_z_ref, diff_h_ref, lines_e_ref, diff_e_ref, mask_ref, done_ref, *refs,
 ):
     last = exchange == 1
     targets, refs = refs[3:6], refs[6:]
@@ -378,11 +374,10 @@
     copies = []
     def make_block_moments(group):
         first = half * group
-        centre = block_ref[first + 1 : first + half + 1].reshape(span, cols)
-        grad_i = dot(diff_e_ref[:span, :span], centre)
-        grad_x = dot(centre, diff_x_ref[...])
-        grad_z = block_ref[first + 2 : first + half + 2].astype(f32) - block_ref[first : first + half].astype(f32)
-        return moments(grad_i, grad_x, grad_z.reshape(span, cols))
+        planes = [block_ref[first + k : first + half + k].reshape(span, cols) for k in range(3)]
+        grad_i = dot(diff_e_ref[...], planes[1])
+        grad_x = dot(planes[1], diff_x_ref[...])
+        return moments(grad_i, grad_x, dot(diff_z_ref[...], jnp.concatenate([planes[0], planes[2]], axis=0)))
 
     def make_edge(group, comp, term):
         first = half * group
@@ -405,21 +400,15 @@
             copy.start()
             copies.append(copy)
 
-    for comp, term in enumerate(make_block_moments(0)):
-        make_edge(0, comp, term)
-    later = make_block_moments(1)
-    tensor_of(edge_ref[:half], smooth_ref, tensor_ref.at[0])
-    for k in range(half):
-        if k < 6:
-            make_edge(1, k, later[k])
-        finish(0, k)
-    if last:
-        send(0)
-    tensor_of(edge_ref[half:], smooth_ref, tensor_ref.at[1])
-    for k in range(half):
-        finish(1, k)
-    if last:
-        send(1)
+    for group in range(2):
+        for comp, term in enumerate(make_block_moments(group)):
+            make_edge(group, comp, term)
+    for group in range(2):
+        tensor_of(edge_ref[half * group : half * (group + 1)], smooth_ref, tensor_ref.at[group])
+        for k in range(half):
+            finish(group, k)
+        if last:
+            send(group)
     for copy in finished + copies:
         copy.wait()
 
@@ -448,14 +437,15 @@
     work = half * 1024 * 2 * 256 * 256
     packed_rows = -(-REACH * (depths + 2) // 16) * 16
 
-    span = EDGE * count
-    lines, diff_i, diff_x, smooth, pack_h, diff_h, lines_e, diff_e, pick, mask = call(
+    span = EDGE * SLOTS
+    lines, diff_i, diff_x, diff_z, smooth, pack_h, diff_h, lines_e, diff_e, pick, mask = call(
         "tables_kernel",
         lambda *refs: tables_kernel(depths, *refs),
         [
             ((rows, rows), bf16),
             ((rows, rows), bf16),
             ((cols, cols), bf16),
+            ((rows, 2 * rows), bf16),
             ((cols, cols), bf16),
             ((256, 256), bf16),
             ((128 * TILES, 512), bf16),
@@ -474,7 +464,7 @@
     chunks = rows // EDGE - 2
     lined = [((count, chunks, 6, EDGE, cols), bf16), ((2, 6, count, EDGE, cols), f32)]
     moment_slots = [pltpu.VMEM((2, 6, rows, cols), bf16)] * 2
-    inner, part = call("lines_kernel", lines_kernel, lined, moment_slots, [vol, lines, diff_i, diff_x], flops=work // 4)
+    inner, part = call("lines_kernel", lines_kernel, lined, moment_slots, [vol, lines, diff_i, diff_x, diff_z], flops=work // 4)
     packed = ((packed_rows, cols), bf16)
     halo, near, far = call(
         "rows_kernel",
@@ -495,7 +485,7 @@
     border = ((6 * EDGE * chunks, 256), f32)
     ready = [((3, count // 2 - 2, EDGE * chunks, cols), f32)]
     own_scratch = moment_slots + [pltpu.VMEM((2, 6 * EDGE * chunks, cols), f32), pltpu.VMEM(*ready[0]), pltpu.SemaphoreType.DMA((count // 4 - 1, 3))]
-    shared = [vol, lines, diff_i, diff_x, smooth, halo, diff_h, pack_h, mask]
+    shared = [vol, lines, diff_i, diff_x, diff_z, smooth, halo, diff_h, pack_h, mask]
     inner, part, *outs_in, done, part_h, border = call(
         "first_own_kernel",
         lambda *refs: own_kernel(0, *refs),
@@ -521,7 +511,7 @@
     )
 
     end_rows = (3, count, EDGE, cols)
-    tables = [smooth, pack_h, diff_x, diff_h, lines_e, diff_e, mask]
+    tables = [smooth, pack_h, diff_x, diff_z, diff_h, lines_e, diff_e, mask]
     scratch = [
         pltpu.VMEM((8 + packed_rows, cols), f32),
         pltpu.VMEM((depths, EDGE, cols), bf16),

time: 19.7 us -> 19.6 us (level)
  Pallas kernels: 12.9 us -> 12.4 us
    pallas_call x9, Pallas kernels: 12.9 us -> 12.4 us  [call(): pl.pallas_call(kernel, out_shape=tuple((jax.ShapeDtypeStruct(*out) for ou...]
  transfers between devices with their start and end apart: 4 -> 4, of which waited for: 0 -> 1; matrix products, arithmetic and copies ran while one was open for 0% -> 0% of each run, Pallas kernels for 47% -> 45%
where the time goes in v13:
time: 19.6 us; the launch traced here: 19.4 us
  Pallas kernels  12.4 us (63%)
  starting transfers between devices  5.7 us (29%)
  between operations  0.71 us (4%)
  local copies, waits for them, and re-layouts  0.45 us (2%)
    pallas_call x9, Pallas kernels, call(): pl.pallas_call(kernel, out_shape=tuple((jax.ShapeDtypeStruct(*out) for ou...  12.4 us
    ppermute x1, starting transfers between devices, body(): far_in = lax.ppermute(far, 'il', swap)  2.94 us
    ppermute x1, starting transfers between devices, body(): relayed_in = lax.ppermute(relayed, 'il', onward)  2.16 us
    ppermute x1, starting transfers between devices, body(): side = lax.ppermute(send, 'xl', [(0, 1), (1, 0)])  0.52 us
    unnamed x2, local copies, waits for them, and re-layouts  0.45 us
  transfers between devices with their start and end apart: 4, of which 1 were waited for; matrix products, arithmetic and copies ran while one was open for 0% of the time, Pallas kernels for 45%

profile of v13, /device:TPU:0, one launch (start us, length us, event | category | flops | bytes accessed | tf_op | source)
XLA Modules:
  0.0 19.4 jit_solution(12085983568055209141)
XLA Ops:
  0.6 0.0 copy-start
  0.6 0.8 %tables_kernel.1 = (bf16[128,128]{1,0:T(8,128)(2,1)S(1)}, bf16[128,128]{1,0:T(8,128)(2,1)S(1)}, bf16[256,256]{1,0:T(8,128)(2,1)S(1)}, bf16[128,256]{1,0:T(8,128)...) custom-call(), custom_call_target="tpu_custom_call" | custom-call | flops 1073741824 | tf_op jit(solution)/shard_map/tables_kernel/pallas_call | solution.py:417
  1.5 0.4 %copy-done = bf16[18,128,256]{2,1,0:T(8,128)(2,1)S(1)} copy-done((bf16[18,128,256]{2,1,0:T(8,128)(2,1)S(1)}, bf16[18,128,256]{2,1,0:T(8,128)(2,1)}, u32[]{:S(2)}) %copy-start) | copy-done | bytes 1179672
  1.9 0.5 %pack_kernel.1 = (bf16[18,128,256]{2,1,0:T(8,128)(2,1)S(1)}, bf16[3,128,128]{2,1,0:T(8,128)(2,1)S(1)}, bf16[3,128,128]{2,1,0:T(8,128)(2,1)S(1)}) custom-call(bf16[18,128,256]{2,1,0:T(8,128)(2,1)S(1)} %copy-done, bf16[256,256]{1,0:T(8,128)(2,1)S(1)} %get-tuple-element.39.pick_ref), custom_call_target="tpu_custom_call" | custom-call | tf_op jit(solution)/shard_map/pack_kernel/pallas_call | solution.py:417
  2.4 0.5 %collective-permute-start = (bf16[3,128,128]{2,1,0:T(8,128)(2,1)S(1)}, bf16[3,128,128]{2,1,0:T(8,128)(2,1)S(1)}, u32[]{:S(2)}, u32[]{:S(2)}) collective-permute-start(bf16[3,128,128]{2,1,0:T(8,128)(2,1)S(1)} %get-tuple-element.42), channel_id=1, source_target_pairs={{0,1},{1,0},{2,3},{3,2},{4,5},{5,4},{6,7},{7,6},{8,9},{9,8},{10,11... | collective-permute-start | bytes 294920 | tf_op jit(solution)/shard_map/ppermute | solution.py:463
  2.9 0.9 %lines_kernel.1 = (bf16[16,6,6,16,256]{4,3,2,1,0:T(8,128)(2,1)S(1)}, f32[2,6,16,16,256]{4,3,2,1,0:T(8,128)S(1)}) custom-call(bf16[18,128,256]{2,1,0:T(8,128)(2,1)S(1)} %get-tuple-element.40.vol_ref.refs_0_, bf16[128,128]{1,0:T(8,128)(2,1)S(1)} %get-tuple-element.43.lines_ref.refs_1_, bf16[128,128]{1,0:T(8,128)(2,1)S(1)} %get-tuple-element.44.diff_i_ref.refs_2_, ...), custom_call_target="tpu_custom_call" | custom-call | flops 268435456 | tf_op jit(solution)/shard_map/lines_kernel/pallas_call | solution.py:417
  3.9 0.0 collective-permute-done.side_ref
  3.9 0.1 rows_kernel.1
  4.0 2.9 %collective-permute-start.1 = (bf16[208,256]{1,0:T(8,128)(2,1)S(1)}, bf16[208,256]{1,0:T(8,128)(2,1)S(1)}, u32[]{:S(2)}, u32[]{:S(2)}) collective-permute-start(bf16[208,256]{1,0:T(8,128)(2,1)S(1)} %get-tuple-element.49), channel_id=1, source_target_pairs={{0,2},{2,0},{4,6},{6,4},{8,10},{10,8},{12,14},{14,12},{1,3},{3,1},... | collective-permute-start | bytes 319496 | tf_op jit(solution)/shard_map/ppermute | solution.py:480
  7.0 0.1 collective-permute-start.3
  7.0 3.5 %first_own_kernel.1 = (bf16[16,6,6,16,256]{4,3,2,1,0:T(8,128)(2,1)S(1)}, f32[2,6,16,16,256]{4,3,2,1,0:T(8,128)S(1)}, f32[16,128,256]{2,1,0:T(8,128)}, f32[16,128...) custom-call(bf16[18,128,256]{2,1,0:T(8,128)(2,1)S(1)} %get-tuple-ele, ...), custom_call_target="tpu_custom_call", output_to_operand_aliasing={{0}: (10, {}), {1}: (11, {})} | custom-call | flops 3221225472 | tf_op jit(solution)/shard_map/first_own_kernel/pallas_call | solution.py:417
  10.6 0.1 collective-permute-done.1.rows_ref
  10.7 2.2 %collective-permute-start.2 = (bf16[208,256]{1,0:T(8,128)(2,1)S(1)}, bf16[208,256]{1,0:T(8,128)(2,1)S(1)}, u32[]{:S(2)}, u32[]{:S(2)}) collective-permute-start(bf16[208,256]{1,0:T(8,128)(2,1)S(1)} %relay_kernel.1), channel_id=1, source_target_pairs={{0,4},{4,8},{8,12},{12,14},{6,2},{10,6},{14,10},{2,0},{1,5},{5,9},... | collective-permute-start | bytes 319496 | tf_op jit(solution)/shard_map/ppermute | solution.py:500
  12.9 2.4 %second_own_kernel.1 = (bf16[16,6,6,16,256]{4,3,2,1,0:T(8,128)(2,1)S(1)}, f32[2,6,16,16,256]{4,3,2,1,0:T(8,128)S(1)}, f32[16,128,256]{2,1,0:T(8,128)}, f32[16,12...) custom-call(bf16[18,128,256]{2,1,0:T(8,128)(2,1)S(1)} %get-tuple-ele, ...), custom_call_target="tpu_custom_call", output_to_operand_aliasing={{0}: (10, {}), {1}: (11, {}), {2}: (14, {}), {3}: (15, {}),... | custom-call | flops 3221225472 | tf_op jit(solution)/shard_map/second_own_kernel/pallas_call | solution.py:417
  15.3 0.0 collective-permute-done.3.refs_2_
  15.3 1.8 %near_end_kernel.1 = (f32[16,128,256]{2,1,0:T(8,128)}, f32[16,128,256]{2,1,0:T(8,128)}, f32[16,128,256]{2,1,0:T(8,128)}, f32[3,16,16,256]{3,2,1,0:T(8,128)S(1)}) custom-call(bf16[18,128,256]{2,1,0:T(8,128)(2,1)S(1)} %get-tuple-element.40.vol_ref.refs_0_, ...), custom_call_target="tpu_custom_call", output_to_operand_aliasing={{0}: (14, {}), {1}: (15, {}), {2}: (16, {})} | custom-call | flops 1073741824 | tf_op jit(solution)/shard_map/near_end_kernel/pallas_call | solution.py:417
  17.2 0.0 collective-permute-done.2.refs_2_
  17.2 2.2 %far_end_kernel.1 = (f32[16,128,256]{2,1,0:T(8,128)}, f32[16,128,256]{2,1,0:T(8,128)}, f32[16,128,256]{2,1,0:T(8,128)}) custom-call(bf16[18,128,256]{2,1,0:T(8,128)(2,1)S(1)} %get-tuple-element.40.vol_ref.refs_0_, bf16[128,384]{1,0:T(8,128)(2,1)S(1)} %get-tuple-element.48.refs_6_.refs_1_, ...), custom_call_target="tpu_custom_call", output_to_operand_aliasing={{0}: (14, {}), {1}: (15, {}), {2}: (16, {})} | custom-call | flops 1073741824 | tf_op jit(solution)/shard_map/far_end_kernel/pallas_call | solution.py:417
  (1 shorter events, 0.0 us)
Async XLA Ops:
  0.6 1.3 %copy-start = (bf16[18,128,256]{2,1,0:T(8,128)(2,1)S(1)}, bf16[18,128,256]{2,1,0:T(8,128)(2,1)}, u32[]{:S(2)}) copy-start(bf16[18,128,256]{2,1,0:T(8,128)(2,1)} %vol_ref.1) | copy-start | bytes 3538948
  2.4 1.5 %collective-permute-start = (bf16[3,128,128]{2,1,0:T(8,128)(2,1)S(1)}, bf16[3,128,128]{2,1,0:T(8,128)(2,1)S(1)}, u32[]{:S(2)}, u32[]{:S(2)}) collective-permute-start(bf16[3,128,128]{2,1,0:T(8,128)(2,1)S(1)} %get-tuple-element.42), channel_id=1, source_target_pairs={{0,1},{1,0},{2,3},{3,2},{4,5},{5,4},{6,7},{7,6},{8,9},{9,8},{10,11... | collective-permute-start | bytes 294920 | tf_op jit(solution)/shard_map/ppermute | solution.py:463
  4.0 6.7 %collective-permute-start.1 = (bf16[208,256]{1,0:T(8,128)(2,1)S(1)}, bf16[208,256]{1,0:T(8,128)(2,1)S(1)}, u32[]{:S(2)}, u32[]{:S(2)}) collective-permute-start(bf16[208,256]{1,0:T(8,128)(2,1)S(1)} %get-tuple-element.49), channel_id=1, source_target_pairs={{0,2},{2,0},{4,6},{6,4},{8,10},{10,8},{12,14},{14,12},{1,3},{3,1},... | collective-permute-start | bytes 319496 | tf_op jit(solution)/shard_map/ppermute | solution.py:480
  7.0 8.4 %collective-permute-start.3 = (bf16[208,256]{1,0:T(8,128)(2,1)S(1)}, bf16[208,256]{1,0:T(8,128)(2,1)S(1)}, u32[]{:S(2)}, u32[]{:S(2)}) collective-permute-start(bf16[208,256]{1,0:T(8,128)(2,1)S(1)} %get-tuple-element.66), channel_id=1, source_target_pairs={{0,2},{2,0},{4,6},{6,4},{8,10},{10,8},{12,14},{14,12},{1,3},{3,1},... | collective-permute-start | bytes 319496 | tf_op jit(solution)/shard_map/ppermute | solution.py:481
  10.7 6.5 %collective-permute-start.2 = (bf16[208,256]{1,0:T(8,128)(2,1)S(1)}, bf16[208,256]{1,0:T(8,128)(2,1)S(1)}, u32[]{:S(2)}, u32[]{:S(2)}) collective-permute-start(bf16[208,256]{1,0:T(8,128)(2,1)S(1)} %relay_kernel.1), channel_id=1, source_target_pairs={{0,4},{4,8},{8,12},{12,14},{6,2},{10,6},{14,10},{2,0},{1,5},{5,9},... | collective-permute-start | bytes 319496 | tf_op jit(solution)/shard_map/ppermute | solution.py:500

commit v14 on v11

--- a/solution.py
+++ b/solution.py
@@ -49,11 +49,6 @@
 
 def dot(left, right):
     return jnp.dot(left, right, preferred_element_type=jnp.float32)
-
-
-def reciprocal(value):
-    guess = pl.reciprocal(value, approx=True)
-    return guess * (2.0 - value * guess)
 
 
 def halo_plane(lane, tile, depths):
@@ -176,10 +171,6 @@
     far_ref[...] = packed_ref[1].astype(jnp.bfloat16)
 
 
-def relay_kernel(rows_ref, after_ref, out_ref):
-    out_ref[...] = rows_ref[...]
-
-
 def moments(grad_i, grad_x, grad_z):
     terms = (
         grad_i * grad_i,
@@ -239,12 +230,11 @@
     lanes = (pl.multiple_of(128 * x, 128), pl.multiple_of(128 - 128 * x, 128))
     for half, lane in zip(halves, lanes):
         a, b, c, d, e, f = [half[EDGE * comp : EDGE * (comp + 1)] for comp in range(6)]
-        low = c + 1e-6
-        guess = pl.reciprocal(low, approx=True)
-        inverse = guess * (low * guess - 2.0)
+        low = -1e-6 - c
+        inverse = pl.reciprocal(low, approx=True)
         spread = (a - b) * (a - c) + (b - c) * (b - c) + 3.0 * (d * d + e * e + f * f)
         root = spread * lax.rsqrt(jnp.maximum(spread, TINY))
-        store(pl.ds(lane, 128), (e * inverse, f * inverse, root * reciprocal(a + b + low)))
+        store(pl.ds(lane, 128), (e * inverse, f * inverse, root * pl.reciprocal(a + b - low, approx=True)))
 
 
 def border_of(packed, slot, mask_ref):
@@ -254,69 +244,58 @@
 
 
 def own_kernel(
-    stage, vol_ref, lines_ref, diff_i_ref, smooth_ref, halo_ref, diff_h_ref, pack_h_ref, mask_ref,
-    inner_in_ref, part_in_ref, *refs,
+    vol_ref, lines_ref, diff_i_ref, smooth_ref, halo_ref, diff_h_ref, pack_h_ref, mask_ref, inner_in_ref, part_in_ref,
+    part_ref, dip_i_ref, dip_x_ref, plan_ref, later_ref, part_h_ref,
+    inner_ref, border_ref, even_ref, odd_ref, tensor_ref, out_ref, sems,
 ):
-    if stage == 0:
-        inner_ref, part_ref, *targets, later_ref, part_h_ref, border_ref, even_ref, odd_ref, tensor_ref, out_ref, sems = refs
-        both = dot(halo_ref[...], diff_h_ref[...])
-        grad_i = dot(diff_i_ref[...], halo_ref[:, :256])
-        lined_h = [[] for chunk in range(inner_ref.shape[1])]
-        for comp, term in enumerate(moments(grad_i, both[:, 256:], both[:, :256])):
-            summed = dot(lines_ref[...], term)
-            for chunk, parts in enumerate(lined_h):
-                parts.append(summed[EDGE * (chunk + 1) : EDGE * (chunk + 2)].astype(jnp.bfloat16))
-            part_h_ref[0, comp] = summed[:EDGE]
-            part_h_ref[1, comp] = summed[EDGE * (len(lined_h) + 1) :]
-        border_ref[...] = dot(jnp.concatenate(sum(lined_h, []), axis=0), pack_h_ref[...])
-        finished = []
-    else:
-        border_ref, done_ref, *refs = refs
-        inner_ref, part_ref, *targets, later_ref, even_ref, odd_ref, tensor_ref, out_ref, sems, done_sems = refs[3:]
-        finished = []
     count, chunks = inner_ref.shape[:2]
-    pairs, inner = count // 4, EDGE * chunks
+    inner = EDGE * chunks
     slots = (even_ref, odd_ref)
-
-    def place(target, pair):
-        return target.at[pl.ds(2 * pair, 2), pl.ds(EDGE, inner)]
-
-    if stage == 1:
-        for n, target in enumerate(targets):
-            finished.append(pltpu.make_async_copy(done_ref.at[n], place(target, pairs - 1), done_sems.at[n]))
-            finished[-1].start()
-
-    half = count // 2
-    ahead = range(2 * HEAD, half + 2 * AHEAD) if stage == 0 else range(half + 2 * AHEAD, count)
-    tensor_of(inner_ref[half * stage], smooth_ref, tensor_ref.at[0])
-    for step in range(half):
-        z = half * stage + step
-        later = ahead[step] if step < len(ahead) else None
+    targets = (dip_i_ref, dip_x_ref, plan_ref)
+    inner_ref[: 2 * HEAD] = inner_in_ref[...]
+
+    both = dot(halo_ref[...], diff_h_ref[...])
+    grad_i = dot(diff_i_ref[...], halo_ref[:, :256])
+    lined_h = [[] for chunk in range(chunks)]
+    for comp, term in enumerate(moments(grad_i, both[:, 256:], both[:, :256])):
+        summed = dot(lines_ref[...], term)
+        for chunk, parts in enumerate(lined_h):
+            parts.append(summed[EDGE * (chunk + 1) : EDGE * (chunk + 2)].astype(jnp.bfloat16))
+        part_h_ref[0, comp] = summed[:EDGE]
+        part_h_ref[1, comp] = summed[EDGE * (chunks + 1) :]
+    border_ref[...] = dot(jnp.concatenate(sum(lined_h, []), axis=0), pack_h_ref[...])
+
+    copies = []
+    tensor_of(inner_ref[0], smooth_ref, tensor_ref.at[0])
+    for z in range(count):
+        later = z + 2 * HEAD if z + 2 * HEAD < count else None
         if later is not None and later % 2 == 0:
             make_moments(later // 2, vol_ref, mask_ref, slots[later // 2 % 2])
-        if step < half - 1:
-            tensor_of(inner_ref[z + 1], smooth_ref, tensor_ref.at[(step + 1) % 2])
+        if z < count - 1:
+            tensor_of(inner_ref[z + 1], smooth_ref, tensor_ref.at[(z + 1) % 2])
+        group = 128 * (z // SLOTS)
         for chunk in range(chunks):
             rows = slice(EDGE * chunk, EDGE * (chunk + 1))
             part = slice(6 * EDGE * chunk, 6 * EDGE * (chunk + 1))
 
             def store(lanes, values):
                 for n, value in enumerate(values):
-                    if step >= half - 2:
-                        later_ref[n, step % 2, rows, lanes] = value
+                    if z >= count - 2:
+                        later_ref[n, z % 2, rows, lanes] = value
                     else:
-                        out_ref[n, step, rows, lanes] = value
-
-            border = border_of(border_ref[part, 128 * stage : 128 * (stage + 1)], z % SLOTS, mask_ref)
-            attributes(tensor_ref[step % 2, part], border, store)
+                        out_ref[n, z, rows, lanes] = value
+
+            border = border_of(border_ref[part, group : group + 128], z % SLOTS, mask_ref)
+            attributes(tensor_ref[z % 2, part], border, store)
             if later is not None:
                 make_lines(later, chunk, lines_ref, slots[later // 2 % 2], inner_ref, part_ref)
-        if step % 2 == 1 and step < half - 2:
+        if z % 2 == 1 and z < count - 2:
+            depth = pl.ds(z - 1, 2)
             for n, target in enumerate(targets):
-                source = out_ref.at[n, pl.ds(step - 1, 2)]
-                finished.append(pltpu.make_async_copy(source, place(target, z // 2), sems.at[step // 2, n]))
-                finished[-1].start()
-    for copy in finished:
+                place = target.at[depth, pl.ds(EDGE, inner)]
+                copies.append(pltpu.make_async_copy(out_ref.at[n, depth], place, sems.at[z // 2, n]))
+                copies[-1].start()
+    for copy in copies:
         copy.wait()
 
 
@@ -327,9 +306,9 @@
     last = exchange == 1
     targets, refs = refs[3:6], refs[6:]
     if last:
-        packed_ref, block_ref, block_h_ref, border_ref, edge_ref, tensor_ref, out_ref, done_sems, sems = refs
+        packed_ref, block_ref, block_h_ref, border_ref, edge_ref, out_ref, done_sems, sems = refs
     else:
-        out_ref, packed_ref, block_ref, block_h_ref, border_ref, edge_ref, tensor_ref, done_sems = refs
+        out_ref, packed_ref, block_ref, block_h_ref, border_ref, edge_ref, done_sems = refs
     depths, rows, cols = vol_ref.shape
     count, half = depths - 2, (depths - 2) // 2
     bf16, f32 = jnp.bfloat16, jnp.float32
@@ -392,13 +371,13 @@
         summed = part_ref[end, comp, first : first + half] + outer.reshape(half, EDGE, cols)
         edge_ref[first : first + half, comp] = summed.astype(bf16)
 
-    def finish(group, k):
+    def finish(group, k, tensor):
         def store(lanes, values):
             for n, value in enumerate(values):
                 out_ref[n, half * group + k, :, lanes] = value
 
         border = border_of(border_ref[:, 128 * group : 128 * (group + 1)], k, mask_ref)
-        attributes(tensor_ref[group, 6 * EDGE * k : 6 * EDGE * (k + 1)], border, store)
+        attributes(tensor, border, store)
 
     def send(group):
         depth = pl.ds(half * group, half)
@@ -407,21 +386,15 @@
             copy.start()
             copies.append(copy)
 
-    for comp, term in enumerate(make_block_moments(0)):
-        make_edge(0, comp, term)
-    later = make_block_moments(1)
-    tensor_of(edge_ref[:half], smooth_ref, tensor_ref.at[0])
-    for k in range(half):
-        if k < 6:
-            make_edge(1, k, later[k])
-        finish(0, k)
-    if last:
-        send(0)
-    tensor_of(edge_ref[half:], smooth_ref, tensor_ref.at[1])
-    for k in range(half):
-        finish(1, k)
-    if last:
-        send(1)
+    for group in range(2):
+        for comp, term in enumerate(make_block_moments(group)):
+            make_edge(group, comp, term)
+    for group in range(2):
+        tensor = dot(edge_ref[half * group : half * (group + 1)].reshape(6 * span, cols), smooth_ref[...])
+        for k in range(half):
+            finish(group, k, tensor[6 * EDGE * k : 6 * EDGE * (k + 1)])
+        if last:
+            send(group)
     for copy in finished + copies:
         copy.wait()
 
@@ -473,9 +446,16 @@
     vol, send, own = call("pack_kernel", pack_kernel, [(volume.shape, bf16), halo_tile, halo_tile], [], [volume, pick])
     side = lax.ppermute(send, "xl", [(0, 1), (1, 0)])
     chunks = rows // EDGE - 2
-    lined = [((count, chunks, 6, EDGE, cols), bf16), ((2, 6, count, EDGE, cols), f32)]
     moment_slots = [pltpu.VMEM((2, 6, rows, cols), bf16)] * 2
-    inner, part = call("lines_kernel", lines_kernel, lined, moment_slots, [vol, lines, mask], flops=work // 4)
+    partial = ((2, 6, count, EDGE, cols), f32)
+    inner, part = call(
+        "lines_kernel",
+        lines_kernel,
+        [((2 * HEAD, chunks, 6, EDGE, cols), bf16), partial],
+        moment_slots,
+        [vol, lines, mask],
+        flops=work // 4,
+    )
     packed = ((packed_rows, cols), bf16)
     halo, near, far = call(
         "rows_kernel",
@@ -485,40 +465,29 @@
         [vol, own, side, part],
         in_specs=[WHOLE] * 3 + [ANYWHERE],
     )
-    swap = [(i, i ^ 1) for i in range(il)]
-    onward = [(i, i + 2) for i in range(0, il - 2, 2)] + [(il - 2, il - 1)]
-    onward += [(i, i - 2) for i in range(3, il, 2)] + [(1, 0)]
-    far_in = lax.ppermute(far, "il", swap)
-    near_in = lax.ppermute(near, "il", swap)
+    pairs = [(i, i + 1) for i in range(1, il - 1, 2)]
+    far_in = lax.ppermute(far, "il", pairs + [(j, i) for i, j in pairs] + [(0, 0), (il - 1, il - 1)])
+    near_in = lax.ppermute(near, "il", [(i, i ^ 1) for i in range(il)])
 
     outs = [((count, rows, cols), f32)] * 3
-    saved = ((3, 2, EDGE * chunks, cols), f32)
-    border = ((6 * EDGE * chunks, 256), f32)
-    ready = [((3, count // 2 - 2, EDGE * chunks, cols), f32)]
-    own_scratch = moment_slots + [pltpu.VMEM((2, 6 * EDGE * chunks, cols), f32), pltpu.VMEM(*ready[0]), pltpu.SemaphoreType.DMA((count // 4 - 1, 3))]
-    shared = [vol, lines, diff_i, smooth, halo, diff_h, pack_h, mask]
-    inner, part, *outs_in, done, part_h, border = call(
-        "first_own_kernel",
-        lambda *refs: own_kernel(0, *refs),
-        lined + outs + [saved, ((2, 6, EDGE, 256), f32), border],
-        own_scratch,
-        shared + [inner, part],
-        out_specs=(WHOLE,) * 2 + (IN_HBM,) * 3 + (WHOLE,) * 3,
-        flops=3 * work,
-        aliases={len(shared) + n: n for n in range(2)},
-    )
-    (relayed,) = call("relay_kernel", relay_kernel, [packed], [], [far_in, done], in_specs=[WHOLE, ANYWHERE])
-    relayed_in = lax.ppermute(relayed, "il", onward)
-    inner, part, *outs_in, done = call(
-        "second_own_kernel",
-        lambda *refs: own_kernel(1, *refs),
-        lined + outs + [saved],
-        own_scratch + [pltpu.SemaphoreType.DMA((3,))],
-        shared + [inner, part, border, done] + outs_in,
-        in_specs=[WHOLE] * (len(shared) + 4) + [IN_HBM] * 3,
-        out_specs=(WHOLE,) * 2 + (IN_HBM,) * 3 + (WHOLE,),
-        flops=3 * work,
-        aliases={len(shared): 0, len(shared) + 1: 1} | {len(shared) + 4 + n: 2 + n for n in range(3)},
+    operands = [vol, lines, diff_i, smooth, halo, diff_h, pack_h, mask, inner, part]
+    part, *outs_in, done, part_h = call(
+        "own_kernel",
+        own_kernel,
+        [partial, *outs, ((3, 2, EDGE * chunks, cols), f32), ((2, 6, EDGE, 256), f32)],
+        [
+            pltpu.VMEM((count, chunks, 6, EDGE, cols), bf16),
+            pltpu.VMEM((6 * EDGE * chunks, 256), f32),
+            *moment_slots,
+            pltpu.VMEM((2, 6 * EDGE * chunks, cols), f32),
+            pltpu.VMEM((3, count - 2, EDGE * chunks, cols), f32),
+            pltpu.SemaphoreType.DMA((half - 1, 3)),
+        ],
+        operands,
+        out_specs=(WHOLE,) + (IN_HBM,) * 3 + (WHOLE,) * 2,
+        flops=5 * work,
+        limit=24,
+        aliases={len(operands) - 1: 0},
     )
 
     end_rows = (3, count, EDGE, cols)
@@ -529,7 +498,6 @@
         pltpu.VMEM((EDGE, 128 * TILES), bf16),
         pltpu.VMEM((6 * EDGE, 256), f32),
         pltpu.VMEM((count, 6, EDGE, cols), bf16),
-        pltpu.VMEM((2, half * 6 * EDGE, cols), f32),
     ]
     sems = pltpu.SemaphoreType.DMA((3,))
     operands = [vol, halo, near_in, part, part_h, *tables, done]
@@ -544,7 +512,7 @@
         flops=work,
         aliases={len(operands) + n: n for n in range(3)},
     )
-    operands = [vol, halo, relayed_in, part, part_h, *tables, done]
+    operands = [vol, halo, far_in, part, part_h, *tables, done]
     return call(
         "far_end_kernel",
         lambda *refs: end_kernel(1, *refs),

time: 19.7 us -> 19 us (0.964)
  Pallas kernels: 12.3 us -> 10.5 us
  starting transfers between devices: 5.7 us -> 6.88 us
    pallas_call x9 -> x7, Pallas kernels: 12.3 us -> 10.5 us  [call(): pl.pallas_call(kernel, out_shape=tuple((jax.ShapeDtypeStruct(*out) for ou...]
    ppermute x3 -> x2, starting transfers between devices: 5.18 us -> 6.36 us  [the longest x1 5.69 us: body(): near_in = lax.ppermute(near, 'il', [(i, i ^ 1) for i in range(il)])]
  transfers between devices with their start and end apart: 4 -> 3, of which waited for: 1 -> 1; matrix products, arithmetic and copies ran while one was open for 0% -> 0% of each run, Pallas kernels for 45% -> 38%
where the time goes in v14:
time: 19 us; the launch traced here: 18.9 us
  Pallas kernels  10.5 us (55%)
  starting transfers between devices  6.88 us (36%)
  between operations  0.7 us (4%)
  local copies, waits for them, and re-layouts  0.52 us (3%)
  waiting for transfers between devices  0.25 us (1%)
    pallas_call x7, Pallas kernels, call(): pl.pallas_call(kernel, out_shape=tuple((jax.ShapeDtypeStruct(*out) for ou...  10.5 us
    ppermute x1, starting transfers between devices, body(): near_in = lax.ppermute(near, 'il', [(i, i ^ 1) for i in range(il)])  5.69 us
    ppermute x1, starting transfers between devices, body(): lax.ppermute(far, 'il', pairs + [(j, i) for i, j in pairs] + [(0, 0), (il...  0.67 us
    ppermute x1, starting transfers between devices, body(): side = lax.ppermute(send, 'xl', [(0, 1), (1, 0)])  0.52 us
    unnamed x2, local copies, waits for them, and re-layouts  0.52 us
  transfers between devices with their start and end apart: 3, of which 1 were waited for; matrix products, arithmetic and copies ran while one was open for 0% of the time, Pallas kernels for 38%

profile of v14, /device:TPU:0, one launch (start us, length us, event | category | flops | bytes accessed | tf_op | source)
XLA Modules:
  0.0 18.9 jit_solution(11664013790838371112)
XLA Ops:
  0.6 0.0 copy-start
  0.6 0.7 %tables_kernel.1 = (bf16[128,128]{1,0:T(8,128)(2,1)S(1)}, bf16[128,128]{1,0:T(8,128)(2,1)S(1)}, bf16[256,256]{1,0:T(8,128)(2,1)S(1)}, bf16[256,256]{1,0:T(8,128)...) custom-call(), custom_call_target="tpu_custom_call" | custom-call | flops 1073741824 | tf_op jit(solution)/shard_map/tables_kernel/pallas_call | solution.py:403
  1.4 0.5 %copy-done = bf16[18,128,256]{2,1,0:T(8,128)(2,1)S(1)} copy-done((bf16[18,128,256]{2,1,0:T(8,128)(2,1)S(1)}, bf16[18,128,256]{2,1,0:T(8,128)(2,1)}, u32[]{:S(2)}) %copy-start) | copy-done | bytes 1179672
  1.9 0.5 %pack_kernel.1 = (bf16[18,128,256]{2,1,0:T(8,128)(2,1)S(1)}, bf16[3,128,128]{2,1,0:T(8,128)(2,1)S(1)}, bf16[3,128,128]{2,1,0:T(8,128)(2,1)S(1)}) custom-call(bf16[18,128,256]{2,1,0:T(8,128)(2,1)S(1)} %copy-done, bf16[256,256]{1,0:T(8,128)(2,1)S(1)} %get-tuple-element.30.pick_ref), custom_call_target="tpu_custom_call" | custom-call | tf_op jit(solution)/shard_map/pack_kernel/pallas_call | solution.py:403
  2.4 0.5 %collective-permute-start = (bf16[3,128,128]{2,1,0:T(8,128)(2,1)S(1)}, bf16[3,128,128]{2,1,0:T(8,128)(2,1)S(1)}, u32[]{:S(2)}, u32[]{:S(2)}) collective-permute-start(bf16[3,128,128]{2,1,0:T(8,128)(2,1)S(1)} %get-tuple-element.33), channel_id=1, source_target_pairs={{0,1},{1,0},{2,3},{3,2},{4,5},{5,4},{6,7},{7,6},{8,9},{9,8},{10,11... | collective-permute-start | bytes 294920 | tf_op jit(solution)/shard_map/ppermute | solution.py:447
  2.9 0.7 %lines_kernel.1 = (bf16[4,6,6,16,256]{4,3,2,1,0:T(8,128)(2,1)S(1)}, f32[2,6,16,16,256]{4,3,2,1,0:T(8,128)S(1)}) custom-call(bf16[18,128,256]{2,1,0:T(8,128)(2,1)S(1)} %get-tuple-element.31.vol_ref.refs_0_, bf16[128,128]{1,0:T(8,128)(2,1)S(1)} %get-tuple-element.34.lines_ref, f32[3,8,128]{2,1,0:T(8,128)S(1)} %get-tuple-element.35.mask_ref.refs_10_), custom_call_target="tpu_custom_call" | custom-call | flops 268435456 | tf_op jit(solution)/shard_map/lines_kernel/pallas_call | solution.py:403
  3.6 0.2 %collective-permute-done.side_ref = bf16[3,128,128]{2,1,0:T(8,128)(2,1)S(1)} collective-permute-done((bf16[3,128,128]{2,1,0:T(8,128)(2,1)S(1)}, bf16[3,128,128]{2,1,0:T(8,128)(2,1)S(1)}, u32[]{:S(2)}, u32[]{:S(2)}) %collective-permute-start) | collective-permute-done | bytes 98336 | tf_op jit(solution)/shard_map/ppermute | solution.py:447
  3.9 0.1 rows_kernel.1
  4.0 0.7 %collective-permute-start.1 = (bf16[208,256]{1,0:T(8,128)(2,1)S(1)}, bf16[208,256]{1,0:T(8,128)(2,1)S(1)}, u32[]{:S(2)}, u32[]{:S(2)}) collective-permute-start(bf16[208,256]{1,0:T(8,128)(2,1)S(1)} %get-tuple-element.38), channel_id=1, source_target_pairs={{2,4},{6,8},{10,12},{4,2},{8,6},{12,10},{0,0},{14,14},{3,5},{7,9},... | collective-permute-start | bytes 319496 | tf_op jit(solution)/shard_map/ppermute | solution.py:469
  4.7 5.7 %collective-permute-start.2 = (bf16[208,256]{1,0:T(8,128)(2,1)S(1)}, bf16[208,256]{1,0:T(8,128)(2,1)S(1)}, u32[]{:S(2)}, u32[]{:S(2)}) collective-permute-start(bf16[208,256]{1,0:T(8,128)(2,1)S(1)} %get-tuple-element.48), channel_id=1, source_target_pairs={{0,2},{2,0},{4,6},{6,4},{8,10},{10,8},{12,14},{14,12},{1,3},{3,1},... | collective-permute-start | bytes 319496 | tf_op jit(solution)/shard_map/ppermute | solution.py:470
  10.4 5.0 %own_kernel.1 = (f32[2,6,16,16,256]{4,3,2,1,0:T(8,128)S(1)}, f32[16,128,256]{2,1,0:T(8,128)}, f32[16,128,256]{2,1,0:T(8,128)}, f32[16,128,256]{2,1,0:T(8,128)}, ...) custom-call(bf16[18,128,256]{2,1,0:T(8,128)(2,1)S(1)} %get-tuple-element.31.vol_ref.r, ...), custom_call_target="tpu_custom_call", output_to_operand_aliasing={{0}: (9, {})} | custom-call | flops 5368709120 | tf_op jit(solution)/shard_map/own_kernel/pallas_call | solution.py:403
  15.4 0.0 collective-permute-done.2.refs_2_
  15.4 1.5 %near_end_kernel.1 = (f32[16,128,256]{2,1,0:T(8,128)}, f32[16,128,256]{2,1,0:T(8,128)}, f32[16,128,256]{2,1,0:T(8,128)}, f32[3,16,16,256]{3,2,1,0:T(8,128)S(1)}) custom-call(bf16[18,128,256]{2,1,0:T(8,128)(2,1)S(1)} %get-tuple-element.31.vol_ref.refs_0_, ...), custom_call_target="tpu_custom_call", output_to_operand_aliasing={{0}: (12, {}), {1}: (13, {}), {2}: (14, {})} | custom-call | flops 1073741824 | tf_op jit(solution)/shard_map/near_end_kernel/pallas_call | solution.py:403
  16.9 0.0 collective-permute-done.1.refs_2_
  16.9 1.9 %far_end_kernel.1 = (f32[16,128,256]{2,1,0:T(8,128)}, f32[16,128,256]{2,1,0:T(8,128)}, f32[16,128,256]{2,1,0:T(8,128)}) custom-call(bf16[18,128,256]{2,1,0:T(8,128)(2,1)S(1)} %get-tuple-element.31.vol_ref.refs_0_, bf16[128,384]{1,0:T(8,128)(2,1)S(1)} %get-tuple-element.37.halo_ref.refs_1_, ...), custom_call_target="tpu_custom_call", output_to_operand_aliasing={{0}: (12, {}), {1}: (13, {}), {2}: (14, {})} | custom-call | flops 1073741824 | tf_op jit(solution)/shard_map/far_end_kernel/pallas_call | solution.py:403
Async XLA Ops:
  0.6 1.3 %copy-start = (bf16[18,128,256]{2,1,0:T(8,128)(2,1)S(1)}, bf16[18,128,256]{2,1,0:T(8,128)(2,1)}, u32[]{:S(2)}) copy-start(bf16[18,128,256]{2,1,0:T(8,128)(2,1)} %vol_ref.1) | copy-start | bytes 3538948
  2.4 1.5 %collective-permute-start = (bf16[3,128,128]{2,1,0:T(8,128)(2,1)S(1)}, bf16[3,128,128]{2,1,0:T(8,128)(2,1)S(1)}, u32[]{:S(2)}, u32[]{:S(2)}) collective-permute-start(bf16[3,128,128]{2,1,0:T(8,128)(2,1)S(1)} %get-tuple-element.33), channel_id=1, source_target_pairs={{0,1},{1,0},{2,3},{3,2},{4,5},{5,4},{6,7},{7,6},{8,9},{9,8},{10,11... | collective-permute-start | bytes 294920 | tf_op jit(solution)/shard_map/ppermute | solution.py:447
  4.0 12.9 %collective-permute-start.1 = (bf16[208,256]{1,0:T(8,128)(2,1)S(1)}, bf16[208,256]{1,0:T(8,128)(2,1)S(1)}, u32[]{:S(2)}, u32[]{:S(2)}) collective-permute-start(bf16[208,256]{1,0:T(8,128)(2,1)S(1)} %get-tuple-element.38), channel_id=1, source_target_pairs={{2,4},{6,8},{10,12},{4,2},{8,6},{12,10},{0,0},{14,14},{3,5},{7,9},... | collective-permute-start | bytes 319496 | tf_op jit(solution)/shard_map/ppermute | solution.py:469
  4.7 10.7 %collective-permute-start.2 = (bf16[208,256]{1,0:T(8,128)(2,1)S(1)}, bf16[208,256]{1,0:T(8,128)(2,1)S(1)}, u32[]{:S(2)}, u32[]{:S(2)}) collective-permute-start(bf16[208,256]{1,0:T(8,128)(2,1)S(1)} %get-tuple-element.48), channel_id=1, source_target_pairs={{0,2},{2,0},{4,6},{6,4},{8,10},{10,8},{12,14},{14,12},{1,3},{3,1},... | collective-permute-start | bytes 319496 | tf_op jit(solution)/shard_map/ppermute | solution.py:470

commit v15 on v14

--- a/solution.py
+++ b/solution.py
@@ -465,9 +465,9 @@
         [vol, own, side, part],
         in_specs=[WHOLE] * 3 + [ANYWHERE],
     )
+    near_in = lax.ppermute(near, "il", [(i, i ^ 1) for i in range(il)])
     pairs = [(i, i + 1) for i in range(1, il - 1, 2)]
     far_in = lax.ppermute(far, "il", pairs + [(j, i) for i, j in pairs] + [(0, 0), (il - 1, il - 1)])
-    near_in = lax.ppermute(near, "il", [(i, i ^ 1) for i in range(il)])
 
     outs = [((count, rows, cols), f32)] * 3
     operands = [vol, lines, diff_i, smooth, halo, diff_h, pack_h, mask, inner, part]

time: 19 us -> 19 us (level)
  no operation moved by 1% of the time
where the time goes in v15:
time: 19 us; the launch traced here: 18.9 us
  Pallas kernels  10.5 us (55%)
  starting transfers between devices  6.88 us (36%)
  between operations  0.7 us (4%)
  local copies, waits for them, and re-layouts  0.52 us (3%)
  waiting for transfers between devices  0.25 us (1%)
    pallas_call x7, Pallas kernels, call(): pl.pallas_call(kernel, out_shape=tuple((jax.ShapeDtypeStruct(*out) for ou...  10.5 us
    ppermute x1, starting transfers between devices, body(): near_in = lax.ppermute(near, 'il', [(i, i ^ 1) for i in range(il)])  5.69 us
    ppermute x1, starting transfers between devices, body(): lax.ppermute(far, 'il', pairs + [(j, i) for i, j in pairs] + [(0, 0), (il...  0.67 us
    ppermute x1, starting transfers between devices, body(): side = lax.ppermute(send, 'xl', [(0, 1), (1, 0)])  0.52 us
    unnamed x2, local copies, waits for them, and re-layouts  0.52 us
  transfers between devices with their start and end apart: 3, of which 1 were waited for; matrix products, arithmetic and copies ran while one was open for 0% of the time, Pallas kernels for 38%

profile of v15, /device:TPU:0, one launch (start us, length us, event | category | flops | bytes accessed | tf_op | source)
XLA Modules:
  0.0 18.9 jit_solution(11664013790838371112)
XLA Ops:
  0.6 0.0 copy-start
  0.6 0.7 %tables_kernel.1 = (bf16[128,128]{1,0:T(8,128)(2,1)S(1)}, bf16[128,128]{1,0:T(8,128)(2,1)S(1)}, bf16[256,256]{1,0:T(8,128)(2,1)S(1)}, bf16[256,256]{1,0:T(8,128)...) custom-call(), custom_call_target="tpu_custom_call" | custom-call | flops 1073741824 | tf_op jit(solution)/shard_map/tables_kernel/pallas_call | solution.py:403
  1.4 0.5 %copy-done = bf16[18,128,256]{2,1,0:T(8,128)(2,1)S(1)} copy-done((bf16[18,128,256]{2,1,0:T(8,128)(2,1)S(1)}, bf16[18,128,256]{2,1,0:T(8,128)(2,1)}, u32[]{:S(2)}) %copy-start) | copy-done | bytes 1179672
  1.9 0.5 %pack_kernel.1 = (bf16[18,128,256]{2,1,0:T(8,128)(2,1)S(1)}, bf16[3,128,128]{2,1,0:T(8,128)(2,1)S(1)}, bf16[3,128,128]{2,1,0:T(8,128)(2,1)S(1)}) custom-call(bf16[18,128,256]{2,1,0:T(8,128)(2,1)S(1)} %copy-done, bf16[256,256]{1,0:T(8,128)(2,1)S(1)} %get-tuple-element.30.pick_ref), custom_call_target="tpu_custom_call" | custom-call | tf_op jit(solution)/shard_map/pack_kernel/pallas_call | solution.py:403
  2.4 0.5 %collective-permute-start = (bf16[3,128,128]{2,1,0:T(8,128)(2,1)S(1)}, bf16[3,128,128]{2,1,0:T(8,128)(2,1)S(1)}, u32[]{:S(2)}, u32[]{:S(2)}) collective-permute-start(bf16[3,128,128]{2,1,0:T(8,128)(2,1)S(1)} %get-tuple-element.33), channel_id=1, source_target_pairs={{0,1},{1,0},{2,3},{3,2},{4,5},{5,4},{6,7},{7,6},{8,9},{9,8},{10,11... | collective-permute-start | bytes 294920 | tf_op jit(solution)/shard_map/ppermute | solution.py:447
  2.9 0.7 %lines_kernel.1 = (bf16[4,6,6,16,256]{4,3,2,1,0:T(8,128)(2,1)S(1)}, f32[2,6,16,16,256]{4,3,2,1,0:T(8,128)S(1)}) custom-call(bf16[18,128,256]{2,1,0:T(8,128)(2,1)S(1)} %get-tuple-element.31.vol_ref.refs_0_, bf16[128,128]{1,0:T(8,128)(2,1)S(1)} %get-tuple-element.34.lines_ref, f32[3,8,128]{2,1,0:T(8,128)S(1)} %get-tuple-element.35.mask_ref.refs_10_), custom_call_target="tpu_custom_call" | custom-call | flops 268435456 | tf_op jit(solution)/shard_map/lines_kernel/pallas_call | solution.py:403
  3.6 0.2 %collective-permute-done.side_ref = bf16[3,128,128]{2,1,0:T(8,128)(2,1)S(1)} collective-permute-done((bf16[3,128,128]{2,1,0:T(8,128)(2,1)S(1)}, bf16[3,128,128]{2,1,0:T(8,128)(2,1)S(1)}, u32[]{:S(2)}, u32[]{:S(2)}) %collective-permute-start) | collective-permute-done | bytes 98336 | tf_op jit(solution)/shard_map/ppermute | solution.py:447
  3.9 0.1 rows_kernel.1
  4.0 0.7 %collective-permute-start.1 = (bf16[208,256]{1,0:T(8,128)(2,1)S(1)}, bf16[208,256]{1,0:T(8,128)(2,1)S(1)}, u32[]{:S(2)}, u32[]{:S(2)}) collective-permute-start(bf16[208,256]{1,0:T(8,128)(2,1)S(1)} %get-tuple-element.38), channel_id=1, source_target_pairs={{2,4},{6,8},{10,12},{4,2},{8,6},{12,10},{0,0},{14,14},{3,5},{7,9},... | collective-permute-start | bytes 319496 | tf_op jit(solution)/shard_map/ppermute | solution.py:470
  4.7 5.7 %collective-permute-start.2 = (bf16[208,256]{1,0:T(8,128)(2,1)S(1)}, bf16[208,256]{1,0:T(8,128)(2,1)S(1)}, u32[]{:S(2)}, u32[]{:S(2)}) collective-permute-start(bf16[208,256]{1,0:T(8,128)(2,1)S(1)} %get-tuple-element.48), channel_id=1, source_target_pairs={{0,2},{2,0},{4,6},{6,4},{8,10},{10,8},{12,14},{14,12},{1,3},{3,1},... | collective-permute-start | bytes 319496 | tf_op jit(solution)/shard_map/ppermute | solution.py:468
  10.4 5.0 %own_kernel.1 = (f32[2,6,16,16,256]{4,3,2,1,0:T(8,128)S(1)}, f32[16,128,256]{2,1,0:T(8,128)}, f32[16,128,256]{2,1,0:T(8,128)}, f32[16,128,256]{2,1,0:T(8,128)}, ...) custom-call(bf16[18,128,256]{2,1,0:T(8,128)(2,1)S(1)} %get-tuple-element.31.vol_ref.r, ...), custom_call_target="tpu_custom_call", output_to_operand_aliasing={{0}: (9, {})} | custom-call | flops 5368709120 | tf_op jit(solution)/shard_map/own_kernel/pallas_call | solution.py:403
  15.4 0.0 collective-permute-done.2.refs_2_
  15.4 1.5 %near_end_kernel.1 = (f32[16,128,256]{2,1,0:T(8,128)}, f32[16,128,256]{2,1,0:T(8,128)}, f32[16,128,256]{2,1,0:T(8,128)}, f32[3,16,16,256]{3,2,1,0:T(8,128)S(1)}) custom-call(bf16[18,128,256]{2,1,0:T(8,128)(2,1)S(1)} %get-tuple-element.31.vol_ref.refs_0_, ...), custom_call_target="tpu_custom_call", output_to_operand_aliasing={{0}: (12, {}), {1}: (13, {}), {2}: (14, {})} | custom-call | flops 1073741824 | tf_op jit(solution)/shard_map/near_end_kernel/pallas_call | solution.py:403
  16.9 0.0 collective-permute-done.1.refs_2_
  16.9 1.9 %far_end_kernel.1 = (f32[16,128,256]{2,1,0:T(8,128)}, f32[16,128,256]{2,1,0:T(8,128)}, f32[16,128,256]{2,1,0:T(8,128)}) custom-call(bf16[18,128,256]{2,1,0:T(8,128)(2,1)S(1)} %get-tuple-element.31.vol_ref.refs_0_, bf16[128,384]{1,0:T(8,128)(2,1)S(1)} %get-tuple-element.37.halo_ref.refs_1_, ...), custom_call_target="tpu_custom_call", output_to_operand_aliasing={{0}: (12, {}), {1}: (13, {}), {2}: (14, {})} | custom-call | flops 1073741824 | tf_op jit(solution)/shard_map/far_end_kernel/pallas_call | solution.py:403
Async XLA Ops:
  0.6 1.3 %copy-start = (bf16[18,128,256]{2,1,0:T(8,128)(2,1)S(1)}, bf16[18,128,256]{2,1,0:T(8,128)(2,1)}, u32[]{:S(2)}) copy-start(bf16[18,128,256]{2,1,0:T(8,128)(2,1)} %vol_ref.1) | copy-start | bytes 3538948
  2.4 1.5 %collective-permute-start = (bf16[3,128,128]{2,1,0:T(8,128)(2,1)S(1)}, bf16[3,128,128]{2,1,0:T(8,128)(2,1)S(1)}, u32[]{:S(2)}, u32[]{:S(2)}) collective-permute-start(bf16[3,128,128]{2,1,0:T(8,128)(2,1)S(1)} %get-tuple-element.33), channel_id=1, source_target_pairs={{0,1},{1,0},{2,3},{3,2},{4,5},{5,4},{6,7},{7,6},{8,9},{9,8},{10,11... | collective-permute-start | bytes 294920 | tf_op jit(solution)/shard_map/ppermute | solution.py:447
  4.0 12.9 %collective-permute-start.1 = (bf16[208,256]{1,0:T(8,128)(2,1)S(1)}, bf16[208,256]{1,0:T(8,128)(2,1)S(1)}, u32[]{:S(2)}, u32[]{:S(2)}) collective-permute-start(bf16[208,256]{1,0:T(8,128)(2,1)S(1)} %get-tuple-element.38), channel_id=1, source_target_pairs={{2,4},{6,8},{10,12},{4,2},{8,6},{12,10},{0,0},{14,14},{3,5},{7,9},... | collective-permute-start | bytes 319496 | tf_op jit(solution)/shard_map/ppermute | solution.py:470
  4.7 10.7 %collective-permute-start.2 = (bf16[208,256]{1,0:T(8,128)(2,1)S(1)}, bf16[208,256]{1,0:T(8,128)(2,1)S(1)}, u32[]{:S(2)}, u32[]{:S(2)}) collective-permute-start(bf16[208,256]{1,0:T(8,128)(2,1)S(1)} %get-tuple-element.48), channel_id=1, source_target_pairs={{0,2},{2,0},{4,6},{6,4},{8,10},{10,8},{12,14},{14,12},{1,3},{3,1},... | collective-permute-start | bytes 319496 | tf_op jit(solution)/shard_map/ppermute | solution.py:468

commit v16 on v11

--- a/solution.py
+++ b/solution.py
@@ -49,11 +49,6 @@
 
 def dot(left, right):
     return jnp.dot(left, right, preferred_element_type=jnp.float32)
-
-
-def reciprocal(value):
-    guess = pl.reciprocal(value, approx=True)
-    return guess * (2.0 - value * guess)
 
 
 def halo_plane(lane, tile, depths):
@@ -239,12 +234,11 @@
     lanes = (pl.multiple_of(128 * x, 128), pl.multiple_of(128 - 128 * x, 128))
     for half, lane in zip(halves, lanes):
         a, b, c, d, e, f = [half[EDGE * comp : EDGE * (comp + 1)] for comp in range(6)]
-        low = c + 1e-6
-        guess = pl.reciprocal(low, approx=True)
-        inverse = guess * (low * guess - 2.0)
+        low = -1e-6 - c
+        inverse = pl.reciprocal(low, approx=True)
         spread = (a - b) * (a - c) + (b - c) * (b - c) + 3.0 * (d * d + e * e + f * f)
         root = spread * lax.rsqrt(jnp.maximum(spread, TINY))
-        store(pl.ds(lane, 128), (e * inverse, f * inverse, root * reciprocal(a + b + low)))
+        store(pl.ds(lane, 128), (e * inverse, f * inverse, root * pl.reciprocal(a + b - low, approx=True)))
 
 
 def border_of(packed, slot, mask_ref):
@@ -327,9 +321,9 @@
     last = exchange == 1
     targets, refs = refs[3:6], refs[6:]
     if last:
-        packed_ref, block_ref, block_h_ref, border_ref, edge_ref, tensor_ref, out_ref, done_sems, sems = refs
+        packed_ref, block_ref, block_h_ref, border_ref, edge_ref, out_ref, done_sems, sems = refs
     else:
-        out_ref, packed_ref, block_ref, block_h_ref, border_ref, edge_ref, tensor_ref, done_sems = refs
+        out_ref, packed_ref, block_ref, block_h_ref, border_ref, edge_ref, done_sems = refs
     depths, rows, cols = vol_ref.shape
     count, half = depths - 2, (depths - 2) // 2
     bf16, f32 = jnp.bfloat16, jnp.float32
@@ -392,13 +386,13 @@
         summed = part_ref[end, comp, first : first + half] + outer.reshape(half, EDGE, cols)
         edge_ref[first : first + half, comp] = summed.astype(bf16)
 
-    def finish(group, k):
+    def finish(group, k, tensor):
         def store(lanes, values):
             for n, value in enumerate(values):
                 out_ref[n, half * group + k, :, lanes] = value
 
         border = border_of(border_ref[:, 128 * group : 128 * (group + 1)], k, mask_ref)
-        attributes(tensor_ref[group, 6 * EDGE * k : 6 * EDGE * (k + 1)], border, store)
+        attributes(tensor, border, store)
 
     def send(group):
         depth = pl.ds(half * group, half)
@@ -407,21 +401,15 @@
             copy.start()
             copies.append(copy)
 
-    for comp, term in enumerate(make_block_moments(0)):
-        make_edge(0, comp, term)
-    later = make_block_moments(1)
-    tensor_of(edge_ref[:half], smooth_ref, tensor_ref.at[0])
-    for k in range(half):
-        if k < 6:
-            make_edge(1, k, later[k])
-        finish(0, k)
-    if last:
-        send(0)
-    tensor_of(edge_ref[half:], smooth_ref, tensor_ref.at[1])
-    for k in range(half):
-        finish(1, k)
-    if last:
-        send(1)
+    for group in range(2):
+        for comp, term in enumerate(make_block_moments(group)):
+            make_edge(group, comp, term)
+    for group in range(2):
+        tensor = dot(edge_ref[half * group : half * (group + 1)].reshape(6 * span, cols), smooth_ref[...])
+        for k in range(half):
+            finish(group, k, tensor[6 * EDGE * k : 6 * EDGE * (k + 1)])
+        if last:
+            send(group)
     for copy in finished + copies:
         copy.wait()
 
@@ -486,9 +474,9 @@
         in_specs=[WHOLE] * 3 + [ANYWHERE],
     )
     swap = [(i, i ^ 1) for i in range(il)]
-    onward = [(i, i + 2) for i in range(0, il - 2, 2)] + [(il - 2, il - 1)]
-    onward += [(i, i - 2) for i in range(3, il, 2)] + [(1, 0)]
-    far_in = lax.ppermute(far, "il", swap)
+    ring = [(i, i - 2) for i in range(2, il, 2)] + [(0, 1)]
+    ring += [(i, i + 2) for i in range(1, il - 2, 2)] + [(il - 1, il - 2)]
+    far_in = lax.ppermute(far, "il", ring)
     near_in = lax.ppermute(near, "il", swap)
 
     outs = [((count, rows, cols), f32)] * 3
@@ -508,7 +496,7 @@
         aliases={len(shared) + n: n for n in range(2)},
     )
     (relayed,) = call("relay_kernel", relay_kernel, [packed], [], [far_in, done], in_specs=[WHOLE, ANYWHERE])
-    relayed_in = lax.ppermute(relayed, "il", onward)
+    relayed_in = lax.ppermute(relayed, "il", swap)
     inner, part, *outs_in, done = call(
         "second_own_kernel",
         lambda *refs: own_kernel(1, *refs),
@@ -529,7 +517,6 @@
         pltpu.VMEM((EDGE, 128 * TILES), bf16),
         pltpu.VMEM((6 * EDGE, 256), f32),
         pltpu.VMEM((count, 6, EDGE, cols), bf16),
-        pltpu.VMEM((2, half * 6 * EDGE, cols), f32),
     ]
     sems = pltpu.SemaphoreType.DMA((3,))
     operands = [vol, halo, near_in, part, part_h, *tables, done]

time: 19.7 us -> 19 us (0.964)
  Pallas kernels: 12.3 us -> 11.5 us
    ppermute x1, starting transfers between devices: 0.08 us -> 1.58 us  [body(): near_in = lax.ppermute(near, 'il', swap)]
    ppermute x2, starting transfers between devices: 5.1 us -> 3.71 us  [the longest x1 2.92 us: body(): far_in = lax.ppermute(far, 'il', ring)]
    pallas_call x9, Pallas kernels: 12.3 us -> 11.5 us  [call(): pl.pallas_call(kernel, out_shape=tuple((jax.ShapeDtypeStruct(*out) for ou...]
  transfers between devices with their start and end apart: 4 -> 4, of which waited for: 1 -> 1; matrix products, arithmetic and copies ran while one was open for 0% -> 0% of each run, Pallas kernels for 45% -> 44%
where the time goes in v16:
time: 19 us; the launch traced here: 18.8 us
  Pallas kernels  11.5 us (61%)
  starting transfers between devices  5.81 us (31%)
  between operations  0.72 us (4%)
  local copies, waits for them, and re-layouts  0.52 us (3%)
  waiting for transfers between devices  0.26 us (1%)
    pallas_call x9, Pallas kernels, call(): pl.pallas_call(kernel, out_shape=tuple((jax.ShapeDtypeStruct(*out) for ou...  11.5 us
    ppermute x1, starting transfers between devices, body(): far_in = lax.ppermute(far, 'il', ring)  2.92 us
    ppermute x1, starting transfers between devices, body(): near_in = lax.ppermute(near, 'il', swap)  1.58 us
    ppermute x1, starting transfers between devices, body(): relayed_in = lax.ppermute(relayed, 'il', swap)  0.79 us
    ppermute x1, starting transfers between devices, body(): side = lax.ppermute(send, 'xl', [(0, 1), (1, 0)])  0.52 us
    unnamed x2, local copies, waits for them, and re-layouts  0.52 us
  transfers between devices with their start and end apart: 4, of which 1 were waited for; matrix products, arithmetic and copies ran while one was open for 0% of the time, Pallas kernels for 44%

profile of v16, /device:TPU:0, one launch (start us, length us, event | category | flops | bytes accessed | tf_op | source)
XLA Modules:
  0.0 18.8 jit_solution(14869613307306962899)
XLA Ops:
  0.6 0.0 copy-start
  0.6 0.7 %tables_kernel.1 = (bf16[128,128]{1,0:T(8,128)(2,1)S(1)}, bf16[128,128]{1,0:T(8,128)(2,1)S(1)}, bf16[256,256]{1,0:T(8,128)(2,1)S(1)}, bf16[256,256]{1,0:T(8,128)...) custom-call(), custom_call_target="tpu_custom_call" | custom-call | flops 1073741824 | tf_op jit(solution)/shard_map/tables_kernel/pallas_call | solution.py:418
  1.4 0.5 %copy-done = bf16[18,128,256]{2,1,0:T(8,128)(2,1)S(1)} copy-done((bf16[18,128,256]{2,1,0:T(8,128)(2,1)S(1)}, bf16[18,128,256]{2,1,0:T(8,128)(2,1)}, u32[]{:S(2)}) %copy-start) | copy-done | bytes 1179672
  1.9 0.5 %pack_kernel.1 = (bf16[18,128,256]{2,1,0:T(8,128)(2,1)S(1)}, bf16[3,128,128]{2,1,0:T(8,128)(2,1)S(1)}, bf16[3,128,128]{2,1,0:T(8,128)(2,1)S(1)}) custom-call(bf16[18,128,256]{2,1,0:T(8,128)(2,1)S(1)} %copy-done, bf16[256,256]{1,0:T(8,128)(2,1)S(1)} %get-tuple-element.37.pick_ref), custom_call_target="tpu_custom_call" | custom-call | tf_op jit(solution)/shard_map/pack_kernel/pallas_call | solution.py:418
  2.4 0.5 %collective-permute-start = (bf16[3,128,128]{2,1,0:T(8,128)(2,1)S(1)}, bf16[3,128,128]{2,1,0:T(8,128)(2,1)S(1)}, u32[]{:S(2)}, u32[]{:S(2)}) collective-permute-start(bf16[3,128,128]{2,1,0:T(8,128)(2,1)S(1)} %get-tuple-element.40), channel_id=1, source_target_pairs={{0,1},{1,0},{2,3},{3,2},{4,5},{5,4},{6,7},{7,6},{8,9},{9,8},{10,11... | collective-permute-start | bytes 294920 | tf_op jit(solution)/shard_map/ppermute | solution.py:462
  2.9 0.7 %lines_kernel.1 = (bf16[16,6,6,16,256]{4,3,2,1,0:T(8,128)(2,1)S(1)}, f32[2,6,16,16,256]{4,3,2,1,0:T(8,128)S(1)}) custom-call(bf16[18,128,256]{2,1,0:T(8,128)(2,1)S(1)} %get-tuple-element.38.vol_ref.refs_0_, bf16[128,128]{1,0:T(8,128)(2,1)S(1)} %get-tuple-element.41.lines_ref.refs_1_, f32[3,8,128]{2,1,0:T(8,128)S(1)} %get-tuple-element.42.mask_ref.refs_7_.refs_10_), custom_call_target="tpu_custom_call" | custom-call | flops 268435456 | tf_op jit(solution)/shard_map/lines_kernel/pallas_call | solution.py:418
  3.6 0.2 %collective-permute-done.side_ref = bf16[3,128,128]{2,1,0:T(8,128)(2,1)S(1)} collective-permute-done((bf16[3,128,128]{2,1,0:T(8,128)(2,1)S(1)}, bf16[3,128,128]{2,1,0:T(8,128)(2,1)S(1)}, u32[]{:S(2)}, u32[]{:S(2)}) %collective-permute-start) | collective-permute-done | bytes 98336 | tf_op jit(solution)/shard_map/ppermute | solution.py:462
  3.9 0.1 rows_kernel.1
  4.0 2.9 %collective-permute-start.1 = (bf16[208,256]{1,0:T(8,128)(2,1)S(1)}, bf16[208,256]{1,0:T(8,128)(2,1)S(1)}, u32[]{:S(2)}, u32[]{:S(2)}) collective-permute-start(bf16[208,256]{1,0:T(8,128)(2,1)S(1)} %get-tuple-element.45), channel_id=1, source_target_pairs={{4,0},{8,4},{12,8},{0,2},{2,6},{6,10},{10,14},{14,12},{5,1},{9,5},... | collective-permute-start | bytes 319496 | tf_op jit(solution)/shard_map/ppermute | solution.py:479
  7.0 1.6 %collective-permute-start.3 = (bf16[208,256]{1,0:T(8,128)(2,1)S(1)}, bf16[208,256]{1,0:T(8,128)(2,1)S(1)}, u32[]{:S(2)}, u32[]{:S(2)}) collective-permute-start(bf16[208,256]{1,0:T(8,128)(2,1)S(1)} %get-tuple-element.62), channel_id=1, source_target_pairs={{0,2},{2,0},{4,6},{6,4},{8,10},{10,8},{12,14},{14,12},{1,3},{3,1},... | collective-permute-start | bytes 319496 | tf_op jit(solution)/shard_map/ppermute | solution.py:480
  8.5 3.5 %first_own_kernel.1 = (bf16[16,6,6,16,256]{4,3,2,1,0:T(8,128)(2,1)S(1)}, f32[2,6,16,16,256]{4,3,2,1,0:T(8,128)S(1)}, f32[16,128,256]{2,1,0:T(8,128)}, f32[16,128...) custom-call(bf16[18,128,256]{2,1,0:T(8,128)(2,1)S(1)} %get-tuple-ele, ...), custom_call_target="tpu_custom_call", output_to_operand_aliasing={{0}: (8, {}), {1}: (9, {})} | custom-call | flops 3221225472 | tf_op jit(solution)/shard_map/first_own_kernel/pallas_call | solution.py:418
  12.0 0.0 collective-permute-done.1.rows_ref
  12.1 0.8 %collective-permute-start.2 = (bf16[208,256]{1,0:T(8,128)(2,1)S(1)}, bf16[208,256]{1,0:T(8,128)(2,1)S(1)}, u32[]{:S(2)}, u32[]{:S(2)}) collective-permute-start(bf16[208,256]{1,0:T(8,128)(2,1)S(1)} %relay_kernel.1), channel_id=1, source_target_pairs={{0,2},{2,0},{4,6},{6,4},{8,10},{10,8},{12,14},{14,12},{1,3},{3,1},... | collective-permute-start | bytes 319496 | tf_op jit(solution)/shard_map/ppermute | solution.py:499
  12.8 2.5 %second_own_kernel.1 = (bf16[16,6,6,16,256]{4,3,2,1,0:T(8,128)(2,1)S(1)}, f32[2,6,16,16,256]{4,3,2,1,0:T(8,128)S(1)}, f32[16,128,256]{2,1,0:T(8,128)}, f32[16,12...) custom-call(bf16[18,128,256]{2,1,0:T(8,128)(2,1)S(1)} %get-tuple-ele, ...), custom_call_target="tpu_custom_call", output_to_operand_aliasing={{0}: (8, {}), {1}: (9, {}), {2}: (12, {}), {3}: (13, {}), {... | custom-call | flops 3221225472 | tf_op jit(solution)/shard_map/second_own_kernel/pallas_call | solution.py:418
  15.4 0.0 collective-permute-done.3.refs_2_
  15.4 1.5 %near_end_kernel.1 = (f32[16,128,256]{2,1,0:T(8,128)}, f32[16,128,256]{2,1,0:T(8,128)}, f32[16,128,256]{2,1,0:T(8,128)}, f32[3,16,16,256]{3,2,1,0:T(8,128)S(1)}) custom-call(bf16[18,128,256]{2,1,0:T(8,128)(2,1)S(1)} %get-tuple-element.38.vol_ref.refs_0_, ...), custom_call_target="tpu_custom_call", output_to_operand_aliasing={{0}: (12, {}), {1}: (13, {}), {2}: (14, {})} | custom-call | flops 1073741824 | tf_op jit(solution)/shard_map/near_end_kernel/pallas_call | solution.py:418
  16.9 0.0 collective-permute-done.2.refs_2_
  16.9 1.9 %far_end_kernel.1 = (f32[16,128,256]{2,1,0:T(8,128)}, f32[16,128,256]{2,1,0:T(8,128)}, f32[16,128,256]{2,1,0:T(8,128)}) custom-call(bf16[18,128,256]{2,1,0:T(8,128)(2,1)S(1)} %get-tuple-element.38.vol_ref.refs_0_, bf16[128,384]{1,0:T(8,128)(2,1)S(1)} %get-tuple-element.44.refs_4_.refs_1_, ...), custom_call_target="tpu_custom_call", output_to_operand_aliasing={{0}: (12, {}), {1}: (13, {}), {2}: (14, {})} | custom-call | flops 1073741824 | tf_op jit(solution)/shard_map/far_end_kernel/pallas_call | solution.py:418
  (1 shorter events, 0.0 us)
Async XLA Ops:
  0.6 1.3 %copy-start = (bf16[18,128,256]{2,1,0:T(8,128)(2,1)S(1)}, bf16[18,128,256]{2,1,0:T(8,128)(2,1)}, u32[]{:S(2)}) copy-start(bf16[18,128,256]{2,1,0:T(8,128)(2,1)} %vol_ref.1) | copy-start | bytes 3538948
  2.4 1.5 %collective-permute-start = (bf16[3,128,128]{2,1,0:T(8,128)(2,1)S(1)}, bf16[3,128,128]{2,1,0:T(8,128)(2,1)S(1)}, u32[]{:S(2)}, u32[]{:S(2)}) collective-permute-start(bf16[3,128,128]{2,1,0:T(8,128)(2,1)S(1)} %get-tuple-element.40), channel_id=1, source_target_pairs={{0,1},{1,0},{2,3},{3,2},{4,5},{5,4},{6,7},{7,6},{8,9},{9,8},{10,11... | collective-permute-start | bytes 294920 | tf_op jit(solution)/shard_map/ppermute | solution.py:462
  4.0 8.0 %collective-permute-start.1 = (bf16[208,256]{1,0:T(8,128)(2,1)S(1)}, bf16[208,256]{1,0:T(8,128)(2,1)S(1)}, u32[]{:S(2)}, u32[]{:S(2)}) collective-permute-start(bf16[208,256]{1,0:T(8,128)(2,1)S(1)} %get-tuple-element.45), channel_id=1, source_target_pairs={{4,0},{8,4},{12,8},{0,2},{2,6},{6,10},{10,14},{14,12},{5,1},{9,5},... | collective-permute-start | bytes 319496 | tf_op jit(solution)/shard_map/ppermute | solution.py:479
  7.0 8.4 %collective-permute-start.3 = (bf16[208,256]{1,0:T(8,128)(2,1)S(1)}, bf16[208,256]{1,0:T(8,128)(2,1)S(1)}, u32[]{:S(2)}, u32[]{:S(2)}) collective-permute-start(bf16[208,256]{1,0:T(8,128)(2,1)S(1)} %get-tuple-element.62), channel_id=1, source_target_pairs={{0,2},{2,0},{4,6},{6,4},{8,10},{10,8},{12,14},{14,12},{1,3},{3,1},... | collective-permute-start | bytes 319496 | tf_op jit(solution)/shard_map/ppermute | solution.py:480
  12.1 4.8 %collective-permute-start.2 = (bf16[208,256]{1,0:T(8,128)(2,1)S(1)}, bf16[208,256]{1,0:T(8,128)(2,1)S(1)}, u32[]{:S(2)}, u32[]{:S(2)}) collective-permute-start(bf16[208,256]{1,0:T(8,128)(2,1)S(1)} %relay_kernel.1), channel_id=1, source_target_pairs={{0,2},{2,0},{4,6},{6,4},{8,10},{10,8},{12,14},{14,12},{1,3},{3,1},... | collective-permute-start | bytes 319496 | tf_op jit(solution)/shard_map/ppermute | solution.py:499

commit v17 on v15

--- a/solution.py
+++ b/solution.py
@@ -300,8 +300,8 @@
 
 
 def end_kernel(
-    exchange, vol_ref, halo_ref, rows_ref, part_ref, part_h_ref,
-    smooth_ref, pack_h_ref, diff_h_ref, lines_e_ref, diff_e_ref, mask_ref, done_ref, *refs,
+    exchange, done_ref, vol_ref, halo_ref, rows_ref, part_ref, part_h_ref,
+    smooth_ref, pack_h_ref, diff_h_ref, lines_e_ref, diff_e_ref, mask_ref, *refs,
 ):
     last = exchange == 1
     targets, refs = refs[3:6], refs[6:]
@@ -500,7 +500,7 @@
         pltpu.VMEM((count, 6, EDGE, cols), bf16),
     ]
     sems = pltpu.SemaphoreType.DMA((3,))
-    operands = [vol, halo, near_in, part, part_h, *tables, done]
+    operands = [done, vol, halo, near_in, part, part_h, *tables]
     *outs_in, done = call(
         "near_end_kernel",
         lambda *refs: end_kernel(0, *refs),
@@ -512,7 +512,7 @@
         flops=work,
         aliases={len(operands) + n: n for n in range(3)},
     )
-    operands = [vol, halo, far_in, part, part_h, *tables, done]
+    operands = [done, vol, halo, far_in, part, part_h, *tables]
     return call(
         "far_end_kernel",
         lambda *refs: end_kernel(1, *refs),

time: 19 us -> 17.6 us (0.926)
  the two profiles are of different devices: /device:TPU:0 before, /device:TPU:6 now
where the time goes in v17:
time: 17.6 us; the launch traced here: 17.4 us
  Pallas kernels  10.5 us (60%)
  starting transfers between devices  5.07 us (29%)
  between operations  0.71 us (4%)
  waiting for transfers between devices  0.59 us (3%)
  local copies, waits for them, and re-layouts  0.52 us (3%)
    pallas_call x7, Pallas kernels, call(): pl.pallas_call(kernel, out_shape=tuple((jax.ShapeDtypeStruct(*out) for ou...  10.5 us
    ppermute x1, starting transfers between devices, body(): lax.ppermute(far, 'il', pairs + [(j, i) for i, j in pairs] + [(0, 0), (il...  4.43 us
    ppermute x1, waiting for transfers between devices, body(): side = lax.ppermute(send, 'xl', [(0, 1), (1, 0)])  0.59 us
    ppermute x1, starting transfers between devices, body(): near_in = lax.ppermute(near, 'il', [(i, i ^ 1) for i in range(il)])  0.57 us
    unnamed x2, local copies, waits for them, and re-layouts  0.52 us
  transfers between devices with their start and end apart: 3, of which 1 were waited for; matrix products, arithmetic and copies ran while one was open for 0% of the time, Pallas kernels for 41%

profile of v17, /device:TPU:6, one launch (start us, length us, event | category | flops | bytes accessed | tf_op | source)
XLA Modules:
  0.0 17.4 jit_solution(6312012271834698001)
XLA Ops:
  0.6 0.0 copy-start
  0.6 0.7 %tables_kernel.1 = (bf16[128,128]{1,0:T(8,128)(2,1)S(1)}, bf16[128,128]{1,0:T(8,128)(2,1)S(1)}, bf16[256,256]{1,0:T(8,128)(2,1)S(1)}, bf16[256,256]{1,0:T(8,128)...) custom-call(), custom_call_target="tpu_custom_call" | custom-call | flops 1073741824 | tf_op jit(solution)/shard_map/tables_kernel/pallas_call | solution.py:403
  1.4 0.5 %copy-done = bf16[18,128,256]{2,1,0:T(8,128)(2,1)S(1)} copy-done((bf16[18,128,256]{2,1,0:T(8,128)(2,1)S(1)}, bf16[18,128,256]{2,1,0:T(8,128)(2,1)}, u32[]{:S(2)}) %copy-start) | copy-done | bytes 1179672
  1.9 0.5 %pack_kernel.1 = (bf16[18,128,256]{2,1,0:T(8,128)(2,1)S(1)}, bf16[3,128,128]{2,1,0:T(8,128)(2,1)S(1)}, bf16[3,128,128]{2,1,0:T(8,128)(2,1)S(1)}) custom-call(bf16[18,128,256]{2,1,0:T(8,128)(2,1)S(1)} %copy-done, bf16[256,256]{1,0:T(8,128)(2,1)S(1)} %get-tuple-element.30.pick_ref), custom_call_target="tpu_custom_call" | custom-call | tf_op jit(solution)/shard_map/pack_kernel/pallas_call | solution.py:403
  2.4 0.1 collective-permute-start
  2.5 0.7 %lines_kernel.1 = (bf16[4,6,6,16,256]{4,3,2,1,0:T(8,128)(2,1)S(1)}, f32[2,6,16,16,256]{4,3,2,1,0:T(8,128)S(1)}) custom-call(bf16[18,128,256]{2,1,0:T(8,128)(2,1)S(1)} %get-tuple-element.31.vol_ref.refs_1_, bf16[128,128]{1,0:T(8,128)(2,1)S(1)} %get-tuple-element.32.lines_ref, f32[3,8,128]{2,1,0:T(8,128)S(1)} %get-tuple-element.37.mask_ref.refs_11_), custom_call_target="tpu_custom_call" | custom-call | flops 268435456 | tf_op jit(solution)/shard_map/lines_kernel/pallas_call | solution.py:403
  3.2 0.6 %collective-permute-done.side_ref = bf16[3,128,128]{2,1,0:T(8,128)(2,1)S(1)} collective-permute-done((bf16[3,128,128]{2,1,0:T(8,128)(2,1)S(1)}, bf16[3,128,128]{2,1,0:T(8,128)(2,1)S(1)}, u32[]{:S(2)}, u32[]{:S(2)}) %collective-permute-start) | collective-permute-done | bytes 98336 | tf_op jit(solution)/shard_map/ppermute | solution.py:447
  3.8 0.1 rows_kernel.1
  3.9 0.6 %collective-permute-start.1 = (bf16[208,256]{1,0:T(8,128)(2,1)S(1)}, bf16[208,256]{1,0:T(8,128)(2,1)S(1)}, u32[]{:S(2)}, u32[]{:S(2)}) collective-permute-start(bf16[208,256]{1,0:T(8,128)(2,1)S(1)} %get-tuple-element.44), channel_id=1, source_target_pairs={{0,2},{2,0},{4,6},{6,4},{8,10},{10,8},{12,14},{14,12},{1,3},{3,1},... | collective-permute-start | bytes 319496 | tf_op jit(solution)/shard_map/ppermute | solution.py:468
  4.5 4.4 %collective-permute-start.2 = (bf16[208,256]{1,0:T(8,128)(2,1)S(1)}, bf16[208,256]{1,0:T(8,128)(2,1)S(1)}, u32[]{:S(2)}, u32[]{:S(2)}) collective-permute-start(bf16[208,256]{1,0:T(8,128)(2,1)S(1)} %get-tuple-element.53), channel_id=1, source_target_pairs={{2,4},{6,8},{10,12},{4,2},{8,6},{12,10},{0,0},{14,14},{3,5},{7,9},... | collective-permute-start | bytes 319496 | tf_op jit(solution)/shard_map/ppermute | solution.py:470
  8.9 5.0 %own_kernel.1 = (f32[2,6,16,16,256]{4,3,2,1,0:T(8,128)S(1)}, f32[16,128,256]{2,1,0:T(8,128)}, f32[16,128,256]{2,1,0:T(8,128)}, f32[16,128,256]{2,1,0:T(8,128)}, ...) custom-call(bf16[18,128,256]{2,1,0:T(8,128)(2,1)S(1)} %get-tuple-element.31.vol_ref.r, ...), custom_call_target="tpu_custom_call", output_to_operand_aliasing={{0}: (9, {})} | custom-call | flops 5368709120 | tf_op jit(solution)/shard_map/own_kernel/pallas_call | solution.py:403
  14.0 0.0 collective-permute-done.1.refs_3_
  14.0 1.5 %near_end_kernel.1 = (f32[16,128,256]{2,1,0:T(8,128)}, f32[16,128,256]{2,1,0:T(8,128)}, f32[16,128,256]{2,1,0:T(8,128)}, f32[3,16,16,256]{3,2,1,0:T(8,128)S(1)}) custom-call(f32[3,2,96,256]{3,2,1,0:T(8,128)S(1)} %get-tuple-element.43.refs_0_, ...), custom_call_target="tpu_custom_call", output_to_operand_aliasing={{0}: (12, {}), {1}: (13, {}), {2}: (14, {})} | custom-call | flops 1073741824 | tf_op jit(solution)/shard_map/near_end_kernel/pallas_call | solution.py:403
  15.5 0.0 collective-permute-done.2.refs_3_
  15.5 1.9 %far_end_kernel.1 = (f32[16,128,256]{2,1,0:T(8,128)}, f32[16,128,256]{2,1,0:T(8,128)}, f32[16,128,256]{2,1,0:T(8,128)}) custom-call(f32[3,16,16,256]{3,2,1,0:T(8,128)S(1)} %get-tuple-element.52.refs_0_, bf16[18,128,256]{2,1,0:T(8,128)(2,1)S(1)} %get-tuple-element.31.vol_ref.refs_1_, ...), custom_call_target="tpu_custom_call", output_to_operand_aliasing={{0}: (12, {}), {1}: (13, {}), {2}: (14, {})} | custom-call | flops 1073741824 | tf_op jit(solution)/shard_map/far_end_kernel/pallas_call | solution.py:403
Async XLA Ops:
  0.6 1.3 %copy-start = (bf16[18,128,256]{2,1,0:T(8,128)(2,1)S(1)}, bf16[18,128,256]{2,1,0:T(8,128)(2,1)}, u32[]{:S(2)}) copy-start(bf16[18,128,256]{2,1,0:T(8,128)(2,1)} %vol_ref.1) | copy-start | bytes 3538948
  2.4 1.4 %collective-permute-start = (bf16[3,128,128]{2,1,0:T(8,128)(2,1)S(1)}, bf16[3,128,128]{2,1,0:T(8,128)(2,1)S(1)}, u32[]{:S(2)}, u32[]{:S(2)}) collective-permute-start(bf16[3,128,128]{2,1,0:T(8,128)(2,1)S(1)} %get-tuple-element.36), channel_id=1, source_target_pairs={{0,1},{1,0},{2,3},{3,2},{4,5},{5,4},{6,7},{7,6},{8,9},{9,8},{10,11... | collective-permute-start | bytes 294920 | tf_op jit(solution)/shard_map/ppermute | solution.py:447
  3.9 10.0 %collective-permute-start.1 = (bf16[208,256]{1,0:T(8,128)(2,1)S(1)}, bf16[208,256]{1,0:T(8,128)(2,1)S(1)}, u32[]{:S(2)}, u32[]{:S(2)}) collective-permute-start(bf16[208,256]{1,0:T(8,128)(2,1)S(1)} %get-tuple-element.44), channel_id=1, source_target_pairs={{0,2},{2,0},{4,6},{6,4},{8,10},{10,8},{12,14},{14,12},{1,3},{3,1},... | collective-permute-start | bytes 319496 | tf_op jit(solution)/shard_map/ppermute | solution.py:468
  4.5 11.0 %collective-permute-start.2 = (bf16[208,256]{1,0:T(8,128)(2,1)S(1)}, bf16[208,256]{1,0:T(8,128)(2,1)S(1)}, u32[]{:S(2)}, u32[]{:S(2)}) collective-permute-start(bf16[208,256]{1,0:T(8,128)(2,1)S(1)} %get-tuple-element.53), channel_id=1, source_target_pairs={{2,4},{6,8},{10,12},{4,2},{8,6},{12,10},{0,0},{14,14},{3,5},{7,9},... | collective-permute-start | bytes 319496 | tf_op jit(solution)/shard_map/ppermute | solution.py:470

commit v18 on v17

--- a/solution.py
+++ b/solution.py
@@ -15,8 +15,8 @@
 EDGE = 16
 OWN = 2
 TINY = float(np.finfo(np.float32).tiny)
-HEAD = 2
-AHEAD = 2
+HEAD = 3
+AHEAD = 3
 FAR = -1000
 WHOLE = pl.BlockSpec(memory_space=pltpu.VMEM)
 IN_HBM = pl.BlockSpec(memory_space=pltpu.HBM)
@@ -111,13 +111,16 @@
             diff_h_ref[part, out : out + 128] = jnp.where(same, difference(plane, centre), 0.0).astype(bf16)
             diff_h_ref[part, 256 + out : 384 + out] = jnp.where(plane == centre, across, 0.0).astype(bf16)
 
-    source, lane = iota((cols, 256), 0), iota((cols, 256), 1)
+    source, lane = iota((128, 256), 0), iota((128, 256), 1)
     place = lax.rem(lane, SIDE)
     low, high = place < SIDE - OWN, place >= OWN
-    sent = jnp.where(x == 0, jnp.where(low, cols - (SIDE - OWN) + place, FAR), jnp.where(high, place - OWN, FAR))
+    sent = jnp.where(x == 0, jnp.where(low, 128 - (SIDE - OWN) + place, FAR), jnp.where(high, place - OWN, FAR))
     low, high = place < OWN, place >= SIDE - OWN
-    kept = jnp.where(x == 0, jnp.where(low, cols - OWN + place, FAR), jnp.where(high, place - (SIDE - OWN), FAR))
-    pick_ref[...] = jnp.where(source == jnp.where(lane < 128, sent, kept), 1.0, 0.0).astype(bf16)
+    kept = jnp.where(x == 0, jnp.where(low, 128 - OWN + place, FAR), jnp.where(high, place - (SIDE - OWN), FAR))
+    pick = jnp.where(source == jnp.where(lane < 128, sent, kept), 1.0, 0.0)
+    slot = lax.div(lax.rem(lane, 128), SIDE)
+    for index in range(SLOTS):
+        pick_ref[128 * index : 128 * (index + 1)] = jnp.where(slot == index, pick, 0.0).astype(bf16)
     lane = iota((8, 128), 1)
     border = jnp.where(x == 0, lane - (128 - SIDE), lane)
     mask_ref[0] = jnp.where((border >= 0) & (border < SIDE), 1.0, 0.0)
@@ -127,18 +130,12 @@
 
 def pack_kernel(vol_ref, pick_ref, copy_ref, send_ref, own_ref):
     depths, rows, cols = vol_ref.shape
-    slot = lax.div(lax.rem(iota((rows, 256), 1), 128), SIDE)
+    edge = pl.ds(pl.multiple_of((cols - 128) * (1 - lax.axis_index("xl")), 128), 128)
     copy_ref[...] = vol_ref[...]
-    picked = dot(vol_ref[...].reshape(depths * rows, cols), pick_ref[...])
     for tile in range(TILES):
-        if tile < 2:
-            planes = [(1 + SLOTS * tile + index, index) for index in range(SLOTS)]
-        else:
-            planes = [(0, 0), (depths - 1, 1)]
-        packed = jnp.zeros((rows, 256), jnp.float32)
-        for plane, index in planes:
-            packed = jnp.where(slot == index, picked[rows * plane : rows * (plane + 1)], packed)
-        packed = packed.astype(jnp.bfloat16)
+        planes = (0, depths - 1) if tile == 2 else range(1 + SLOTS * tile, 1 + SLOTS * (tile + 1))
+        beside = jnp.concatenate([vol_ref[plane, :, edge] for plane in planes], axis=1)
+        packed = dot(beside, pick_ref[: beside.shape[1]]).astype(jnp.bfloat16)
         send_ref[tile] = packed[:, :128]
         own_ref[tile] = packed[:, 128:]
 
@@ -326,23 +323,20 @@
     for copy in finished:
         copy.start()
 
-    packed_ref[:8] = jnp.zeros_like(packed_ref[:8])
+    rows_in = rows_ref[...].astype(f32)
     if last:
         il = lax.axis_index("il")
         outside = (low & (il == 0)) | (jnp.logical_not(low) & (il == lax.axis_size("il") - 1))
-        packed_ref[8:] = jnp.where(outside, 0.0, rows_ref[...].astype(f32))
-    else:
-        packed_ref[8:] = rows_ref[...].astype(f32)
+        rows_in = jnp.where(outside, 0.0, rows_in)
+    packed_ref[...] = pltpu.roll(rows_in, jnp.where(low, 0, EDGE - REACH), 0)
+    place = iota((EDGE, cols), 0)
+    received = jnp.where(low, place, EDGE - 1 - place) < REACH
 
     def joined(row, own):
         lanes = own.shape[1]
-        before = packed_ref[8 + row : 8 + row + EDGE, :lanes]
-        after = packed_ref[8 + row - (EDGE - REACH) : 8 + row + REACH, :lanes]
-        own = own.astype(f32)
-        place = iota(own.shape, 0)
-        first = jnp.where(place < REACH, before, pltpu.roll(own, REACH, 0))
-        second = jnp.where(place < EDGE - REACH, pltpu.roll(own, EDGE - REACH, 0), after)
-        return jnp.where(low, first, second).astype(bf16)
+        rows_in = packed_ref[row : row + EDGE, :lanes]
+        own = pltpu.roll(own.astype(f32), jnp.where(low, REACH, EDGE - REACH), 0)
+        return jnp.where(received[:, :lanes], rows_in, own).astype(bf16)
 
     for depth in range(depths):
         block_ref[depth] = joined(REACH * depth, vol_ref[depth, pl.ds(start, EDGE)])
@@ -435,7 +429,7 @@
             ((128 * TILES, 512), bf16),
             ((2, span, span), bf16),
             ((EDGE, EDGE), bf16),
-            ((cols, 256), bf16),
+            ((128 * SLOTS, 256), bf16),
             ((3, 8, 128), f32),
         ],
         [],
@@ -493,7 +487,7 @@
     end_rows = (3, count, EDGE, cols)
     tables = [smooth, pack_h, diff_h, lines_e, diff_e, mask]
     scratch = [
-        pltpu.VMEM((8 + packed_rows, cols), f32),
+        pltpu.VMEM((packed_rows, cols), f32),
         pltpu.VMEM((depths, EDGE, cols), bf16),
         pltpu.VMEM((EDGE, 128 * TILES), bf16),
         pltpu.VMEM((6 * EDGE, 256), f32),

time: 17.6 us -> 17.3 us (0.983)
  the two profiles are of different devices: /device:TPU:6 before, /device:TPU:4 now
where the time goes in v18:
time: 17.3 us; the launch traced here: 17.2 us
  Pallas kernels  10.6 us (61%)
  starting transfers between devices  5.06 us (29%)
  between operations  0.72 us (4%)
  local copies, waits for them, and re-layouts  0.48 us (3%)
  waiting for transfers between devices  0.34 us (2%)
    pallas_call x7, Pallas kernels, call(): pl.pallas_call(kernel, out_shape=tuple((jax.ShapeDtypeStruct(*out) for ou...  10.6 us
    ppermute x1, starting transfers between devices, body(): lax.ppermute(far, 'il', pairs + [(j, i) for i, j in pairs] + [(0, 0), (il...  4.92 us
    unnamed x2, local copies, waits for them, and re-layouts  0.48 us
  transfers between devices with their start and end apart: 3, of which 1 were waited for; matrix products, arithmetic and copies ran while one was open for 0% of the time, Pallas kernels for 42%

profile of v18, /device:TPU:4, one launch (start us, length us, event | category | flops | bytes accessed | tf_op | source)
XLA Modules:
  0.0 17.2 jit_solution(1816167672779447423)
XLA Ops:
  0.6 0.0 copy-start
  0.6 0.8 %tables_kernel.1 = (bf16[128,128]{1,0:T(8,128)(2,1)S(1)}, bf16[128,128]{1,0:T(8,128)(2,1)S(1)}, bf16[256,256]{1,0:T(8,128)(2,1)S(1)}, bf16[256,256]{1,0:T(8,128)...) custom-call(), custom_call_target="tpu_custom_call" | custom-call | flops 1073741824 | tf_op jit(solution)/shard_map/tables_kernel/pallas_call | solution.py:397
  1.4 0.5 %copy-done = bf16[18,128,256]{2,1,0:T(8,128)(2,1)S(1)} copy-done((bf16[18,128,256]{2,1,0:T(8,128)(2,1)S(1)}, bf16[18,128,256]{2,1,0:T(8,128)(2,1)}, u32[]{:S(2)}) %copy-start) | copy-done | bytes 1179672
  1.9 0.4 %pack_kernel.1 = (bf16[18,128,256]{2,1,0:T(8,128)(2,1)S(1)}, bf16[3,128,128]{2,1,0:T(8,128)(2,1)S(1)}, bf16[3,128,128]{2,1,0:T(8,128)(2,1)S(1)}) custom-call(bf16[18,128,256]{2,1,0:T(8,128)(2,1)S(1)} %copy-done, bf16[1024,256]{1,0:T(8,128)(2,1)S(1)} %get-tuple-element.30.pick_ref), custom_call_target="tpu_custom_call" | custom-call | tf_op jit(solution)/shard_map/pack_kernel/pallas_call | solution.py:397
  2.3 0.1 collective-permute-start
  2.4 0.9 %lines_kernel.1 = (bf16[6,6,6,16,256]{4,3,2,1,0:T(8,128)(2,1)S(1)}, f32[2,6,16,16,256]{4,3,2,1,0:T(8,128)S(1)}) custom-call(bf16[18,128,256]{2,1,0:T(8,128)(2,1)S(1)} %get-tuple-element.31.vol_ref.refs_1_, bf16[128,128]{1,0:T(8,128)(2,1)S(1)} %get-tuple-element.32.lines_ref, f32[3,8,128]{2,1,0:T(8,128)S(1)} %get-tuple-element.37.mask_ref.refs_11_), custom_call_target="tpu_custom_call" | custom-call | flops 268435456 | tf_op jit(solution)/shard_map/lines_kernel/pallas_call | solution.py:397
  3.3 0.3 %collective-permute-done.side_ref = bf16[3,128,128]{2,1,0:T(8,128)(2,1)S(1)} collective-permute-done((bf16[3,128,128]{2,1,0:T(8,128)(2,1)S(1)}, bf16[3,128,128]{2,1,0:T(8,128)(2,1)S(1)}, u32[]{:S(2)}, u32[]{:S(2)}) %collective-permute-start) | collective-permute-done | bytes 98336 | tf_op jit(solution)/shard_map/ppermute | solution.py:441
  3.7 0.1 rows_kernel.1
  3.8 0.1 collective-permute-start.1
  3.9 4.9 %collective-permute-start.2 = (bf16[208,256]{1,0:T(8,128)(2,1)S(1)}, bf16[208,256]{1,0:T(8,128)(2,1)S(1)}, u32[]{:S(2)}, u32[]{:S(2)}) collective-permute-start(bf16[208,256]{1,0:T(8,128)(2,1)S(1)} %get-tuple-element.53), channel_id=1, source_target_pairs={{2,4},{6,8},{10,12},{4,2},{8,6},{12,10},{0,0},{14,14},{3,5},{7,9},... | collective-permute-start | bytes 319496 | tf_op jit(solution)/shard_map/ppermute | solution.py:464
  8.8 4.8 %own_kernel.1 = (f32[2,6,16,16,256]{4,3,2,1,0:T(8,128)S(1)}, f32[16,128,256]{2,1,0:T(8,128)}, f32[16,128,256]{2,1,0:T(8,128)}, f32[16,128,256]{2,1,0:T(8,128)}, ...) custom-call(bf16[18,128,256]{2,1,0:T(8,128)(2,1)S(1)} %get-tuple-element.31.vol_ref.r, ...), custom_call_target="tpu_custom_call", output_to_operand_aliasing={{0}: (9, {})} | custom-call | flops 5368709120 | tf_op jit(solution)/shard_map/own_kernel/pallas_call | solution.py:397
  13.7 0.0 collective-permute-done.1.refs_3_
  13.7 1.5 %near_end_kernel.1 = (f32[16,128,256]{2,1,0:T(8,128)}, f32[16,128,256]{2,1,0:T(8,128)}, f32[16,128,256]{2,1,0:T(8,128)}, f32[3,16,16,256]{3,2,1,0:T(8,128)S(1)}) custom-call(f32[3,2,96,256]{3,2,1,0:T(8,128)S(1)} %get-tuple-element.43.refs_0_, ...), custom_call_target="tpu_custom_call", output_to_operand_aliasing={{0}: (12, {}), {1}: (13, {}), {2}: (14, {})} | custom-call | flops 1073741824 | tf_op jit(solution)/shard_map/near_end_kernel/pallas_call | solution.py:397
  15.2 0.0 collective-permute-done.2.refs_3_
  15.2 2.0 %far_end_kernel.1 = (f32[16,128,256]{2,1,0:T(8,128)}, f32[16,128,256]{2,1,0:T(8,128)}, f32[16,128,256]{2,1,0:T(8,128)}) custom-call(f32[3,16,16,256]{3,2,1,0:T(8,128)S(1)} %get-tuple-element.52.refs_0_, bf16[18,128,256]{2,1,0:T(8,128)(2,1)S(1)} %get-tuple-element.31.vol_ref.refs_1_, ...), custom_call_target="tpu_custom_call", output_to_operand_aliasing={{0}: (12, {}), {1}: (13, {}), {2}: (14, {})} | custom-call | flops 1073741824 | tf_op jit(solution)/shard_map/far_end_kernel/pallas_call | solution.py:397
Async XLA Ops:
  0.6 1.3 %copy-start = (bf16[18,128,256]{2,1,0:T(8,128)(2,1)S(1)}, bf16[18,128,256]{2,1,0:T(8,128)(2,1)}, u32[]{:S(2)}) copy-start(bf16[18,128,256]{2,1,0:T(8,128)(2,1)} %vol_ref.1) | copy-start | bytes 3538948
  2.3 1.4 %collective-permute-start = (bf16[3,128,128]{2,1,0:T(8,128)(2,1)S(1)}, bf16[3,128,128]{2,1,0:T(8,128)(2,1)S(1)}, u32[]{:S(2)}, u32[]{:S(2)}) collective-permute-start(bf16[3,128,128]{2,1,0:T(8,128)(2,1)S(1)} %get-tuple-element.36), channel_id=1, source_target_pairs={{0,1},{1,0},{2,3},{3,2},{4,5},{5,4},{6,7},{7,6},{8,9},{9,8},{10,11... | collective-permute-start | bytes 294920 | tf_op jit(solution)/shard_map/ppermute | solution.py:441
  3.8 9.8 %collective-permute-start.1 = (bf16[208,256]{1,0:T(8,128)(2,1)S(1)}, bf16[208,256]{1,0:T(8,128)(2,1)S(1)}, u32[]{:S(2)}, u32[]{:S(2)}) collective-permute-start(bf16[208,256]{1,0:T(8,128)(2,1)S(1)} %get-tuple-element.44), channel_id=1, source_target_pairs={{0,2},{2,0},{4,6},{6,4},{8,10},{10,8},{12,14},{14,12},{1,3},{3,1},... | collective-permute-start | bytes 319496 | tf_op jit(solution)/shard_map/ppermute | solution.py:462
  3.9 11.3 %collective-permute-start.2 = (bf16[208,256]{1,0:T(8,128)(2,1)S(1)}, bf16[208,256]{1,0:T(8,128)(2,1)S(1)}, u32[]{:S(2)}, u32[]{:S(2)}) collective-permute-start(bf16[208,256]{1,0:T(8,128)(2,1)S(1)} %get-tuple-element.53), channel_id=1, source_target_pairs={{2,4},{6,8},{10,12},{4,2},{8,6},{12,10},{0,0},{14,14},{3,5},{7,9},... | collective-permute-start | bytes 319496 | tf_op jit(solution)/shard_map/ppermute | solution.py:464

commit v19 on v18

--- a/solution.py
+++ b/solution.py
@@ -296,100 +296,91 @@
         copy.wait()
 
 
-def end_kernel(
-    exchange, done_ref, vol_ref, halo_ref, rows_ref, part_ref, part_h_ref,
-    smooth_ref, pack_h_ref, diff_h_ref, lines_e_ref, diff_e_ref, mask_ref, *refs,
+def ends_kernel(
+    done_ref, vol_ref, halo_ref, near_ref, far_ref, part_ref, part_h_ref,
+    smooth_ref, pack_h_ref, diff_h_ref, lines_e_ref, diff_e_ref, mask_ref, in_i_ref, in_x_ref, in_p_ref,
+    dip_i_ref, dip_x_ref, plan_ref,
+    packed_ref, block_ref, block_h_ref, border_ref, edge_ref, out_ref, done_sems, sems,
 ):
-    last = exchange == 1
-    targets, refs = refs[3:6], refs[6:]
-    if last:
-        packed_ref, block_ref, block_h_ref, border_ref, edge_ref, out_ref, done_sems, sems = refs
-    else:
-        out_ref, packed_ref, block_ref, block_h_ref, border_ref, edge_ref, done_sems = refs
     depths, rows, cols = vol_ref.shape
     count, half = depths - 2, (depths - 2) // 2
     bf16, f32 = jnp.bfloat16, jnp.float32
-    low = low_end(exchange)
-    end = jnp.where(low, 0, 1)
-    start = pl.multiple_of(jnp.where(low, 0, rows - EDGE), EDGE)
-    other = pl.multiple_of(jnp.where(low, rows - EDGE, 0), EDGE)
-    finished = []
+    span = EDGE * half
+    targets = (dip_i_ref, dip_x_ref, plan_ref)
+    copies = []
     for n, target in enumerate(targets):
-        if last:
-            place = target.at[:, pl.ds(other, EDGE)]
-        else:
-            place = target.at[pl.ds(count - 2, 2), pl.ds(EDGE, rows - 2 * EDGE)]
-        finished.append(pltpu.make_async_copy(done_ref.at[n], place, done_sems.at[n]))
-    for copy in finished:
-        copy.start()
-
-    rows_in = rows_ref[...].astype(f32)
-    if last:
-        il = lax.axis_index("il")
-        outside = (low & (il == 0)) | (jnp.logical_not(low) & (il == lax.axis_size("il") - 1))
-        rows_in = jnp.where(outside, 0.0, rows_in)
-    packed_ref[...] = pltpu.roll(rows_in, jnp.where(low, 0, EDGE - REACH), 0)
-    place = iota((EDGE, cols), 0)
-    received = jnp.where(low, place, EDGE - 1 - place) < REACH
-
-    def joined(row, own):
-        lanes = own.shape[1]
-        rows_in = packed_ref[row : row + EDGE, :lanes]
-        own = pltpu.roll(own.astype(f32), jnp.where(low, REACH, EDGE - REACH), 0)
-        return jnp.where(received[:, :lanes], rows_in, own).astype(bf16)
-
-    for depth in range(depths):
-        block_ref[depth] = joined(REACH * depth, vol_ref[depth, pl.ds(start, EDGE)])
-    own_h = halo_ref[pl.ds(start, EDGE)]
-    block_h_ref[:, :256] = joined(REACH * depths, own_h[:, :256])
-    block_h_ref[:, 256:] = joined(REACH * (depths + 1), own_h[:, 256:])
-
-    both = dot(block_h_ref[...], diff_h_ref[...])
-    grad_i = dot(diff_e_ref[...], block_h_ref[:, :256])
-    lined_h = []
-    for comp, term in enumerate(moments(grad_i, both[:, 256:], both[:, :256])):
-        summed = part_h_ref[end, comp] + dot(lines_e_ref[exchange, :EDGE, :EDGE], term)
-        lined_h.append(summed.astype(bf16))
-    border_ref[...] = dot(jnp.concatenate(lined_h, axis=0), pack_h_ref[...])
-
-    span = EDGE * half
-    copies = []
-    def make_block_moments(group):
+        place = target.at[pl.ds(count - 2, 2), pl.ds(EDGE, rows - 2 * EDGE)]
+        copies.append(pltpu.make_async_copy(done_ref.at[n], place, done_sems.at[n]))
+        copies[-1].start()
+    lows = [low_end(exchange) for exchange in range(2)]
+    ends = [jnp.where(low, 0, 1) for low in lows]
+    starts = [pl.multiple_of(jnp.where(low, 0, rows - EDGE), EDGE) for low in lows]
+
+    def prepare(exchange, rows_ref):
+        low, start, end = lows[exchange], starts[exchange], ends[exchange]
+        rows_in = rows_ref[...].astype(f32)
+        if exchange == 1:
+            il = lax.axis_index("il")
+            outside = (low & (il == 0)) | (jnp.logical_not(low) & (il == lax.axis_size("il") - 1))
+            rows_in = jnp.where(outside, 0.0, rows_in)
+        packed_ref[exchange] = pltpu.roll(rows_in, jnp.where(low, 0, EDGE - REACH), 0)
+        place = iota((EDGE, cols), 0)
+        received = jnp.where(low, place, EDGE - 1 - place) < REACH
+
+        def joined(row, own):
+            lanes = own.shape[1]
+            own = pltpu.roll(own.astype(f32), jnp.where(low, REACH, EDGE - REACH), 0)
+            return jnp.where(received[:, :lanes], packed_ref[exchange, row : row + EDGE, :lanes], own).astype(bf16)
+
+        for depth in range(depths):
+            block_ref[exchange, depth] = joined(REACH * depth, vol_ref[depth, pl.ds(start, EDGE)])
+        own_h = halo_ref[pl.ds(start, EDGE)]
+        block_h_ref[exchange, :, :256] = joined(REACH * depths, own_h[:, :256])
+        block_h_ref[exchange, :, 256:] = joined(REACH * (depths + 1), own_h[:, 256:])
+
+        both = dot(block_h_ref[exchange], diff_h_ref[...])
+        grad_i = dot(diff_e_ref[...], block_h_ref[exchange, :, :256])
+        lined_h = []
+        for comp, term in enumerate(moments(grad_i, both[:, 256:], both[:, :256])):
+            summed = part_h_ref[end, comp] + dot(lines_e_ref[exchange, :EDGE, :EDGE], term)
+            lined_h.append(summed.astype(bf16))
+        border_ref[exchange] = dot(jnp.concatenate(lined_h, axis=0), pack_h_ref[...])
+
+    def make_edges(exchange, group):
         first = half * group
-        planes = [block_ref[first + k : first + half + k].astype(f32).reshape(span, cols) for k in range(3)]
-        return moments(*gradients(*planes, mask_ref))
-
-    def make_edge(group, comp, term):
+        planes = [block_ref[exchange, first + k : first + half + k].astype(f32).reshape(span, cols) for k in range(3)]
+        for comp, term in enumerate(moments(*gradients(*planes, mask_ref))):
+            outer = dot(lines_e_ref[exchange], term)
+            summed = part_ref[ends[exchange], comp, first : first + half] + outer.reshape(half, EDGE, cols)
+            edge_ref[exchange, first : first + half, comp] = summed.astype(bf16)
+
+    def finish(exchange, group):
         first = half * group
-        outer = dot(lines_e_ref[exchange, :span, :span], term)
-        summed = part_ref[end, comp, first : first + half] + outer.reshape(half, EDGE, cols)
-        edge_ref[first : first + half, comp] = summed.astype(bf16)
-
-    def finish(group, k, tensor):
-        def store(lanes, values):
-            for n, value in enumerate(values):
-                out_ref[n, half * group + k, :, lanes] = value
-
-        border = border_of(border_ref[:, 128 * group : 128 * (group + 1)], k, mask_ref)
-        attributes(tensor, border, store)
-
-    def send(group):
-        depth = pl.ds(half * group, half)
+        own = edge_ref[exchange, first : first + half].reshape(6 * span, cols)
+        tensor = dot(own, smooth_ref[...])
+        for k in range(half):
+
+            def store(lanes, values):
+                for n, value in enumerate(values):
+                    out_ref[exchange, n, first + k, :, lanes] = value
+
+            border = border_of(border_ref[exchange, :, 128 * group : 128 * (group + 1)], k, mask_ref)
+            attributes(tensor[6 * EDGE * k : 6 * EDGE * (k + 1)], border, store)
+        depth = pl.ds(first, half)
         for n, target in enumerate(targets):
-            copy = pltpu.make_async_copy(out_ref.at[n, depth], target.at[depth, pl.ds(start, EDGE)], sems.at[group, n])
-            copy.start()
-            copies.append(copy)
-
-    for group in range(2):
-        for comp, term in enumerate(make_block_moments(group)):
-            make_edge(group, comp, term)
-    for group in range(2):
-        tensor = dot(edge_ref[half * group : half * (group + 1)].reshape(6 * span, cols), smooth_ref[...])
-        for k in range(half):
-            finish(group, k, tensor[6 * EDGE * k : 6 * EDGE * (k + 1)])
-        if last:
-            send(group)
-    for copy in finished + copies:
+            place = target.at[depth, pl.ds(starts[exchange], EDGE)]
+            copies.append(pltpu.make_async_copy(out_ref.at[exchange, n, depth], place, sems.at[exchange, group, n]))
+            copies[-1].start()
+
+    for exchange, rows_ref in enumerate((near_ref, far_ref)):
+        prepare(exchange, rows_ref)
+    for exchange in range(2):
+        for group in range(2):
+            make_edges(exchange, group)
+    for exchange in range(2):
+        for group in range(2):
+            finish(exchange, group)
+    for copy in copies:
         copy.wait()
 
 
@@ -484,38 +475,26 @@
         aliases={len(operands) - 1: 0},
     )
 
-    end_rows = (3, count, EDGE, cols)
-    tables = [smooth, pack_h, diff_h, lines_e, diff_e, mask]
-    scratch = [
-        pltpu.VMEM((packed_rows, cols), f32),
-        pltpu.VMEM((depths, EDGE, cols), bf16),
-        pltpu.VMEM((EDGE, 128 * TILES), bf16),
-        pltpu.VMEM((6 * EDGE, 256), f32),
-        pltpu.VMEM((count, 6, EDGE, cols), bf16),
-    ]
-    sems = pltpu.SemaphoreType.DMA((3,))
-    operands = [done, vol, halo, near_in, part, part_h, *tables]
-    *outs_in, done = call(
-        "near_end_kernel",
-        lambda *refs: end_kernel(0, *refs),
-        outs + [(end_rows, f32)],
-        scratch + [sems],
-        operands + outs_in,
-        in_specs=[WHOLE] * len(operands) + [IN_HBM] * 3,
-        out_specs=(IN_HBM,) * 3 + (WHOLE,),
-        flops=work,
-        aliases={len(operands) + n: n for n in range(3)},
-    )
-    operands = [done, vol, halo, far_in, part, part_h, *tables]
+    operands = [done, vol, halo, near_in, far_in, part, part_h, smooth, pack_h, diff_h, lines_e, diff_e, mask]
     return call(
-        "far_end_kernel",
-        lambda *refs: end_kernel(1, *refs),
+        "ends_kernel",
+        ends_kernel,
         outs,
-        scratch + [pltpu.VMEM(end_rows, f32), sems, pltpu.SemaphoreType.DMA((2, 3))],
+        [
+            pltpu.VMEM((2, packed_rows, cols), f32),
+            pltpu.VMEM((2, depths, EDGE, cols), bf16),
+            pltpu.VMEM((2, EDGE, 128 * TILES), bf16),
+            pltpu.VMEM((2, 6 * EDGE, 256), f32),
+            pltpu.VMEM((2, count, 6, EDGE, cols), bf16),
+            pltpu.VMEM((2, 3, count, EDGE, cols), f32),
+            pltpu.SemaphoreType.DMA((3,)),
+            pltpu.SemaphoreType.DMA((2, 2, 3)),
+        ],
         operands + outs_in,
         in_specs=[WHOLE] * len(operands) + [IN_HBM] * 3,
         out_specs=(IN_HBM,) * 3,
-        flops=work,
+        flops=2 * work,
+        limit=24,
         aliases={len(operands) + n: n for n in range(3)},
     )
 

time: 17.3 us -> 17 us (0.983)
  the two profiles are of different devices: /device:TPU:4 before, /device:TPU:14 now
where the time goes in v19:
time: 17 us; the launch traced here: 16.8 us
  Pallas kernels  10.2 us (60%)
  starting transfers between devices  5.07 us (30%)
  between operations  0.71 us (4%)
  local copies, waits for them, and re-layouts  0.48 us (3%)
  waiting for transfers between devices  0.34 us (2%)
    pallas_call x6, Pallas kernels, call(): pl.pallas_call(kernel, out_shape=tuple((jax.ShapeDtypeStruct(*out) for ou...  10.2 us
    ppermute x1, starting transfers between devices, body(): lax.ppermute(far, 'il', pairs + [(j, i) for i, j in pairs] + [(0, 0), (il...  4.43 us
    ppermute x1, starting transfers between devices, body(): near_in = lax.ppermute(near, 'il', [(i, i ^ 1) for i in range(il)])  0.57 us
    unnamed x2, local copies, waits for them, and re-layouts  0.48 us
  transfers between devices with their start and end apart: 3, of which 1 were waited for; matrix products, arithmetic and copies ran while one was open for 0% of the time, Pallas kernels for 34%

profile of v19, /device:TPU:14, one launch (start us, length us, event | category | flops | bytes accessed | tf_op | source)
XLA Modules:
  0.0 16.8 jit_solution(14575239616647806895)
XLA Ops:
  0.6 0.0 copy-start
  0.6 0.8 %tables_kernel.1 = (bf16[128,128]{1,0:T(8,128)(2,1)S(1)}, bf16[128,128]{1,0:T(8,128)(2,1)S(1)}, bf16[256,256]{1,0:T(8,128)(2,1)S(1)}, bf16[256,256]{1,0:T(8,128)...) custom-call(), custom_call_target="tpu_custom_call" | custom-call | flops 1073741824 | tf_op jit(solution)/shard_map/tables_kernel/pallas_call | solution.py:388
  1.4 0.5 %copy-done = bf16[18,128,256]{2,1,0:T(8,128)(2,1)S(1)} copy-done((bf16[18,128,256]{2,1,0:T(8,128)(2,1)S(1)}, bf16[18,128,256]{2,1,0:T(8,128)(2,1)}, u32[]{:S(2)}) %copy-start) | copy-done | bytes 1179672
  1.9 0.4 %pack_kernel.1 = (bf16[18,128,256]{2,1,0:T(8,128)(2,1)S(1)}, bf16[3,128,128]{2,1,0:T(8,128)(2,1)S(1)}, bf16[3,128,128]{2,1,0:T(8,128)(2,1)S(1)}) custom-call(bf16[18,128,256]{2,1,0:T(8,128)(2,1)S(1)} %copy-done, bf16[1024,256]{1,0:T(8,128)(2,1)S(1)} %get-tuple-element.26.pick_ref), custom_call_target="tpu_custom_call" | custom-call | tf_op jit(solution)/shard_map/pack_kernel/pallas_call | solution.py:388
  2.3 0.1 collective-permute-start
  2.4 0.9 %lines_kernel.1 = (bf16[6,6,6,16,256]{4,3,2,1,0:T(8,128)(2,1)S(1)}, f32[2,6,16,16,256]{4,3,2,1,0:T(8,128)S(1)}) custom-call(bf16[18,128,256]{2,1,0:T(8,128)(2,1)S(1)} %get-tuple-element.27.vol_ref, bf16[128,128]{1,0:T(8,128)(2,1)S(1)} %get-tuple-element.28.lines_ref, f32[3,8,128]{2,1,0:T(8,128)S(1)} %get-tuple-element.33.mask_ref), custom_call_target="tpu_custom_call" | custom-call | flops 268435456 | tf_op jit(solution)/shard_map/lines_kernel/pallas_call | solution.py:388
  3.3 0.3 %collective-permute-done.side_ref = bf16[3,128,128]{2,1,0:T(8,128)(2,1)S(1)} collective-permute-done((bf16[3,128,128]{2,1,0:T(8,128)(2,1)S(1)}, bf16[3,128,128]{2,1,0:T(8,128)(2,1)S(1)}, u32[]{:S(2)}, u32[]{:S(2)}) %collective-permute-start) | collective-permute-done | bytes 98336 | tf_op jit(solution)/shard_map/ppermute | solution.py:432
  3.7 0.2 rows_kernel.1
  3.8 0.6 %collective-permute-start.1 = (bf16[208,256]{1,0:T(8,128)(2,1)S(1)}, bf16[208,256]{1,0:T(8,128)(2,1)S(1)}, u32[]{:S(2)}, u32[]{:S(2)}) collective-permute-start(bf16[208,256]{1,0:T(8,128)(2,1)S(1)} %get-tuple-element.40), channel_id=1, source_target_pairs={{0,2},{2,0},{4,6},{6,4},{8,10},{10,8},{12,14},{14,12},{1,3},{3,1},... | collective-permute-start | bytes 319496 | tf_op jit(solution)/shard_map/ppermute | solution.py:453
  4.4 4.4 %collective-permute-start.2 = (bf16[208,256]{1,0:T(8,128)(2,1)S(1)}, bf16[208,256]{1,0:T(8,128)(2,1)S(1)}, u32[]{:S(2)}, u32[]{:S(2)}) collective-permute-start(bf16[208,256]{1,0:T(8,128)(2,1)S(1)} %get-tuple-element.41), channel_id=1, source_target_pairs={{2,4},{6,8},{10,12},{4,2},{8,6},{12,10},{0,0},{14,14},{3,5},{7,9},... | collective-permute-start | bytes 319496 | tf_op jit(solution)/shard_map/ppermute | solution.py:455
  8.8 4.9 %own_kernel.1 = (f32[2,6,16,16,256]{4,3,2,1,0:T(8,128)S(1)}, f32[16,128,256]{2,1,0:T(8,128)}, f32[16,128,256]{2,1,0:T(8,128)}, f32[16,128,256]{2,1,0:T(8,128)}, ...) custom-call(bf16[18,128,256]{2,1,0:T(8,128)(2,1)S(1)} %get-tuple-element.27.vol_ref, ...), custom_call_target="tpu_custom_call", output_to_operand_aliasing={{0}: (9, {})} | custom-call | flops 5368709120 | tf_op jit(solution)/shard_map/own_kernel/pallas_call | solution.py:388
  13.7 0.0 collective-permute-done.1.near_ref
  13.7 0.0 collective-permute-done.2.far_ref
  13.7 3.1 %ends_kernel.1 = (f32[16,128,256]{2,1,0:T(8,128)}, f32[16,128,256]{2,1,0:T(8,128)}, f32[16,128,256]{2,1,0:T(8,128)}) custom-call(f32[3,2,96,256]{3,2,1,0:T(8,128)S(1)} %get-tuple-element.39.done_ref, bf16[18,128,256]{2,1,0:T(8,128)(2,1)S(1)} %get-tuple-element.27.vol_ref, ...), custom_call_target="tpu_custom_call", output_to_operand_aliasing={{0}: (13, {}), {1}: (14, {}), {2}: (15, {})} | custom-call | flops 2147483648 | tf_op jit(solution)/shard_map/ends_kernel/pallas_call | solution.py:388
Async XLA Ops:
  0.6 1.3 %copy-start = (bf16[18,128,256]{2,1,0:T(8,128)(2,1)S(1)}, bf16[18,128,256]{2,1,0:T(8,128)(2,1)}, u32[]{:S(2)}) copy-start(bf16[18,128,256]{2,1,0:T(8,128)(2,1)} %vol_ref.1) | copy-start | bytes 3538948
  2.3 1.4 %collective-permute-start = (bf16[3,128,128]{2,1,0:T(8,128)(2,1)S(1)}, bf16[3,128,128]{2,1,0:T(8,128)(2,1)S(1)}, u32[]{:S(2)}, u32[]{:S(2)}) collective-permute-start(bf16[3,128,128]{2,1,0:T(8,128)(2,1)S(1)} %get-tuple-element.32), channel_id=1, source_target_pairs={{0,1},{1,0},{2,3},{3,2},{4,5},{5,4},{6,7},{7,6},{8,9},{9,8},{10,11... | collective-permute-start | bytes 294920 | tf_op jit(solution)/shard_map/ppermute | solution.py:432
  3.8 9.9 %collective-permute-start.1 = (bf16[208,256]{1,0:T(8,128)(2,1)S(1)}, bf16[208,256]{1,0:T(8,128)(2,1)S(1)}, u32[]{:S(2)}, u32[]{:S(2)}) collective-permute-start(bf16[208,256]{1,0:T(8,128)(2,1)S(1)} %get-tuple-element.40), channel_id=1, source_target_pairs={{0,2},{2,0},{4,6},{6,4},{8,10},{10,8},{12,14},{14,12},{1,3},{3,1},... | collective-permute-start | bytes 319496 | tf_op jit(solution)/shard_map/ppermute | solution.py:453
  4.4 9.3 %collective-permute-start.2 = (bf16[208,256]{1,0:T(8,128)(2,1)S(1)}, bf16[208,256]{1,0:T(8,128)(2,1)S(1)}, u32[]{:S(2)}, u32[]{:S(2)}) collective-permute-start(bf16[208,256]{1,0:T(8,128)(2,1)S(1)} %get-tuple-element.41), channel_id=1, source_target_pairs={{2,4},{6,8},{10,12},{4,2},{8,6},{12,10},{0,0},{14,14},{3,5},{7,9},... | collective-permute-start | bytes 319496 | tf_op jit(solution)/shard_map/ppermute | solution.py:455

commit v20 on v19

--- a/solution.py
+++ b/solution.py
@@ -17,6 +17,7 @@
 TINY = float(np.finfo(np.float32).tiny)
 HEAD = 3
 AHEAD = 3
+LATER = 6
 FAR = -1000
 WHOLE = pl.BlockSpec(memory_space=pltpu.VMEM)
 IN_HBM = pl.BlockSpec(memory_space=pltpu.HBM)
@@ -277,8 +278,8 @@
 
             def store(lanes, values):
                 for n, value in enumerate(values):
-                    if z >= count - 2:
-                        later_ref[n, z % 2, rows, lanes] = value
+                    if z >= count - LATER:
+                        later_ref[n, z - (count - LATER), rows, lanes] = value
                     else:
                         out_ref[n, z, rows, lanes] = value
 
@@ -286,7 +287,7 @@
             attributes(tensor_ref[z % 2, part], border, store)
             if later is not None:
                 make_lines(later, chunk, lines_ref, slots[later // 2 % 2], inner_ref, part_ref)
-        if z % 2 == 1 and z < count - 2:
+        if z % 2 == 1 and z < count - LATER:
             depth = pl.ds(z - 1, 2)
             for n, target in enumerate(targets):
                 place = target.at[depth, pl.ds(EDGE, inner)]
@@ -309,7 +310,7 @@
     targets = (dip_i_ref, dip_x_ref, plan_ref)
     copies = []
     for n, target in enumerate(targets):
-        place = target.at[pl.ds(count - 2, 2), pl.ds(EDGE, rows - 2 * EDGE)]
+        place = target.at[pl.ds(count - LATER, LATER), pl.ds(EDGE, rows - 2 * EDGE)]
         copies.append(pltpu.make_async_copy(done_ref.at[n], place, done_sems.at[n]))
         copies[-1].start()
     lows = [low_end(exchange) for exchange in range(2)]
@@ -459,14 +460,14 @@
     part, *outs_in, done, part_h = call(
         "own_kernel",
         own_kernel,
-        [partial, *outs, ((3, 2, EDGE * chunks, cols), f32), ((2, 6, EDGE, 256), f32)],
+        [partial, *outs, ((3, LATER, EDGE * chunks, cols), f32), ((2, 6, EDGE, 256), f32)],
         [
             pltpu.VMEM((count, chunks, 6, EDGE, cols), bf16),
             pltpu.VMEM((6 * EDGE * chunks, 256), f32),
             *moment_slots,
             pltpu.VMEM((2, 6 * EDGE * chunks, cols), f32),
-            pltpu.VMEM((3, count - 2, EDGE * chunks, cols), f32),
-            pltpu.SemaphoreType.DMA((half - 1, 3)),
+            pltpu.VMEM((3, count - LATER, EDGE * chunks, cols), f32),
+            pltpu.SemaphoreType.DMA(((count - LATER) // 2, 3)),
         ],
         operands,
         out_specs=(WHOLE,) + (IN_HBM,) * 3 + (WHOLE,) * 2,

time: 17 us -> 16.8 us (0.988)
  Pallas kernels: 10.2 us -> 10 us
  transfers between devices with their start and end apart: 3 -> 3, of which waited for: 1 -> 1; matrix products, arithmetic and copies ran while one was open for 0% -> 0% of each run, Pallas kernels for 34% -> 33%
where the time goes in v20:
time: 16.8 us; the launch traced here: 16.6 us
  Pallas kernels  10 us (60%)
  starting transfers between devices  5.07 us (30%)
  between operations  0.71 us (4%)
  local copies, waits for them, and re-layouts  0.48 us (3%)
  waiting for transfers between devices  0.35 us (2%)
    pallas_call x6, Pallas kernels, call(): pl.pallas_call(kernel, out_shape=tuple((jax.ShapeDtypeStruct(*out) for ou...  10 us
    ppermute x1, starting transfers between devices, body(): lax.ppermute(far, 'il', pairs + [(j, i) for i, j in pairs] + [(0, 0), (il...  4.43 us
    ppermute x1, starting transfers between devices, body(): near_in = lax.ppermute(near, 'il', [(i, i ^ 1) for i in range(il)])  0.57 us
    unnamed x2, local copies, waits for them, and re-layouts  0.48 us
    ppermute x1, waiting for transfers between devices, body(): side = lax.ppermute(send, 'xl', [(0, 1), (1, 0)])  0.34 us
  transfers between devices with their start and end apart: 3, of which 1 were waited for; matrix products, arithmetic and copies ran while one was open for 0% of the time, Pallas kernels for 33%

profile of v20, /device:TPU:14, one launch (start us, length us, event | category | flops | bytes accessed | tf_op | source)
XLA Modules:
  0.0 16.6 jit_solution(9566134046968287086)
XLA Ops:
  0.6 0.0 copy-start
  0.6 0.8 %tables_kernel.1 = (bf16[128,128]{1,0:T(8,128)(2,1)S(1)}, bf16[128,128]{1,0:T(8,128)(2,1)S(1)}, bf16[256,256]{1,0:T(8,128)(2,1)S(1)}, bf16[256,256]{1,0:T(8,128)...) custom-call(), custom_call_target="tpu_custom_call" | custom-call | flops 1073741824 | tf_op jit(solution)/shard_map/tables_kernel/pallas_call | solution.py:389
  1.4 0.5 %copy-done = bf16[18,128,256]{2,1,0:T(8,128)(2,1)S(1)} copy-done((bf16[18,128,256]{2,1,0:T(8,128)(2,1)S(1)}, bf16[18,128,256]{2,1,0:T(8,128)(2,1)}, u32[]{:S(2)}) %copy-start) | copy-done | bytes 1179672
  1.9 0.4 %pack_kernel.1 = (bf16[18,128,256]{2,1,0:T(8,128)(2,1)S(1)}, bf16[3,128,128]{2,1,0:T(8,128)(2,1)S(1)}, bf16[3,128,128]{2,1,0:T(8,128)(2,1)S(1)}) custom-call(bf16[18,128,256]{2,1,0:T(8,128)(2,1)S(1)} %copy-done, bf16[1024,256]{1,0:T(8,128)(2,1)S(1)} %get-tuple-element.26.pick_ref), custom_call_target="tpu_custom_call" | custom-call | tf_op jit(solution)/shard_map/pack_kernel/pallas_call | solution.py:389
  2.3 0.1 collective-permute-start
  2.4 0.9 %lines_kernel.1 = (bf16[6,6,6,16,256]{4,3,2,1,0:T(8,128)(2,1)S(1)}, f32[2,6,16,16,256]{4,3,2,1,0:T(8,128)S(1)}) custom-call(bf16[18,128,256]{2,1,0:T(8,128)(2,1)S(1)} %get-tuple-element.27.vol_ref, bf16[128,128]{1,0:T(8,128)(2,1)S(1)} %get-tuple-element.28.lines_ref, f32[3,8,128]{2,1,0:T(8,128)S(1)} %get-tuple-element.33.mask_ref), custom_call_target="tpu_custom_call" | custom-call | flops 268435456 | tf_op jit(solution)/shard_map/lines_kernel/pallas_call | solution.py:389
  3.3 0.3 %collective-permute-done.side_ref = bf16[3,128,128]{2,1,0:T(8,128)(2,1)S(1)} collective-permute-done((bf16[3,128,128]{2,1,0:T(8,128)(2,1)S(1)}, bf16[3,128,128]{2,1,0:T(8,128)(2,1)S(1)}, u32[]{:S(2)}, u32[]{:S(2)}) %collective-permute-start) | collective-permute-done | bytes 98336 | tf_op jit(solution)/shard_map/ppermute | solution.py:433
  3.7 0.1 rows_kernel.1
  3.8 0.6 %collective-permute-start.1 = (bf16[208,256]{1,0:T(8,128)(2,1)S(1)}, bf16[208,256]{1,0:T(8,128)(2,1)S(1)}, u32[]{:S(2)}, u32[]{:S(2)}) collective-permute-start(bf16[208,256]{1,0:T(8,128)(2,1)S(1)} %get-tuple-element.40), channel_id=1, source_target_pairs={{0,2},{2,0},{4,6},{6,4},{8,10},{10,8},{12,14},{14,12},{1,3},{3,1},... | collective-permute-start | bytes 319496 | tf_op jit(solution)/shard_map/ppermute | solution.py:454
  4.4 4.4 %collective-permute-start.2 = (bf16[208,256]{1,0:T(8,128)(2,1)S(1)}, bf16[208,256]{1,0:T(8,128)(2,1)S(1)}, u32[]{:S(2)}, u32[]{:S(2)}) collective-permute-start(bf16[208,256]{1,0:T(8,128)(2,1)S(1)} %get-tuple-element.41), channel_id=1, source_target_pairs={{2,4},{6,8},{10,12},{4,2},{8,6},{12,10},{0,0},{14,14},{3,5},{7,9},... | collective-permute-start | bytes 319496 | tf_op jit(solution)/shard_map/ppermute | solution.py:456
  8.8 4.6 %own_kernel.1 = (f32[2,6,16,16,256]{4,3,2,1,0:T(8,128)S(1)}, f32[16,128,256]{2,1,0:T(8,128)}, f32[16,128,256]{2,1,0:T(8,128)}, f32[16,128,256]{2,1,0:T(8,128)}, ...) custom-call(bf16[18,128,256]{2,1,0:T(8,128)(2,1)S(1)} %get-tuple-element.27.vol_ref, ...), custom_call_target="tpu_custom_call", output_to_operand_aliasing={{0}: (9, {})} | custom-call | flops 5368709120 | tf_op jit(solution)/shard_map/own_kernel/pallas_call | solution.py:389
  13.4 0.0 collective-permute-done.1.near_ref
  13.4 0.0 collective-permute-done.2.far_ref
  13.5 3.2 %ends_kernel.1 = (f32[16,128,256]{2,1,0:T(8,128)}, f32[16,128,256]{2,1,0:T(8,128)}, f32[16,128,256]{2,1,0:T(8,128)}) custom-call(f32[3,6,96,256]{3,2,1,0:T(8,128)S(1)} %get-tuple-element.39.done_ref, bf16[18,128,256]{2,1,0:T(8,128)(2,1)S(1)} %get-tuple-element.27.vol_ref, ...), custom_call_target="tpu_custom_call", output_to_operand_aliasing={{0}: (13, {}), {1}: (14, {}), {2}: (15, {})} | custom-call | flops 2147483648 | tf_op jit(solution)/shard_map/ends_kernel/pallas_call | solution.py:389
Async XLA Ops:
  0.6 1.3 %copy-start = (bf16[18,128,256]{2,1,0:T(8,128)(2,1)S(1)}, bf16[18,128,256]{2,1,0:T(8,128)(2,1)}, u32[]{:S(2)}) copy-start(bf16[18,128,256]{2,1,0:T(8,128)(2,1)} %vol_ref.1) | copy-start | bytes 3538948
  2.3 1.4 %collective-permute-start = (bf16[3,128,128]{2,1,0:T(8,128)(2,1)S(1)}, bf16[3,128,128]{2,1,0:T(8,128)(2,1)S(1)}, u32[]{:S(2)}, u32[]{:S(2)}) collective-permute-start(bf16[3,128,128]{2,1,0:T(8,128)(2,1)S(1)} %get-tuple-element.32), channel_id=1, source_target_pairs={{0,1},{1,0},{2,3},{3,2},{4,5},{5,4},{6,7},{7,6},{8,9},{9,8},{10,11... | collective-permute-start | bytes 294920 | tf_op jit(solution)/shard_map/ppermute | solution.py:433
  3.8 9.6 %collective-permute-start.1 = (bf16[208,256]{1,0:T(8,128)(2,1)S(1)}, bf16[208,256]{1,0:T(8,128)(2,1)S(1)}, u32[]{:S(2)}, u32[]{:S(2)}) collective-permute-start(bf16[208,256]{1,0:T(8,128)(2,1)S(1)} %get-tuple-element.40), channel_id=1, source_target_pairs={{0,2},{2,0},{4,6},{6,4},{8,10},{10,8},{12,14},{14,12},{1,3},{3,1},... | collective-permute-start | bytes 319496 | tf_op jit(solution)/shard_map/ppermute | solution.py:454
  4.4 9.1 %collective-permute-start.2 = (bf16[208,256]{1,0:T(8,128)(2,1)S(1)}, bf16[208,256]{1,0:T(8,128)(2,1)S(1)}, u32[]{:S(2)}, u32[]{:S(2)}) collective-permute-start(bf16[208,256]{1,0:T(8,128)(2,1)S(1)} %get-tuple-element.41), channel_id=1, source_target_pairs={{2,4},{6,8},{10,12},{4,2},{8,6},{12,10},{0,0},{14,14},{3,5},{7,9},... | collective-permute-start | bytes 319496 | tf_op jit(solution)/shard_map/ppermute | solution.py:456

commit v21 on v20

--- a/solution.py
+++ b/solution.py
@@ -17,7 +17,7 @@
 TINY = float(np.finfo(np.float32).tiny)
 HEAD = 3
 AHEAD = 3
-LATER = 6
+LATER = 8
 FAR = -1000
 WHOLE = pl.BlockSpec(memory_space=pltpu.VMEM)
 IN_HBM = pl.BlockSpec(memory_space=pltpu.HBM)
@@ -287,11 +287,11 @@
             attributes(tensor_ref[z % 2, part], border, store)
             if later is not None:
                 make_lines(later, chunk, lines_ref, slots[later // 2 % 2], inner_ref, part_ref)
-        if z % 2 == 1 and z < count - LATER:
-            depth = pl.ds(z - 1, 2)
+        if z == count - LATER - 1:
+            depth = pl.ds(0, count - LATER)
             for n, target in enumerate(targets):
                 place = target.at[depth, pl.ds(EDGE, inner)]
-                copies.append(pltpu.make_async_copy(out_ref.at[n, depth], place, sems.at[z // 2, n]))
+                copies.append(pltpu.make_async_copy(out_ref.at[n], place, sems.at[n]))
                 copies[-1].start()
     for copy in copies:
         copy.wait()
@@ -467,7 +467,7 @@
             *moment_slots,
             pltpu.VMEM((2, 6 * EDGE * chunks, cols), f32),
             pltpu.VMEM((3, count - LATER, EDGE * chunks, cols), f32),
-            pltpu.SemaphoreType.DMA(((count - LATER) // 2, 3)),
+            pltpu.SemaphoreType.DMA((3,)),
         ],
         operands,
         out_specs=(WHOLE,) + (IN_HBM,) * 3 + (WHOLE,) * 2,

time: 16.8 us -> 17.4 us (1.036)
  the two profiles are of different devices: /device:TPU:14 before, /device:TPU:4 now
where the time goes in v21:
time: 17.4 us; the launch traced here: 17.2 us
  Pallas kernels  10.6 us (61%)
  starting transfers between devices  5.06 us (29%)
  between operations  0.71 us (4%)
  local copies, waits for them, and re-layouts  0.48 us (3%)
  waiting for transfers between devices  0.34 us (2%)
    pallas_call x6, Pallas kernels, call(): pl.pallas_call(kernel, out_shape=tuple((jax.ShapeDtypeStruct(*out) for ou...  10.6 us
    ppermute x1, starting transfers between devices, body(): lax.ppermute(far, 'il', pairs + [(j, i) for i, j in pairs] + [(0, 0), (il...  4.92 us
    unnamed x2, local copies, waits for them, and re-layouts  0.48 us
  transfers between devices with their start and end apart: 3, of which 1 were waited for; matrix products, arithmetic and copies ran while one was open for 0% of the time, Pallas kernels for 35%

profile of v21, /device:TPU:4, one launch (start us, length us, event | category | flops | bytes accessed | tf_op | source)
XLA Modules:
  0.0 17.2 jit_solution(4505719809443635253)
XLA Ops:
  0.6 0.0 copy-start
  0.6 0.8 %tables_kernel.1 = (bf16[128,128]{1,0:T(8,128)(2,1)S(1)}, bf16[128,128]{1,0:T(8,128)(2,1)S(1)}, bf16[256,256]{1,0:T(8,128)(2,1)S(1)}, bf16[256,256]{1,0:T(8,128)...) custom-call(), custom_call_target="tpu_custom_call" | custom-call | flops 1073741824 | tf_op jit(solution)/shard_map/tables_kernel/pallas_call | solution.py:389
  1.4 0.5 %copy-done = bf16[18,128,256]{2,1,0:T(8,128)(2,1)S(1)} copy-done((bf16[18,128,256]{2,1,0:T(8,128)(2,1)S(1)}, bf16[18,128,256]{2,1,0:T(8,128)(2,1)}, u32[]{:S(2)}) %copy-start) | copy-done | bytes 1179672
  1.9 0.4 %pack_kernel.1 = (bf16[18,128,256]{2,1,0:T(8,128)(2,1)S(1)}, bf16[3,128,128]{2,1,0:T(8,128)(2,1)S(1)}, bf16[3,128,128]{2,1,0:T(8,128)(2,1)S(1)}) custom-call(bf16[18,128,256]{2,1,0:T(8,128)(2,1)S(1)} %copy-done, bf16[1024,256]{1,0:T(8,128)(2,1)S(1)} %get-tuple-element.26.pick_ref), custom_call_target="tpu_custom_call" | custom-call | tf_op jit(solution)/shard_map/pack_kernel/pallas_call | solution.py:389
  2.3 0.1 collective-permute-start
  2.4 0.9 %lines_kernel.1 = (bf16[6,6,6,16,256]{4,3,2,1,0:T(8,128)(2,1)S(1)}, f32[2,6,16,16,256]{4,3,2,1,0:T(8,128)S(1)}) custom-call(bf16[18,128,256]{2,1,0:T(8,128)(2,1)S(1)} %get-tuple-element.27.vol_ref, bf16[128,128]{1,0:T(8,128)(2,1)S(1)} %get-tuple-element.28.lines_ref, f32[3,8,128]{2,1,0:T(8,128)S(1)} %get-tuple-element.33.mask_ref), custom_call_target="tpu_custom_call" | custom-call | flops 268435456 | tf_op jit(solution)/shard_map/lines_kernel/pallas_call | solution.py:389
  3.3 0.3 %collective-permute-done.side_ref = bf16[3,128,128]{2,1,0:T(8,128)(2,1)S(1)} collective-permute-done((bf16[3,128,128]{2,1,0:T(8,128)(2,1)S(1)}, bf16[3,128,128]{2,1,0:T(8,128)(2,1)S(1)}, u32[]{:S(2)}, u32[]{:S(2)}) %collective-permute-start) | collective-permute-done | bytes 98336 | tf_op jit(solution)/shard_map/ppermute | solution.py:433
  3.7 0.1 rows_kernel.1
  3.8 0.1 collective-permute-start.1
  3.9 4.9 %collective-permute-start.2 = (bf16[208,256]{1,0:T(8,128)(2,1)S(1)}, bf16[208,256]{1,0:T(8,128)(2,1)S(1)}, u32[]{:S(2)}, u32[]{:S(2)}) collective-permute-start(bf16[208,256]{1,0:T(8,128)(2,1)S(1)} %get-tuple-element.41), channel_id=1, source_target_pairs={{2,4},{6,8},{10,12},{4,2},{8,6},{12,10},{0,0},{14,14},{3,5},{7,9},... | collective-permute-start | bytes 319496 | tf_op jit(solution)/shard_map/ppermute | solution.py:456
  8.8 5.0 %own_kernel.1 = (f32[2,6,16,16,256]{4,3,2,1,0:T(8,128)S(1)}, f32[16,128,256]{2,1,0:T(8,128)}, f32[16,128,256]{2,1,0:T(8,128)}, f32[16,128,256]{2,1,0:T(8,128)}, ...) custom-call(bf16[18,128,256]{2,1,0:T(8,128)(2,1)S(1)} %get-tuple-element.27.vol_ref, ...), custom_call_target="tpu_custom_call", output_to_operand_aliasing={{0}: (9, {})} | custom-call | flops 5368709120 | tf_op jit(solution)/shard_map/own_kernel/pallas_call | solution.py:389
  13.9 0.0 collective-permute-done.1.near_ref
  13.9 0.0 collective-permute-done.2.far_ref
  13.9 3.4 %ends_kernel.1 = (f32[16,128,256]{2,1,0:T(8,128)}, f32[16,128,256]{2,1,0:T(8,128)}, f32[16,128,256]{2,1,0:T(8,128)}) custom-call(f32[3,8,96,256]{3,2,1,0:T(8,128)S(1)} %get-tuple-element.39.done_ref, bf16[18,128,256]{2,1,0:T(8,128)(2,1)S(1)} %get-tuple-element.27.vol_ref, ...), custom_call_target="tpu_custom_call", output_to_operand_aliasing={{0}: (13, {}), {1}: (14, {}), {2}: (15, {})} | custom-call | flops 2147483648 | tf_op jit(solution)/shard_map/ends_kernel/pallas_call | solution.py:389
Async XLA Ops:
  0.6 1.3 %copy-start = (bf16[18,128,256]{2,1,0:T(8,128)(2,1)S(1)}, bf16[18,128,256]{2,1,0:T(8,128)(2,1)}, u32[]{:S(2)}) copy-start(bf16[18,128,256]{2,1,0:T(8,128)(2,1)} %vol_ref.1) | copy-start | bytes 3538948
  2.3 1.4 %collective-permute-start = (bf16[3,128,128]{2,1,0:T(8,128)(2,1)S(1)}, bf16[3,128,128]{2,1,0:T(8,128)(2,1)S(1)}, u32[]{:S(2)}, u32[]{:S(2)}) collective-permute-start(bf16[3,128,128]{2,1,0:T(8,128)(2,1)S(1)} %get-tuple-element.32), channel_id=1, source_target_pairs={{0,1},{1,0},{2,3},{3,2},{4,5},{5,4},{6,7},{7,6},{8,9},{9,8},{10,11... | collective-permute-start | bytes 294920 | tf_op jit(solution)/shard_map/ppermute | solution.py:433
  3.8 10.0 %collective-permute-start.1 = (bf16[208,256]{1,0:T(8,128)(2,1)S(1)}, bf16[208,256]{1,0:T(8,128)(2,1)S(1)}, u32[]{:S(2)}, u32[]{:S(2)}) collective-permute-start(bf16[208,256]{1,0:T(8,128)(2,1)S(1)} %get-tuple-element.40), channel_id=1, source_target_pairs={{0,2},{2,0},{4,6},{6,4},{8,10},{10,8},{12,14},{14,12},{1,3},{3,1},... | collective-permute-start | bytes 319496 | tf_op jit(solution)/shard_map/ppermute | solution.py:454
  3.9 10.0 %collective-permute-start.2 = (bf16[208,256]{1,0:T(8,128)(2,1)S(1)}, bf16[208,256]{1,0:T(8,128)(2,1)S(1)}, u32[]{:S(2)}, u32[]{:S(2)}) collective-permute-start(bf16[208,256]{1,0:T(8,128)(2,1)S(1)} %get-tuple-element.41), channel_id=1, source_target_pairs={{2,4},{6,8},{10,12},{4,2},{8,6},{12,10},{0,0},{14,14},{3,5},{7,9},... | collective-permute-start | bytes 319496 | tf_op jit(solution)/shard_map/ppermute | solution.py:456

commit v22 on v20

--- a/solution.py
+++ b/solution.py
@@ -18,6 +18,7 @@
 HEAD = 3
 AHEAD = 3
 LATER = 6
+SHARED = 2
 FAR = -1000
 WHOLE = pl.BlockSpec(memory_space=pltpu.VMEM)
 IN_HBM = pl.BlockSpec(memory_space=pltpu.HBM)
@@ -218,6 +219,24 @@
                 make_lines(2 * pair + k, comp, lines_ref, slots[pair % 2], inner_ref, part_ref)
 
 
+def shared_lines_kernel(
+    parity, vol_ref, lines_ref, mask_ref, rows_ref, part_in_ref, *refs,
+):
+    inner_ref, part_ref, rows_out_ref, even_ref, odd_ref = refs[-5:]
+    rows_out_ref[...] = rows_ref[...]
+
+    @pl.when(lax.rem(lax.axis_index("il"), 2) == parity)
+    def _():
+        for index in range(SHARED):
+            pair, slot = HEAD + index, (even_ref, odd_ref)[index % 2]
+            make_moments(pair, vol_ref, mask_ref, slot)
+            for k in range(2):
+                z = 2 * pair + k
+                for comp in range(6):
+                    summed = dot(lines_ref[...], slot[k, comp])
+                    store_chunks(summed, comp, inner_ref.at[2 * index + k], part_ref.at[:, :, z])
+
+
 def tensor_of(own, smooth_ref, tensor_ref):
     tensor_ref[...] = dot(own.reshape(-1, own.shape[-1]), smooth_ref[...])
 
@@ -242,15 +261,19 @@
 
 
 def own_kernel(
-    vol_ref, lines_ref, diff_i_ref, smooth_ref, halo_ref, diff_h_ref, pack_h_ref, mask_ref, inner_in_ref, part_in_ref,
+    vol_ref, lines_ref, diff_i_ref, smooth_ref, halo_ref, diff_h_ref, pack_h_ref, mask_ref, inner_in_ref, shared_ref, part_in_ref,
     part_ref, dip_i_ref, dip_x_ref, plan_ref, later_ref, part_h_ref,
     inner_ref, border_ref, even_ref, odd_ref, tensor_ref, out_ref, sems,
 ):
-    count, chunks = inner_ref.shape[:2]
+    count, chunks = vol_ref.shape[0] - 2, inner_ref.shape[1]
     inner = EDGE * chunks
     slots = (even_ref, odd_ref)
     targets = (dip_i_ref, dip_x_ref, plan_ref)
-    inner_ref[: 2 * HEAD] = inner_in_ref[...]
+    ready, known = 2 * HEAD, 2 * (HEAD + SHARED)
+
+    def inner_of(z):
+        return inner_in_ref[z] if z < ready else shared_ref[z - ready] if z < known else inner_ref[z - known]
+
 
     both = dot(halo_ref[...], diff_h_ref[...])
     grad_i = dot(diff_i_ref[...], halo_ref[:, :256])
@@ -264,13 +287,13 @@
     border_ref[...] = dot(jnp.concatenate(sum(lined_h, []), axis=0), pack_h_ref[...])
 
     copies = []
-    tensor_of(inner_ref[0], smooth_ref, tensor_ref.at[0])
+    tensor_of(inner_of(0), smooth_ref, tensor_ref.at[0])
     for z in range(count):
-        later = z + 2 * HEAD if z + 2 * HEAD < count else None
+        later = z + known if z + known < count else None
         if later is not None and later % 2 == 0:
             make_moments(later // 2, vol_ref, mask_ref, slots[later // 2 % 2])
         if z < count - 1:
-            tensor_of(inner_ref[z + 1], smooth_ref, tensor_ref.at[(z + 1) % 2])
+            tensor_of(inner_of(z + 1), smooth_ref, tensor_ref.at[(z + 1) % 2])
         group = 128 * (z // SLOTS)
         for chunk in range(chunks):
             rows = slice(EDGE * chunk, EDGE * (chunk + 1))
@@ -286,7 +309,8 @@
             border = border_of(border_ref[part, group : group + 128], z % SLOTS, mask_ref)
             attributes(tensor_ref[z % 2, part], border, store)
             if later is not None:
-                make_lines(later, chunk, lines_ref, slots[later // 2 % 2], inner_ref, part_ref)
+                summed = dot(lines_ref[...], slots[later // 2 % 2][later % 2, chunk])
+                store_chunks(summed, chunk, inner_ref.at[later - known], part_ref.at[:, :, later])
         if z % 2 == 1 and z < count - LATER:
             depth = pl.ds(z - 1, 2)
             for n, target in enumerate(targets):
@@ -453,16 +477,37 @@
     )
     near_in = lax.ppermute(near, "il", [(i, i ^ 1) for i in range(il)])
     pairs = [(i, i + 1) for i in range(1, il - 1, 2)]
+    shared_shape = ((2 * SHARED, chunks, 6, EDGE, cols), bf16)
+    operands = [vol, lines, mask, far, part]
+    shared, part, far = call(
+        "odd_lines_kernel",
+        lambda *refs: shared_lines_kernel(1, *refs),
+        [shared_shape, partial, packed],
+        moment_slots,
+        operands,
+        flops=work // 4,
+        aliases={4: 1},
+    )
     far_in = lax.ppermute(far, "il", pairs + [(j, i) for i, j in pairs] + [(0, 0), (il - 1, il - 1)])
+    operands = [vol, lines, mask, far, part, shared]
+    shared, part, _ = call(
+        "even_lines_kernel",
+        lambda *refs: shared_lines_kernel(0, *refs),
+        [shared_shape, partial, packed],
+        moment_slots,
+        operands,
+        flops=work // 4,
+        aliases={4: 1, 5: 0},
+    )
 
     outs = [((count, rows, cols), f32)] * 3
-    operands = [vol, lines, diff_i, smooth, halo, diff_h, pack_h, mask, inner, part]
+    operands = [vol, lines, diff_i, smooth, halo, diff_h, pack_h, mask, inner, shared, part]
     part, *outs_in, done, part_h = call(
         "own_kernel",
         own_kernel,
         [partial, *outs, ((3, LATER, EDGE * chunks, cols), f32), ((2, 6, EDGE, 256), f32)],
         [
-            pltpu.VMEM((count, chunks, 6, EDGE, cols), bf16),
+            pltpu.VMEM((count - 2 * (HEAD + SHARED), chunks, 6, EDGE, cols), bf16),
             pltpu.VMEM((6 * EDGE * chunks, 256), f32),
             *moment_slots,
             pltpu.VMEM((2, 6 * EDGE * chunks, cols), f32),

time: 16.8 us -> 17.1 us (1.018)
  the two profiles are of different devices: /device:TPU:14 before, /device:TPU:26 now
where the time goes in v22:
time: 17.1 us; the launch traced here: 16.9 us
  Pallas kernels  10.7 us (63%)
  starting transfers between devices  4.65 us (27%)
  between operations  0.71 us (4%)
  local copies, waits for them, and re-layouts  0.48 us (3%)
  waiting for transfers between devices  0.35 us (2%)
    pallas_call x8, Pallas kernels, call(): pl.pallas_call(kernel, out_shape=tuple((jax.ShapeDtypeStruct(*out) for ou...  10.7 us
    ppermute x1, starting transfers between devices, body(): lax.ppermute(far, 'il', pairs + [(j, i) for i, j in pairs] + [(0, 0), (il...  3 us
    ppermute x1, starting transfers between devices, body(): near_in = lax.ppermute(near, 'il', [(i, i ^ 1) for i in range(il)])  1.59 us
    unnamed x2, local copies, waits for them, and re-layouts  0.48 us
    ppermute x1, waiting for transfers between devices, body(): side = lax.ppermute(send, 'xl', [(0, 1), (1, 0)])  0.34 us
  transfers between devices with their start and end apart: 3, of which 1 were waited for; matrix products, arithmetic and copies ran while one was open for 0% of the time, Pallas kernels for 37%

profile of v22, /device:TPU:26, one launch (start us, length us, event | category | flops | bytes accessed | tf_op | source)
XLA Modules:
  0.0 16.9 jit_solution(18233256277275675109)
XLA Ops:
  0.6 0.0 copy-start
  0.6 0.8 %tables_kernel.1 = (bf16[128,128]{1,0:T(8,128)(2,1)S(1)}, bf16[128,128]{1,0:T(8,128)(2,1)S(1)}, bf16[256,256]{1,0:T(8,128)(2,1)S(1)}, bf16[256,256]{1,0:T(8,128)...) custom-call(), custom_call_target="tpu_custom_call" | custom-call | flops 1073741824 | tf_op jit(solution)/shard_map/tables_kernel/pallas_call | solution.py:413
  1.4 0.5 %copy-done = bf16[18,128,256]{2,1,0:T(8,128)(2,1)S(1)} copy-done((bf16[18,128,256]{2,1,0:T(8,128)(2,1)S(1)}, bf16[18,128,256]{2,1,0:T(8,128)(2,1)}, u32[]{:S(2)}) %copy-start) | copy-done | bytes 1179672
  1.9 0.4 %pack_kernel.1 = (bf16[18,128,256]{2,1,0:T(8,128)(2,1)S(1)}, bf16[3,128,128]{2,1,0:T(8,128)(2,1)S(1)}, bf16[3,128,128]{2,1,0:T(8,128)(2,1)S(1)}) custom-call(bf16[18,128,256]{2,1,0:T(8,128)(2,1)S(1)} %copy-done, bf16[1024,256]{1,0:T(8,128)(2,1)S(1)} %get-tuple-element.31.pick_ref), custom_call_target="tpu_custom_call" | custom-call | tf_op jit(solution)/shard_map/pack_kernel/pallas_call | solution.py:413
  2.3 0.1 collective-permute-start
  2.4 0.9 %lines_kernel.1 = (bf16[6,6,6,16,256]{4,3,2,1,0:T(8,128)(2,1)S(1)}, f32[2,6,16,16,256]{4,3,2,1,0:T(8,128)S(1)}) custom-call(bf16[18,128,256]{2,1,0:T(8,128)(2,1)S(1)} %get-tuple-element.32.vol_ref.refs_0_, bf16[128,128]{1,0:T(8,128)(2,1)S(1)} %get-tuple-element.33.lines_ref.refs_1_, f32[3,8,128]{2,1,0:T(8,128)S(1)} %get-tuple-element.38.mask_ref.refs_2_), custom_call_target="tpu_custom_call" | custom-call | flops 268435456 | tf_op jit(solution)/shard_map/lines_kernel/pallas_call | solution.py:413
  3.3 0.3 %collective-permute-done.side_ref = bf16[3,128,128]{2,1,0:T(8,128)(2,1)S(1)} collective-permute-done((bf16[3,128,128]{2,1,0:T(8,128)(2,1)S(1)}, bf16[3,128,128]{2,1,0:T(8,128)(2,1)S(1)}, u32[]{:S(2)}, u32[]{:S(2)}) %collective-permute-start) | collective-permute-done | bytes 98336 | tf_op jit(solution)/shard_map/ppermute | solution.py:457
  3.7 0.1 rows_kernel.1
  3.8 1.6 %collective-permute-start.1 = (bf16[208,256]{1,0:T(8,128)(2,1)S(1)}, bf16[208,256]{1,0:T(8,128)(2,1)S(1)}, u32[]{:S(2)}, u32[]{:S(2)}) collective-permute-start(bf16[208,256]{1,0:T(8,128)(2,1)S(1)} %get-tuple-element.51), channel_id=1, source_target_pairs={{0,2},{2,0},{4,6},{6,4},{8,10},{10,8},{12,14},{14,12},{1,3},{3,1},... | collective-permute-start | bytes 319496 | tf_op jit(solution)/shard_map/ppermute | solution.py:478
  5.4 3.0 %collective-permute-start.2 = (bf16[208,256]{1,0:T(8,128)(2,1)S(1)}, bf16[208,256]{1,0:T(8,128)(2,1)S(1)}, u32[]{:S(2)}, u32[]{:S(2)}) collective-permute-start(bf16[208,256]{1,0:T(8,128)(2,1)S(1)} %get-tuple-element.45.refs_3_), channel_id=1, source_target_pairs={{2,4},{6,8},{10,12},{4,2},{8,6},{12,10},{0,0},{14,14},{3,5},{7,9},... | collective-permute-start | bytes 319496 | tf_op jit(solution)/shard_map/ppermute | solution.py:491
  8.4 1.4 %even_lines_kernel.1 = (bf16[4,6,6,16,256]{4,3,2,1,0:T(8,128)(2,1)S(1)}, f32[2,6,16,16,256]{4,3,2,1,0:T(8,128)S(1)}, bf16[208,256]{1,0:T(8,128)(2,1)}) custom-call(bf16[18,128,256]{2,1,0:T(8,128)(2,1)S(1)} %get-tuple-element.32.vol_ref.refs_0_, ...), custom_call_target="tpu_custom_call", output_to_operand_aliasing={{1}: (4, {}), {0}: (5, {})} | custom-call | flops 268435456 | tf_op jit(solution)/shard_map/even_lines_kernel/pallas_call | solution.py:413
  9.8 3.9 %own_kernel.1 = (f32[2,6,16,16,256]{4,3,2,1,0:T(8,128)S(1)}, f32[16,128,256]{2,1,0:T(8,128)}, f32[16,128,256]{2,1,0:T(8,128)}, f32[16,128,256]{2,1,0:T(8,128)}, ...) custom-call(bf16[18,128,256]{2,1,0:T(8,128)(2,1)S(1)} %get-tuple-element.32.vol_ref., ...), custom_call_target="tpu_custom_call", output_to_operand_aliasing={{0}: (10, {})} | custom-call | flops 5368709120 | tf_op jit(solution)/shard_map/own_kernel/pallas_call | solution.py:413
  13.7 0.0 collective-permute-done.1.near_ref
  13.7 0.0 collective-permute-done.2.far_ref
  13.7 3.2 %ends_kernel.1 = (f32[16,128,256]{2,1,0:T(8,128)}, f32[16,128,256]{2,1,0:T(8,128)}, f32[16,128,256]{2,1,0:T(8,128)}) custom-call(f32[3,6,96,256]{3,2,1,0:T(8,128)S(1)} %get-tuple-element.50.done_ref, bf16[18,128,256]{2,1,0:T(8,128)(2,1)S(1)} %get-tuple-element.32.vol_ref.refs_0_, ...), custom_call_target="tpu_custom_call", output_to_operand_aliasing={{0}: (13, {}), {1}: (14, {}), {2}: (15, {})} | custom-call | flops 2147483648 | tf_op jit(solution)/shard_map/ends_kernel/pallas_call | solution.py:413
  (1 shorter events, 0.0 us)
Async XLA Ops:
  0.6 1.3 %copy-start = (bf16[18,128,256]{2,1,0:T(8,128)(2,1)S(1)}, bf16[18,128,256]{2,1,0:T(8,128)(2,1)}, u32[]{:S(2)}) copy-start(bf16[18,128,256]{2,1,0:T(8,128)(2,1)} %vol_ref.1) | copy-start | bytes 3538948
  2.3 1.4 %collective-permute-start = (bf16[3,128,128]{2,1,0:T(8,128)(2,1)S(1)}, bf16[3,128,128]{2,1,0:T(8,128)(2,1)S(1)}, u32[]{:S(2)}, u32[]{:S(2)}) collective-permute-start(bf16[3,128,128]{2,1,0:T(8,128)(2,1)S(1)} %get-tuple-element.37), channel_id=1, source_target_pairs={{0,1},{1,0},{2,3},{3,2},{4,5},{5,4},{6,7},{7,6},{8,9},{9,8},{10,11... | collective-permute-start | bytes 294920 | tf_op jit(solution)/shard_map/ppermute | solution.py:457
  3.8 9.9 %collective-permute-start.1 = (bf16[208,256]{1,0:T(8,128)(2,1)S(1)}, bf16[208,256]{1,0:T(8,128)(2,1)S(1)}, u32[]{:S(2)}, u32[]{:S(2)}) collective-permute-start(bf16[208,256]{1,0:T(8,128)(2,1)S(1)} %get-tuple-element.51), channel_id=1, source_target_pairs={{0,2},{2,0},{4,6},{6,4},{8,10},{10,8},{12,14},{14,12},{1,3},{3,1},... | collective-permute-start | bytes 319496 | tf_op jit(solution)/shard_map/ppermute | solution.py:478
  5.4 8.3 %collective-permute-start.2 = (bf16[208,256]{1,0:T(8,128)(2,1)S(1)}, bf16[208,256]{1,0:T(8,128)(2,1)S(1)}, u32[]{:S(2)}, u32[]{:S(2)}) collective-permute-start(bf16[208,256]{1,0:T(8,128)(2,1)S(1)} %get-tuple-element.45.refs_3_), channel_id=1, source_target_pairs={{2,4},{6,8},{10,12},{4,2},{8,6},{12,10},{0,0},{14,14},{3,5},{7,9},... | collective-permute-start | bytes 319496 | tf_op jit(solution)/shard_map/ppermute | solution.py:491

commit v23 on v22

--- a/solution.py
+++ b/solution.py
@@ -220,10 +220,13 @@
 
 
 def shared_lines_kernel(
-    parity, vol_ref, lines_ref, mask_ref, rows_ref, part_in_ref, *refs,
+    parity, vol_ref, lines_ref, mask_ref, part_in_ref, *refs,
 ):
-    inner_ref, part_ref, rows_out_ref, even_ref, odd_ref = refs[-5:]
-    rows_out_ref[...] = rows_ref[...]
+    if parity == 1:
+        rows_ref, inner_ref, part_ref, rows_out_ref, even_ref, odd_ref = refs
+        rows_out_ref[...] = rows_ref[...]
+    else:
+        shared_in_ref, inner_ref, part_ref, even_ref, odd_ref = refs
 
     @pl.when(lax.rem(lax.axis_index("il"), 2) == parity)
     def _():
@@ -478,7 +481,7 @@
     near_in = lax.ppermute(near, "il", [(i, i ^ 1) for i in range(il)])
     pairs = [(i, i + 1) for i in range(1, il - 1, 2)]
     shared_shape = ((2 * SHARED, chunks, 6, EDGE, cols), bf16)
-    operands = [vol, lines, mask, far, part]
+    operands = [vol, lines, mask, part, far]
     shared, part, far = call(
         "odd_lines_kernel",
         lambda *refs: shared_lines_kernel(1, *refs),
@@ -486,18 +489,18 @@
         moment_slots,
         operands,
         flops=work // 4,
-        aliases={4: 1},
+        aliases={3: 1},
     )
     far_in = lax.ppermute(far, "il", pairs + [(j, i) for i, j in pairs] + [(0, 0), (il - 1, il - 1)])
-    operands = [vol, lines, mask, far, part, shared]
-    shared, part, _ = call(
+    operands = [vol, lines, mask, part, shared]
+    shared, part = call(
         "even_lines_kernel",
         lambda *refs: shared_lines_kernel(0, *refs),
-        [shared_shape, partial, packed],
+        [shared_shape, partial],
         moment_slots,
         operands,
         flops=work // 4,
-        aliases={4: 1, 5: 0},
+        aliases={3: 1, 4: 0},
     )
 
     outs = [((count, rows, cols), f32)] * 3

time: 17.1 us -> 16.4 us (0.959)
  the two profiles are of different devices: /device:TPU:26 before, /device:TPU:18 now
where the time goes in v23:
time: 16.4 us; the launch traced here: 16.3 us
  Pallas kernels  10.1 us (62%)
  starting transfers between devices  4.65 us (28%)
  between operations  0.72 us (4%)
  local copies, waits for them, and re-layouts  0.48 us (3%)
  waiting for transfers between devices  0.35 us (2%)
    pallas_call x8, Pallas kernels, call(): pl.pallas_call(kernel, out_shape=tuple((jax.ShapeDtypeStruct(*out) for ou...  10.1 us
    ppermute x1, starting transfers between devices, body(): lax.ppermute(far, 'il', pairs + [(j, i) for i, j in pairs] + [(0, 0), (il...  2.99 us
    ppermute x1, starting transfers between devices, body(): near_in = lax.ppermute(near, 'il', [(i, i ^ 1) for i in range(il)])  1.58 us
    unnamed x2, local copies, waits for them, and re-layouts  0.48 us
    ppermute x1, waiting for transfers between devices, body(): side = lax.ppermute(send, 'xl', [(0, 1), (1, 0)])  0.35 us
  transfers between devices with their start and end apart: 3, of which 1 were waited for; matrix products, arithmetic and copies ran while one was open for 0% of the time, Pallas kernels for 34%

profile of v23, /device:TPU:18, one launch (start us, length us, event | category | flops | bytes accessed | tf_op | source)
XLA Modules:
  0.0 16.3 jit_solution(10629895070780341863)
XLA Ops:
  0.6 0.0 copy-start
  0.6 0.8 %tables_kernel.1 = (bf16[128,128]{1,0:T(8,128)(2,1)S(1)}, bf16[128,128]{1,0:T(8,128)(2,1)S(1)}, bf16[256,256]{1,0:T(8,128)(2,1)S(1)}, bf16[256,256]{1,0:T(8,128)...) custom-call(), custom_call_target="tpu_custom_call" | custom-call | flops 1073741824 | tf_op jit(solution)/shard_map/tables_kernel/pallas_call | solution.py:416
  1.4 0.5 %copy-done = bf16[18,128,256]{2,1,0:T(8,128)(2,1)S(1)} copy-done((bf16[18,128,256]{2,1,0:T(8,128)(2,1)S(1)}, bf16[18,128,256]{2,1,0:T(8,128)(2,1)}, u32[]{:S(2)}) %copy-start) | copy-done | bytes 1179672
  1.9 0.4 %pack_kernel.1 = (bf16[18,128,256]{2,1,0:T(8,128)(2,1)S(1)}, bf16[3,128,128]{2,1,0:T(8,128)(2,1)S(1)}, bf16[3,128,128]{2,1,0:T(8,128)(2,1)S(1)}) custom-call(bf16[18,128,256]{2,1,0:T(8,128)(2,1)S(1)} %copy-done, bf16[1024,256]{1,0:T(8,128)(2,1)S(1)} %get-tuple-element.31.pick_ref), custom_call_target="tpu_custom_call" | custom-call | tf_op jit(solution)/shard_map/pack_kernel/pallas_call | solution.py:416
  2.3 0.1 collective-permute-start
  2.4 0.9 %lines_kernel.1 = (bf16[6,6,6,16,256]{4,3,2,1,0:T(8,128)(2,1)S(1)}, f32[2,6,16,16,256]{4,3,2,1,0:T(8,128)S(1)}) custom-call(bf16[18,128,256]{2,1,0:T(8,128)(2,1)S(1)} %get-tuple-element.32.vol_ref.refs_0_, bf16[128,128]{1,0:T(8,128)(2,1)S(1)} %get-tuple-element.33.lines_ref.refs_1_, f32[3,8,128]{2,1,0:T(8,128)S(1)} %get-tuple-element.38.mask_ref.refs_2_), custom_call_target="tpu_custom_call" | custom-call | flops 268435456 | tf_op jit(solution)/shard_map/lines_kernel/pallas_call | solution.py:416
  3.3 0.3 %collective-permute-done.side_ref = bf16[3,128,128]{2,1,0:T(8,128)(2,1)S(1)} collective-permute-done((bf16[3,128,128]{2,1,0:T(8,128)(2,1)S(1)}, bf16[3,128,128]{2,1,0:T(8,128)(2,1)S(1)}, u32[]{:S(2)}, u32[]{:S(2)}) %collective-permute-start) | collective-permute-done | bytes 98336 | tf_op jit(solution)/shard_map/ppermute | solution.py:460
  3.7 0.2 rows_kernel.1
  3.8 1.6 %collective-permute-start.1 = (bf16[208,256]{1,0:T(8,128)(2,1)S(1)}, bf16[208,256]{1,0:T(8,128)(2,1)S(1)}, u32[]{:S(2)}, u32[]{:S(2)}) collective-permute-start(bf16[208,256]{1,0:T(8,128)(2,1)S(1)} %get-tuple-element.50), channel_id=1, source_target_pairs={{0,2},{2,0},{4,6},{6,4},{8,10},{10,8},{12,14},{14,12},{1,3},{3,1},... | collective-permute-start | bytes 319496 | tf_op jit(solution)/shard_map/ppermute | solution.py:481
  5.4 3.0 %collective-permute-start.2 = (bf16[208,256]{1,0:T(8,128)(2,1)S(1)}, bf16[208,256]{1,0:T(8,128)(2,1)S(1)}, u32[]{:S(2)}, u32[]{:S(2)}) collective-permute-start(bf16[208,256]{1,0:T(8,128)(2,1)S(1)} %get-tuple-element.51), channel_id=1, source_target_pairs={{2,4},{6,8},{10,12},{4,2},{8,6},{12,10},{0,0},{14,14},{3,5},{7,9},... | collective-permute-start | bytes 319496 | tf_op jit(solution)/shard_map/ppermute | solution.py:494
  8.4 0.7 %even_lines_kernel.1 = (bf16[4,6,6,16,256]{4,3,2,1,0:T(8,128)(2,1)S(1)}, f32[2,6,16,16,256]{4,3,2,1,0:T(8,128)S(1)}) custom-call(bf16[18,128,256]{2,1,0:T(8,128)(2,1)S(1)} %get-tuple-element.32.vol_ref.refs_0_, bf16[128,128]{1,0:T(8,128)(2,1)S(1)} %get-tuple-element.33.lines_ref.refs_1_, ...), custom_call_target="tpu_custom_call", output_to_operand_aliasing={{1}: (3, {}), {0}: (4, {})} | custom-call | flops 268435456 | tf_op jit(solution)/shard_map/even_lines_kernel/pallas_call | solution.py:416
  9.1 3.9 %own_kernel.1 = (f32[2,6,16,16,256]{4,3,2,1,0:T(8,128)S(1)}, f32[16,128,256]{2,1,0:T(8,128)}, f32[16,128,256]{2,1,0:T(8,128)}, f32[16,128,256]{2,1,0:T(8,128)}, ...) custom-call(bf16[18,128,256]{2,1,0:T(8,128)(2,1)S(1)} %get-tuple-element.32.vol_ref., ...), custom_call_target="tpu_custom_call", output_to_operand_aliasing={{0}: (10, {})} | custom-call | flops 5368709120 | tf_op jit(solution)/shard_map/own_kernel/pallas_call | solution.py:416
  13.1 0.0 collective-permute-done.1.near_ref
  13.1 0.0 collective-permute-done.2.far_ref
  13.1 3.2 %ends_kernel.1 = (f32[16,128,256]{2,1,0:T(8,128)}, f32[16,128,256]{2,1,0:T(8,128)}, f32[16,128,256]{2,1,0:T(8,128)}) custom-call(f32[3,6,96,256]{3,2,1,0:T(8,128)S(1)} %get-tuple-element.49.done_ref, bf16[18,128,256]{2,1,0:T(8,128)(2,1)S(1)} %get-tuple-element.32.vol_ref.refs_0_, ...), custom_call_target="tpu_custom_call", output_to_operand_aliasing={{0}: (13, {}), {1}: (14, {}), {2}: (15, {})} | custom-call | flops 2147483648 | tf_op jit(solution)/shard_map/ends_kernel/pallas_call | solution.py:416
  (1 shorter events, 0.0 us)
Async XLA Ops:
  0.6 1.3 %copy-start = (bf16[18,128,256]{2,1,0:T(8,128)(2,1)S(1)}, bf16[18,128,256]{2,1,0:T(8,128)(2,1)}, u32[]{:S(2)}) copy-start(bf16[18,128,256]{2,1,0:T(8,128)(2,1)} %vol_ref.1) | copy-start | bytes 3538948
  2.3 1.4 %collective-permute-start = (bf16[3,128,128]{2,1,0:T(8,128)(2,1)S(1)}, bf16[3,128,128]{2,1,0:T(8,128)(2,1)S(1)}, u32[]{:S(2)}, u32[]{:S(2)}) collective-permute-start(bf16[3,128,128]{2,1,0:T(8,128)(2,1)S(1)} %get-tuple-element.37), channel_id=1, source_target_pairs={{0,1},{1,0},{2,3},{3,2},{4,5},{5,4},{6,7},{7,6},{8,9},{9,8},{10,11... | collective-permute-start | bytes 294920 | tf_op jit(solution)/shard_map/ppermute | solution.py:460
  3.8 9.3 %collective-permute-start.1 = (bf16[208,256]{1,0:T(8,128)(2,1)S(1)}, bf16[208,256]{1,0:T(8,128)(2,1)S(1)}, u32[]{:S(2)}, u32[]{:S(2)}) collective-permute-start(bf16[208,256]{1,0:T(8,128)(2,1)S(1)} %get-tuple-element.50), channel_id=1, source_target_pairs={{0,2},{2,0},{4,6},{6,4},{8,10},{10,8},{12,14},{14,12},{1,3},{3,1},... | collective-permute-start | bytes 319496 | tf_op jit(solution)/shard_map/ppermute | solution.py:481
  5.4 7.7 %collective-permute-start.2 = (bf16[208,256]{1,0:T(8,128)(2,1)S(1)}, bf16[208,256]{1,0:T(8,128)(2,1)S(1)}, u32[]{:S(2)}, u32[]{:S(2)}) collective-permute-start(bf16[208,256]{1,0:T(8,128)(2,1)S(1)} %get-tuple-element.51), channel_id=1, source_target_pairs={{2,4},{6,8},{10,12},{4,2},{8,6},{12,10},{0,0},{14,14},{3,5},{7,9},... | collective-permute-start | bytes 319496 | tf_op jit(solution)/shard_map/ppermute | solution.py:494

commit v24 on v23

--- a/solution.py
+++ b/solution.py
@@ -15,7 +15,7 @@
 EDGE = 16
 OWN = 2
 TINY = float(np.finfo(np.float32).tiny)
-HEAD = 3
+HEAD = 4
 AHEAD = 3
 LATER = 6
 SHARED = 2

time: 16.4 us -> 16.6 us (1.012)
  waiting for transfers between devices: 0.35 us -> 0.56 us
    ppermute x1, waiting for transfers between devices: 0.01 us -> 0.47 us  [body(): lax.ppermute(far, 'il', pairs + [(j, i) for i, j in pairs] + [(0, 0), (il...]
    ppermute x1, waiting for transfers between devices: 0.35 us -> 0.09 us  [body(): side = lax.ppermute(send, 'xl', [(0, 1), (1, 0)])]
  transfers between devices with their start and end apart: 3 -> 3, of which waited for: 1 -> 2; matrix products, arithmetic and copies ran while one was open for 0% -> 0% of each run, Pallas kernels for 34% -> 34%
where the time goes in v24:
time: 16.6 us; the launch traced here: 16.4 us
  Pallas kernels  10 us (60%)
  starting transfers between devices  4.65 us (28%)
  between operations  0.71 us (4%)
  waiting for transfers between devices  0.56 us (3%)
  local copies, waits for them, and re-layouts  0.48 us (3%)
    pallas_call x8, Pallas kernels, call(): pl.pallas_call(kernel, out_shape=tuple((jax.ShapeDtypeStruct(*out) for ou...  10 us
    ppermute x1, starting transfers between devices, body(): lax.ppermute(far, 'il', pairs + [(j, i) for i, j in pairs] + [(0, 0), (il...  2.99 us
    ppermute x1, starting transfers between devices, body(): near_in = lax.ppermute(near, 'il', [(i, i ^ 1) for i in range(il)])  1.58 us
    unnamed x2, local copies, waits for them, and re-layouts  0.48 us
    ppermute x1, waiting for transfers between devices, body(): lax.ppermute(far, 'il', pairs + [(j, i) for i, j in pairs] + [(0, 0), (il...  0.47 us
  transfers between devices with their start and end apart: 3, of which 2 were waited for; matrix products, arithmetic and copies ran while one was open for 0% of the time, Pallas kernels for 34%

profile of v24, /device:TPU:18, one launch (start us, length us, event | category | flops | bytes accessed | tf_op | source)
XLA Modules:
  0.0 16.4 jit_solution(14644227532152502149)
XLA Ops:
  0.6 0.0 copy-start
  0.6 0.8 %tables_kernel.1 = (bf16[128,128]{1,0:T(8,128)(2,1)S(1)}, bf16[128,128]{1,0:T(8,128)(2,1)S(1)}, bf16[256,256]{1,0:T(8,128)(2,1)S(1)}, bf16[256,256]{1,0:T(8,128)...) custom-call(), custom_call_target="tpu_custom_call" | custom-call | flops 1073741824 | tf_op jit(solution)/shard_map/tables_kernel/pallas_call | solution.py:416
  1.4 0.5 %copy-done = bf16[18,128,256]{2,1,0:T(8,128)(2,1)S(1)} copy-done((bf16[18,128,256]{2,1,0:T(8,128)(2,1)S(1)}, bf16[18,128,256]{2,1,0:T(8,128)(2,1)}, u32[]{:S(2)}) %copy-start) | copy-done | bytes 1179672
  1.9 0.4 %pack_kernel.1 = (bf16[18,128,256]{2,1,0:T(8,128)(2,1)S(1)}, bf16[3,128,128]{2,1,0:T(8,128)(2,1)S(1)}, bf16[3,128,128]{2,1,0:T(8,128)(2,1)S(1)}) custom-call(bf16[18,128,256]{2,1,0:T(8,128)(2,1)S(1)} %copy-done, bf16[1024,256]{1,0:T(8,128)(2,1)S(1)} %get-tuple-element.31.pick_ref), custom_call_target="tpu_custom_call" | custom-call | tf_op jit(solution)/shard_map/pack_kernel/pallas_call | solution.py:416
  2.3 0.1 collective-permute-start
  2.4 1.2 %lines_kernel.1 = (bf16[8,6,6,16,256]{4,3,2,1,0:T(8,128)(2,1)S(1)}, f32[2,6,16,16,256]{4,3,2,1,0:T(8,128)S(1)}) custom-call(bf16[18,128,256]{2,1,0:T(8,128)(2,1)S(1)} %get-tuple-element.32.vol_ref.refs_0_, bf16[128,128]{1,0:T(8,128)(2,1)S(1)} %get-tuple-element.33.lines_ref.refs_1_, f32[3,8,128]{2,1,0:T(8,128)S(1)} %get-tuple-element.38.mask_ref.refs_2_), custom_call_target="tpu_custom_call" | custom-call | flops 268435456 | tf_op jit(solution)/shard_map/lines_kernel/pallas_call | solution.py:416
  3.6 0.1 collective-permute-done.side_ref
  3.7 0.2 rows_kernel.1
  3.8 1.6 %collective-permute-start.1 = (bf16[208,256]{1,0:T(8,128)(2,1)S(1)}, bf16[208,256]{1,0:T(8,128)(2,1)S(1)}, u32[]{:S(2)}, u32[]{:S(2)}) collective-permute-start(bf16[208,256]{1,0:T(8,128)(2,1)S(1)} %get-tuple-element.50), channel_id=1, source_target_pairs={{0,2},{2,0},{4,6},{6,4},{8,10},{10,8},{12,14},{14,12},{1,3},{3,1},... | collective-permute-start | bytes 319496 | tf_op jit(solution)/shard_map/ppermute | solution.py:481
  5.4 3.0 %collective-permute-start.2 = (bf16[208,256]{1,0:T(8,128)(2,1)S(1)}, bf16[208,256]{1,0:T(8,128)(2,1)S(1)}, u32[]{:S(2)}, u32[]{:S(2)}) collective-permute-start(bf16[208,256]{1,0:T(8,128)(2,1)S(1)} %get-tuple-element.51), channel_id=1, source_target_pairs={{2,4},{6,8},{10,12},{4,2},{8,6},{12,10},{0,0},{14,14},{3,5},{7,9},... | collective-permute-start | bytes 319496 | tf_op jit(solution)/shard_map/ppermute | solution.py:494
  8.4 0.7 %even_lines_kernel.1 = (bf16[4,6,6,16,256]{4,3,2,1,0:T(8,128)(2,1)S(1)}, f32[2,6,16,16,256]{4,3,2,1,0:T(8,128)S(1)}) custom-call(bf16[18,128,256]{2,1,0:T(8,128)(2,1)S(1)} %get-tuple-element.32.vol_ref.refs_0_, bf16[128,128]{1,0:T(8,128)(2,1)S(1)} %get-tuple-element.33.lines_ref.refs_1_, ...), custom_call_target="tpu_custom_call", output_to_operand_aliasing={{1}: (3, {}), {0}: (4, {})} | custom-call | flops 268435456 | tf_op jit(solution)/shard_map/even_lines_kernel/pallas_call | solution.py:416
  9.1 3.6 %own_kernel.1 = (f32[2,6,16,16,256]{4,3,2,1,0:T(8,128)S(1)}, f32[16,128,256]{2,1,0:T(8,128)}, f32[16,128,256]{2,1,0:T(8,128)}, f32[16,128,256]{2,1,0:T(8,128)}, ...) custom-call(bf16[18,128,256]{2,1,0:T(8,128)(2,1)S(1)} %get-tuple-element.32.vol_ref., ...), custom_call_target="tpu_custom_call", output_to_operand_aliasing={{0}: (10, {})} | custom-call | flops 5368709120 | tf_op jit(solution)/shard_map/own_kernel/pallas_call | solution.py:416
  12.8 0.0 collective-permute-done.1.near_ref
  12.8 0.5 %collective-permute-done.2.far_ref = bf16[208,256]{1,0:T(8,128)(2,1)S(1)} collective-permute-done((bf16[208,256]{1,0:T(8,128)(2,1)S(1)}, bf16[208,256]{1,0:T(8,128)(2,1)S(1)}, u32[]{:S(2)}, u32[]{:S(2)}) %collective-permute-start.2) | collective-permute-done | bytes 106528 | tf_op jit(solution)/shard_map/ppermute | solution.py:494
  13.2 3.2 %ends_kernel.1 = (f32[16,128,256]{2,1,0:T(8,128)}, f32[16,128,256]{2,1,0:T(8,128)}, f32[16,128,256]{2,1,0:T(8,128)}) custom-call(f32[3,6,96,256]{3,2,1,0:T(8,128)S(1)} %get-tuple-element.49.done_ref, bf16[18,128,256]{2,1,0:T(8,128)(2,1)S(1)} %get-tuple-element.32.vol_ref.refs_0_, ...), custom_call_target="tpu_custom_call", output_to_operand_aliasing={{0}: (13, {}), {1}: (14, {}), {2}: (15, {})} | custom-call | flops 2147483648 | tf_op jit(solution)/shard_map/ends_kernel/pallas_call | solution.py:416
  (1 shorter events, 0.0 us)
Async XLA Ops:
  0.6 1.3 %copy-start = (bf16[18,128,256]{2,1,0:T(8,128)(2,1)S(1)}, bf16[18,128,256]{2,1,0:T(8,128)(2,1)}, u32[]{:S(2)}) copy-start(bf16[18,128,256]{2,1,0:T(8,128)(2,1)} %vol_ref.1) | copy-start | bytes 3538948
  2.3 1.4 %collective-permute-start = (bf16[3,128,128]{2,1,0:T(8,128)(2,1)S(1)}, bf16[3,128,128]{2,1,0:T(8,128)(2,1)S(1)}, u32[]{:S(2)}, u32[]{:S(2)}) collective-permute-start(bf16[3,128,128]{2,1,0:T(8,128)(2,1)S(1)} %get-tuple-element.37), channel_id=1, source_target_pairs={{0,1},{1,0},{2,3},{3,2},{4,5},{5,4},{6,7},{7,6},{8,9},{9,8},{10,11... | collective-permute-start | bytes 294920 | tf_op jit(solution)/shard_map/ppermute | solution.py:460
  3.8 8.9 %collective-permute-start.1 = (bf16[208,256]{1,0:T(8,128)(2,1)S(1)}, bf16[208,256]{1,0:T(8,128)(2,1)S(1)}, u32[]{:S(2)}, u32[]{:S(2)}) collective-permute-start(bf16[208,256]{1,0:T(8,128)(2,1)S(1)} %get-tuple-element.50), channel_id=1, source_target_pairs={{0,2},{2,0},{4,6},{6,4},{8,10},{10,8},{12,14},{14,12},{1,3},{3,1},... | collective-permute-start | bytes 319496 | tf_op jit(solution)/shard_map/ppermute | solution.py:481
  5.4 7.8 %collective-permute-start.2 = (bf16[208,256]{1,0:T(8,128)(2,1)S(1)}, bf16[208,256]{1,0:T(8,128)(2,1)S(1)}, u32[]{:S(2)}, u32[]{:S(2)}) collective-permute-start(bf16[208,256]{1,0:T(8,128)(2,1)S(1)} %get-tuple-element.51), channel_id=1, source_target_pairs={{2,4},{6,8},{10,12},{4,2},{8,6},{12,10},{0,0},{14,14},{3,5},{7,9},... | collective-permute-start | bytes 319496 | tf_op jit(solution)/shard_map/ppermute | solution.py:494
